TPU v7x, 32 devices: a whole 2x2x4 slice. The times are simulated.
32 devices in a mesh: groups: 2 (over y), clus: 4 (over z), sub: 2 (over x), rhs: 2 (over core).
Axes of the slice: x: 2, y: 2, z: 4, core: 2. Of those that a mesh axis runs over, the one named last changes fastest.
Arguments:
- positions: bfloat16 [128, 3, 512], P(('groups', 'clus'), None, 'sub'), parts along dimension 0, may hold values from -1 to 1
- areas: bfloat16 [128, 512], P(('groups', 'clus'), 'sub'), parts along dimension 0, may hold values from 0.5 to 2
- density: bfloat16 [128, 64, 512], P(('groups', 'clus'), 'rhs', 'sub'), parts along dimension 0, may hold values from -6 to 6
- cotangent: bfloat16 [128, 64, 512], P(('groups', 'clus'), 'rhs', 'sub'), parts along dimension 0, may hold values from -0.59765625 to 0.59765625
- matching: int32 [5, 128], P(None, 'groups'), parts along dimension 1, may hold values from 0 to 63, as said below
- connect: int32 [128, 4, 512], P(('groups', 'clus'), None, 'sub'), parts along dimension 0, may hold values from 0 to 32767, as said below
Outputs:
- potential: bfloat16 [128, 64, 512], P(('groups', 'clus'), 'rhs', 'sub'), parts along dimension 0
- node_grad: float32 [3, 65536], P(None, ('groups', 'clus', 'sub')), parts along dimension 1
There are 2 independent parts, one for each index of `groups`. A program takes and returns all parts, laid end to end along the dimension named above; each array names one. Nothing has to cross between parts.
Inputs may be any that keep to these rules, and one draw needn't show every extreme that they name: matching[r, c] is the cluster paired with cluster c in round r: the pairing is mutual, and never pairs two clusters of the same index of clus (c // 16). In each round, of the 16 clusters of one index of clus at most 6 are paired with clusters of any one other index, and every index reaches 6 with some other index. `connect`: the corners of panel a of cluster c are (c * 512 + a + t + k) mod 32768 for k = 0, 1, 32, 33 in this order, with one whole number t of -8 to 8 for each panel.
All inputs are finite; a program needn't handle non-finite values.
Results may differ from a plain program's by a relative error of at most 0.0051.
Values may be sent and summed in bfloat16 or wider, within the bound.
No kernel may reach another device: no remote copies, remote signals or barrier semaphores. Data moves between devices by JAX's collectives and lax.ppermute only.
A program may use at most 64 MiB of HBM per device.

v0:
```python
import jax
import jax.numpy as jnp
from jax import lax
from jax.sharding import PartitionSpec as P

CP = 512
ROUNDS = 5


core_radius = 0.25
edge_reach = 64
jitter_reach = 8
corner_steps = (0, 1, 32, 33)


def from_behind(value, axis, steps):
    count = lax.axis_size(axis)
    pairs = [(source, (source + steps) % count) for source in range(count)]
    return lax.ppermute(value, axis, pairs)


def pair_terms(items):
    own_pos, own_area, own_dens, own_cot, partner = items
    here = own_pos.astype(jnp.float32)
    there = partner[:, 0:3].astype(jnp.float32)
    distance_sq = jnp.zeros((here.shape[0], here.shape[2], there.shape[2]), jnp.float32)
    for coord in range(3):
        distance_sq = distance_sq + (here[:, coord, :, None] - there[:, coord, None, :]) ** 2
    inverse = 1.0 / jnp.sqrt(distance_sq + core_radius * core_radius)
    factor = CP ** (-0.5)
    weight_there = factor * partner[:, 3].astype(jnp.float32)
    kernel = (weight_there[:, None, :] * inverse).astype(jnp.bfloat16)
    width = own_dens.shape[1]
    mate_dens = partner[:, 4 : 4 + width]
    potential_term = jnp.einsum(
        "gcb,gab->gca", mate_dens, kernel, preferred_element_type=jnp.float32
    )
    inv_cube = inverse * inverse * inverse
    product = jnp.einsum("gca,gcb->gab", own_cot, mate_dens, preferred_element_type=jnp.float32)
    weighted = weight_there[:, None, :] * inv_cube * product
    augmented = jnp.concatenate(
        [there, jnp.ones((there.shape[0], 1, there.shape[2]), jnp.float32)], axis=1
    )
    target_sums = jnp.einsum("gkb,gab->gka", augmented, weighted, precision=lax.Precision.HIGHEST)
    gradient = target_sums[:, :3] - here * target_sums[:, 3:4]
    mate_cot = partner[:, 4 + width :]
    product_two = jnp.einsum("gca,gcb->gab", own_dens, mate_cot, preferred_element_type=jnp.float32)
    weight_here = factor * own_area.astype(jnp.float32)
    weighted_two = weight_here[:, :, None] * inv_cube * product_two
    source_sums = jnp.einsum(
        "gkb,gab->gka", augmented, weighted_two, precision=lax.Precision.HIGHEST
    )
    gradient = gradient + (source_sums[:, :3] - here * source_sums[:, 3:4])
    return (potential_term, gradient)


def paired(array):
    return array.reshape((array.shape[0] // 2, 2) + array.shape[1:])


def unpaired(array):
    return array.reshape((array.shape[0] * 2,) + array.shape[2:])


def on_device(positions, areas, density, cotangent, matching, connect):
    clus_count = lax.axis_size("clus")
    sub_count = lax.axis_size("sub")
    device = lax.axis_index("clus")
    sub_place = lax.axis_index("sub")
    per_device = positions.shape[0]
    row_count = positions.shape[2]
    capacity = 2 * ((per_device // 2 + clus_count - 2) // (clus_count - 1))
    payload = jnp.concatenate([positions, areas[:, None, :], density, cotangent], axis=1)
    slot_shape = payload.shape[1:]
    local_index = jnp.arange(per_device, dtype=jnp.int32)
    earlier = local_index[None, :] < local_index[:, None]
    potential_sum = jnp.zeros(density.shape, jnp.float32)
    panel_grad = jnp.zeros((per_device, 3, row_count), jnp.float32)
    for round_idx in range(ROUNDS):
        pairing = matching[round_idx].reshape(clus_count, per_device)
        partners = lax.dynamic_index_in_dim(pairing, device, 0, keepdims=False)
        target_dev = partners // per_device
        send_slot = jnp.sum(
            ((target_dev[None, :] == target_dev[:, None]) & earlier).astype(jnp.int32), axis=1
        )
        source_rows = pairing[target_dev]
        position_in = partners % per_device
        preceding = local_index[None, :] < position_in[:, None]
        recv_slot = jnp.sum(
            ((source_rows // per_device == device) & preceding).astype(jnp.int32), axis=1
        )
        outbox = jnp.zeros((clus_count * capacity,) + slot_shape, jnp.bfloat16)
        outbox = outbox.at[target_dev * capacity + send_slot].set(payload)
        received = lax.all_to_all(
            outbox.reshape((clus_count, capacity) + slot_shape),
            "clus",
            split_axis=0,
            concat_axis=0,
            tiled=True,
        )
        arrived = received.reshape((clus_count * capacity,) + slot_shape)[
            target_dev * capacity + recv_slot
        ]
        partner = lax.all_gather(arrived, "sub", axis=2, tiled=True)
        results = lax.map(
            pair_terms,
            (paired(positions), paired(areas), paired(density), paired(cotangent), paired(partner)),
        )
        potential_sum = potential_sum + unpaired(results[0])
        panel_grad = panel_grad + unpaired(results[1])
    potential = potential_sum.astype(jnp.bfloat16)
    grad_total = lax.psum(panel_grad, "rhs")
    full_panels = row_count * sub_count
    nodes_total = per_device * clus_count * full_panels
    span = per_device * full_panels
    cluster_first = (device * per_device + local_index) * full_panels
    panel_first = sub_place * row_count + jnp.arange(row_count, dtype=jnp.int32)
    base_ids = cluster_first[:, None] + panel_first[None, :]
    jitter = (connect[:, 0, :] - base_ids + jitter_reach) % nodes_total - jitter_reach
    quarter = jnp.transpose(0.25 * grad_total, (1, 0, 2))
    dense_terms = jnp.zeros((3, per_device, full_panels), jnp.float32)
    dense_terms = lax.dynamic_update_slice(dense_terms, quarter, (0, 0, sub_place * row_count))
    dense_jitter = jnp.full((per_device, full_panels), 4 * jitter_reach, jnp.int32)
    dense_jitter = lax.dynamic_update_slice(dense_jitter, jitter, (0, sub_place * row_count))
    flat_terms = dense_terms.reshape(3, span)
    flat_jitter = dense_jitter.reshape(1, span)
    spread = jnp.zeros((3, span + 2 * jitter_reach), jnp.float32)
    for offset in range(-jitter_reach, jitter_reach + 1):
        masked = jnp.where(flat_jitter == offset, flat_terms, 0.0)
        start = offset + jitter_reach
        spread = spread.at[:, start : start + span].add(masked)
    window_terms = jnp.zeros((3, span + 2 * edge_reach), jnp.float32)
    for step in corner_steps:
        start = edge_reach - jitter_reach + step
        window_terms = window_terms.at[:, start : start + span + 2 * jitter_reach].add(spread)
    lower_rim = window_terms[:, :edge_reach]
    upper_rim = window_terms[:, edge_reach + span :]
    inner = window_terms[:, edge_reach : edge_reach + span]
    from_below = from_behind(upper_rim, "clus", 1)
    from_above = from_behind(lower_rim, "clus", -1)
    inner = inner.at[:, :edge_reach].add(from_below)
    inner = inner.at[:, span - edge_reach :].add(from_above)
    node_grad = lax.psum_scatter(inner, "sub", scatter_dimension=1, tiled=True)
    return (potential, node_grad)


def solution(mesh):
    placed = (
        P(("groups", "clus"), None, "sub"),
        P(("groups", "clus"), "sub"),
        P(("groups", "clus"), "rhs", "sub"),
        P(("groups", "clus"), "rhs", "sub"),
        P(None, "groups"),
        P(("groups", "clus"), None, "sub"),
    )
    return jax.shard_map(
        on_device,
        mesh=mesh,
        in_specs=placed,
        out_specs=(P(("groups", "clus"), "rhs", "sub"), P(None, ("groups", "clus", "sub"))),
        check_vma=False,
    )
```

profile of v0, /device:TPU:0, one launch (start us, length us, event | category | flops | bytes accessed | tf_op | source)
XLA Modules:
  0.0 486.3 jit_solution(12667505658234739018)
XLA Ops:
  10.5 1.3 pad_maximum_fusion
  11.7 1.0 broadcast.1700.clone.3
  12.8 2.6 scatter_fusion
  15.4 6.3 %all-to-all-start = ((bf16[4,6,68,256]{3,2,1,0:T(8,128)(2,1)}), bf16[4,6,68,256]{3,2,1,0:T(8,128)(2,1)S(1)}, u32[]{:S(2)}, u32[]{:S(2)}) async-start(bf16[4,6,68,256]{3,2,1,0:T(8,128)(2,1)} %bitcast.46), calls=%async_computation | async-start | bytes 1769472 | tf_op jit(solution)/shard_map/all_to_all | solution.py:94
  23.1 1.0 broadcast.1700.clone.2
  24.0 2.6 scatter_fusion.2
  26.7 17.2 %all-to-all-done = bf16[4,6,68,256]{3,2,1,0:T(8,128)(2,1)S(1)} async-done(((bf16[4,6,68,256]{3,2,1,0:T(8,128)(2,1)}), bf16[4,6,68,256]{3,2,1,0:T(8,128)(2,1)S(1)}, u32[]{:S(2)}, u32[]{:S(2)}) %all-to-all-start) | async-done | bytes 835616 | tf_op jit(solution)/shard_map/all_to_all | solution.py:94
  43.9 3.5 all-to-all-start.2
  47.6 1.4 gather_fusion.1
  49.9 1.0 broadcast.1700.clone.1
  50.9 2.6 scatter_fusion.3
  53.6 15.5 %all-to-all-done.2 = bf16[4,6,68,256]{3,2,1,0:T(8,128)(2,1)S(1)} async-done(((bf16[4,6,68,256]{3,2,1,0:T(8,128)(2,1)}), bf16[4,6,68,256]{3,2,1,0:T(8,128)(2,1)S(1)}, u32[]{:S(2)}, u32[]{:S(2)}) %all-to-all-start.2) | async-done | bytes 835616 | tf_op jit(solution)/shard_map/all_to_all | solution.py:94
  69.1 3.5 all-to-all-start.3
  72.7 1.4 gather_fusion.5
  75.1 1.0 broadcast.1700.clone
  76.1 2.6 scatter_fusion.4
  78.7 15.6 %all-to-all-done.3 = bf16[4,6,68,256]{3,2,1,0:T(8,128)(2,1)S(1)} async-done(((bf16[4,6,68,256]{3,2,1,0:T(8,128)(2,1)}), bf16[4,6,68,256]{3,2,1,0:T(8,128)(2,1)S(1)}, u32[]{:S(2)}, u32[]{:S(2)}) %all-to-all-start.3) | async-done | bytes 835616 | tf_op jit(solution)/shard_map/all_to_all | solution.py:94
  94.3 3.5 all-to-all-start.4
  97.9 1.4 gather_fusion.7
  100.3 1.0 broadcast.1700.clone.4
  101.3 2.6 scatter_fusion.1
  104.0 15.5 %all-to-all-done.4 = bf16[4,6,68,256]{3,2,1,0:T(8,128)(2,1)S(1)} async-done(((bf16[4,6,68,256]{3,2,1,0:T(8,128)(2,1)}), bf16[4,6,68,256]{3,2,1,0:T(8,128)(2,1)S(1)}, u32[]{:S(2)}, u32[]{:S(2)}) %all-to-all-start.4) | async-done | bytes 835616 | tf_op jit(solution)/shard_map/all_to_all | solution.py:94
  119.5 3.5 all-to-all-start.1
  123.1 1.4 gather_fusion.9
  146.7 1.5 gather_fusion.3
  148.5 43.9 %while.83 = (s32[]{:T(128)}, f32[8,2,32,256]{3,2,1,0:T(8,128)S(1)}, f32[8,2,3,256]{3,2,1,0:T(4,128)S(1)}, bf16[8,2,68,512]{3,2,1,0:T(8,128)(2,1)}, bf16[8,2,3,25...) while((s32[]{:T(128)}, f32[8,2,32,256]{3,2,1,0:T(8,128)S(1)}, ...), condition=%wide.region_4.5_spmd, body=%wide.region_3.4_spmd.sunk | while | flops 85213696 | bytes 5075073 | solution.py:105
  151.3 1.0 fusion.310
  153.0 1.0 fusion.309
  162.2 1.0 fusion.310
  191.4 1.0 fusion.309
  192.5 43.9 %while.85 = (s32[]{:T(128)}, f32[8,2,32,256]{3,2,1,0:T(8,128)S(1)}, f32[8,2,3,256]{3,2,1,0:T(4,128)S(1)}, bf16[8,2,68,512]{3,2,1,0:T(8,128)(2,1)}, bf16[8,2,3,25...) while((s32[]{:T(128)}, f32[8,2,32,256]{3,2,1,0:T(8,128)S(1)}, ...), condition=%wide.region_14.15_spmd, body=%wide.region_13.14_spmd.sunk | while | flops 85213696 | bytes 5075073 | solution.py:105
  195.2 1.0 fusion.342
  200.7 1.0 fusion.342
  202.5 1.0 fusion.341
  206.2 1.0 fusion.342
  236.5 43.9 %while.86 = (s32[]{:T(128)}, f32[8,2,32,256]{3,2,1,0:T(8,128)S(1)}, f32[8,2,3,256]{3,2,1,0:T(4,128)S(1)}, bf16[8,2,68,512]{3,2,1,0:T(8,128)(2,1)}, bf16[8,2,3,25...) while((s32[]{:T(128)}, f32[8,2,32,256]{3,2,1,0:T(8,128)S(1)}, ...), condition=%wide.region_19.20_spmd, body=%wide.region_18.19_spmd.sunk | while | flops 85213696 | bytes 5075073 | solution.py:105
  280.4 43.9 %while.87 = (s32[]{:T(128)}, f32[8,2,32,256]{3,2,1,0:T(8,128)S(1)}, f32[8,2,3,256]{3,2,1,0:T(4,128)S(1)}, bf16[8,2,68,512]{3,2,1,0:T(8,128)(2,1)}, bf16[8,2,3,25...) while((s32[]{:T(128)}, f32[8,2,32,256]{3,2,1,0:T(8,128)S(1)}, ...), condition=%wide.region_24.25_spmd, body=%wide.region_23.24_spmd.sunk | while | flops 85213696 | bytes 5075073 | solution.py:105
  324.4 43.9 %while.84 = (s32[]{:T(128)}, f32[8,2,32,256]{3,2,1,0:T(8,128)S(1)}, f32[8,2,3,256]{3,2,1,0:T(4,128)S(1)}, bf16[8,2,68,512]{3,2,1,0:T(8,128)(2,1)}, bf16[8,2,3,25...) while((s32[]{:T(128)}, f32[8,2,32,256]{3,2,1,0:T(8,128)S(1)}, ...), condition=%wide.region_9.10_spmd, body=%wide.region_8.9_spmd.sunk | while | flops 85213696 | bytes 5075073 | solution.py:105
  368.4 3.5 psum.7
  372.0 1.3 select_select_fusion
  374.2 1.4 scatter-add.79
  376.5 1.2 scatter-add.80
  378.5 1.2 scatter-add.81
  380.5 1.2 scatter-add.84
  382.5 1.2 scatter-add.85
  384.5 1.2 scatter-add.86
  386.4 1.2 scatter-add.89
  388.4 1.2 scatter-add.90
  390.4 1.2 scatter-add.91
  392.4 1.2 scatter-add.94
  394.3 1.2 scatter-add.95
  396.3 1.2 scatter-add.96
  398.4 1.2 scatter-add.99
  400.3 1.2 scatter-add.100
  402.2 1.2 scatter-add.101
  403.6 1.2 scatter-add.104
  406.3 1.2 scatter-add.106
  408.3 1.2 scatter-add.109
  410.3 1.2 scatter-add.110
  411.6 1.9 collective-permute-start
  414.3 1.9 collective-permute-start.1
  418.2 2.6 copy.26
  421.7 54.9 %reduce-scatter.4.cloned.1.call-done = f32[4096,3]{1,0:T(8,128)} async-done(((f32[8192,3]{1,0:T(8,128)}), f32[4096,3]{1,0:T(8,128)}) %reduce-scatter.4.cloned.1.call-update) | async-done | bytes 49168
  476.6 2.8 copy.27
  (1029 shorter events, 255.2 us)
Async XLA Ops:
  15.4 28.5 %all-to-all-start = ((bf16[4,6,68,256]{3,2,1,0:T(8,128)(2,1)}), bf16[4,6,68,256]{3,2,1,0:T(8,128)(2,1)S(1)}, u32[]{:S(2)}, u32[]{:S(2)}) async-start(bf16[4,6,68,256]{3,2,1,0:T(8,128)(2,1)} %bitcast.46), calls=%async_computation | async-start | bytes 1769472 | tf_op jit(solution)/shard_map/all_to_all | solution.py:94
  43.9 25.2 %all-to-all-start.2 = ((bf16[4,6,68,256]{3,2,1,0:T(8,128)(2,1)}), bf16[4,6,68,256]{3,2,1,0:T(8,128)(2,1)S(1)}, u32[]{:S(2)}, u32[]{:S(2)}) async-start(bf16[4,6,68,256]{3,2,1,0:T(8,128)(2,1)} %bitcast.71), calls=%async_computation.2 | async-start | bytes 1769472 | tf_op jit(solution)/shard_map/all_to_all | solution.py:94
  47.4 101.0 %all-gather.11.cloned.1.call-start = ((), (), s32[]{:S(2)}) async-start(), calls=%async_computation.6 | async-start | bytes 1769472 | tf_op jit(solution)/shard_map/all_gather | solution.py:104
  69.1 25.2 %all-to-all-start.3 = ((bf16[4,6,68,256]{3,2,1,0:T(8,128)(2,1)}), bf16[4,6,68,256]{3,2,1,0:T(8,128)(2,1)S(1)}, u32[]{:S(2)}, u32[]{:S(2)}) async-start(bf16[4,6,68,256]{3,2,1,0:T(8,128)(2,1)} %bitcast.82), calls=%async_computation.3 | async-start | bytes 1769472 | tf_op jit(solution)/shard_map/all_to_all | solution.py:94
  72.6 119.8 %all-gather.15.cloned.1.call-start = ((), (), s32[]{:S(2)}) async-start(), calls=%async_computation.8 | async-start | bytes 1769472 | tf_op jit(solution)/shard_map/all_gather | solution.py:104
  94.3 25.2 %all-to-all-start.4 = ((bf16[4,6,68,256]{3,2,1,0:T(8,128)(2,1)}), bf16[4,6,68,256]{3,2,1,0:T(8,128)(2,1)S(1)}, u32[]{:S(2)}, u32[]{:S(2)}) async-start(bf16[4,6,68,256]{3,2,1,0:T(8,128)(2,1)} %bitcast.93), calls=%async_computation.4 | async-start | bytes 1769472 | tf_op jit(solution)/shard_map/all_to_all | solution.py:94
  97.8 138.6 %all-gather.17.cloned.1.call-start = ((), (), s32[]{:S(2)}) async-start(), calls=%async_computation.9 | async-start | bytes 1769472 | tf_op jit(solution)/shard_map/all_gather | solution.py:104
  119.5 27.2 %all-to-all-start.1 = ((bf16[4,6,68,256]{3,2,1,0:T(8,128)(2,1)}), bf16[4,6,68,256]{3,2,1,0:T(8,128)(2,1)S(1)}, u32[]{:S(2)}, u32[]{:S(2)}) async-start(bf16[4,6,68,256]{3,2,1,0:T(8,128)(2,1)} %bitcast.60), calls=%async_computation.1 | async-start | bytes 1769472 | tf_op jit(solution)/shard_map/all_to_all | solution.py:94
  123.0 1.6 copy-start.2
  123.0 1.6 slice-start
  123.0 157.4 %all-gather.19.cloned.1.call-start = ((), (), s32[]{:S(2)}) async-start(), calls=%async_computation.10 | async-start | bytes 1769472 | tf_op jit(solution)/shard_map/all_gather | solution.py:104
  124.5 199.8 %all-gather.13.cloned.1.call-start = ((), (), s32[]{:S(2)}) async-start(), calls=%async_computation.7 | async-start | bytes 1769472 | tf_op jit(solution)/shard_map/all_gather | solution.py:104
  146.7 1.8 copy-start
  146.7 1.8 copy-start.1
  148.2 328.4 %reduce-scatter.4.cloned.1.call-start = ((), (), s32[]{:S(2)}) async-start(), calls=%async_computation.11 | async-start | bytes 6291456
  368.3 5.1 %copy-start.15 = (pred[2,4,8,128]{3,1,2,0:T(4,128)(4,1)S(1)}, pred[2,4,8,128]{3,1,2,0:T(4,128)(4,1)}, u32[]{:S(2)}) copy-start(pred[2,4,8,128]{3,1,2,0:T(4,128)(4,1)} %copy.76) | copy-start | bytes 24580
  368.3 7.4 %copy-start.14 = (pred[2,4,8,128]{3,1,2,0:T(4,128)(4,1)S(1)}, pred[2,4,8,128]{3,1,2,0:T(4,128)(4,1)}, u32[]{:S(2)}) copy-start(pred[2,4,8,128]{3,1,2,0:T(4,128)(4,1)} %copy.77) | copy-start | bytes 24580
  368.4 9.3 %copy-start.13 = (pred[2,4,8,128]{3,1,2,0:T(4,128)(4,1)S(1)}, pred[2,4,8,128]{3,1,2,0:T(4,128)(4,1)}, u32[]{:S(2)}) copy-start(pred[2,4,8,128]{3,1,2,0:T(4,128)(4,1)} %copy.78) | copy-start | bytes 24580
  373.4 6.3 %copy-start.12 = (pred[2,4,8,128]{3,1,2,0:T(4,128)(4,1)S(1)}, pred[2,4,8,128]{3,1,2,0:T(4,128)(4,1)}, u32[]{:S(2)}) copy-start(pred[2,4,8,128]{3,1,2,0:T(4,128)(4,1)} %copy.79) | copy-start | bytes 24580
  374.2 7.5 %copy-start.11 = (pred[2,4,8,128]{3,1,2,0:T(4,128)(4,1)S(1)}, pred[2,4,8,128]{3,1,2,0:T(4,128)(4,1)}, u32[]{:S(2)}) copy-start(pred[2,4,8,128]{3,1,2,0:T(4,128)(4,1)} %copy.80) | copy-start | bytes 24580
  376.5 7.2 %copy-start.10 = (pred[2,4,8,128]{3,1,2,0:T(4,128)(4,1)S(1)}, pred[2,4,8,128]{3,1,2,0:T(4,128)(4,1)}, u32[]{:S(2)}) copy-start(pred[2,4,8,128]{3,1,2,0:T(4,128)(4,1)} %copy.81) | copy-start | bytes 24580
  378.5 7.3 %copy-start.9 = (pred[2,4,8,128]{3,1,2,0:T(4,128)(4,1)S(1)}, pred[2,4,8,128]{3,1,2,0:T(4,128)(4,1)}, u32[]{:S(2)}) copy-start(pred[2,4,8,128]{3,1,2,0:T(4,128)(4,1)} %copy.82) | copy-start | bytes 24580
  380.5 7.1 %copy-start.8 = (pred[2,4,8,128]{3,1,2,0:T(4,128)(4,1)S(1)}, pred[2,4,8,128]{3,1,2,0:T(4,128)(4,1)}, u32[]{:S(2)}) copy-start(pred[2,4,8,128]{3,1,2,0:T(4,128)(4,1)} %copy.83) | copy-start | bytes 24580
  382.5 7.1 %copy-start.7 = (pred[2,4,8,128]{3,1,2,0:T(4,128)(4,1)S(1)}, pred[2,4,8,128]{3,1,2,0:T(4,128)(4,1)}, u32[]{:S(2)}) copy-start(pred[2,4,8,128]{3,1,2,0:T(4,128)(4,1)} %copy.84) | copy-start | bytes 24580
  384.5 7.2 %copy-start.6 = (pred[2,4,8,128]{3,1,2,0:T(4,128)(4,1)S(1)}, pred[2,4,8,128]{3,1,2,0:T(4,128)(4,1)}, u32[]{:S(2)}) copy-start(pred[2,4,8,128]{3,1,2,0:T(4,128)(4,1)} %copy.85) | copy-start | bytes 24580
  386.4 7.2 %copy-start.5 = (pred[2,4,8,128]{3,1,2,0:T(4,128)(4,1)S(1)}, pred[2,4,8,128]{3,1,2,0:T(4,128)(4,1)}, u32[]{:S(2)}) copy-start(pred[2,4,8,128]{3,1,2,0:T(4,128)(4,1)} %copy.86) | copy-start | bytes 24580
  388.4 7.2 %copy-start.4 = (pred[2,4,8,128]{3,1,2,0:T(4,128)(4,1)S(1)}, pred[2,4,8,128]{3,1,2,0:T(4,128)(4,1)}, u32[]{:S(2)}) copy-start(pred[2,4,8,128]{3,1,2,0:T(4,128)(4,1)} %copy.87) | copy-start | bytes 24580
  390.4 7.1 %copy-start.3 = (pred[2,4,8,128]{3,1,2,0:T(4,128)(4,1)S(1)}, pred[2,4,8,128]{3,1,2,0:T(4,128)(4,1)}, u32[]{:S(2)}) copy-start(pred[2,4,8,128]{3,1,2,0:T(4,128)(4,1)} %copy.88) | copy-start | bytes 24580
  411.6 5.4 %collective-permute-start = (f32[3,64]{1,0:T(4,128)S(1)}, f32[3,64]{1,0:T(4,128)S(1)}, u32[]{:S(2)}, u32[]{:S(2)}) collective-permute-start(f32[3,64]{1,0:T(4,128)S(1)} %get-tuple-element.669), channel_id=1, source_target_pairs={{0,4},{4,8},{8,12},{12,0},{1,5},{5,9},{9,13},{13,1},{2,6},{6,10},{... | collective-permute-start | bytes 2312 | tf_op jit(solution)/shard_map/ppermute | solution.py:19
  414.3 3.6 collective-permute-start.1
Sparse Core Ops, SparseCore 0:
  49.8 24.1 all-gather.10
  75.5 23.6 all-gather.14
  100.8 23.5 all-gather.16
  125.8 23.4 all-gather.18
  150.6 22.7 all-gather.12
  420.9 55.6 reduce-scatter.3
where the time goes:
time: 488 us; the launch traced here: 486 us
  matrix products  172 us (35%)
  waiting for transfers between devices  120 us (25%)
  local copies, waits for them, and re-layouts  109 us (22%)
  other arithmetic  37.2 us (8%)
  starting transfers between devices  24.6 us (5%)
  between operations  15.1 us (3%)
  loops' own time  5.28 us (1%)
    all_to_all x5, waiting for transfers between devices, on_device(): lax.all_to_all(outbox.reshape((clus_count, capacity) + slot_shape), 'clus...  63.9 us
    unnamed x7, waiting for transfers between devices  55 us
    dot_general x40, matrix products, pair_terms(): jnp.einsum('gkb,gab->gka', augmented, weighted, precision=lax.Precision.H...  38.5 us
    dot_general x40, matrix products, pair_terms(): jnp.einsum('gkb,gab->gka', augmented, weighted_two, precision=lax.Precisi...  38.5 us
    squeeze x40, local copies, waits for them, and re-layouts, on_device(): lax.map(pair_terms, (paired(positions), paired(areas), paired(density), p...  37.1 us
    dot_general x40, matrix products, pair_terms(): jnp.einsum('gca,gcb->gab', own_cot, mate_dens, preferred_element_type=jnp...  32.4 us
    dot_general x40, matrix products, pair_terms(): jnp.einsum('gcb,gab->gca', mate_dens, kernel, preferred_element_type=jnp....  32.1 us
    another operation x43, other arithmetic  31.2 us
  transfers between devices with their start and end apart: 13, of which 7 were waited for; matrix products, arithmetic and copies ran while one was open for 46% of the time, Pallas kernels for 0%

commit v1 on v0

v1 whole, which is shorter than its diff:
```python
import functools

import jax
import jax.numpy as jnp
from jax import lax
from jax.experimental import pallas as pl
from jax.experimental.pallas import tpu as pltpu
from jax.sharding import PartitionSpec as P

CP = 512
ROUNDS = 5

core_radius = 0.25
jitter_reach = 8
LANES = 128
AUG = 16


def shifted(value, axis, steps):
    count = lax.axis_size(axis)
    pairs = [(source, (source + steps) % count) for source in range(count)]
    return lax.ppermute(value, axis, pairs)


def three_parts(value):
    parts = []
    for _ in range(3):
        part = value.astype(jnp.bfloat16).astype(jnp.float32)
        parts.append(part)
        value = value - part
    return parts


def pick(index, choices):
    out = choices[0]
    for place in range(1, len(choices)):
        out = jnp.where(index == place, choices[place], out)
    return out


def own_kernel(pos_ref, aug_ref, aug32):
    pos = [pos_ref[coord].astype(jnp.float32) for coord in range(3)]
    square = pos[0] * pos[0] + pos[1] * pos[1] + pos[2] * pos[2] + core_radius * core_radius
    ones = jnp.ones_like(square)
    rows = [-2.0 * value for value in pos] + three_parts(square) + [ones] * 3
    aug32[...] = jnp.zeros(aug32.shape, jnp.float32)
    for row, value in enumerate(rows):
        aug32[:, row, :] = value
    aug_ref[...] = aug32[...].astype(jnp.bfloat16)


def step_kernel(step, cap, first, *refs):
    if first:
        items, source_ref, cot_ref, own_ref, pos_ref = refs[:5]
        refs = refs[5:]
    else:
        items, source_ref, cot_ref, own_ref, pos_ref, pot_in, grad_in = refs[:7]
        refs = refs[7:]
    pot_ref, grad_ref, back_ref, aug32, aug, aug_t, dens_t, weight, target, back = refs
    clusters, width, panels = cot_ref.shape
    quarter = source_ref.shape[1]
    base = clusters * width

    there = [
        source_ref[base + coord * clusters : base + (coord + 1) * clusters, :].astype(jnp.float32)
        for coord in range(3)
    ]
    area = source_ref[base + 3 * clusters : base + 4 * clusters, :].astype(jnp.float32)
    square = there[0] * there[0] + there[1] * there[1] + there[2] * there[2]
    ones = jnp.ones_like(square)
    aug32[...] = jnp.zeros(aug32.shape, jnp.float32)
    for row, value in enumerate(there + [ones] * 3 + three_parts(square)):
        aug32[:, row, :] = value
    weight_t = (CP ** (-0.5) * area).T
    for cluster in range(clusters):
        rows = aug32[cluster]
        aug[cluster] = rows.astype(jnp.bfloat16)
        aug_t[cluster] = rows.T.astype(jnp.bfloat16)
        dens = source_ref[cluster * width : (cluster + 1) * width, :]
        dens_t[cluster] = dens.T
        weight[cluster] = jnp.broadcast_to(weight_t[:, cluster : cluster + 1], (quarter, LANES))
    target[...] = jnp.zeros(target.shape, jnp.float32)
    back[...] = jnp.zeros(back.shape, jnp.float32)
    if first:
        pot_ref[...] = jnp.zeros(pot_ref.shape, jnp.float32)
    else:
        pot_ref[...] = pot_in[...]

    chunk = 256

    def one_item(place):
        code = items[step * (cap + 1) + 1 + place]
        here = code // clusters
        mate = code % clusters
        mate_dens = source_ref[pl.ds(pl.multiple_of(mate * width, width), width), :]
        mate_dens_t = dens_t[mate]
        mate_aug_t = aug_t[mate]
        mate_aug = aug[mate]
        mate_weight = weight[mate]
        mate_weight = jnp.concatenate([mate_weight] * (chunk // LANES), axis=1)
        total = jnp.zeros((AUG, quarter), jnp.float32)
        for start in range(0, panels, chunk):
            cols = slice(start, start + chunk)
            own = own_ref[here, :, cols]
            distance_sq = jnp.dot(mate_aug_t, own, preferred_element_type=jnp.float32)
            product = jnp.dot(mate_dens_t, cot_ref[here, :, cols], preferred_element_type=jnp.float32)
            inverse = lax.rsqrt(distance_sq)
            kernel = mate_weight * inverse
            weighted = ((inverse * inverse) * (kernel * product)).astype(jnp.bfloat16)
            pot_ref[here, :, cols] += jnp.dot(
                mate_dens, kernel.astype(jnp.bfloat16), preferred_element_type=jnp.float32
            )
            target[here, :, cols] += jnp.dot(
                mate_aug, weighted, preferred_element_type=jnp.float32
            )[:8]
            total = total + lax.dot_general(
                own, weighted, (((1,), (1,)), ((), ())), preferred_element_type=jnp.float32
            )
        back[mate] += total[:8]

    count = items[step * (cap + 1)]

    @pl.loop(0, count // 2)
    def _(pair):
        one_item(2 * pair)
        one_item(2 * pair + 1)

    @pl.when(count % 2 == 1)
    def _():
        one_item(count - 1)

    for coord in range(3):
        value = target[:, coord, :] - pos_ref[coord].astype(jnp.float32) * target[:, 3, :]
        if not first:
            value = value + grad_in[coord]
        grad_ref[coord] = value
        back_ref[coord] = -0.5 * back[:, coord, :] - there[coord] * back[:, 6, :]


def run_step(step, cap, items, source, cot, own, pos, carried):
    clusters, width, panels = cot.shape
    quarter = source.shape[1]
    first = carried is None
    vmem = pl.BlockSpec(memory_space=pltpu.VMEM)
    smem = pl.BlockSpec(memory_space=pltpu.SMEM)
    operands = (items, source, cot, own, pos) + (() if first else carried)
    pairs = cap * panels * quarter
    return pl.pallas_call(
        functools.partial(step_kernel, step, cap, first),
        out_shape=(
            jax.ShapeDtypeStruct((clusters, width, panels), jnp.float32),
            jax.ShapeDtypeStruct((3, clusters, panels), jnp.float32),
            jax.ShapeDtypeStruct((3, clusters, quarter), jnp.float32),
        ),
        in_specs=[smem] + [vmem] * (len(operands) - 1),
        out_specs=(vmem, vmem, vmem),
        scratch_shapes=[
            pltpu.VMEM((clusters, AUG, quarter), jnp.float32),
            pltpu.VMEM((clusters, AUG, quarter), jnp.bfloat16),
            pltpu.VMEM((clusters, quarter, AUG), jnp.bfloat16),
            pltpu.VMEM((clusters, quarter, width), jnp.bfloat16),
            pltpu.VMEM((clusters, quarter, LANES), jnp.float32),
            pltpu.VMEM((clusters, 8, panels), jnp.float32),
            pltpu.VMEM((clusters, 8, quarter), jnp.float32),
        ],
        compiler_params=pltpu.CompilerParams(vmem_limit_bytes=32 * 1024 * 1024),
        cost_estimate=pl.CostEstimate(
            flops=2 * pairs * (2 * width + 3 * AUG), bytes_accessed=6 * 2**20, transcendentals=pairs
        ),
        name=f"near_field_{step}",
    )(*operands)


def node_kernel(grad_ref, jitter_ref, main_ref, rims_ref):
    clusters, panels = jitter_ref.shape
    wide = panels + 2 * LANES
    jitter = jitter_ref[...]
    side = jnp.zeros((clusters, LANES), jnp.float32)
    row_at = lax.broadcasted_iota(jnp.int32, (clusters, LANES), 0)
    rims_ref[...] = jnp.zeros(rims_ref.shape, jnp.float32)
    for coord in range(3):
        terms = 0.25 * grad_ref[coord]
        spread = jnp.zeros((clusters, wide), jnp.float32)
        for offset in range(-jitter_reach, jitter_reach + 1):
            masked = jnp.where(jitter == offset, terms, 0.0)
            masked = jnp.concatenate([side, masked, side], axis=1)
            spread = spread + pltpu.roll(masked, offset % wide, 1)
        spread = spread + pltpu.roll(spread, 1, 1)
        spread = spread + pltpu.roll(spread, 32, 1)
        below = spread[:, :LANES]
        above = spread[:, LANES + panels :]
        inner = spread[:, LANES : LANES + panels]
        first = jnp.where(row_at == 0, 0.0, pltpu.roll(above, 1, 0))
        last = jnp.where(row_at == clusters - 1, 0.0, pltpu.roll(below, clusters - 1, 0))
        inner = jnp.concatenate(
            [
                inner[:, :LANES] + first,
                inner[:, LANES : panels - LANES],
                inner[:, panels - LANES :] + last,
            ],
            axis=1,
        )
        for cluster in range(clusters):
            main_ref[coord : coord + 1, cluster * panels : (cluster + 1) * panels] = inner[
                cluster : cluster + 1
            ]
        rims_ref[0, coord : coord + 1, :] = below[:1]
        rims_ref[1, coord : coord + 1, :] = above[clusters - 1 :]


def on_device(positions, areas, density, cotangent, matching, connect):
    clus_count = lax.axis_size("clus")
    sub_count = lax.axis_size("sub")
    rhs_count = lax.axis_size("rhs")
    device = lax.axis_index("clus")
    sub_place = lax.axis_index("sub")
    core = lax.axis_index("rhs")
    clusters, rhs, row_count = density.shape
    panels = row_count * sub_count
    quarter = row_count // rhs_count
    width = rhs * rhs_count
    vmem = pl.BlockSpec(memory_space=pltpu.VMEM)

    def part_of(array, place):
        return pick(
            place % rhs_count,
            [array[..., at * quarter : (at + 1) * quarter] for at in range(rhs_count)],
        )

    blocks = [part_of(density, core)]
    for step in range(1, rhs_count):
        blocks.append(shifted(part_of(density, core + step), "rhs", step))
    by_coord = jnp.transpose(positions, (1, 0, 2))
    placed = jnp.concatenate([by_coord, areas[None]], axis=0)
    source = jnp.concatenate(
        [
            jnp.concatenate(blocks, axis=1).reshape(clusters * width, quarter),
            part_of(placed, core).reshape(4 * clusters, quarter),
        ],
        axis=0,
    )

    per_round = 2 * ((clusters // 2 + clus_count - 2) // (clus_count - 1))
    cap = ROUNDS * per_round
    partners = lax.dynamic_slice_in_dim(matching, device * clusters, clusters, 1).reshape(-1)
    here = jnp.tile(jnp.arange(clusters, dtype=jnp.int32), ROUNDS)
    code = here * clusters + partners % clusters
    behind = (device - partners // clusters) % clus_count
    total_items = ROUNDS * clusters
    order = jnp.arange(total_items, dtype=jnp.int32)
    rank = jnp.sum(
        ((behind[None, :] == behind[:, None]) & (order[None, :] < order[:, None])).astype(jnp.int32),
        axis=1,
    )
    steps = jnp.arange(1, clus_count, dtype=jnp.int32)
    member = behind[None, :] == steps[:, None]
    slots = jnp.arange(cap, dtype=jnp.int32)
    chosen = member[:, None, :] & (rank[None, None, :] == slots[None, :, None])
    listed = jnp.sum(jnp.where(chosen, code[None, None, :], 0), axis=2)
    counts = jnp.sum(member.astype(jnp.int32), axis=1)
    items = jnp.concatenate([counts[:, None], listed], axis=1).reshape(-1)

    cluster_at = jnp.arange(clusters, dtype=jnp.int32)
    first_ids = (device * clusters + cluster_at) * panels
    base_ids = first_ids[:, None] + (
        sub_place * row_count + jnp.arange(row_count, dtype=jnp.int32)
    )[None, :]
    nodes_total = clus_count * clusters * panels
    jitter = (connect[:, 0, :] - base_ids + jitter_reach) % nodes_total - jitter_reach
    local = jnp.concatenate(
        [
            cotangent.reshape(clusters * rhs, row_count),
            by_coord.reshape(3 * clusters, row_count),
            jitter.astype(jnp.bfloat16),
        ],
        axis=0,
    )
    found = [local] + [shifted(local, "sub", step) for step in range(1, sub_count)]
    whole = jnp.concatenate(
        [
            pick((sub_place - place) % sub_count, found)
            for place in range(sub_count)
        ],
        axis=1,
    )
    cot_half = whole[: clusters * rhs].reshape(clusters, rhs, panels)
    cot_blocks = [cot_half] + [shifted(cot_half, "rhs", step) for step in range(1, rhs_count)]
    cot = jnp.concatenate(cot_blocks, axis=1)
    pos = whole[clusters * rhs : clusters * (rhs + 3)].reshape(3, clusters, panels)
    jitter_all = whole[clusters * (rhs + 3) :].astype(jnp.int32)
    own = pl.pallas_call(
        own_kernel,
        out_shape=jax.ShapeDtypeStruct((clusters, AUG, panels), jnp.bfloat16),
        in_specs=[vmem],
        out_specs=vmem,
        scratch_shapes=[pltpu.VMEM((clusters, AUG, panels), jnp.float32)],
        compiler_params=pltpu.CompilerParams(vmem_limit_bytes=16 * 1024 * 1024),
        name="target_rows",
    )(pos)

    carried = None
    returned = jnp.zeros((3, clusters, quarter), jnp.float32)
    for step in range(1, clus_count):
        source = shifted(source, "clus", 1)
        pot, grad, back = run_step(step - 1, cap, items, source, cot, own, pos, carried)
        carried = (pot, grad)
        returned = returned + shifted(back, "clus", -step)

    at = sub_place * row_count + core * quarter
    own_part = lax.dynamic_slice_in_dim(grad, at, quarter, 2) + returned
    grad = lax.dynamic_update_slice_in_dim(grad, own_part, at, 2)
    share = clusters // sub_count

    def share_of(array, place):
        return pick(
            place % sub_count,
            [array[..., at * share : (at + 1) * share, :] for at in range(sub_count)],
        )

    summed = share_of(grad, sub_place)
    for step in range(1, sub_count):
        summed = summed + shifted(share_of(grad, sub_place + step), "sub", step)
    gathered = summed
    for step in range(1, rhs_count):
        gathered = gathered + shifted(summed, "rhs", step)
    main, rims = pl.pallas_call(
        node_kernel,
        out_shape=(
            jax.ShapeDtypeStruct((3, share * panels), jnp.float32),
            jax.ShapeDtypeStruct((2, 8, LANES), jnp.float32),
        ),
        in_specs=[vmem, vmem],
        out_specs=(vmem, vmem),
        compiler_params=pltpu.CompilerParams(vmem_limit_bytes=16 * 1024 * 1024),
        name="node_terms",
    )(gathered, share_of(jitter_all, sub_place))
    from_above = shifted(rims[0], ("clus", "sub"), -1)[:3]
    from_below = shifted(rims[1], ("clus", "sub"), 1)[:3]
    node_grad = jnp.concatenate(
        [main[:, :LANES] + from_below, main[:, LANES:-LANES], main[:, -LANES:] + from_above], axis=1
    )

    half = pot[:, :rhs]
    for step in range(1, rhs_count):
        half = half + shifted(pot[:, step * rhs : (step + 1) * rhs], "rhs", -step)

    def panels_of(array, place):
        return pick(
            place % sub_count,
            [array[..., at * row_count : (at + 1) * row_count] for at in range(sub_count)],
        )

    potential = panels_of(half, sub_place)
    for step in range(1, sub_count):
        potential = potential + shifted(panels_of(half, sub_place + step), "sub", step)
    return (potential.astype(jnp.bfloat16), node_grad)


def solution(mesh):
    placed = (
        P(("groups", "clus"), None, "sub"),
        P(("groups", "clus"), "sub"),
        P(("groups", "clus"), "rhs", "sub"),
        P(("groups", "clus"), "rhs", "sub"),
        P(None, "groups"),
        P(("groups", "clus"), None, "sub"),
    )
    return jax.shard_map(
        on_device,
        mesh=mesh,
        in_specs=placed,
        out_specs=(P(("groups", "clus"), "rhs", "sub"), P(None, ("groups", "clus", "sub"))),
        check_vma=False,
    )
```

time: 488 us -> 106 us (0.22)
  matrix products: 172 us -> 0 us
  local copies, waits for them, and re-layouts: 109 us -> 1.39 us
  waiting for transfers between devices: 120 us -> 40.7 us
  Pallas kernels: 0 us -> 41.2 us
  other arithmetic: 37.2 us -> 5.54 us
  between operations: 15.1 us -> 0.98 us
  starting transfers between devices: 24.6 us -> 16.4 us
  loops' own time: 5.28 us -> 0 us
    dot_general x200 -> x0, matrix products: 172 us -> none  [the longest x40 38.5 us: pair_terms(): jnp.einsum('gkb,gab->gka', augmented, weighted, precision=lax.Precision.H...]
    all_to_all x5 -> x0, waiting for transfers between devices: 63.9 us -> none  [on_device(): lax.all_to_all(outbox.reshape((clus_count, capacity) + slot_shape), 'clus...]
    unnamed x7 -> x0, waiting for transfers between devices: 55 us -> none
    pallas_call x0 -> x5, Pallas kernels: none -> 41.2 us  [the longest x3 40.5 us: run_step(): pl.pallas_call(functools.partial(step_kernel, step, cap, first), out_shap...]
    ppermute x2 -> x15, waiting for transfers between devices: 0.88 us -> 40.7 us  [shifted(): return lax.ppermute(value, axis, pairs)]
    squeeze x40 -> x1, local copies, waits for them, and re-layouts: 37.1 us -> 0.01 us  [on_device(): from_below = shifted(rims[1], ('clus', 'sub'), 1)[:3]]
    another operation x43 -> x0, other arithmetic: 31.2 us -> none
    scatter-add x23 -> x0, local copies, waits for them, and re-layouts: 23.6 us -> none  [the longest x17 19.5 us: on_device(): spread = spread.at[:, start:start + span].add(masked)]
  transfers between devices with their start and end apart: 13 -> 15, of which waited for: 7 -> 8; matrix products, arithmetic and copies ran while one was open for 46% -> 5% of each run, Pallas kernels for 0% -> 39%
where the time goes in v1:
time: 106 us
  Pallas kernels  41.2 us (39%)
  waiting for transfers between devices  40.7 us (38%)
  starting transfers between devices  16.4 us (15%)
  other arithmetic  5.54 us (5%)
  local copies, waits for them, and re-layouts  1.39 us (1%)
    ppermute x15, waiting for transfers between devices, shifted(): return lax.ppermute(value, axis, pairs)  40.7 us
    pallas_call x3, Pallas kernels, run_step(): pl.pallas_call(functools.partial(step_kernel, step, cap, first), out_shap...  40.5 us
    ppermute x15, starting transfers between devices, shifted(): return lax.ppermute(value, axis, pairs)  16.4 us
  transfers between devices with their start and end apart: 15, of which 8 were waited for; matrix products, arithmetic and copies ran while one was open for 5% of the time, Pallas kernels for 39%

profile of v1, /device:TPU:0, one launch (start us, length us, event | category | flops | bytes accessed | tf_op | source)
XLA Modules:
  0.0 106.2 jit_solution(11633886846848912570)
XLA Ops:
  0.6 0.0 copy-start
  0.6 0.0 copy-start.2
  0.7 0.0 copy-start.1
  0.7 1.0 broadcast_select_fusion.3
  1.7 0.5 collective-permute-start
  2.3 0.9 slice.79
  3.1 0.1 fusion.5
  3.2 1.0 pad_maximum_fusion.1
  4.2 2.6 %collective-permute-start.4 = (bf16[576,256]{1,0:T(8,128)(2,1)S(1)}, bf16[576,256]{1,0:T(8,128)(2,1)S(1)}, u32[]{:S(2)}, u32[]{:S(2)}) collective-permute-start(bf16[576,256]{1,0:T(8,128)(2,1)S(1)} %pad_maximum_fusion.1), channel_id=1, source_target_pairs={{0,2},{2,0},{1,3},{3,1},{4,6},{6,4},{5,7},{7,5},{8,10},{10,8},{9,1... | collective-permute-start | bytes 884744 | tf_op jit(solution)/shard_map/ppermute | solution.py:22
  6.8 0.0 copy-done
  6.8 0.1 constant_dynamic-slice_fusion
  6.9 0.1 reshape.198
  6.9 0.1 mul.31
  7.0 0.2 convert_reduce_fusion
  7.3 0.7 fusion.7
  8.0 0.0 collective-permute-done
  8.1 1.6 %collective-permute-start.1 = (bf16[1088,128]{1,0:T(8,128)(2,1)S(1)}, bf16[1088,128]{1,0:T(8,128)(2,1)S(1)}, u32[]{:S(2)}, u32[]{:S(2)}) collective-permute-start(bf16[1088,128]{1,0:T(8,128)(2,1)S(1)} %pad_maximum_fusion.2), channel_id=1, source_target_pairs={{0,4},{4,8},{8,12},{12,0},{1,5},{5,9},{9,13},{13,1},{2,6},{6,10},{... | collective-permute-start | bytes 835592 | tf_op jit(solution)/shard_map/ppermute | solution.py:22
  9.7 4.7 %collective-permute-done.4 = bf16[576,256]{1,0:T(8,128)(2,1)S(1)} collective-permute-done((bf16[576,256]{1,0:T(8,128)(2,1)S(1)}, bf16[576,256]{1,0:T(8,128)(2,1)S(1)}, u32[]{:S(2)}, u32[]{:S(2)}) %collective-permute-start.4) | collective-permute-done | bytes 294944 | tf_op jit(solution)/shard_map/ppermute | solution.py:22
  14.4 0.0 copy-done.2
  14.4 0.0 copy-done.1
  14.4 0.1 broadcast_select_fusion
  14.6 0.1 collective-permute-start.5
  14.7 4.1 %collective-permute-done.1.refs_1_ = bf16[1088,128]{1,0:T(8,128)(2,1)S(1)} collective-permute-done((bf16[1088,128]{1,0:T(8,128)(2,1)S(1)}, bf16[1088,128]{1,0:T(8,128)(2,1)S(1)}, u32[]{:S(2)}, u32[]{:S(2)}) %collective-permute-start.1) | collective-permute-done | bytes 278560 | tf_op jit(solution)/shard_map/ppermute | solution.py:22
  18.7 0.0 collective-permute-start.2
  18.8 0.2 convert_reduce_fusion.1
  18.9 0.1 copy.10
  19.0 0.1 select_reduce_fusion
  19.2 0.1 pad_add_fusion
  19.3 0.1 reshape.199.refs_0_
  19.3 9.2 %collective-permute-done.2.refs_1_ = bf16[1088,128]{1,0:T(8,128)(2,1)S(1)} collective-permute-done((bf16[1088,128]{1,0:T(8,128)(2,1)S(1)}, bf16[1088,128]{1,0:T(8,128)(2,1)S(1)}, u32[]{:S(2)}, u32[]{:S(2)}) %collective-permute-start.2) | collective-permute-done | bytes 278560 | tf_op jit(solution)/shard_map/ppermute | solution.py:22
  28.5 0.0 collective-permute-start.3
  28.6 0.1 target_rows.1.refs_3_
  28.7 0.0 collective-permute-done.5
  28.7 0.1 pad_maximum_fusion.refs_2_
  28.8 13.3 %near_field_0.1 = (f32[16,64,512]{2,1,0:T(8,128)S(1)}, f32[3,16,512]{2,1,0:T(8,128)S(1)}, f32[3,16,128]{2,1,0:T(8,128)S(1)}) custom-call(s32[93]{0:T(128)S(1)} %reshape.199.refs_0_, bf16[1088,128]{1,0:T(8,128)(2,1)S(1)} %collective-permute-done.1.refs_1_, bf16[16,64,512]{2,1,0:T(8,128)(2,1)S(1)} %pad_maximum_fusion.refs_2_, ...), custom_call_target="tpu_custom_call" | custom-call | flops 692060160 | bytes 6291456 | tf_op jit(solution)/shard_map/near_field_0/pallas_call | solution.py:148
  42.1 12.3 %near_field_1.1 = (f32[16,64,512]{2,1,0:T(8,128)S(1)}, f32[3,16,512]{2,1,0:T(8,128)S(1)}, f32[3,16,128]{2,1,0:T(8,128)S(1)}) custom-call(s32[93]{0:T(128)S(1)} %reshape.199.refs_0_, bf16[1088,128]{1,0:T(8,128)(2,1)S(1)} %collective-permute-done.2.refs_1_, bf16[16,64,512]{2,1,0:T(8,128)(2,1)S(1)} %pad_maximum_fusion.refs_2_, ...), custom_call_target="tpu_custom_call" | custom-call | flops 692060160 | bytes 6291456 | tf_op jit(solution)/shard_map/near_field_1/pallas_call | solution.py:148
  54.3 0.5 collective-permute-start.9
  54.9 5.2 %collective-permute-start.8 = (f32[3,16,128]{2,1,0:T(8,128)S(1)}, f32[3,16,128]{2,1,0:T(8,128)S(1)}, u32[]{:S(2)}, u32[]{:S(2)}) collective-permute-start(f32[3,16,128]{2,1,0:T(8,128)S(1)} %get-tuple-element.19), channel_id=1, source_target_pairs={{0,12},{4,0},{8,4},{12,8},{1,13},{5,1},{9,5},{13,9},{2,14},{6,2},{... | collective-permute-start | bytes 73736 | tf_op jit(solution)/shard_map/ppermute | solution.py:22
  60.1 0.0 collective-permute-done.3.refs_1_
  60.1 15.0 %near_field_2.1 = (f32[16,64,512]{2,1,0:T(8,128)S(1)}, f32[3,16,512]{2,1,0:T(8,128)S(1)}, f32[3,16,128]{2,1,0:T(8,128)S(1)}) custom-call(s32[93]{0:T(128)S(1)} %reshape.199.refs_0_, bf16[1088,128]{1,0:T(8,128)(2,1)S(1)} %collective-permute-done.3.refs_1_, bf16[16,64,512]{2,1,0:T(8,128)(2,1)S(1)} %pad_maximum_fusion.refs_2_, ...), custom_call_target="tpu_custom_call" | custom-call | flops 692060160 | bytes 6291456 | tf_op jit(solution)/shard_map/near_field_2/pallas_call | solution.py:148
  75.1 0.1 collective-permute-start.10
  75.2 0.1 slice.83
  75.3 0.1 collective-permute-start.6
  75.4 0.0 collective-permute-done.9
  75.4 0.0 collective-permute-done.8
  75.4 5.4 %collective-permute-done.10 = f32[3,16,128]{2,1,0:T(8,128)S(1)} collective-permute-done((f32[3,16,128]{2,1,0:T(8,128)S(1)}, f32[3,16,128]{2,1,0:T(8,128)S(1)}, u32[]{:S(2)}, u32[]{:S(2)}) %collective-permute-start.10) | collective-permute-done | bytes 24608 | tf_op jit(solution)/shard_map/ppermute | solution.py:22
  80.8 0.8 collective-permute-start.11
  81.7 3.3 %collective-permute-done.11 = f32[3,8,512]{2,1,0:T(8,128)S(1)} collective-permute-done((f32[3,8,512]{2,1,0:T(8,128)S(1)}, f32[3,8,512]{2,1,0:T(8,128)S(1)}, u32[]{:S(2)}, u32[]{:S(2)}) %collective-permute-start.11) | collective-permute-done | bytes 49184 | tf_op jit(solution)/shard_map/ppermute | solution.py:22
  85.0 0.1 collective-permute-start.12
  85.1 1.2 %collective-permute-done.12 = f32[3,8,512]{2,1,0:T(8,128)S(1)} collective-permute-done((f32[3,8,512]{2,1,0:T(8,128)S(1)}, f32[3,8,512]{2,1,0:T(8,128)S(1)}, u32[]{:S(2)}, u32[]{:S(2)}) %collective-permute-start.12) | collective-permute-done | bytes 49184 | tf_op jit(solution)/shard_map/ppermute | solution.py:22
  86.3 0.5 node_terms.1
  86.8 0.8 collective-permute-start.13
  87.7 3.9 %collective-permute-start.14 = (f32[8,128]{1,0:T(8,128)S(1)}, f32[8,128]{1,0:T(8,128)S(1)}, u32[]{:S(2)}, u32[]{:S(2)}) collective-permute-start(f32[8,128]{1,0:T(8,128)S(1)} %get-tuple-element.33), channel_id=1, source_target_pairs={{0,14},{2,0},{4,2},{6,4},{8,6},{10,8},{12,10},{14,12},{1,15},{3,1}... | collective-permute-start | bytes 12296 | tf_op jit(solution)/shard_map/ppermute | solution.py:22
  91.6 0.0 collective-permute-done.6
  91.6 0.2 slice_add_fusion
  91.8 0.1 slice_select_fusion
  91.9 0.1 collective-permute-start.7
  92.0 1.2 %collective-permute-done.13 = f32[8,128]{1,0:T(8,128)S(1)} collective-permute-done((f32[8,128]{1,0:T(8,128)S(1)}, f32[8,128]{1,0:T(8,128)S(1)}, u32[]{:S(2)}, u32[]{:S(2)}) %collective-permute-start.13) | collective-permute-done | bytes 4128 | tf_op jit(solution)/shard_map/ppermute | solution.py:22
  93.2 0.0 collective-permute-done.14
  93.2 0.6 pad_maximum_fusion.4
  93.8 11.6 %collective-permute-done.7 = f32[16,32,256]{2,1,0:T(8,128)S(1)} collective-permute-done((f32[16,32,256]{2,1,0:T(8,128)S(1)}, f32[16,32,256]{2,1,0:T(8,128)S(1)}, u32[]{:S(2)}, u32[]{:S(2)}) %collective-permute-start.7) | collective-permute-done | bytes 524320 | tf_op jit(solution)/shard_map/ppermute | solution.py:22
  105.4 0.8 add_convert_fusion
  (19 shorter events, 0.2 us)
Async XLA Ops:
  0.6 6.2 %copy-start = (s32[5,64]{1,0:T(8,128)S(1)}, s32[5,64]{1,0:T(8,128)}, u32[]{:S(2)}) copy-start(s32[5,64]{1,0:T(8,128)} %param.10) | copy-start | bytes 3844
  0.6 13.8 %copy-start.2 = (bf16[16,3,256]{2,0,1:T(8,128)(2,1)S(1)}, bf16[16,3,256]{2,0,1:T(8,128)(2,1)}, u32[]{:S(2)}) copy-start(bf16[16,3,256]{2,0,1:T(8,128)(2,1)} %param.6) | copy-start | bytes 73732
  0.7 13.8 %copy-start.1 = (bf16[16,32,256]{2,1,0:T(8,128)(2,1)S(1)}, bf16[16,32,256]{2,1,0:T(8,128)(2,1)}, u32[]{:S(2)}) copy-start(bf16[16,32,256]{2,1,0:T(8,128)(2,1)} %param.9) | copy-start | bytes 786436
  1.7 6.3 %collective-permute-start = (bf16[16,32,128]{2,1,0:T(8,128)(2,1)S(1)}, bf16[16,32,128]{2,1,0:T(8,128)(2,1)S(1)}, u32[]{:S(2)}, u32[]{:S(2)}) collective-permute-start(bf16[16,32,128]{2,1,0:T(8,128)(2,1)S(1)} %get-tuple-element.29), channel_id=1, source_target_pairs={{0,1},{1,0},{2,3},{3,2},{4,5},{5,4},{6,7},{7,6},{8,9},{9,8},{10,11... | collective-permute-start | bytes 393224 | tf_op jit(solution)/shard_map/ppermute | solution.py:22
  4.2 10.2 %collective-permute-start.4 = (bf16[576,256]{1,0:T(8,128)(2,1)S(1)}, bf16[576,256]{1,0:T(8,128)(2,1)S(1)}, u32[]{:S(2)}, u32[]{:S(2)}) collective-permute-start(bf16[576,256]{1,0:T(8,128)(2,1)S(1)} %pad_maximum_fusion.1), channel_id=1, source_target_pairs={{0,2},{2,0},{1,3},{3,1},{4,6},{6,4},{5,7},{7,5},{8,10},{10,8},{9,1... | collective-permute-start | bytes 884744 | tf_op jit(solution)/shard_map/ppermute | solution.py:22
  8.1 10.7 %collective-permute-start.1 = (bf16[1088,128]{1,0:T(8,128)(2,1)S(1)}, bf16[1088,128]{1,0:T(8,128)(2,1)S(1)}, u32[]{:S(2)}, u32[]{:S(2)}) collective-permute-start(bf16[1088,128]{1,0:T(8,128)(2,1)S(1)} %pad_maximum_fusion.2), channel_id=1, source_target_pairs={{0,4},{4,8},{8,12},{12,0},{1,5},{5,9},{9,13},{13,1},{2,6},{6,10},{... | collective-permute-start | bytes 835592 | tf_op jit(solution)/shard_map/ppermute | solution.py:22
  14.6 14.1 %collective-permute-start.5 = (bf16[16,32,512]{2,1,0:T(8,128)(2,1)S(1)}, bf16[16,32,512]{2,1,0:T(8,128)(2,1)S(1)}, u32[]{:S(2)}, u32[]{:S(2)}) collective-permute-start(bf16[16,32,512]{2,1,0:T(8,128)(2,1)S(1)} %bitcast.28), channel_id=1, source_target_pairs={{0,1},{1,0},{2,3},{3,2},{4,5},{5,4},{6,7},{7,6},{8,9},{9,8},{10,11... | collective-permute-start | bytes 1572872 | tf_op jit(solution)/shard_map/ppermute | solution.py:22
  18.7 9.8 %collective-permute-start.2 = (bf16[1088,128]{1,0:T(8,128)(2,1)S(1)}, bf16[1088,128]{1,0:T(8,128)(2,1)S(1)}, u32[]{:S(2)}, u32[]{:S(2)}) collective-permute-start(bf16[1088,128]{1,0:T(8,128)(2,1)S(1)} %collective-permute-done.1.refs_1_), channel_id=1, source_target_pairs={{0,4},{4,8},{8,12},{12,0},{1,5},{5,9},{9,13},{13,1},{2,6},{6,10},{... | collective-permute-start | bytes 835592 | tf_op jit(solution)/shard_map/ppermute | solution.py:22
  28.5 31.5 %collective-permute-start.3 = (bf16[1088,128]{1,0:T(8,128)(2,1)S(1)}, bf16[1088,128]{1,0:T(8,128)(2,1)S(1)}, u32[]{:S(2)}, u32[]{:S(2)}) collective-permute-start(bf16[1088,128]{1,0:T(8,128)(2,1)S(1)} %collective-permute-done.2.refs_1_), channel_id=1, source_target_pairs={{0,4},{4,8},{8,12},{12,0},{1,5},{5,9},{9,13},{13,1},{2,6},{6,10},{... | collective-permute-start | bytes 835592 | tf_op jit(solution)/shard_map/ppermute | solution.py:22
  54.3 21.0 %collective-permute-start.9 = (f32[3,16,128]{2,1,0:T(8,128)S(1)}, f32[3,16,128]{2,1,0:T(8,128)S(1)}, u32[]{:S(2)}, u32[]{:S(2)}) collective-permute-start(f32[3,16,128]{2,1,0:T(8,128)S(1)} %get-tuple-element.20), channel_id=1, source_target_pairs={{0,8},{4,12},{8,0},{12,4},{1,9},{5,13},{9,1},{13,5},{2,10},{6,14},... | collective-permute-start | bytes 73736 | tf_op jit(solution)/shard_map/ppermute | solution.py:22
  54.9 20.5 %collective-permute-start.8 = (f32[3,16,128]{2,1,0:T(8,128)S(1)}, f32[3,16,128]{2,1,0:T(8,128)S(1)}, u32[]{:S(2)}, u32[]{:S(2)}) collective-permute-start(f32[3,16,128]{2,1,0:T(8,128)S(1)} %get-tuple-element.19), channel_id=1, source_target_pairs={{0,12},{4,0},{8,4},{12,8},{1,13},{5,1},{9,5},{13,9},{2,14},{6,2},{... | collective-permute-start | bytes 73736 | tf_op jit(solution)/shard_map/ppermute | solution.py:22
  75.1 5.7 %collective-permute-start.10 = (f32[3,16,128]{2,1,0:T(8,128)S(1)}, f32[3,16,128]{2,1,0:T(8,128)S(1)}, u32[]{:S(2)}, u32[]{:S(2)}) collective-permute-start(f32[3,16,128]{2,1,0:T(8,128)S(1)} %get-tuple-element.21), channel_id=1, source_target_pairs={{0,4},{4,8},{8,12},{12,0},{1,5},{5,9},{9,13},{13,1},{2,6},{6,10},{... | collective-permute-start | bytes 73736 | tf_op jit(solution)/shard_map/ppermute | solution.py:22
  75.3 16.3 %collective-permute-start.6 = (f32[16,32,512]{2,1,0:T(8,128)S(1)}, f32[16,32,512]{2,1,0:T(8,128)S(1)}, u32[]{:S(2)}, u32[]{:S(2)}) collective-permute-start(f32[16,32,512]{2,1,0:T(8,128)S(1)} %slice.83), channel_id=1, source_target_pairs={{0,1},{1,0},{2,3},{3,2},{4,5},{5,4},{6,7},{7,6},{8,9},{9,8},{10,11... | collective-permute-start | bytes 3145736 | tf_op jit(solution)/shard_map/ppermute | solution.py:22
  80.8 4.2 %collective-permute-start.11 = (f32[3,8,512]{2,1,0:T(8,128)S(1)}, f32[3,8,512]{2,1,0:T(8,128)S(1)}, u32[]{:S(2)}, u32[]{:S(2)}) collective-permute-start(f32[3,8,512]{2,1,0:T(8,128)S(1)} %slice_select_fusion.1), channel_id=1, source_target_pairs={{0,2},{2,0},{1,3},{3,1},{4,6},{6,4},{5,7},{7,5},{8,10},{10,8},{9,1... | collective-permute-start | bytes 147464 | tf_op jit(solution)/shard_map/ppermute | solution.py:22
  85.0 1.3 %collective-permute-start.12 = (f32[3,8,512]{2,1,0:T(8,128)S(1)}, f32[3,8,512]{2,1,0:T(8,128)S(1)}, u32[]{:S(2)}, u32[]{:S(2)}) collective-permute-start(f32[3,8,512]{2,1,0:T(8,128)S(1)} %select_add_fusion), channel_id=1, source_target_pairs={{0,1},{1,0},{2,3},{3,2},{4,5},{5,4},{6,7},{7,6},{8,9},{9,8},{10,11... | collective-permute-start | bytes 147464 | tf_op jit(solution)/shard_map/ppermute | solution.py:22
  86.8 6.4 %collective-permute-start.13 = (f32[8,128]{1,0:T(8,128)S(1)}, f32[8,128]{1,0:T(8,128)S(1)}, u32[]{:S(2)}, u32[]{:S(2)}) collective-permute-start(f32[8,128]{1,0:T(8,128)S(1)} %get-tuple-element.32), channel_id=1, source_target_pairs={{0,2},{2,4},{4,6},{6,8},{8,10},{10,12},{12,14},{14,0},{1,3},{3,5},... | collective-permute-start | bytes 12296 | tf_op jit(solution)/shard_map/ppermute | solution.py:22
  87.7 5.5 %collective-permute-start.14 = (f32[8,128]{1,0:T(8,128)S(1)}, f32[8,128]{1,0:T(8,128)S(1)}, u32[]{:S(2)}, u32[]{:S(2)}) collective-permute-start(f32[8,128]{1,0:T(8,128)S(1)} %get-tuple-element.33), channel_id=1, source_target_pairs={{0,14},{2,0},{4,2},{6,4},{8,6},{10,8},{12,10},{14,12},{1,15},{3,1}... | collective-permute-start | bytes 12296 | tf_op jit(solution)/shard_map/ppermute | solution.py:22
  91.9 13.5 %collective-permute-start.7 = (f32[16,32,256]{2,1,0:T(8,128)S(1)}, f32[16,32,256]{2,1,0:T(8,128)S(1)}, u32[]{:S(2)}, u32[]{:S(2)}) collective-permute-start(f32[16,32,256]{2,1,0:T(8,128)S(1)} %slice_select_fusion), channel_id=1, source_target_pairs={{0,2},{2,0},{1,3},{3,1},{4,6},{6,4},{5,7},{7,5},{8,10},{10,8},{9,1... | collective-permute-start | bytes 1572872 | tf_op jit(solution)/shard_map/ppermute | solution.py:22

commit v2 on v1

--- a/solution.py
+++ b/solution.py
@@ -49,14 +49,19 @@
     aug_ref[...] = aug32[...].astype(jnp.bfloat16)
 
 
-def step_kernel(step, cap, first, *refs):
-    if first:
-        items, source_ref, cot_ref, own_ref, pos_ref = refs[:5]
-        refs = refs[5:]
+def step_kernel(step, length, first, last, *refs):
+    items, source_ref, cot_ref, own_ref = refs[:4]
+    refs = refs[4:]
+    if not first:
+        acc_in = refs[0]
+        refs = refs[1:]
+    if last:
+        pos_ref, pot_ref, pot_out_ref, grad_ref, back_ref, acc = refs[:6]
+        refs = refs[6:]
     else:
-        items, source_ref, cot_ref, own_ref, pos_ref, pot_in, grad_in = refs[:7]
-        refs = refs[7:]
-    pot_ref, grad_ref, back_ref, aug32, aug, aug_t, dens_t, weight, target, back = refs
+        acc, back_ref = refs[:2]
+        refs = refs[2:]
+    aug32, aug_t, dens_t, left, weight, back, dist_a, dist_b, prod_a, prod_b, both_a, both_b = refs
     clusters, width, panels = cot_ref.shape
     quarter = source_ref.shape[1]
     base = clusters * width
@@ -72,97 +77,118 @@
     for row, value in enumerate(there + [ones] * 3 + three_parts(square)):
         aug32[:, row, :] = value
     weight_t = (CP ** (-0.5) * area).T
+    left[...] = jnp.zeros(left.shape, left.dtype)
     for cluster in range(clusters):
         rows = aug32[cluster]
-        aug[cluster] = rows.astype(jnp.bfloat16)
+        left[cluster, width:, quarter:] = rows.astype(jnp.bfloat16)
         aug_t[cluster] = rows.T.astype(jnp.bfloat16)
         dens = source_ref[cluster * width : (cluster + 1) * width, :]
+        left[cluster, :width, :quarter] = dens
         dens_t[cluster] = dens.T
         weight[cluster] = jnp.broadcast_to(weight_t[:, cluster : cluster + 1], (quarter, LANES))
-    target[...] = jnp.zeros(target.shape, jnp.float32)
+    weight[clusters] = jnp.zeros((quarter, LANES), jnp.float32)
     back[...] = jnp.zeros(back.shape, jnp.float32)
     if first:
-        pot_ref[...] = jnp.zeros(pot_ref.shape, jnp.float32)
+        acc[...] = jnp.zeros(acc.shape, jnp.float32)
     else:
-        pot_ref[...] = pot_in[...]
-
-    chunk = 256
-
-    def one_item(place):
-        code = items[step * (cap + 1) + 1 + place]
-        here = code // clusters
-        mate = code % clusters
-        mate_dens = source_ref[pl.ds(pl.multiple_of(mate * width, width), width), :]
-        mate_dens_t = dens_t[mate]
-        mate_aug_t = aug_t[mate]
-        mate_aug = aug[mate]
-        mate_weight = weight[mate]
-        mate_weight = jnp.concatenate([mate_weight] * (chunk // LANES), axis=1)
-        total = jnp.zeros((AUG, quarter), jnp.float32)
-        for start in range(0, panels, chunk):
-            cols = slice(start, start + chunk)
-            own = own_ref[here, :, cols]
-            distance_sq = jnp.dot(mate_aug_t, own, preferred_element_type=jnp.float32)
-            product = jnp.dot(mate_dens_t, cot_ref[here, :, cols], preferred_element_type=jnp.float32)
-            inverse = lax.rsqrt(distance_sq)
-            kernel = mate_weight * inverse
-            weighted = ((inverse * inverse) * (kernel * product)).astype(jnp.bfloat16)
-            pot_ref[here, :, cols] += jnp.dot(
-                mate_dens, kernel.astype(jnp.bfloat16), preferred_element_type=jnp.float32
+        acc[...] = acc_in[...]
+    dist_b[...] = jnp.ones(dist_b.shape, jnp.float32)
+    prod_b[...] = jnp.zeros(prod_b.shape, jnp.float32)
+    both_a[...] = jnp.zeros(both_a.shape, both_a.dtype)
+
+    def decoded(place):
+        code = items[step * length + place]
+        return code // (2 * clusters), code % (2 * clusters)
+
+    def raw(place, dist, prod):
+        here, mate = decoded(place)
+        mate = mate % clusters
+        dist[...] = jnp.dot(aug_t[mate], own_ref[here], preferred_element_type=jnp.float32)
+        prod[...] = jnp.dot(dens_t[mate], cot_ref[here], preferred_element_type=jnp.float32)
+
+    def pointwise(place, dist, prod, both):
+        _, mate = decoded(place)
+        scale = weight[mate]
+        for start in range(0, panels, LANES):
+            cols = slice(start, start + LANES)
+            inverse = lax.rsqrt(dist[:, cols])
+            kernel = scale * inverse
+            both[:quarter, cols] = kernel.astype(jnp.bfloat16)
+            both[quarter:, cols] = ((inverse * inverse) * (kernel * prod[:, cols])).astype(jnp.bfloat16)
+
+    def summed(place, both):
+        here, mate = decoded(place)
+        mate = mate % clusters
+        acc[here] += jnp.dot(left[mate], both[...], preferred_element_type=jnp.float32)
+        back[mate] += lax.dot_general(
+            own_ref[here],
+            both[quarter:, :],
+            (((1,), (1,)), ((), ())),
+            preferred_element_type=jnp.float32,
+        )[:8]
+
+    @pl.loop(0, items[step * length])
+    def _(pair):
+        turn = 2 * pair + 1
+        summed(turn, both_a)
+        pointwise(turn + 1, dist_b, prod_b, both_b)
+        raw(turn + 2, dist_a, prod_a)
+        summed(turn + 1, both_b)
+        pointwise(turn + 2, dist_a, prod_a, both_a)
+        raw(turn + 3, dist_b, prod_b)
+
+    for coord in range(3):
+        back_ref[coord] = -0.5 * back[:, coord, :] - there[coord] * back[:, 6, :]
+    if last:
+        for coord in range(3):
+            grad_ref[coord] = (
+                acc[:, width + coord, :]
+                - pos_ref[coord].astype(jnp.float32) * acc[:, width + 3, :]
             )
-            target[here, :, cols] += jnp.dot(
-                mate_aug, weighted, preferred_element_type=jnp.float32
-            )[:8]
-            total = total + lax.dot_general(
-                own, weighted, (((1,), (1,)), ((), ())), preferred_element_type=jnp.float32
-            )
-        back[mate] += total[:8]
-
-    count = items[step * (cap + 1)]
-
-    @pl.loop(0, count // 2)
-    def _(pair):
-        one_item(2 * pair)
-        one_item(2 * pair + 1)
-
-    @pl.when(count % 2 == 1)
-    def _():
-        one_item(count - 1)
-
-    for coord in range(3):
-        value = target[:, coord, :] - pos_ref[coord].astype(jnp.float32) * target[:, 3, :]
-        if not first:
-            value = value + grad_in[coord]
-        grad_ref[coord] = value
-        back_ref[coord] = -0.5 * back[:, coord, :] - there[coord] * back[:, 6, :]
-
-
-def run_step(step, cap, items, source, cot, own, pos, carried):
+        rhs = pot_ref.shape[1]
+        pot_ref[...] = acc[:, :rhs, :]
+        pot_out_ref[...] = acc[:, rhs:width, :].astype(jnp.bfloat16)
+
+
+def run_step(step, length, items, source, cot, own, pos, rhs, carried, last):
     clusters, width, panels = cot.shape
     quarter = source.shape[1]
     first = carried is None
     vmem = pl.BlockSpec(memory_space=pltpu.VMEM)
     smem = pl.BlockSpec(memory_space=pltpu.SMEM)
-    operands = (items, source, cot, own, pos) + (() if first else carried)
-    pairs = cap * panels * quarter
+    operands = (items, source, cot, own)
+    if not first:
+        operands += (carried,)
+    acc_shape = (clusters, width + AUG, panels)
+    back_shape = jax.ShapeDtypeStruct((3, clusters, quarter), jnp.float32)
+    scratch = [
+        pltpu.VMEM((clusters, AUG, quarter), jnp.float32),
+        pltpu.VMEM((clusters, quarter, AUG), jnp.bfloat16),
+        pltpu.VMEM((clusters, quarter, width), jnp.bfloat16),
+        pltpu.VMEM((clusters, width + AUG, 2 * quarter), jnp.bfloat16),
+        pltpu.VMEM((clusters + 1, quarter, LANES), jnp.float32),
+        pltpu.VMEM((clusters, 8, quarter), jnp.float32),
+    ]
+    scratch += [pltpu.VMEM((quarter, panels), jnp.float32)] * 4
+    scratch += [pltpu.VMEM((2 * quarter, panels), jnp.bfloat16)] * 2
+    if last:
+        operands += (pos,)
+        out_shape = (
+            jax.ShapeDtypeStruct((clusters, rhs, panels), jnp.float32),
+            jax.ShapeDtypeStruct((clusters, width - rhs, panels), jnp.bfloat16),
+            jax.ShapeDtypeStruct((3, clusters, panels), jnp.float32),
+            back_shape,
+        )
+        scratch = [pltpu.VMEM(acc_shape, jnp.float32)] + scratch
+    else:
+        out_shape = (jax.ShapeDtypeStruct(acc_shape, jnp.float32), back_shape)
+    pairs = (length - 6) * panels * quarter
     return pl.pallas_call(
-        functools.partial(step_kernel, step, cap, first),
-        out_shape=(
-            jax.ShapeDtypeStruct((clusters, width, panels), jnp.float32),
-            jax.ShapeDtypeStruct((3, clusters, panels), jnp.float32),
-            jax.ShapeDtypeStruct((3, clusters, quarter), jnp.float32),
-        ),
+        functools.partial(step_kernel, step, length, first, last),
+        out_shape=out_shape,
         in_specs=[smem] + [vmem] * (len(operands) - 1),
-        out_specs=(vmem, vmem, vmem),
-        scratch_shapes=[
-            pltpu.VMEM((clusters, AUG, quarter), jnp.float32),
-            pltpu.VMEM((clusters, AUG, quarter), jnp.bfloat16),
-            pltpu.VMEM((clusters, quarter, AUG), jnp.bfloat16),
-            pltpu.VMEM((clusters, quarter, width), jnp.bfloat16),
-            pltpu.VMEM((clusters, quarter, LANES), jnp.float32),
-            pltpu.VMEM((clusters, 8, panels), jnp.float32),
-            pltpu.VMEM((clusters, 8, quarter), jnp.float32),
-        ],
+        out_specs=(vmem,) * len(out_shape),
+        scratch_shapes=scratch,
         compiler_params=pltpu.CompilerParams(vmem_limit_bytes=32 * 1024 * 1024),
         cost_estimate=pl.CostEstimate(
             flops=2 * pairs * (2 * width + 3 * AUG), bytes_accessed=6 * 2**20, transcendentals=pairs
@@ -244,7 +270,7 @@
     cap = ROUNDS * per_round
     partners = lax.dynamic_slice_in_dim(matching, device * clusters, clusters, 1).reshape(-1)
     here = jnp.tile(jnp.arange(clusters, dtype=jnp.int32), ROUNDS)
-    code = here * clusters + partners % clusters
+    code = here * (2 * clusters) + partners % clusters
     behind = (device - partners // clusters) % clus_count
     total_items = ROUNDS * clusters
     order = jnp.arange(total_items, dtype=jnp.int32)
@@ -256,9 +282,11 @@
     member = behind[None, :] == steps[:, None]
     slots = jnp.arange(cap, dtype=jnp.int32)
     chosen = member[:, None, :] & (rank[None, None, :] == slots[None, :, None])
-    listed = jnp.sum(jnp.where(chosen, code[None, None, :], 0), axis=2)
-    counts = jnp.sum(member.astype(jnp.int32), axis=1)
-    items = jnp.concatenate([counts[:, None], listed], axis=1).reshape(-1)
+    listed = jnp.sum(jnp.where(chosen, code[None, None, :] - clusters, 0), axis=2) + clusters
+    turns = (jnp.sum(member.astype(jnp.int32), axis=1) + 3) // 2
+    length = cap + 6
+    items = jnp.pad(listed, ((0, 0), (3, 3)), constant_values=clusters)
+    items = jnp.concatenate([turns[:, None], items[:, 1:]], axis=1).reshape(-1)
 
     cluster_at = jnp.arange(clusters, dtype=jnp.int32)
     first_ids = (device * clusters + cluster_at) * panels
@@ -275,6 +303,7 @@
         ],
         axis=0,
     )
+    local, source = lax.optimization_barrier((local, source))
     found = [local] + [shifted(local, "sub", step) for step in range(1, sub_count)]
     whole = jnp.concatenate(
         [
@@ -299,12 +328,38 @@
     )(pos)
 
     carried = None
+    backs = []
+    for step in range(1, clus_count):
+        if step > 2:
+            source, backs[step - 3] = lax.optimization_barrier((source, backs[step - 3]))
+        source = shifted(source, "clus", 1)
+        last = step == clus_count - 1
+        results = run_step(step - 1, length, items, source, cot, own, pos, rhs, carried, last)
+        if last:
+            pot, pot_out, grad, back = results
+        else:
+            carried, back = results
+        backs.append(back)
     returned = jnp.zeros((3, clusters, quarter), jnp.float32)
     for step in range(1, clus_count):
-        source = shifted(source, "clus", 1)
-        pot, grad, back = run_step(step - 1, cap, items, source, cot, own, pos, carried)
-        carried = (pot, grad)
-        returned = returned + shifted(back, "clus", -step)
+        returned = returned + shifted(backs[step - 1], "clus", -step)
+
+    half = pot
+    for step in range(1, rhs_count):
+        arrived = shifted(pot_out[:, (step - 1) * rhs : step * rhs], "rhs", -step)
+        half = half + arrived.astype(jnp.float32)
+    half, returned = lax.optimization_barrier((half, returned))
+
+    def panels_of(array, place):
+        return pick(
+            place % sub_count,
+            [array[..., at * row_count : (at + 1) * row_count] for at in range(sub_count)],
+        )
+
+    potential = panels_of(half, sub_place)
+    for step in range(1, sub_count):
+        sent = panels_of(half, sub_place + step).astype(jnp.bfloat16)
+        potential = potential + shifted(sent, "sub", step).astype(jnp.float32)
 
     at = sub_place * row_count + core * quarter
     own_part = lax.dynamic_slice_in_dim(grad, at, quarter, 2) + returned
@@ -323,6 +378,7 @@
     gathered = summed
     for step in range(1, rhs_count):
         gathered = gathered + shifted(summed, "rhs", step)
+    gathered, potential = lax.optimization_barrier((gathered, potential))
     main, rims = pl.pallas_call(
         node_kernel,
         out_shape=(
@@ -339,20 +395,6 @@
     node_grad = jnp.concatenate(
         [main[:, :LANES] + from_below, main[:, LANES:-LANES], main[:, -LANES:] + from_above], axis=1
     )
-
-    half = pot[:, :rhs]
-    for step in range(1, rhs_count):
-        half = half + shifted(pot[:, step * rhs : (step + 1) * rhs], "rhs", -step)
-
-    def panels_of(array, place):
-        return pick(
-            place % sub_count,
-            [array[..., at * row_count : (at + 1) * row_count] for at in range(sub_count)],
-        )
-
-    potential = panels_of(half, sub_place)
-    for step in range(1, sub_count):
-        potential = potential + shifted(panels_of(half, sub_place + step), "sub", step)
     return (potential.astype(jnp.bfloat16), node_grad)
 
 

time: 106 us -> 71.6 us (0.68)
  Pallas kernels: 41.2 us -> 24.1 us
  waiting for transfers between devices: 40.7 us -> 23.9 us
    pallas_call x3, Pallas kernels: 40.5 us -> 23.4 us  [run_step(): pl.pallas_call(functools.partial(step_kernel, step, length, first, last),...]
    ppermute x15, waiting for transfers between devices: 40.7 us -> 23.9 us  [shifted(): return lax.ppermute(value, axis, pairs)]
  transfers between devices with their start and end apart: 15 -> 15, of which waited for: 8 -> 11; matrix products, arithmetic and copies ran while one was open for 5% -> 6% of each run, Pallas kernels for 39% -> 22%
where the time goes in v2:
time: 71.6 us; the launch traced here: 71.4 us
  Pallas kernels  24.1 us (34%)
  waiting for transfers between devices  23.9 us (33%)
  starting transfers between devices  15.7 us (22%)
  other arithmetic  5.42 us (8%)
  local copies, waits for them, and re-layouts  1.36 us (2%)
  between operations  0.95 us (1%)
    ppermute x15, waiting for transfers between devices, shifted(): return lax.ppermute(value, axis, pairs)  23.9 us
    pallas_call x3, Pallas kernels, run_step(): pl.pallas_call(functools.partial(step_kernel, step, length, first, last),...  23.4 us
    ppermute x15, starting transfers between devices, shifted(): return lax.ppermute(value, axis, pairs)  15.7 us
    select_n x5, other arithmetic, pick(): out = jnp.where(index == place, choices[place], out)  1.8 us
  transfers between devices with their start and end apart: 15, of which 11 were waited for; matrix products, arithmetic and copies ran while one was open for 6% of the time, Pallas kernels for 22%

profile of v2, /device:TPU:0, one launch (start us, length us, event | category | flops | bytes accessed | tf_op | source)
XLA Modules:
  0.0 71.4 jit_solution(3804969976072406955)
XLA Ops:
  0.6 0.0 copy-start
  0.7 1.0 %broadcast_select_fusion.3 = (bf16[16,32,128]{2,1,0:T(8,128)(2,1)S(1)}, bf16[16,32,128]{2,1,0:T(8,128)(2,1)S(1)}) fusion(pred[]{:T(512)S(6)} %eq.94, bf16[16,32,256]{2,1,0:T(8,128)(2,1)} %param.8, pred[]{:T(512)S(6)} %eq.95), kind=kLoop, calls=%fused_computation.15 | loop fusion | flops 131072 | bytes 524290 | tf_op jit(solution)/shard_map/jit(_where)/select_n | solution.py:37
  1.7 0.5 collective-permute-start
  2.2 0.0 copy-done
  2.2 0.1 constant_dynamic-slice_fusion
  2.3 0.1 reshape.254
  2.4 0.1 mul.34
  2.5 0.2 convert_reduce_fusion
  2.7 0.2 convert_reduce_fusion.1
  2.9 0.9 %slice.73 = s32[16,1,256]{2,1,0:T(1,128)S(1)} slice(s32[16,4,256]{2,1,0:T(4,128)} %param.11), slice={[0:16], [0:1], [0:256]} | slice | bytes 32768 | tf_op jit(solution)/shard_map/slice | solution.py:297
  3.7 0.1 fusion.5
  3.8 0.7 %fusion.7 = bf16[4,16,128]{2,1,0:T(8,128)(2,1)S(1)} fusion(bf16[3,16,256]{2,1,0:T(8,128)(2,1)} %bitcast.31, bf16[1,16,256]{2,1,0:T(8,128)(2,1)} %bitcast.34, pred[]{:T(512)S(6)} %eq.94), kind=kLoop, calls=%fused_computation.35 | loop fusion | flops 73728 | bytes 49153 | tf_op jit(solution)/shard_map/jit(_where)/select_n | solution.py:37
  4.6 0.1 copy.10
  4.7 1.0 %pad_maximum_fusion.1 = bf16[576,256]{1,0:T(8,128)(2,1)S(1)} fusion(bf16[16,256]{1,0:T(8,128)(2,1)S(1)} %fusion.5, bf16[48,256]{1,0:T(8,128)(2,1)} %bitcast.32, bf16[512,256]{1,0:T(8,128)(2,1)} %bitcast.30), kind=kLoop, calls=%fused_computation.9 | loop fusion | flops 884736 | bytes 589824 | tf_op jit(solution)/shard_map/concatenate | solution.py:298
  5.7 0.0 collective-permute-done
  5.7 2.6 %collective-permute-start.3 = (bf16[576,256]{1,0:T(8,128)(2,1)S(1)}, bf16[576,256]{1,0:T(8,128)(2,1)S(1)}, u32[]{:S(2)}, u32[]{:S(2)}) collective-permute-start(bf16[576,256]{1,0:T(8,128)(2,1)S(1)} %pad_maximum_fusion.1), channel_id=1, source_target_pairs={{0,2},{2,0},{1,3},{3,1},{4,6},{6,4},{5,7},{7,5},{8,10},{10,8},{9,1... | collective-permute-start | bytes 884744 | tf_op jit(solution)/shard_map/ppermute | solution.py:22
  8.3 0.1 select_reduce_fusion
  8.5 1.6 %collective-permute-start.1 = (bf16[1088,128]{1,0:T(8,128)(2,1)S(1)}, bf16[1088,128]{1,0:T(8,128)(2,1)S(1)}, u32[]{:S(2)}, u32[]{:S(2)}) collective-permute-start(bf16[1088,128]{1,0:T(8,128)(2,1)S(1)} %pad_maximum_fusion.2), channel_id=1, source_target_pairs={{0,4},{4,8},{8,12},{12,0},{1,5},{5,9},{9,13},{13,1},{2,6},{6,10},{... | collective-permute-start | bytes 835592 | tf_op jit(solution)/shard_map/ppermute | solution.py:22
  10.1 5.9 %collective-permute-done.3 = bf16[576,256]{1,0:T(8,128)(2,1)S(1)} collective-permute-done((bf16[576,256]{1,0:T(8,128)(2,1)S(1)}, bf16[576,256]{1,0:T(8,128)(2,1)S(1)}, u32[]{:S(2)}, u32[]{:S(2)}) %collective-permute-start.3) | collective-permute-done | bytes 294944 | tf_op jit(solution)/shard_map/ppermute | solution.py:22
  16.1 0.1 collective-permute-start.4
  16.2 0.1 pad_slice_fusion.6
  16.2 0.1 pad_add_fusion
  16.3 0.1 reshape.255.refs_0_
  16.4 2.8 %collective-permute-done.1.refs_1_ = bf16[1088,128]{1,0:T(8,128)(2,1)S(1)} collective-permute-done((bf16[1088,128]{1,0:T(8,128)(2,1)S(1)}, bf16[1088,128]{1,0:T(8,128)(2,1)S(1)}, u32[]{:S(2)}, u32[]{:S(2)}) %collective-permute-start.1) | collective-permute-done | bytes 278560 | tf_op jit(solution)/shard_map/ppermute | solution.py:22
  19.2 0.0 collective-permute-start.2
  19.2 0.1 target_rows.1.refs_3_
  19.3 0.0 collective-permute-done.4
  19.3 0.1 pad_maximum_fusion.refs_2_
  19.4 7.7 %near_field_0.1 = (f32[16,80,512]{2,1,0:T(8,128)S(1)}, f32[3,16,128]{2,1,0:T(8,128)S(1)}) custom-call(s32[108]{0:T(128)S(1)} %reshape.255.refs_0_, bf16[1088,128]{1,0:T(8,128)(2,1)S(1)} %collective-permute-done.1.refs_1_, bf16[16,64,512]{2,1,0:T(8,128)(2,1)S(1)} %pad_maximum_fusion.refs_2_, bf16[16,16,512]{2,1,0:T(8,128)(2,1)S(1)} %target_rows.1.refs_3_), custom_call_target="tpu_custom_call" | custom-call | flops 692060160 | bytes 6291456 | tf_op jit(solution)/shard_map/near_field_0/pallas_call | solution.py:186
  27.1 1.9 %collective-permute-done.2.refs_1_ = bf16[1088,128]{1,0:T(8,128)(2,1)S(1)} collective-permute-done((bf16[1088,128]{1,0:T(8,128)(2,1)S(1)}, bf16[1088,128]{1,0:T(8,128)(2,1)S(1)}, u32[]{:S(2)}, u32[]{:S(2)}) %collective-permute-start.2) | collective-permute-done | bytes 278560 | tf_op jit(solution)/shard_map/ppermute | solution.py:22
  29.0 0.0 collective-permute-start.5
  29.0 8.0 %near_field_1.1 = (f32[16,80,512]{2,1,0:T(8,128)S(1)}, f32[3,16,128]{2,1,0:T(8,128)S(1)}) custom-call(s32[108]{0:T(128)S(1)} %reshape.255.refs_0_, bf16[1088,128]{1,0:T(8,128)(2,1)S(1)} %collective-permute-done.2.refs_1_, bf16[16,64,512]{2,1,0:T(8,128)(2,1)S(1)} %pad_maximum_fusion.refs_2_, bf16[16,16,512]{2,1,0:T(8,128)(2,1)S(1)} %target_rows.1.refs_3_, ...), custom_call_target="tpu_custom_call" | custom-call | flops 692060160 | bytes 6291456 | tf_op jit(solution)/shard_map/near_field_1/pallas_call | solution.py:186
  37.0 0.9 %collective-permute-done.5.refs_1_ = bf16[1088,128]{1,0:T(8,128)(2,1)S(1)} collective-permute-done((bf16[1088,128]{1,0:T(8,128)(2,1)S(1)}, bf16[1088,128]{1,0:T(8,128)(2,1)S(1)}, u32[]{:S(2)}, u32[]{:S(2)}) %collective-permute-start.5) | collective-permute-done | bytes 278560 | tf_op jit(solution)/shard_map/ppermute | solution.py:22
  37.8 7.7 %near_field_2.1 = (f32[16,32,512]{2,1,0:T(8,128)S(1)}, bf16[16,32,512]{2,1,0:T(8,128)(2,1)S(1)}, f32[3,16,512]{2,1,0:T(8,128)S(1)}, f32[3,16,128]{2,1,0:T(8,128)S(1)}) custom-call(s32[108]{0:T(128)S(1)} %reshape.255.refs_0_, bf16[1088,128]{1,0:T(8,128)(2,1)S(1)} %collective-permute-done.5.refs_1_, bf16[16,64,512]{2,1,0:T(8,128)(2,1)S(1)} %pad_maximum_fusion.refs_2_, ...), custom_call_target="tpu_custom_call" | custom-call | flops 692060160 | bytes 6291456 | tf_op jit(solution)/shard_map/near_field_2/pallas_call | solution.py:186
  45.6 0.1 collective-permute-start.6
  45.7 3.0 %collective-permute-start.7 = (f32[3,16,128]{2,1,0:T(8,128)S(1)}, f32[3,16,128]{2,1,0:T(8,128)S(1)}, u32[]{:S(2)}, u32[]{:S(2)}) collective-permute-start(f32[3,16,128]{2,1,0:T(8,128)S(1)} %get-tuple-element.29), channel_id=1, source_target_pairs={{0,12},{4,0},{8,4},{12,8},{1,13},{5,1},{9,5},{13,9},{2,14},{6,2},{... | collective-permute-start | bytes 73736 | tf_op jit(solution)/shard_map/ppermute | solution.py:22
  48.7 0.0 collective-permute-start.8
  48.7 0.8 %collective-permute-start.9 = (f32[3,16,128]{2,1,0:T(8,128)S(1)}, f32[3,16,128]{2,1,0:T(8,128)S(1)}, u32[]{:S(2)}, u32[]{:S(2)}) collective-permute-start(f32[3,16,128]{2,1,0:T(8,128)S(1)} %get-tuple-element.31), channel_id=1, source_target_pairs={{0,4},{4,8},{8,12},{12,0},{1,5},{5,9},{9,13},{13,1},{2,6},{6,10},{... | collective-permute-start | bytes 73736 | tf_op jit(solution)/shard_map/ppermute | solution.py:22
  49.5 0.7 %collective-permute-done.7 = f32[3,16,128]{2,1,0:T(8,128)S(1)} collective-permute-done((f32[3,16,128]{2,1,0:T(8,128)S(1)}, f32[3,16,128]{2,1,0:T(8,128)S(1)}, u32[]{:S(2)}, u32[]{:S(2)}) %collective-permute-start.7) | collective-permute-done | bytes 24608 | tf_op jit(solution)/shard_map/ppermute | solution.py:22
  50.2 3.4 %collective-permute-done.8 = f32[3,16,128]{2,1,0:T(8,128)S(1)} collective-permute-done((f32[3,16,128]{2,1,0:T(8,128)S(1)}, f32[3,16,128]{2,1,0:T(8,128)S(1)}, u32[]{:S(2)}, u32[]{:S(2)}) %collective-permute-start.8) | collective-permute-done | bytes 24608 | tf_op jit(solution)/shard_map/ppermute | solution.py:22
  53.7 0.6 collective-permute-done.9
  54.3 0.0 collective-permute-done.6
  54.3 0.2 convert_add_fusion
  54.6 0.8 %collective-permute-start.10 = (f32[3,8,512]{2,1,0:T(8,128)S(1)}, f32[3,8,512]{2,1,0:T(8,128)S(1)}, u32[]{:S(2)}, u32[]{:S(2)}) collective-permute-start(f32[3,8,512]{2,1,0:T(8,128)S(1)} %slice_select_fusion), channel_id=1, source_target_pairs={{0,2},{2,0},{1,3},{3,1},{4,6},{6,4},{5,7},{7,5},{8,10},{10,8},{9,1... | collective-permute-start | bytes 147464 | tf_op jit(solution)/shard_map/ppermute | solution.py:22
  55.4 1.3 %collective-permute-start.12 = (bf16[16,32,256]{2,1,0:T(8,128)(2,1)S(1)}, bf16[16,32,256]{2,1,0:T(8,128)(2,1)S(1)}, u32[]{:S(2)}, u32[]{:S(2)}) collective-permute-start(bf16[16,32,256]{2,1,0:T(8,128)(2,1)S(1)} %select_convert_fusion), channel_id=1, source_target_pairs={{0,2},{2,0},{1,3},{3,1},{4,6},{6,4},{5,7},{7,5},{8,10},{10,8},{9,1... | collective-permute-start | bytes 786440 | tf_op jit(solution)/shard_map/ppermute | solution.py:22
  56.8 2.5 %collective-permute-done.10 = f32[3,8,512]{2,1,0:T(8,128)S(1)} collective-permute-done((f32[3,8,512]{2,1,0:T(8,128)S(1)}, f32[3,8,512]{2,1,0:T(8,128)S(1)}, u32[]{:S(2)}, u32[]{:S(2)}) %collective-permute-start.10) | collective-permute-done | bytes 49184 | tf_op jit(solution)/shard_map/ppermute | solution.py:22
  59.3 0.1 collective-permute-start.11
  59.4 1.2 %collective-permute-done.11 = f32[3,8,512]{2,1,0:T(8,128)S(1)} collective-permute-done((f32[3,8,512]{2,1,0:T(8,128)S(1)}, f32[3,8,512]{2,1,0:T(8,128)S(1)}, u32[]{:S(2)}, u32[]{:S(2)}) %collective-permute-start.11) | collective-permute-done | bytes 49184 | tf_op jit(solution)/shard_map/ppermute | solution.py:22
  60.6 2.5 %collective-permute-done.12 = bf16[16,32,256]{2,1,0:T(8,128)(2,1)S(1)} collective-permute-done((bf16[16,32,256]{2,1,0:T(8,128)(2,1)S(1)}, bf16[16,32,256]{2,1,0:T(8,128)(2,1)S(1)}, u32[]{:S(2)}, u32[]{:S(2)}) %collective-permute-start.12) | collective-permute-done | bytes 262176 | tf_op jit(solution)/shard_map/ppermute | solution.py:22
  63.1 0.8 %convert_add_fusion.1 = bf16[16,32,256]{2,1,0:T(8,128)(2,1)} fusion(bf16[16,32,256]{2,1,0:T(8,128)(2,1)S(1)} %collective-permute-done.12, f32[16,32,512]{2,1,0:T(8,128)S(1)} %convert_add_fusion, pred[]{:T(512)S(6)} %eq.84), kind=kLoop, calls=%fused_computation.7 | loop fusion | flops 524288 | bytes 1572865 | tf_op jit(solution)/shard_map/add | solution.py:362
  63.9 0.5 node_terms.1
  64.4 1.3 %collective-permute-start.13 = (f32[8,128]{1,0:T(8,128)S(1)}, f32[8,128]{1,0:T(8,128)S(1)}, u32[]{:S(2)}, u32[]{:S(2)}) collective-permute-start(f32[8,128]{1,0:T(8,128)S(1)} %get-tuple-element.46), channel_id=1, source_target_pairs={{0,2},{2,4},{4,6},{6,8},{8,10},{10,12},{12,14},{14,0},{1,3},{3,5},... | collective-permute-start | bytes 12296 | tf_op jit(solution)/shard_map/ppermute | solution.py:22
  65.7 3.5 %collective-permute-start.14 = (f32[8,128]{1,0:T(8,128)S(1)}, f32[8,128]{1,0:T(8,128)S(1)}, u32[]{:S(2)}, u32[]{:S(2)}) collective-permute-start(f32[8,128]{1,0:T(8,128)S(1)} %get-tuple-element.47), channel_id=1, source_target_pairs={{0,14},{2,0},{4,2},{6,4},{8,6},{10,8},{12,10},{14,12},{1,15},{3,1}... | collective-permute-start | bytes 12296 | tf_op jit(solution)/shard_map/ppermute | solution.py:22
  69.2 1.6 %collective-permute-done.13 = f32[8,128]{1,0:T(8,128)S(1)} collective-permute-done((f32[8,128]{1,0:T(8,128)S(1)}, f32[8,128]{1,0:T(8,128)S(1)}, u32[]{:S(2)}, u32[]{:S(2)}) %collective-permute-start.13) | collective-permute-done | bytes 4128 | tf_op jit(solution)/shard_map/ppermute | solution.py:22
  70.8 0.0 collective-permute-done.14
  70.8 0.6 pad_maximum_fusion.4
  (25 shorter events, 0.3 us)
Async XLA Ops:
  0.6 1.6 %copy-start = (s32[5,64]{1,0:T(8,128)S(1)}, s32[5,64]{1,0:T(8,128)}, u32[]{:S(2)}) copy-start(s32[5,64]{1,0:T(8,128)} %param.10) | copy-start | bytes 3844
  1.7 4.0 %collective-permute-start = (bf16[16,32,128]{2,1,0:T(8,128)(2,1)S(1)}, bf16[16,32,128]{2,1,0:T(8,128)(2,1)S(1)}, u32[]{:S(2)}, u32[]{:S(2)}) collective-permute-start(bf16[16,32,128]{2,1,0:T(8,128)(2,1)S(1)} %get-tuple-element.43), channel_id=1, source_target_pairs={{0,1},{1,0},{2,3},{3,2},{4,5},{5,4},{6,7},{7,6},{8,9},{9,8},{10,11... | collective-permute-start | bytes 393224 | tf_op jit(solution)/shard_map/ppermute | solution.py:22
  5.7 10.2 %collective-permute-start.3 = (bf16[576,256]{1,0:T(8,128)(2,1)S(1)}, bf16[576,256]{1,0:T(8,128)(2,1)S(1)}, u32[]{:S(2)}, u32[]{:S(2)}) collective-permute-start(bf16[576,256]{1,0:T(8,128)(2,1)S(1)} %pad_maximum_fusion.1), channel_id=1, source_target_pairs={{0,2},{2,0},{1,3},{3,1},{4,6},{6,4},{5,7},{7,5},{8,10},{10,8},{9,1... | collective-permute-start | bytes 884744 | tf_op jit(solution)/shard_map/ppermute | solution.py:22
  8.5 10.7 %collective-permute-start.1 = (bf16[1088,128]{1,0:T(8,128)(2,1)S(1)}, bf16[1088,128]{1,0:T(8,128)(2,1)S(1)}, u32[]{:S(2)}, u32[]{:S(2)}) collective-permute-start(bf16[1088,128]{1,0:T(8,128)(2,1)S(1)} %pad_maximum_fusion.2), channel_id=1, source_target_pairs={{0,4},{4,8},{8,12},{12,0},{1,5},{5,9},{9,13},{13,1},{2,6},{6,10},{... | collective-permute-start | bytes 835592 | tf_op jit(solution)/shard_map/ppermute | solution.py:22
  16.1 3.2 %collective-permute-start.4 = (bf16[16,32,512]{2,1,0:T(8,128)(2,1)S(1)}, bf16[16,32,512]{2,1,0:T(8,128)(2,1)S(1)}, u32[]{:S(2)}, u32[]{:S(2)}) collective-permute-start(bf16[16,32,512]{2,1,0:T(8,128)(2,1)S(1)} %bitcast.27), channel_id=1, source_target_pairs={{0,1},{1,0},{2,3},{3,2},{4,5},{5,4},{6,7},{7,6},{8,9},{9,8},{10,11... | collective-permute-start | bytes 1572872 | tf_op jit(solution)/shard_map/ppermute | solution.py:22
  19.2 9.8 %collective-permute-start.2 = (bf16[1088,128]{1,0:T(8,128)(2,1)S(1)}, bf16[1088,128]{1,0:T(8,128)(2,1)S(1)}, u32[]{:S(2)}, u32[]{:S(2)}) collective-permute-start(bf16[1088,128]{1,0:T(8,128)(2,1)S(1)} %collective-permute-done.1.refs_1_), channel_id=1, source_target_pairs={{0,4},{4,8},{8,12},{12,0},{1,5},{5,9},{9,13},{13,1},{2,6},{6,10},{... | collective-permute-start | bytes 835592 | tf_op jit(solution)/shard_map/ppermute | solution.py:22
  29.0 8.9 %collective-permute-start.5 = (bf16[1088,128]{1,0:T(8,128)(2,1)S(1)}, bf16[1088,128]{1,0:T(8,128)(2,1)S(1)}, u32[]{:S(2)}, u32[]{:S(2)}) collective-permute-start(bf16[1088,128]{1,0:T(8,128)(2,1)S(1)} %collective-permute-done.2.refs_1_), channel_id=1, source_target_pairs={{0,4},{4,8},{8,12},{12,0},{1,5},{5,9},{9,13},{13,1},{2,6},{6,10},{... | collective-permute-start | bytes 835592 | tf_op jit(solution)/shard_map/ppermute | solution.py:22
  45.6 8.7 %collective-permute-start.6 = (bf16[16,32,512]{2,1,0:T(8,128)(2,1)S(1)}, bf16[16,32,512]{2,1,0:T(8,128)(2,1)S(1)}, u32[]{:S(2)}, u32[]{:S(2)}) collective-permute-start(bf16[16,32,512]{2,1,0:T(8,128)(2,1)S(1)} %get-tuple-element.28), channel_id=1, source_target_pairs={{0,1},{1,0},{2,3},{3,2},{4,5},{5,4},{6,7},{7,6},{8,9},{9,8},{10,11... | collective-permute-start | bytes 1572872 | tf_op jit(solution)/shard_map/ppermute | solution.py:22
  45.7 4.6 %collective-permute-start.7 = (f32[3,16,128]{2,1,0:T(8,128)S(1)}, f32[3,16,128]{2,1,0:T(8,128)S(1)}, u32[]{:S(2)}, u32[]{:S(2)}) collective-permute-start(f32[3,16,128]{2,1,0:T(8,128)S(1)} %get-tuple-element.29), channel_id=1, source_target_pairs={{0,12},{4,0},{8,4},{12,8},{1,13},{5,1},{9,5},{13,9},{2,14},{6,2},{... | collective-permute-start | bytes 73736 | tf_op jit(solution)/shard_map/ppermute | solution.py:22
  48.7 5.0 %collective-permute-start.8 = (f32[3,16,128]{2,1,0:T(8,128)S(1)}, f32[3,16,128]{2,1,0:T(8,128)S(1)}, u32[]{:S(2)}, u32[]{:S(2)}) collective-permute-start(f32[3,16,128]{2,1,0:T(8,128)S(1)} %get-tuple-element.30), channel_id=1, source_target_pairs={{0,8},{4,12},{8,0},{12,4},{1,9},{5,13},{9,1},{13,5},{2,10},{6,14},... | collective-permute-start | bytes 73736 | tf_op jit(solution)/shard_map/ppermute | solution.py:22
  48.7 5.6 %collective-permute-start.9 = (f32[3,16,128]{2,1,0:T(8,128)S(1)}, f32[3,16,128]{2,1,0:T(8,128)S(1)}, u32[]{:S(2)}, u32[]{:S(2)}) collective-permute-start(f32[3,16,128]{2,1,0:T(8,128)S(1)} %get-tuple-element.31), channel_id=1, source_target_pairs={{0,4},{4,8},{8,12},{12,0},{1,5},{5,9},{9,13},{13,1},{2,6},{6,10},{... | collective-permute-start | bytes 73736 | tf_op jit(solution)/shard_map/ppermute | solution.py:22
  54.6 4.7 %collective-permute-start.10 = (f32[3,8,512]{2,1,0:T(8,128)S(1)}, f32[3,8,512]{2,1,0:T(8,128)S(1)}, u32[]{:S(2)}, u32[]{:S(2)}) collective-permute-start(f32[3,8,512]{2,1,0:T(8,128)S(1)} %slice_select_fusion), channel_id=1, source_target_pairs={{0,2},{2,0},{1,3},{3,1},{4,6},{6,4},{5,7},{7,5},{8,10},{10,8},{9,1... | collective-permute-start | bytes 147464 | tf_op jit(solution)/shard_map/ppermute | solution.py:22
  55.4 7.6 %collective-permute-start.12 = (bf16[16,32,256]{2,1,0:T(8,128)(2,1)S(1)}, bf16[16,32,256]{2,1,0:T(8,128)(2,1)S(1)}, u32[]{:S(2)}, u32[]{:S(2)}) collective-permute-start(bf16[16,32,256]{2,1,0:T(8,128)(2,1)S(1)} %select_convert_fusion), channel_id=1, source_target_pairs={{0,2},{2,0},{1,3},{3,1},{4,6},{6,4},{5,7},{7,5},{8,10},{10,8},{9,1... | collective-permute-start | bytes 786440 | tf_op jit(solution)/shard_map/ppermute | solution.py:22
  59.3 1.3 %collective-permute-start.11 = (f32[3,8,512]{2,1,0:T(8,128)S(1)}, f32[3,8,512]{2,1,0:T(8,128)S(1)}, u32[]{:S(2)}, u32[]{:S(2)}) collective-permute-start(f32[3,8,512]{2,1,0:T(8,128)S(1)} %select_add_fusion), channel_id=1, source_target_pairs={{0,1},{1,0},{2,3},{3,2},{4,5},{5,4},{6,7},{7,6},{8,9},{9,8},{10,11... | collective-permute-start | bytes 147464 | tf_op jit(solution)/shard_map/ppermute | solution.py:22
  64.4 6.4 %collective-permute-start.13 = (f32[8,128]{1,0:T(8,128)S(1)}, f32[8,128]{1,0:T(8,128)S(1)}, u32[]{:S(2)}, u32[]{:S(2)}) collective-permute-start(f32[8,128]{1,0:T(8,128)S(1)} %get-tuple-element.46), channel_id=1, source_target_pairs={{0,2},{2,4},{4,6},{6,8},{8,10},{10,12},{12,14},{14,0},{1,3},{3,5},... | collective-permute-start | bytes 12296 | tf_op jit(solution)/shard_map/ppermute | solution.py:22
  65.7 5.1 %collective-permute-start.14 = (f32[8,128]{1,0:T(8,128)S(1)}, f32[8,128]{1,0:T(8,128)S(1)}, u32[]{:S(2)}, u32[]{:S(2)}) collective-permute-start(f32[8,128]{1,0:T(8,128)S(1)} %get-tuple-element.47), channel_id=1, source_target_pairs={{0,14},{2,0},{4,2},{6,4},{8,6},{10,8},{12,10},{14,12},{1,15},{3,1}... | collective-permute-start | bytes 12296 | tf_op jit(solution)/shard_map/ppermute | solution.py:22

commit v3 on v2

--- a/solution.py
+++ b/solution.py
@@ -20,6 +20,18 @@
     count = lax.axis_size(axis)
     pairs = [(source, (source + steps) % count) for source in range(count)]
     return lax.ppermute(value, axis, pairs)
+
+
+def moved(value, axes, target):
+    counts = [lax.axis_size(axis) for axis in axes]
+    pairs = []
+    for major in range(counts[0]):
+        for minor in range(counts[1]):
+            goal = target(major, minor)
+            if goal is not None:
+                to_major, to_minor = goal[0] % counts[0], goal[1] % counts[1]
+                pairs.append((major * counts[1] + minor, to_major * counts[1] + to_minor))
+    return lax.ppermute(value, axes, pairs)
 
 
 def three_parts(value):
@@ -49,7 +61,7 @@
     aug_ref[...] = aug32[...].astype(jnp.bfloat16)
 
 
-def step_kernel(step, length, first, last, *refs):
+def step_kernel(step, length, rhs, first, last, *refs):
     items, source_ref, cot_ref, own_ref = refs[:4]
     refs = refs[4:]
     if not first:
@@ -64,7 +76,8 @@
     aug32, aug_t, dens_t, left, weight, back, dist_a, dist_b, prod_a, prod_b, both_a, both_b = refs
     clusters, width, panels = cot_ref.shape
     quarter = source_ref.shape[1]
-    base = clusters * width
+    base = clusters * rhs
+    starts = [0] + list(range(base + 4 * clusters, source_ref.shape[0], base))
 
     there = [
         source_ref[base + coord * clusters : base + (coord + 1) * clusters, :].astype(jnp.float32)
@@ -82,7 +95,9 @@
         rows = aug32[cluster]
         left[cluster, width:, quarter:] = rows.astype(jnp.bfloat16)
         aug_t[cluster] = rows.T.astype(jnp.bfloat16)
-        dens = source_ref[cluster * width : (cluster + 1) * width, :]
+        dens = jnp.concatenate(
+            [source_ref[at + cluster * rhs : at + (cluster + 1) * rhs, :] for at in starts], axis=0
+        )
         left[cluster, :width, :quarter] = dens
         dens_t[cluster] = dens.T
         weight[cluster] = jnp.broadcast_to(weight_t[:, cluster : cluster + 1], (quarter, LANES))
@@ -145,7 +160,6 @@
                 acc[:, width + coord, :]
                 - pos_ref[coord].astype(jnp.float32) * acc[:, width + 3, :]
             )
-        rhs = pot_ref.shape[1]
         pot_ref[...] = acc[:, :rhs, :]
         pot_out_ref[...] = acc[:, rhs:width, :].astype(jnp.bfloat16)
 
@@ -184,7 +198,7 @@
         out_shape = (jax.ShapeDtypeStruct(acc_shape, jnp.float32), back_shape)
     pairs = (length - 6) * panels * quarter
     return pl.pallas_call(
-        functools.partial(step_kernel, step, length, first, last),
+        functools.partial(step_kernel, step, length, rhs, first, last),
         out_shape=out_shape,
         in_specs=[smem] + [vmem] * (len(operands) - 1),
         out_specs=(vmem,) * len(out_shape),
@@ -197,27 +211,34 @@
     )(*operands)
 
 
-def node_kernel(grad_ref, jitter_ref, main_ref, rims_ref):
+def node_kernel(grad_ref, jitter_ref, edge_ref, edge_jitter_ref, main_ref, rims_ref):
     clusters, panels = jitter_ref.shape
     wide = panels + 2 * LANES
-    jitter = jitter_ref[...]
-    side = jnp.zeros((clusters, LANES), jnp.float32)
-    row_at = lax.broadcasted_iota(jnp.int32, (clusters, LANES), 0)
-    rims_ref[...] = jnp.zeros(rims_ref.shape, jnp.float32)
-    for coord in range(3):
-        terms = 0.25 * grad_ref[coord]
-        spread = jnp.zeros((clusters, wide), jnp.float32)
+
+    def spread_of(terms, jitter):
+        side = jnp.zeros((terms.shape[0], LANES), jnp.float32)
+        terms = 0.25 * terms
+        spread = jnp.zeros((terms.shape[0], wide), jnp.float32)
         for offset in range(-jitter_reach, jitter_reach + 1):
             masked = jnp.where(jitter == offset, terms, 0.0)
             masked = jnp.concatenate([side, masked, side], axis=1)
             spread = spread + pltpu.roll(masked, offset % wide, 1)
         spread = spread + pltpu.roll(spread, 1, 1)
-        spread = spread + pltpu.roll(spread, 32, 1)
+        return spread + pltpu.roll(spread, 32, 1)
+
+    jitter = jitter_ref[...]
+    row_at = lax.broadcasted_iota(jnp.int32, (clusters, LANES), 0)
+    rims_ref[...] = jnp.zeros(rims_ref.shape, jnp.float32)
+    edge = spread_of(edge_ref[...], edge_jitter_ref[...])
+    for coord in range(3):
+        spread = spread_of(grad_ref[coord], jitter)
         below = spread[:, :LANES]
         above = spread[:, LANES + panels :]
         inner = spread[:, LANES : LANES + panels]
-        first = jnp.where(row_at == 0, 0.0, pltpu.roll(above, 1, 0))
-        last = jnp.where(row_at == clusters - 1, 0.0, pltpu.roll(below, clusters - 1, 0))
+        before = edge[coord : coord + 1, LANES + panels :]
+        after = edge[3 + coord : 4 + coord, :LANES]
+        first = jnp.where(row_at == 0, before, pltpu.roll(above, 1, 0))
+        last = jnp.where(row_at == clusters - 1, after, pltpu.roll(below, clusters - 1, 0))
         inner = jnp.concatenate(
             [
                 inner[:, :LANES] + first,
@@ -232,6 +253,13 @@
             ]
         rims_ref[0, coord : coord + 1, :] = below[:1]
         rims_ref[1, coord : coord + 1, :] = above[clusters - 1 :]
+
+
+def sum_kernel(*refs):
+    total = refs[0][...]
+    for ref in refs[1:-1]:
+        total = total + ref[...].astype(jnp.float32)
+    refs[-1][...] = total.astype(jnp.bfloat16)
 
 
 def on_device(positions, areas, density, cotangent, matching, connect):
@@ -253,18 +281,22 @@
             [array[..., at * quarter : (at + 1) * quarter] for at in range(rhs_count)],
         )
 
-    blocks = [part_of(density, core)]
-    for step in range(1, rhs_count):
-        blocks.append(shifted(part_of(density, core + step), "rhs", step))
     by_coord = jnp.transpose(positions, (1, 0, 2))
     placed = jnp.concatenate([by_coord, areas[None]], axis=0)
-    source = jnp.concatenate(
+    first_part = jnp.concatenate(
         [
-            jnp.concatenate(blocks, axis=1).reshape(clusters * width, quarter),
+            part_of(density, core).reshape(clusters * rhs, quarter),
             part_of(placed, core).reshape(4 * clusters, quarter),
         ],
         axis=0,
     )
+    arrived = [shifted(first_part, "clus", 1)]
+    for step in range(1, rhs_count):
+        other_part = part_of(density, core + step).reshape(clusters * rhs, quarter)
+        arrived.append(
+            moved(other_part, ("clus", "rhs"), lambda z, c, step=step: (z + 1, c + step))
+        )
+    source = jnp.concatenate(arrived, axis=0)
 
     per_round = 2 * ((clusters // 2 + clus_count - 2) // (clus_count - 1))
     cap = ROUNDS * per_round
@@ -303,7 +335,6 @@
         ],
         axis=0,
     )
-    local, source = lax.optimization_barrier((local, source))
     found = [local] + [shifted(local, "sub", step) for step in range(1, sub_count)]
     whole = jnp.concatenate(
         [
@@ -329,10 +360,16 @@
 
     carried = None
     backs = []
+    returned = jnp.zeros((3, clusters, quarter), jnp.float32)
     for step in range(1, clus_count):
-        if step > 2:
-            source, backs[step - 3] = lax.optimization_barrier((source, backs[step - 3]))
-        source = shifted(source, "clus", 1)
+        if step > 1:
+            if step > 2:
+                source, backs[step - 3] = lax.optimization_barrier((source, backs[step - 3]))
+            source = shifted(source, "clus", 1)
+            if step > 2:
+                home = shifted(backs[step - 3], "clus", 2 - step)
+                source, home = lax.optimization_barrier((source, home))
+                returned = returned + home
         last = step == clus_count - 1
         results = run_step(step - 1, length, items, source, cot, own, pos, rhs, carried, last)
         if last:
@@ -340,15 +377,13 @@
         else:
             carried, back = results
         backs.append(back)
-    returned = jnp.zeros((3, clusters, quarter), jnp.float32)
-    for step in range(1, clus_count):
+    for step in range(max(clus_count - 2, 1), clus_count):
         returned = returned + shifted(backs[step - 1], "clus", -step)
 
     half = pot
     for step in range(1, rhs_count):
         arrived = shifted(pot_out[:, (step - 1) * rhs : step * rhs], "rhs", -step)
         half = half + arrived.astype(jnp.float32)
-    half, returned = lax.optimization_barrier((half, returned))
 
     def panels_of(array, place):
         return pick(
@@ -356,10 +391,19 @@
             [array[..., at * row_count : (at + 1) * row_count] for at in range(sub_count)],
         )
 
-    potential = panels_of(half, sub_place)
+    found = [panels_of(half, sub_place)]
     for step in range(1, sub_count):
-        sent = panels_of(half, sub_place + step).astype(jnp.bfloat16)
-        potential = potential + shifted(sent, "sub", step).astype(jnp.float32)
+        found.append(shifted(panels_of(half, sub_place + step).astype(jnp.bfloat16), "sub", step))
+    found, returned = lax.optimization_barrier((found, returned))
+    potential = pl.pallas_call(
+        sum_kernel,
+        out_shape=jax.ShapeDtypeStruct((clusters, rhs, row_count), jnp.bfloat16),
+        in_specs=[vmem] * sub_count,
+        out_specs=vmem,
+        compiler_params=pltpu.CompilerParams(vmem_limit_bytes=16 * 1024 * 1024),
+        cost_estimate=pl.CostEstimate(flops=2**33, bytes_accessed=2**24, transcendentals=0),
+        name="potential_sum",
+    )(*found)
 
     at = sub_place * row_count + core * quarter
     own_part = lax.dynamic_slice_in_dim(grad, at, quarter, 2) + returned
@@ -367,35 +411,67 @@
     share = clusters // sub_count
 
     def share_of(array, place):
-        return pick(
-            place % sub_count,
-            [array[..., at * share : (at + 1) * share, :] for at in range(sub_count)],
-        )
-
-    summed = share_of(grad, sub_place)
+        own_rows, edges = [], []
+        for at in range(sub_count):
+            own_rows.append(array[:, at * share : (at + 1) * share])
+            none = jnp.zeros_like(array[:, 0])
+            edges.append(
+                [
+                    array[:, at * share - 1] if at > 0 else none,
+                    array[:, (at + 1) * share] if at < sub_count - 1 else none,
+                ]
+            )
+        place = place % sub_count
+        return (
+            pick(place, own_rows),
+            pick(place, [jnp.concatenate(edge, axis=0) for edge in edges]),
+        )
+
+    def packed(rows, edge):
+        edge = jnp.pad(edge, ((0, share - edge.shape[0] % share), (0, 0)))
+        return jnp.concatenate([rows, edge.reshape(-1, share, panels)], axis=0)
+
+    summed = packed(*share_of(grad, sub_place))
     for step in range(1, sub_count):
-        summed = summed + shifted(share_of(grad, sub_place + step), "sub", step)
+        summed = summed + shifted(packed(*share_of(grad, sub_place + step)), "sub", step)
     gathered = summed
     for step in range(1, rhs_count):
         gathered = gathered + shifted(summed, "rhs", step)
-    gathered, potential = lax.optimization_barrier((gathered, potential))
+    edge_terms = gathered[3:].reshape(-1, panels)[:6]
+    own_jitter, edge_jitter = share_of(jitter_all[None], sub_place)
+    edge_jitter = jnp.repeat(edge_jitter, 3, axis=0)
     main, rims = pl.pallas_call(
         node_kernel,
         out_shape=(
             jax.ShapeDtypeStruct((3, share * panels), jnp.float32),
             jax.ShapeDtypeStruct((2, 8, LANES), jnp.float32),
         ),
-        in_specs=[vmem, vmem],
+        in_specs=[vmem] * 4,
         out_specs=(vmem, vmem),
         compiler_params=pltpu.CompilerParams(vmem_limit_bytes=16 * 1024 * 1024),
+        cost_estimate=pl.CostEstimate(flops=2**32, bytes_accessed=2**24, transcendentals=0),
         name="node_terms",
-    )(gathered, share_of(jitter_all, sub_place))
-    from_above = shifted(rims[0], ("clus", "sub"), -1)[:3]
-    from_below = shifted(rims[1], ("clus", "sub"), 1)[:3]
+    )(gathered[:3], own_jitter[0], edge_terms, edge_jitter)
+
+    is_first, is_last = sub_place == 0, sub_place == sub_count - 1
+
+    def rim_goal(z, x):
+        if x == 0:
+            return (z - 1, sub_count - 1)
+        if x == sub_count - 1:
+            return (z + 1, 0)
+        return None
+
+    from_rim = moved(jnp.where(is_first, rims[0], rims[1]), ("clus", "sub"), rim_goal)[:3]
     node_grad = jnp.concatenate(
-        [main[:, :LANES] + from_below, main[:, LANES:-LANES], main[:, -LANES:] + from_above], axis=1
-    )
-    return (potential.astype(jnp.bfloat16), node_grad)
+        [
+            main[:, :LANES] + jnp.where(is_first, from_rim, 0.0),
+            main[:, LANES:-LANES],
+            main[:, -LANES:] + jnp.where(is_last, from_rim, 0.0),
+        ],
+        axis=1,
+    )
+    return (potential, node_grad)
 
 
 def solution(mesh):

time: 71.6 us -> 77.5 us (1.082)
  local copies, waits for them, and re-layouts: 1.36 us -> 4.81 us
  waiting for transfers between devices: 23.9 us -> 20.7 us
  starting transfers between devices: 15.7 us -> 18.8 us
  other arithmetic: 5.42 us -> 6.82 us
  Pallas kernels: 24.1 us -> 25 us
    ppermute x0 -> x2, starting transfers between devices: none -> 5.77 us  [moved(): return lax.ppermute(value, axes, pairs)]
    ppermute x15 -> x12, waiting for transfers between devices: 23.9 us -> 18.3 us  [shifted(): return lax.ppermute(value, axis, pairs)]
    unnamed x2 -> x7, local copies, waits for them, and re-layouts: 0.01 us -> 3.25 us
    ppermute x15 -> x12, starting transfers between devices: 15.7 us -> 13.1 us  [shifted(): return lax.ppermute(value, axis, pairs)]
    ppermute x0 -> x2, waiting for transfers between devices: none -> 2.35 us  [moved(): return lax.ppermute(value, axes, pairs)]
    select_n x5 -> x7, other arithmetic: 1.8 us -> 2.94 us  [pick(): out = jnp.where(index == place, choices[place], out)]
    concatenate x1, other arithmetic: 0.08 us -> 1.12 us  [on_device(): cot = jnp.concatenate(cot_blocks, axis=1)]
    add x3 -> x2, other arithmetic: 0.83 us -> 0.03 us  [the longest x1 0.03 us: on_device(): summed + shifted(packed(*share_of(grad, sub_place + step)), 'sub', step)]
  transfers between devices with their start and end apart: 15 -> 14, of which waited for: 11 -> 8; matrix products, arithmetic and copies ran while one was open for 6% -> 9% of each run, Pallas kernels for 22% -> 21%
where the time goes in v3:
time: 77.5 us; the launch traced here: 77.2 us
  Pallas kernels  25 us (32%)
  waiting for transfers between devices  20.7 us (27%)
  starting transfers between devices  18.8 us (24%)
  other arithmetic  6.82 us (9%)
  local copies, waits for them, and re-layouts  4.81 us (6%)
  between operations  1.05 us (1%)
    pallas_call x3, Pallas kernels, run_step(): pl.pallas_call(functools.partial(step_kernel, step, length, rhs, first, l...  23.4 us
    ppermute x12, waiting for transfers between devices, shifted(): return lax.ppermute(value, axis, pairs)  18.3 us
    ppermute x12, starting transfers between devices, shifted(): return lax.ppermute(value, axis, pairs)  13.1 us
    ppermute x2, starting transfers between devices, moved(): return lax.ppermute(value, axes, pairs)  5.77 us
    unnamed x7, local copies, waits for them, and re-layouts  3.25 us
    select_n x7, other arithmetic, pick(): out = jnp.where(index == place, choices[place], out)  2.94 us
    ppermute x2, waiting for transfers between devices, moved(): return lax.ppermute(value, axes, pairs)  2.35 us
  transfers between devices with their start and end apart: 14, of which 8 were waited for; matrix products, arithmetic and copies ran while one was open for 9% of the time, Pallas kernels for 21%

profile of v3, /device:TPU:0, one launch (start us, length us, event | category | flops | bytes accessed | tf_op | source)
XLA Modules:
  0.0 77.2 jit_solution(8995785829867890291)
XLA Ops:
  0.6 0.0 copy-start
  0.7 1.0 %broadcast_select_fusion.2 = (bf16[16,32,128]{2,1,0:T(8,128)(2,1)S(1)}, bf16[16,32,128]{2,1,0:T(8,128)(2,1)S(1)}) fusion(pred[]{:T(512)S(6)} %eq.104, bf16[16,32,256]{2,1,0:T(8,128)(2,1)} %param.8, pred[]{:T(512)S(6)} %eq.103), kind=kLoop, calls=%fused_computation.13 | loop fusion | flops 131072 | bytes 524290 | tf_op jit(solution)/shard_map/jit(_where)/select_n | solution.py:49
  1.7 2.5 %collective-permute-start.1 = (bf16[512,128]{1,0:T(8,128)(2,1)S(1)}, bf16[512,128]{1,0:T(8,128)(2,1)S(1)}, u32[]{:S(2)}, u32[]{:S(2)}) collective-permute-start(bf16[512,128]{1,0:T(8,128)(2,1)S(1)} %bitcast.55), channel_id=1, source_target_pairs={{0,5},{1,4},{4,9},{5,8},{8,13},{9,12},{12,1},{13,0},{2,7},{3,6},{6... | collective-permute-start | bytes 393224 | tf_op jit(solution)/shard_map/ppermute | solution.py:34
  4.2 0.7 fusion.7
  4.9 1.6 %collective-permute-start = (bf16[576,128]{1,0:T(8,128)(2,1)S(1)}, bf16[576,128]{1,0:T(8,128)(2,1)S(1)}, u32[]{:S(2)}, u32[]{:S(2)}) collective-permute-start(bf16[576,128]{1,0:T(8,128)(2,1)S(1)} %pad_maximum_fusion.2), channel_id=1, source_target_pairs={{0,4},{4,8},{8,12},{12,0},{1,5},{5,9},{9,13},{13,1},{2,6},{6,10},{... | collective-permute-start | bytes 442376 | tf_op jit(solution)/shard_map/ppermute | solution.py:22
  6.6 0.9 %slice.99 = s32[16,1,256]{2,1,0:T(1,128)S(1)} slice(s32[16,4,256]{2,1,0:T(4,128)} %param.11), slice={[0:16], [0:1], [0:256]} | slice | bytes 32768 | tf_op jit(solution)/shard_map/slice | solution.py:329
  7.4 0.1 fusion.5
  7.5 1.0 %pad_maximum_fusion.1 = bf16[576,256]{1,0:T(8,128)(2,1)S(1)} fusion(bf16[16,256]{1,0:T(8,128)(2,1)S(1)} %fusion.5, bf16[48,256]{1,0:T(8,128)(2,1)} %bitcast.53, bf16[512,256]{1,0:T(8,128)(2,1)} %bitcast.49), kind=kLoop, calls=%fused_computation.9 | loop fusion | flops 884736 | bytes 589824 | tf_op jit(solution)/shard_map/concatenate | solution.py:330
  8.5 1.6 %collective-permute-start.3 = (bf16[576,256]{1,0:T(8,128)(2,1)S(1)}, bf16[576,256]{1,0:T(8,128)(2,1)S(1)}, u32[]{:S(2)}, u32[]{:S(2)}) collective-permute-start(bf16[576,256]{1,0:T(8,128)(2,1)S(1)} %pad_maximum_fusion.1), channel_id=1, source_target_pairs={{0,2},{2,0},{1,3},{3,1},{4,6},{6,4},{5,7},{7,5},{8,10},{10,8},{9,1... | collective-permute-start | bytes 884744 | tf_op jit(solution)/shard_map/ppermute | solution.py:22
  10.1 0.0 copy-done
  10.1 0.1 constant_dynamic-slice_fusion
  10.2 0.1 reshape.270
  10.2 0.1 mul.34
  10.3 0.2 convert_reduce_fusion
  10.5 0.2 convert_reduce_fusion.1
  10.7 0.1 copy.28
  10.8 0.1 select_reduce_fusion
  11.0 6.9 %collective-permute-done.3 = bf16[576,256]{1,0:T(8,128)(2,1)S(1)} collective-permute-done((bf16[576,256]{1,0:T(8,128)(2,1)S(1)}, bf16[576,256]{1,0:T(8,128)(2,1)S(1)}, u32[]{:S(2)}, u32[]{:S(2)}) %collective-permute-start.3) | collective-permute-done | bytes 294944 | tf_op jit(solution)/shard_map/ppermute | solution.py:22
  17.9 1.1 %broadcast_select_fusion = (bf16[576,256]{1,0:T(8,128)(2,1)S(1)}, bf16[576,256]{1,0:T(8,128)(2,1)S(1)}) fusion(bf16[576,256]{1,0:T(8,128)(2,1)S(1)} %collective-permute-done.3, pred[]{:T(512)S(6)} %eq.105, bf16[16,256]{1,0:T(8,128)(2,1)S(1)} %fusion.5, bf16[48,256]{1,0:T(8,128)(2,1)} %bitcast.54, bf16[512,256]{1,0:T(8,128)(2,1)} %bitcast.50, pred[]{:T(512)S(6)} %eq.93), kind=kLoop, calls=%fused_computation.10 | loop fusion | flops 1179648 | bytes 1179650 | tf_op jit(solution)/shard_map/jit(_where)/select_n | solution.py:49
  19.1 0.1 collective-permute-start.4
  19.1 0.1 pad_slice_fusion.6
  19.2 0.1 pad_add_fusion
  19.3 0.1 reshape.271.refs_0_
  19.4 0.0 collective-permute-done
  19.4 0.0 collective-permute-done.1
  19.4 1.6 %collective-permute-start.2 = (bf16[1088,128]{1,0:T(8,128)(2,1)S(1)}, bf16[1088,128]{1,0:T(8,128)(2,1)S(1)}, u32[]{:S(2)}, u32[]{:S(2)}) collective-permute-start(bf16[1088,128]{1,0:T(8,128)(2,1)S(1)} %constant_dynamic-update-slice_fusion.refs_1_), channel_id=1, source_target_pairs={{0,4},{4,8},{8,12},{12,0},{1,5},{5,9},{9,13},{13,1},{2,6},{6,10},{... | collective-permute-start | bytes 835592 | tf_op jit(solution)/shard_map/ppermute | solution.py:22
  21.1 0.1 target_rows.1.refs_3_
  21.2 0.0 collective-permute-done.4
  21.2 1.1 %pad_maximum_fusion.refs_2_ = bf16[16,64,512]{2,1,0:T(8,128)(2,1)S(1)} fusion(bf16[16,32,512]{2,1,0:T(8,128)(2,1)} %collective-permute-done.4, bf16[16,32,512]{2,1,0:T(8,128)(2,1)S(1)} %bitcast.48), kind=kLoop, calls=%fused_computation | loop fusion | flops 2097152 | bytes 2097152 | tf_op jit(solution)/shard_map/concatenate | solution.py:348
  22.3 8.5 %near_field_0.1 = (f32[16,80,512]{2,1,0:T(8,128)S(1)}, f32[3,16,128]{2,1,0:T(8,128)S(1)}) custom-call(s32[108]{0:T(128)S(1)} %reshape.271.refs_0_, bf16[1088,128]{1,0:T(8,128)(2,1)S(1)} %constant_dynamic-update-slice_fusion.refs_1_, bf16[16,64,512]{2,1,0:T(8,128)(2,1)S(1)} %pad_maximum_fusion.refs_2_, bf16[16,16,512]{2,1,0:T(8,128)(2,1)S(1)} %target_rows.1.refs_3_), custom_call_target="tpu_custom_call" | custom-call | flops 692060160 | bytes 6291456 | tf_op jit(solution)/shard_map/near_field_0/pallas_call | solution.py:200
  30.9 0.0 copy-start.1
  30.9 1.5 %copy-done.1 = f32[16,80,512]{2,1,0:T(8,128)} copy-done((f32[16,80,512]{2,1,0:T(8,128)}, f32[16,80,512]{2,1,0:T(8,128)S(1)}, u32[]{:S(2)}) %copy-start.1) | copy-done | bytes 2621464
  32.4 0.0 collective-permute-done.2.refs_1_
  32.4 1.1 %collective-permute-start.5 = (bf16[1088,128]{1,0:T(8,128)(2,1)S(1)}, bf16[1088,128]{1,0:T(8,128)(2,1)S(1)}, u32[]{:S(2)}, u32[]{:S(2)}) collective-permute-start(bf16[1088,128]{1,0:T(8,128)(2,1)S(1)} %collective-permute-done.2.refs_1_), channel_id=1, source_target_pairs={{0,4},{4,8},{8,12},{12,0},{1,5},{5,9},{9,13},{13,1},{2,6},{6,10},{... | collective-permute-start | bytes 835592 | tf_op jit(solution)/shard_map/ppermute | solution.py:22
  33.5 2.8 %collective-permute-start.6 = (f32[3,16,128]{2,0,1:T(4,128)S(1)}, f32[3,16,128]{2,0,1:T(4,128)S(1)}, u32[]{:S(2)}, u32[]{:S(2)}) collective-permute-start(f32[3,16,128]{2,0,1:T(4,128)S(1)} %copy.33), channel_id=1, source_target_pairs={{0,12},{4,0},{8,4},{12,8},{1,13},{5,1},{9,5},{13,9},{2,14},{6,2},{... | collective-permute-start | bytes 73736 | tf_op jit(solution)/shard_map/ppermute | solution.py:22
  36.3 0.0 copy-start.2
  36.3 1.7 %copy-done.2 = f32[16,80,512]{2,1,0:T(8,128)S(1)} copy-done((f32[16,80,512]{2,1,0:T(8,128)S(1)}, f32[16,80,512]{2,1,0:T(8,128)}, u32[]{:S(2)}) %copy-start.2) | copy-done | bytes 2621464
  38.0 6.7 %near_field_1.1 = (f32[16,80,512]{2,1,0:T(8,128)S(1)}, f32[3,16,128]{2,1,0:T(8,128)S(1)}) custom-call(s32[108]{0:T(128)S(1)} %reshape.271.refs_0_, bf16[1088,128]{1,0:T(8,128)(2,1)S(1)} %collective-permute-done.2.refs_1_, bf16[16,64,512]{2,1,0:T(8,128)(2,1)S(1)} %pad_maximum_fusion.refs_2_, bf16[16,16,512]{2,1,0:T(8,128)(2,1)S(1)} %target_rows.1.refs_3_, ...), custom_call_target="tpu_custom_call" | custom-call | flops 692060160 | bytes 6291456 | tf_op jit(solution)/shard_map/near_field_1/pallas_call | solution.py:200
  44.7 0.0 collective-permute-done.6
  44.7 0.0 collective-permute-done.5.refs_1_
  44.8 8.2 %near_field_2.1 = (f32[16,32,512]{2,1,0:T(8,128)S(1)}, bf16[16,32,512]{2,1,0:T(8,128)(2,1)S(1)}, f32[3,16,512]{2,1,0:T(8,128)S(1)}, f32[3,16,128]{2,1,0:T(8,128)S(1)}) custom-call(s32[108]{0:T(128)S(1)} %reshape.271.refs_0_, bf16[1088,128]{1,0:T(8,128)(2,1)S(1)} %collective-permute-done.5.refs_1_, bf16[16,64,512]{2,1,0:T(8,128)(2,1)S(1)} %pad_maximum_fusion.refs_2_, ...), custom_call_target="tpu_custom_call" | custom-call | flops 692060160 | bytes 6291456 | tf_op jit(solution)/shard_map/near_field_2/pallas_call | solution.py:200
  52.9 0.1 collective-permute-start.7
  53.1 0.1 collective-permute-start.9
  53.2 1.0 %collective-permute-start.10 = (f32[3,16,128]{2,0,1:T(4,128)S(1)}, f32[3,16,128]{2,0,1:T(4,128)S(1)}, u32[]{:S(2)}, u32[]{:S(2)}) collective-permute-start(f32[3,16,128]{2,0,1:T(4,128)S(1)} %copy.35), channel_id=1, source_target_pairs={{0,4},{4,8},{8,12},{12,0},{1,5},{5,9},{9,13},{13,1},{2,6},{6,10},{... | collective-permute-start | bytes 73736 | tf_op jit(solution)/shard_map/ppermute | solution.py:22
  54.2 0.1 copy.37
  54.3 0.6 collective-permute-done.7
  54.9 0.2 convert_add_fusion
  55.2 1.5 %collective-permute-start.8 = (bf16[16,32,256]{2,1,0:T(8,128)(2,1)S(1)}, bf16[16,32,256]{2,1,0:T(8,128)(2,1)S(1)}, u32[]{:S(2)}, u32[]{:S(2)}) collective-permute-start(bf16[16,32,256]{2,1,0:T(8,128)(2,1)S(1)} %select_convert_fusion), channel_id=1, source_target_pairs={{0,2},{2,0},{1,3},{3,1},{4,6},{6,4},{5,7},{7,5},{8,10},{10,8},{9,1... | collective-permute-start | bytes 786440 | tf_op jit(solution)/shard_map/ppermute | solution.py:22
  56.7 1.3 %collective-permute-done.9 = f32[3,16,128]{2,0,1:T(4,128)S(1)} collective-permute-done((f32[3,16,128]{2,0,1:T(4,128)S(1)}, f32[3,16,128]{2,0,1:T(4,128)S(1)}, u32[]{:S(2)}, u32[]{:S(2)}) %collective-permute-start.9) | collective-permute-done | bytes 24608 | tf_op jit(solution)/shard_map/ppermute | solution.py:22
  58.0 1.0 %collective-permute-done.10 = f32[3,16,128]{2,0,1:T(4,128)S(1)} collective-permute-done((f32[3,16,128]{2,0,1:T(4,128)S(1)}, f32[3,16,128]{2,0,1:T(4,128)S(1)}, u32[]{:S(2)}, u32[]{:S(2)}) %collective-permute-start.10) | collective-permute-done | bytes 24608 | tf_op jit(solution)/shard_map/ppermute | solution.py:22
  59.0 0.1 slice_select_fusion.refs_0_
  59.1 4.5 %collective-permute-done.8.refs_1_ = bf16[16,32,256]{2,1,0:T(8,128)(2,1)S(1)} collective-permute-done((bf16[16,32,256]{2,1,0:T(8,128)(2,1)S(1)}, bf16[16,32,256]{2,1,0:T(8,128)(2,1)S(1)}, u32[]{:S(2)}, u32[]{:S(2)}) %collective-permute-start.8) | collective-permute-done | bytes 262176 | tf_op jit(solution)/shard_map/ppermute | solution.py:22
  63.7 1.5 %collective-permute-start.11 = (f32[4,8,512]{2,1,0:T(8,128)S(1)}, f32[4,8,512]{2,1,0:T(8,128)S(1)}, u32[]{:S(2)}, u32[]{:S(2)}) collective-permute-start(f32[4,8,512]{2,1,0:T(8,128)S(1)} %pad_maximum_fusion.4), channel_id=1, source_target_pairs={{0,2},{2,0},{1,3},{3,1},{4,6},{6,4},{5,7},{7,5},{8,10},{10,8},{9,1... | collective-permute-start | bytes 196616 | tf_op jit(solution)/shard_map/ppermute | solution.py:22
  65.3 2.8 %collective-permute-done.11 = f32[4,8,512]{2,1,0:T(8,128)S(1)} collective-permute-done((f32[4,8,512]{2,1,0:T(8,128)S(1)}, f32[4,8,512]{2,1,0:T(8,128)S(1)}, u32[]{:S(2)}, u32[]{:S(2)}) %collective-permute-start.11) | collective-permute-done | bytes 65568 | tf_op jit(solution)/shard_map/ppermute | solution.py:22
  68.1 0.1 collective-permute-start.12
  68.2 1.2 %collective-permute-done.12 = f32[4,8,512]{2,1,0:T(8,128)S(1)} collective-permute-done((f32[4,8,512]{2,1,0:T(8,128)S(1)}, f32[4,8,512]{2,1,0:T(8,128)S(1)}, u32[]{:S(2)}, u32[]{:S(2)}) %collective-permute-start.12) | collective-permute-done | bytes 65568 | tf_op jit(solution)/shard_map/ppermute | solution.py:22
  69.5 0.7 node_terms.1
  70.2 3.3 %collective-permute-start.13 = (f32[8,128]{1,0:T(8,128)S(1)}, f32[8,128]{1,0:T(8,128)S(1)}, u32[]{:S(2)}, u32[]{:S(2)}) collective-permute-start(f32[8,128]{1,0:T(8,128)S(1)} %select_bitcast_fusion), channel_id=1, source_target_pairs={{0,14},{2,4},{4,2},{6,8},{8,6},{10,12},{12,10},{14,0},{1,15},{3,5}... | collective-permute-start | bytes 12296 | tf_op jit(solution)/shard_map/ppermute | solution.py:34
  73.4 0.7 potential_sum.1
  74.2 2.3 %collective-permute-done.13 = f32[8,128]{1,0:T(8,128)S(1)} collective-permute-done((f32[8,128]{1,0:T(8,128)S(1)}, f32[8,128]{1,0:T(8,128)S(1)}, u32[]{:S(2)}, u32[]{:S(2)}) %collective-permute-start.13) | collective-permute-done | bytes 4128 | tf_op jit(solution)/shard_map/ppermute | solution.py:34
  76.5 0.6 pad_maximum_fusion.5
  (42 shorter events, 0.5 us)
Async XLA Ops:
  0.6 9.4 %copy-start = (s32[5,64]{1,0:T(8,128)S(1)}, s32[5,64]{1,0:T(8,128)}, u32[]{:S(2)}) copy-start(s32[5,64]{1,0:T(8,128)} %param.10) | copy-start | bytes 3844
  1.7 17.7 %collective-permute-start.1 = (bf16[512,128]{1,0:T(8,128)(2,1)S(1)}, bf16[512,128]{1,0:T(8,128)(2,1)S(1)}, u32[]{:S(2)}, u32[]{:S(2)}) collective-permute-start(bf16[512,128]{1,0:T(8,128)(2,1)S(1)} %bitcast.55), channel_id=1, source_target_pairs={{0,5},{1,4},{4,9},{5,8},{8,13},{9,12},{12,1},{13,0},{2,7},{3,6},{6... | collective-permute-start | bytes 393224 | tf_op jit(solution)/shard_map/ppermute | solution.py:34
  4.9 14.4 %collective-permute-start = (bf16[576,128]{1,0:T(8,128)(2,1)S(1)}, bf16[576,128]{1,0:T(8,128)(2,1)S(1)}, u32[]{:S(2)}, u32[]{:S(2)}) collective-permute-start(bf16[576,128]{1,0:T(8,128)(2,1)S(1)} %pad_maximum_fusion.2), channel_id=1, source_target_pairs={{0,4},{4,8},{8,12},{12,0},{1,5},{5,9},{9,13},{13,1},{2,6},{6,10},{... | collective-permute-start | bytes 442376 | tf_op jit(solution)/shard_map/ppermute | solution.py:22
  8.5 9.4 %collective-permute-start.3 = (bf16[576,256]{1,0:T(8,128)(2,1)S(1)}, bf16[576,256]{1,0:T(8,128)(2,1)S(1)}, u32[]{:S(2)}, u32[]{:S(2)}) collective-permute-start(bf16[576,256]{1,0:T(8,128)(2,1)S(1)} %pad_maximum_fusion.1), channel_id=1, source_target_pairs={{0,2},{2,0},{1,3},{3,1},{4,6},{6,4},{5,7},{7,5},{8,10},{10,8},{9,1... | collective-permute-start | bytes 884744 | tf_op jit(solution)/shard_map/ppermute | solution.py:22
  19.1 2.2 %collective-permute-start.4 = (bf16[16,32,512]{2,1,0:T(8,128)(2,1)S(1)}, bf16[16,32,512]{2,1,0:T(8,128)(2,1)}, u32[]{:S(2)}, u32[]{:S(2)}) collective-permute-start(bf16[16,32,512]{2,1,0:T(8,128)(2,1)S(1)} %bitcast.47), channel_id=1, source_target_pairs={{0,1},{1,0},{2,3},{3,2},{4,5},{5,4},{6,7},{7,6},{8,9},{9,8},{10,11... | collective-permute-start | bytes 1572872 | tf_op jit(solution)/shard_map/ppermute | solution.py:22
  19.4 12.9 %collective-permute-start.2 = (bf16[1088,128]{1,0:T(8,128)(2,1)S(1)}, bf16[1088,128]{1,0:T(8,128)(2,1)S(1)}, u32[]{:S(2)}, u32[]{:S(2)}) collective-permute-start(bf16[1088,128]{1,0:T(8,128)(2,1)S(1)} %constant_dynamic-update-slice_fusion.refs_1_), channel_id=1, source_target_pairs={{0,4},{4,8},{8,12},{12,0},{1,5},{5,9},{9,13},{13,1},{2,6},{6,10},{... | collective-permute-start | bytes 835592 | tf_op jit(solution)/shard_map/ppermute | solution.py:22
  30.9 1.5 %copy-start.1 = (f32[16,80,512]{2,1,0:T(8,128)}, f32[16,80,512]{2,1,0:T(8,128)S(1)}, u32[]{:S(2)}) copy-start(f32[16,80,512]{2,1,0:T(8,128)S(1)} %get-tuple-element.23.refs_4_) | copy-start | bytes 7864324
  32.4 12.4 %collective-permute-start.5 = (bf16[1088,128]{1,0:T(8,128)(2,1)S(1)}, bf16[1088,128]{1,0:T(8,128)(2,1)S(1)}, u32[]{:S(2)}, u32[]{:S(2)}) collective-permute-start(bf16[1088,128]{1,0:T(8,128)(2,1)S(1)} %collective-permute-done.2.refs_1_), channel_id=1, source_target_pairs={{0,4},{4,8},{8,12},{12,0},{1,5},{5,9},{9,13},{13,1},{2,6},{6,10},{... | collective-permute-start | bytes 835592 | tf_op jit(solution)/shard_map/ppermute | solution.py:22
  33.5 11.2 %collective-permute-start.6 = (f32[3,16,128]{2,0,1:T(4,128)S(1)}, f32[3,16,128]{2,0,1:T(4,128)S(1)}, u32[]{:S(2)}, u32[]{:S(2)}) collective-permute-start(f32[3,16,128]{2,0,1:T(4,128)S(1)} %copy.33), channel_id=1, source_target_pairs={{0,12},{4,0},{8,4},{12,8},{1,13},{5,1},{9,5},{13,9},{2,14},{6,2},{... | collective-permute-start | bytes 73736 | tf_op jit(solution)/shard_map/ppermute | solution.py:22
  36.3 1.7 %copy-start.2 = (f32[16,80,512]{2,1,0:T(8,128)S(1)}, f32[16,80,512]{2,1,0:T(8,128)}, u32[]{:S(2)}) copy-start(f32[16,80,512]{2,1,0:T(8,128)} %copy-done.1) | copy-start | bytes 7864324
  52.9 2.0 %collective-permute-start.7 = (bf16[16,32,512]{2,1,0:T(8,128)(2,1)S(1)}, bf16[16,32,512]{2,1,0:T(8,128)(2,1)S(1)}, u32[]{:S(2)}, u32[]{:S(2)}) collective-permute-start(bf16[16,32,512]{2,1,0:T(8,128)(2,1)S(1)} %get-tuple-element.26), channel_id=1, source_target_pairs={{0,1},{1,0},{2,3},{3,2},{4,5},{5,4},{6,7},{7,6},{8,9},{9,8},{10,11... | collective-permute-start | bytes 1572872 | tf_op jit(solution)/shard_map/ppermute | solution.py:22
  53.1 4.9 %collective-permute-start.9 = (f32[3,16,128]{2,0,1:T(4,128)S(1)}, f32[3,16,128]{2,0,1:T(4,128)S(1)}, u32[]{:S(2)}, u32[]{:S(2)}) collective-permute-start(f32[3,16,128]{2,0,1:T(4,128)S(1)} %copy.34), channel_id=1, source_target_pairs={{0,8},{4,12},{8,0},{12,4},{1,9},{5,13},{9,1},{13,5},{2,10},{6,14},... | collective-permute-start | bytes 73736 | tf_op jit(solution)/shard_map/ppermute | solution.py:22
  53.2 5.8 %collective-permute-start.10 = (f32[3,16,128]{2,0,1:T(4,128)S(1)}, f32[3,16,128]{2,0,1:T(4,128)S(1)}, u32[]{:S(2)}, u32[]{:S(2)}) collective-permute-start(f32[3,16,128]{2,0,1:T(4,128)S(1)} %copy.35), channel_id=1, source_target_pairs={{0,4},{4,8},{8,12},{12,0},{1,5},{5,9},{9,13},{13,1},{2,6},{6,10},{... | collective-permute-start | bytes 73736 | tf_op jit(solution)/shard_map/ppermute | solution.py:22
  55.2 8.4 %collective-permute-start.8 = (bf16[16,32,256]{2,1,0:T(8,128)(2,1)S(1)}, bf16[16,32,256]{2,1,0:T(8,128)(2,1)S(1)}, u32[]{:S(2)}, u32[]{:S(2)}) collective-permute-start(bf16[16,32,256]{2,1,0:T(8,128)(2,1)S(1)} %select_convert_fusion), channel_id=1, source_target_pairs={{0,2},{2,0},{1,3},{3,1},{4,6},{6,4},{5,7},{7,5},{8,10},{10,8},{9,1... | collective-permute-start | bytes 786440 | tf_op jit(solution)/shard_map/ppermute | solution.py:22
  63.7 4.3 %collective-permute-start.11 = (f32[4,8,512]{2,1,0:T(8,128)S(1)}, f32[4,8,512]{2,1,0:T(8,128)S(1)}, u32[]{:S(2)}, u32[]{:S(2)}) collective-permute-start(f32[4,8,512]{2,1,0:T(8,128)S(1)} %pad_maximum_fusion.4), channel_id=1, source_target_pairs={{0,2},{2,0},{1,3},{3,1},{4,6},{6,4},{5,7},{7,5},{8,10},{10,8},{9,1... | collective-permute-start | bytes 196616 | tf_op jit(solution)/shard_map/ppermute | solution.py:22
  68.1 1.3 %collective-permute-start.12 = (f32[4,8,512]{2,1,0:T(8,128)S(1)}, f32[4,8,512]{2,1,0:T(8,128)S(1)}, u32[]{:S(2)}, u32[]{:S(2)}) collective-permute-start(f32[4,8,512]{2,1,0:T(8,128)S(1)} %copy_add_fusion), channel_id=1, source_target_pairs={{0,1},{1,0},{2,3},{3,2},{4,5},{5,4},{6,7},{7,6},{8,9},{9,8},{10,11... | collective-permute-start | bytes 196616 | tf_op jit(solution)/shard_map/ppermute | solution.py:22
  70.2 6.4 %collective-permute-start.13 = (f32[8,128]{1,0:T(8,128)S(1)}, f32[8,128]{1,0:T(8,128)S(1)}, u32[]{:S(2)}, u32[]{:S(2)}) collective-permute-start(f32[8,128]{1,0:T(8,128)S(1)} %select_bitcast_fusion), channel_id=1, source_target_pairs={{0,14},{2,4},{4,2},{6,8},{8,6},{10,12},{12,10},{14,0},{1,15},{3,5}... | collective-permute-start | bytes 12296 | tf_op jit(solution)/shard_map/ppermute | solution.py:34

commit v4 on v3

--- a/solution.py
+++ b/solution.py
@@ -50,20 +50,30 @@
     return out
 
 
-def own_kernel(pos_ref, aug_ref, aug32):
-    pos = [pos_ref[coord].astype(jnp.float32) for coord in range(3)]
-    square = pos[0] * pos[0] + pos[1] * pos[1] + pos[2] * pos[2] + core_radius * core_radius
-    ones = jnp.ones_like(square)
-    rows = [-2.0 * value for value in pos] + three_parts(square) + [ones] * 3
+def own_kernel(*refs):
+    block_refs, (aug_ref, pos_ref, aug32) = refs[:-3], refs[-3:]
+    clusters = aug_ref.shape[0]
+    row_count = block_refs[0].shape[1]
     aug32[...] = jnp.zeros(aug32.shape, jnp.float32)
-    for row, value in enumerate(rows):
-        aug32[:, row, :] = value
+    for place, block_ref in enumerate(block_refs):
+        cols = slice(place * row_count, (place + 1) * row_count)
+        raw = [block_ref[coord * clusters : (coord + 1) * clusters, :] for coord in range(3)]
+        pos = [value.astype(jnp.float32) for value in raw]
+        square = pos[0] * pos[0] + pos[1] * pos[1] + pos[2] * pos[2] + core_radius * core_radius
+        ones = jnp.ones_like(square)
+        rows = [-2.0 * value for value in pos] + three_parts(square) + [ones] * 3
+        for row, value in enumerate(rows):
+            aug32[:, row, cols] = value
+        for coord in range(3):
+            pos_ref[coord, :, cols] = raw[coord]
     aug_ref[...] = aug32[...].astype(jnp.bfloat16)
 
 
-def step_kernel(step, length, rhs, first, last, *refs):
-    items, source_ref, cot_ref, own_ref = refs[:4]
-    refs = refs[4:]
+def step_kernel(step, length, rhs, blocks, first, last, *refs):
+    items, source_ref, own_ref = refs[:3]
+    cot_refs = refs[3 : 3 + blocks[0] * blocks[1]]
+    width = rhs * blocks[1]
+    refs = refs[3 + len(cot_refs) :]
     if not first:
         acc_in = refs[0]
         refs = refs[1:]
@@ -74,7 +84,7 @@
         acc, back_ref = refs[:2]
         refs = refs[2:]
     aug32, aug_t, dens_t, left, weight, back, dist_a, dist_b, prod_a, prod_b, both_a, both_b = refs
-    clusters, width, panels = cot_ref.shape
+    clusters, _, panels = own_ref.shape
     quarter = source_ref.shape[1]
     base = clusters * rhs
     starts = [0] + list(range(base + 4 * clusters, source_ref.shape[0], base))
@@ -119,7 +129,15 @@
         here, mate = decoded(place)
         mate = mate % clusters
         dist[...] = jnp.dot(aug_t[mate], own_ref[here], preferred_element_type=jnp.float32)
-        prod[...] = jnp.dot(dens_t[mate], cot_ref[here], preferred_element_type=jnp.float32)
+        cot = [
+            jnp.concatenate(
+                [ref[here] for ref in cot_refs[at * blocks[0] : (at + 1) * blocks[0]]], axis=1
+            )
+            for at in range(blocks[1])
+        ]
+        prod[...] = jnp.dot(
+            dens_t[mate], jnp.concatenate(cot, axis=0), preferred_element_type=jnp.float32
+        )
 
     def pointwise(place, dist, prod, both):
         _, mate = decoded(place)
@@ -164,13 +182,17 @@
         pot_out_ref[...] = acc[:, rhs:width, :].astype(jnp.bfloat16)
 
 
-def run_step(step, length, items, source, cot, own, pos, rhs, carried, last):
-    clusters, width, panels = cot.shape
+def run_step(step, length, items, source, cots, own, pos, carried, last):
+    clusters, _, panels = own.shape
     quarter = source.shape[1]
+    rhs = cots[0].shape[1]
+    sub_blocks = panels // cots[0].shape[2]
+    blocks = (sub_blocks, len(cots) // sub_blocks)
+    width = rhs * blocks[1]
     first = carried is None
     vmem = pl.BlockSpec(memory_space=pltpu.VMEM)
     smem = pl.BlockSpec(memory_space=pltpu.SMEM)
-    operands = (items, source, cot, own)
+    operands = (items, source, own, *cots)
     if not first:
         operands += (carried,)
     acc_shape = (clusters, width + AUG, panels)
@@ -198,12 +220,12 @@
         out_shape = (jax.ShapeDtypeStruct(acc_shape, jnp.float32), back_shape)
     pairs = (length - 6) * panels * quarter
     return pl.pallas_call(
-        functools.partial(step_kernel, step, length, rhs, first, last),
+        functools.partial(step_kernel, step, length, rhs, blocks, first, last),
         out_shape=out_shape,
         in_specs=[smem] + [vmem] * (len(operands) - 1),
         out_specs=(vmem,) * len(out_shape),
         scratch_shapes=scratch,
-        compiler_params=pltpu.CompilerParams(vmem_limit_bytes=32 * 1024 * 1024),
+        compiler_params=pltpu.CompilerParams(vmem_limit_bytes=16 * 1024 * 1024),
         cost_estimate=pl.CostEstimate(
             flops=2 * pairs * (2 * width + 3 * AUG), bytes_accessed=6 * 2**20, transcendentals=pairs
         ),
@@ -255,11 +277,15 @@
         rims_ref[1, coord : coord + 1, :] = above[clusters - 1 :]
 
 
-def sum_kernel(*refs):
-    total = refs[0][...]
-    for ref in refs[1:-1]:
+def last_kernel(*refs):
+    found, (main_ref, rim_ref, potential_ref, node_ref) = refs[:-4], refs[-4:]
+    total = found[0][...]
+    for ref in found[1:]:
         total = total + ref[...].astype(jnp.float32)
-    refs[-1][...] = total.astype(jnp.bfloat16)
+    potential_ref[...] = total.astype(jnp.bfloat16)
+    node_ref[...] = main_ref[...]
+    node_ref[:, :LANES] += rim_ref[0]
+    node_ref[:, main_ref.shape[1] - LANES :] += rim_ref[1]
 
 
 def on_device(positions, areas, density, cotangent, matching, connect):
@@ -327,36 +353,32 @@
     )[None, :]
     nodes_total = clus_count * clusters * panels
     jitter = (connect[:, 0, :] - base_ids + jitter_reach) % nodes_total - jitter_reach
-    local = jnp.concatenate(
-        [
-            cotangent.reshape(clusters * rhs, row_count),
-            by_coord.reshape(3 * clusters, row_count),
-            jitter.astype(jnp.bfloat16),
-        ],
-        axis=0,
+    small = jnp.concatenate(
+        [by_coord.reshape(3 * clusters, row_count), jitter.astype(jnp.bfloat16)], axis=0
     )
-    found = [local] + [shifted(local, "sub", step) for step in range(1, sub_count)]
-    whole = jnp.concatenate(
-        [
-            pick((sub_place - place) % sub_count, found)
-            for place in range(sub_count)
-        ],
-        axis=1,
-    )
-    cot_half = whole[: clusters * rhs].reshape(clusters, rhs, panels)
-    cot_blocks = [cot_half] + [shifted(cot_half, "rhs", step) for step in range(1, rhs_count)]
-    cot = jnp.concatenate(cot_blocks, axis=1)
-    pos = whole[clusters * rhs : clusters * (rhs + 3)].reshape(3, clusters, panels)
-    jitter_all = whole[clusters * (rhs + 3) :].astype(jnp.int32)
-    own = pl.pallas_call(
+    smalls = [small] + [shifted(small, "sub", step) for step in range(1, sub_count)]
+    cots = [cotangent] + [shifted(cotangent, "sub", step) for step in range(1, sub_count)]
+    for step in range(1, rhs_count):
+        cots += [shifted(block, "rhs", step) for block in cots[:sub_count]]
+
+    def in_order(blocks):
+        return jnp.concatenate(
+            [pick((sub_place - place) % sub_count, blocks) for place in range(sub_count)], axis=-1
+        )
+
+    jitter_all = in_order([block[3 * clusters :] for block in smalls]).astype(jnp.int32)
+    own, pos = pl.pallas_call(
         own_kernel,
-        out_shape=jax.ShapeDtypeStruct((clusters, AUG, panels), jnp.bfloat16),
-        in_specs=[vmem],
-        out_specs=vmem,
+        out_shape=(
+            jax.ShapeDtypeStruct((clusters, AUG, panels), jnp.bfloat16),
+            jax.ShapeDtypeStruct((3, clusters, panels), jnp.bfloat16),
+        ),
+        in_specs=[vmem] * sub_count,
+        out_specs=(vmem, vmem),
         scratch_shapes=[pltpu.VMEM((clusters, AUG, panels), jnp.float32)],
         compiler_params=pltpu.CompilerParams(vmem_limit_bytes=16 * 1024 * 1024),
         name="target_rows",
-    )(pos)
+    )(*smalls)
 
     carried = None
     backs = []
@@ -371,7 +393,7 @@
                 source, home = lax.optimization_barrier((source, home))
                 returned = returned + home
         last = step == clus_count - 1
-        results = run_step(step - 1, length, items, source, cot, own, pos, rhs, carried, last)
+        results = run_step(step - 1, length, items, source, cots, own, pos, carried, last)
         if last:
             pot, pot_out, grad, back = results
         else:
@@ -385,29 +407,17 @@
         arrived = shifted(pot_out[:, (step - 1) * rhs : step * rhs], "rhs", -step)
         half = half + arrived.astype(jnp.float32)
 
-    def panels_of(array, place):
-        return pick(
-            place % sub_count,
-            [array[..., at * row_count : (at + 1) * row_count] for at in range(sub_count)],
-        )
-
-    found = [panels_of(half, sub_place)]
+    half, grad = lax.optimization_barrier((half, grad))
+    found = [half[..., :row_count]]
     for step in range(1, sub_count):
-        found.append(shifted(panels_of(half, sub_place + step).astype(jnp.bfloat16), "sub", step))
-    found, returned = lax.optimization_barrier((found, returned))
-    potential = pl.pallas_call(
-        sum_kernel,
-        out_shape=jax.ShapeDtypeStruct((clusters, rhs, row_count), jnp.bfloat16),
-        in_specs=[vmem] * sub_count,
-        out_specs=vmem,
-        compiler_params=pltpu.CompilerParams(vmem_limit_bytes=16 * 1024 * 1024),
-        cost_estimate=pl.CostEstimate(flops=2**33, bytes_accessed=2**24, transcendentals=0),
-        name="potential_sum",
-    )(*found)
-
-    at = sub_place * row_count + core * quarter
-    own_part = lax.dynamic_slice_in_dim(grad, at, quarter, 2) + returned
-    grad = lax.dynamic_update_slice_in_dim(grad, own_part, at, 2)
+        sent = half[..., step * row_count : (step + 1) * row_count].astype(jnp.bfloat16)
+        found.append(shifted(sent, "sub", -step))
+
+    grads = [grad[..., at * row_count : (at + 1) * row_count] for at in range(sub_count)]
+    grads[0] = grads[0] + jnp.concatenate(
+        [jnp.where(core == at, returned, 0.0) for at in range(rhs_count)], axis=-1
+    )
+    grad = in_order(grads)
     share = clusters // sub_count
 
     def share_of(array, place):
@@ -449,9 +459,11 @@
         in_specs=[vmem] * 4,
         out_specs=(vmem, vmem),
         compiler_params=pltpu.CompilerParams(vmem_limit_bytes=16 * 1024 * 1024),
-        cost_estimate=pl.CostEstimate(flops=2**32, bytes_accessed=2**24, transcendentals=0),
+        cost_estimate=pl.CostEstimate(flops=2**20, bytes_accessed=2**18, transcendentals=0),
         name="node_terms",
     )(gathered[:3], own_jitter[0], edge_terms, edge_jitter)
+
+    found, rims = lax.optimization_barrier((found, rims))
 
     is_first, is_last = sub_place == 0, sub_place == sub_count - 1
 
@@ -463,14 +475,18 @@
         return None
 
     from_rim = moved(jnp.where(is_first, rims[0], rims[1]), ("clus", "sub"), rim_goal)[:3]
-    node_grad = jnp.concatenate(
-        [
-            main[:, :LANES] + jnp.where(is_first, from_rim, 0.0),
-            main[:, LANES:-LANES],
-            main[:, -LANES:] + jnp.where(is_last, from_rim, 0.0),
-        ],
-        axis=1,
-    )
+    from_rim = jnp.where(is_first, from_rim, 0.0), jnp.where(is_last, from_rim, 0.0)
+    potential, node_grad = pl.pallas_call(
+        last_kernel,
+        out_shape=(
+            jax.ShapeDtypeStruct((clusters, rhs, row_count), jnp.bfloat16),
+            jax.ShapeDtypeStruct(main.shape, jnp.float32),
+        ),
+        in_specs=[vmem] * (sub_count + 2),
+        out_specs=(vmem, vmem),
+        compiler_params=pltpu.CompilerParams(vmem_limit_bytes=16 * 1024 * 1024),
+        name="last_sums",
+    )(*found, main, jnp.stack(from_rim))
     return (potential, node_grad)
 
 

time: 77.5 us -> 70.2 us (0.906)
  starting transfers between devices: 18.8 us -> 14.7 us
  other arithmetic: 6.82 us -> 3.78 us
  local copies, waits for them, and re-layouts: 4.81 us -> 2.58 us
  waiting for transfers between devices: 20.7 us -> 22.7 us
    ppermute x2, waiting for transfers between devices: 2.35 us -> 7.25 us  [moved(): return lax.ppermute(value, axes, pairs)]
    ppermute x2, starting transfers between devices: 5.77 us -> 2.54 us  [moved(): return lax.ppermute(value, axes, pairs)]
    ppermute x12 -> x14, waiting for transfers between devices: 18.3 us -> 15.5 us  [shifted(): return lax.ppermute(value, axis, pairs)]
    unnamed x7, local copies, waits for them, and re-layouts: 3.25 us -> 0.97 us
    concatenate x5 -> x2, other arithmetic: 2.79 us -> 0.83 us  [the longest x1 0.74 us: on_device(): jnp.concatenate([by_coord.reshape(3 * clusters, row_count), jitter.astype...]
    select_n x7 -> x6, other arithmetic: 2.94 us -> 1.87 us  [pick(): out = jnp.where(index == place, choices[place], out)]
    ppermute x12 -> x14, starting transfers between devices: 13.1 us -> 12.1 us  [shifted(): return lax.ppermute(value, axis, pairs)]
  transfers between devices with their start and end apart: 14 -> 16, of which waited for: 8 -> 9; matrix products, arithmetic and copies ran while one was open for 9% -> 7% of each run, Pallas kernels for 21% -> 23%
where the time goes in v4:
time: 70.2 us; the launch traced here: 70.3 us
  Pallas kernels  25.6 us (36%)
  waiting for transfers between devices  22.7 us (32%)
  starting transfers between devices  14.7 us (21%)
  other arithmetic  3.78 us (5%)
  local copies, waits for them, and re-layouts  2.58 us (4%)
  between operations  1.02 us (1%)
    pallas_call x3, Pallas kernels, run_step(): pl.pallas_call(functools.partial(step_kernel, step, length, rhs, blocks,...  23.9 us
    ppermute x14, waiting for transfers between devices, shifted(): return lax.ppermute(value, axis, pairs)  15.5 us
    ppermute x14, starting transfers between devices, shifted(): return lax.ppermute(value, axis, pairs)  12.1 us
    ppermute x2, waiting for transfers between devices, moved(): return lax.ppermute(value, axes, pairs)  7.25 us
    ppermute x2, starting transfers between devices, moved(): return lax.ppermute(value, axes, pairs)  2.54 us
    select_n x6, other arithmetic, pick(): out = jnp.where(index == place, choices[place], out)  1.87 us
  transfers between devices with their start and end apart: 16, of which 9 were waited for; matrix products, arithmetic and copies ran while one was open for 7% of the time, Pallas kernels for 23%

profile of v4, /device:TPU:0, one launch (start us, length us, event | category | flops | bytes accessed | tf_op | source)
XLA Modules:
  0.0 70.3 jit_solution(5200890323707027978)
XLA Ops:
  0.6 0.0 copy-start
  0.6 3.0 %collective-permute-start.4 = (bf16[16,32,256]{2,1,0:T(8,128)(2,1)}, bf16[16,32,256]{2,1,0:T(8,128)(2,1)S(1)}, u32[]{:S(2)}, u32[]{:S(2)}) collective-permute-start(bf16[16,32,256]{2,1,0:T(8,128)(2,1)} %refs_3_.5), channel_id=1, source_target_pairs={{0,2},{2,0},{1,3},{3,1},{4,6},{6,4},{5,7},{7,5},{8,10},{10,8},{9,1... | collective-permute-start | bytes 786440 | tf_op jit(solution)/shard_map/ppermute | solution.py:22
  3.6 0.0 collective-permute-start.5
  3.7 1.0 %broadcast_select_fusion = (bf16[16,32,128]{2,1,0:T(8,128)(2,1)S(1)}, bf16[16,32,128]{2,1,0:T(8,128)(2,1)S(1)}) fusion(pred[]{:T(512)S(6)} %eq.109, bf16[16,32,256]{2,1,0:T(8,128)(2,1)} %param.8, pred[]{:T(512)S(6)} %eq.108), kind=kLoop, calls=%fused_computation.9 | loop fusion | flops 131072 | bytes 524290 | tf_op jit(solution)/shard_map/jit(_where)/select_n | solution.py:49
  4.6 0.0 copy-start.2
  4.7 0.8 %fusion.7 = bf16[4,16,128]{2,1,0:T(8,128)(2,1)S(1)} fusion(bf16[3,16,256]{2,1,0:T(8,128)(2,1)} %bitcast.49, bf16[1,16,256]{2,1,0:T(8,128)(2,1)} %bitcast.52, pred[]{:T(512)S(6)} %eq.108), kind=kLoop, calls=%fused_computation.38 | loop fusion | flops 73728 | bytes 49153 | tf_op jit(solution)/shard_map/jit(_where)/select_n | solution.py:49
  5.5 1.6 %collective-permute-start = (bf16[576,128]{1,0:T(8,128)(2,1)S(1)}, bf16[576,128]{1,0:T(8,128)(2,1)S(1)}, u32[]{:S(2)}, u32[]{:S(2)}) collective-permute-start(bf16[576,128]{1,0:T(8,128)(2,1)S(1)} %pad_maximum_fusion), channel_id=1, source_target_pairs={{0,4},{4,8},{8,12},{12,0},{1,5},{5,9},{9,13},{13,1},{2,6},{6,10},{... | collective-permute-start | bytes 442376 | tf_op jit(solution)/shard_map/ppermute | solution.py:22
  7.1 1.4 %collective-permute-start.1 = (bf16[512,128]{1,0:T(8,128)(2,1)S(1)}, bf16[512,128]{1,0:T(8,128)(2,1)S(1)}, u32[]{:S(2)}, u32[]{:S(2)}) collective-permute-start(bf16[512,128]{1,0:T(8,128)(2,1)S(1)} %bitcast.48), channel_id=1, source_target_pairs={{0,5},{1,4},{4,9},{5,8},{8,13},{9,12},{12,1},{13,0},{2,7},{3,6},{6... | collective-permute-start | bytes 393224 | tf_op jit(solution)/shard_map/ppermute | solution.py:34
  8.5 0.9 %slice.89 = s32[16,1,256]{2,1,0:T(1,128)S(1)} slice(s32[16,4,256]{2,1,0:T(4,128)} %param.11), slice={[0:16], [0:1], [0:256]} | slice | bytes 32768 | tf_op jit(solution)/shard_map/slice | solution.py:355
  9.4 0.1 fusion.5
  9.4 0.7 %pad_maximum_fusion.3.refs_0_ = bf16[64,256]{1,0:T(8,128)(2,1)S(1)} fusion(bf16[16,256]{1,0:T(8,128)(2,1)S(1)} %fusion.5, bf16[48,256]{1,0:T(8,128)(2,1)} %bitcast.50), kind=kLoop, calls=%fused_computation.25 | loop fusion | flops 65536 | bytes 65536 | tf_op jit(solution)/shard_map/concatenate | solution.py:356
  10.2 0.5 collective-permute-start.3
  10.7 0.0 copy-done
  10.7 0.1 constant_dynamic-slice_fusion
  10.8 0.1 reshape.290
  10.9 0.1 mul.30
  11.0 0.2 convert_reduce_fusion
  11.2 0.2 convert_reduce_fusion.1
  11.4 0.2 select_reduce_fusion
  11.5 0.1 copy.28
  11.7 2.3 %collective-permute-done = bf16[576,128]{1,0:T(8,128)(2,1)S(1)} collective-permute-done((bf16[576,128]{1,0:T(8,128)(2,1)S(1)}, bf16[576,128]{1,0:T(8,128)(2,1)S(1)}, u32[]{:S(2)}, u32[]{:S(2)}) %collective-permute-start) | collective-permute-done | bytes 147488 | tf_op jit(solution)/shard_map/ppermute | solution.py:22
  14.0 0.0 collective-permute-done.4.refs_4_
  14.0 0.1 collective-permute-start.6
  14.0 2.1 %collective-permute-done.1 = bf16[512,128]{1,0:T(8,128)(2,1)S(1)} collective-permute-done((bf16[512,128]{1,0:T(8,128)(2,1)S(1)}, bf16[512,128]{1,0:T(8,128)(2,1)S(1)}, u32[]{:S(2)}, u32[]{:S(2)}) %collective-permute-start.1) | collective-permute-done | bytes 131104 | tf_op jit(solution)/shard_map/ppermute | solution.py:34
  16.2 0.1 collective-permute-start.2
  16.2 0.1 pad_slice_fusion.8
  16.3 0.1 pad_add_fusion
  16.4 0.1 reshape.291.refs_0_
  16.5 0.0 collective-permute-done.3.refs_1_
  16.5 0.2 target_rows.1
  16.6 0.0 collective-permute-done.5.refs_5_
  16.7 0.0 collective-permute-done.6.refs_6_
  16.7 0.0 copy-start.1
  16.7 0.9 %copy-done.1 = bf16[16,32,256]{2,1,0:T(8,128)(2,1)S(1)} copy-done((bf16[16,32,256]{2,1,0:T(8,128)(2,1)S(1)}, bf16[16,32,256]{2,1,0:T(8,128)(2,1)}, u32[]{:S(2)}) %copy-start.1) | copy-done | bytes 262168
  17.6 7.0 %near_field_0.1 = (f32[16,80,512]{2,1,0:T(8,128)S(1)}, f32[3,16,128]{2,1,0:T(8,128)S(1)}) custom-call(s32[108]{0:T(128)S(1)} %reshape.291.refs_0_, bf16[1088,128]{1,0:T(8,128)(2,1)S(1)} %constant_dynamic-update-slice_fusion.refs_1_, bf16[16,16,512]{2,1,0:T(8,128)(2,1)S(1)} %get-tuple-element.23.refs_2_, bf16[16,32,256]{2,1,0:T(8,128)(2,1)S(1)} %copy-done.1, ...), custom_call_target="tpu_custom_call" | custom-call | flops 692060160 | bytes 6291456 | tf_op jit(solution)/shard_map/near_field_0/pallas_call | solution.py:222
  24.6 2.1 %collective-permute-done.2.refs_1_ = bf16[1088,128]{1,0:T(8,128)(2,1)S(1)} collective-permute-done((bf16[1088,128]{1,0:T(8,128)(2,1)S(1)}, bf16[1088,128]{1,0:T(8,128)(2,1)S(1)}, u32[]{:S(2)}, u32[]{:S(2)}) %collective-permute-start.2) | collective-permute-done | bytes 278560 | tf_op jit(solution)/shard_map/ppermute | solution.py:22
  26.7 0.9 %collective-permute-start.7 = (bf16[1088,128]{1,0:T(8,128)(2,1)S(1)}, bf16[1088,128]{1,0:T(8,128)(2,1)S(1)}, u32[]{:S(2)}, u32[]{:S(2)}) collective-permute-start(bf16[1088,128]{1,0:T(8,128)(2,1)S(1)} %collective-permute-done.2.refs_1_), channel_id=1, source_target_pairs={{0,4},{4,8},{8,12},{12,0},{1,5},{5,9},{9,13},{13,1},{2,6},{6,10},{... | collective-permute-start | bytes 835592 | tf_op jit(solution)/shard_map/ppermute | solution.py:22
  27.6 0.1 select_bitcast_fusion.1
  27.8 2.9 %collective-permute-start.8 = (f32[3,16,128]{2,0,1:T(4,128)S(1)}, f32[3,16,128]{2,0,1:T(4,128)S(1)}, u32[]{:S(2)}, u32[]{:S(2)}) collective-permute-start(f32[3,16,128]{2,0,1:T(4,128)S(1)} %copy.33), channel_id=1, source_target_pairs={{0,12},{4,0},{8,4},{12,8},{1,13},{5,1},{9,5},{13,9},{2,14},{6,2},{... | collective-permute-start | bytes 73736 | tf_op jit(solution)/shard_map/ppermute | solution.py:22
  30.7 0.0 copy-done.2
  30.7 8.2 %near_field_1.1 = (f32[16,80,512]{2,1,0:T(8,128)S(1)}, f32[3,16,128]{2,1,0:T(8,128)S(1)}) custom-call(s32[108]{0:T(128)S(1)} %reshape.291.refs_0_, bf16[1088,128]{1,0:T(8,128)(2,1)S(1)} %collective-permute-done.2.refs_1_, bf16[16,16,512]{2,1,0:T(8,128)(2,1)S(1)} %get-tuple-element.23.refs_2_, bf16[16,32,256]{2,1,0:T(8,128)(2,1)S(1)} %copy-done.2, ...), custom_call_target="tpu_custom_call" | custom-call | flops 692060160 | bytes 6291456 | tf_op jit(solution)/shard_map/near_field_1/pallas_call | solution.py:222
  38.9 0.0 collective-permute-done.8
  38.9 0.0 collective-permute-done.7.refs_1_
  38.9 8.7 %near_field_2.1 = (f32[16,32,512]{2,1,0:T(8,128)S(1)}, bf16[16,32,512]{2,1,0:T(8,128)(2,1)S(1)}, f32[3,16,512]{2,1,0:T(8,128)S(1)}, f32[3,16,128]{2,1,0:T(8,128)S(1)}) custom-call(s32[108]{0:T(128)S(1)} %reshape.291.refs_0_, bf16[1088,128]{1,0:T(8,128)(2,1)S(1)} %collective-permute-done.7.refs_1_, bf16[16,16,512]{2,1,0:T(8,128)(2,1)S(1)} %get-tuple-element.23.refs_2_, ...), custom_call_target="tpu_custom_call" | custom-call | flops 692060160 | bytes 6291456 | tf_op jit(solution)/shard_map/near_field_2/pallas_call | solution.py:222
  47.7 0.1 collective-permute-start.9
  47.8 0.4 collective-permute-start.11
  48.2 0.3 collective-permute-start.12
  48.5 4.2 %collective-permute-done.11 = f32[3,16,128]{2,0,1:T(4,128)S(1)} collective-permute-done((f32[3,16,128]{2,0,1:T(4,128)S(1)}, f32[3,16,128]{2,0,1:T(4,128)S(1)}, u32[]{:S(2)}, u32[]{:S(2)}) %collective-permute-start.11) | collective-permute-done | bytes 24608 | tf_op jit(solution)/shard_map/ppermute | solution.py:22
  52.7 1.3 %collective-permute-done.12 = f32[3,16,128]{2,0,1:T(4,128)S(1)} collective-permute-done((f32[3,16,128]{2,0,1:T(4,128)S(1)}, f32[3,16,128]{2,0,1:T(4,128)S(1)}, u32[]{:S(2)}, u32[]{:S(2)}) %collective-permute-start.12) | collective-permute-done | bytes 24608 | tf_op jit(solution)/shard_map/ppermute | solution.py:22
  54.0 0.0 collective-permute-done.9
  54.0 0.2 convert_add_fusion
  54.2 0.1 copy.34
  54.5 0.7 %collective-permute-start.13 = (f32[4,8,512]{2,1,0:T(8,128)S(1)}, f32[4,8,512]{2,1,0:T(8,128)S(1)}, u32[]{:S(2)}, u32[]{:S(2)}) collective-permute-start(f32[4,8,512]{2,1,0:T(8,128)S(1)} %pad_maximum_fusion.2), channel_id=1, source_target_pairs={{0,2},{2,0},{1,3},{3,1},{4,6},{6,4},{5,7},{7,5},{8,10},{10,8},{9,1... | collective-permute-start | bytes 196616 | tf_op jit(solution)/shard_map/ppermute | solution.py:22
  55.2 1.4 %collective-permute-start.10 = (bf16[16,32,256]{2,1,0:T(8,128)(2,1)S(1)}, bf16[16,32,256]{2,1,0:T(8,128)(2,1)S(1)}, u32[]{:S(2)}, u32[]{:S(2)}) collective-permute-start(bf16[16,32,256]{2,1,0:T(8,128)(2,1)S(1)} %slice.195), channel_id=1, source_target_pairs={{0,2},{2,0},{1,3},{3,1},{4,6},{6,4},{5,7},{7,5},{8,10},{10,8},{9,1... | collective-permute-start | bytes 786440 | tf_op jit(solution)/shard_map/ppermute | solution.py:22
  56.7 2.9 %collective-permute-done.13 = f32[4,8,512]{2,1,0:T(8,128)S(1)} collective-permute-done((f32[4,8,512]{2,1,0:T(8,128)S(1)}, f32[4,8,512]{2,1,0:T(8,128)S(1)}, u32[]{:S(2)}, u32[]{:S(2)}) %collective-permute-start.13) | collective-permute-done | bytes 65568 | tf_op jit(solution)/shard_map/ppermute | solution.py:22
  59.6 0.1 collective-permute-start.14
  59.8 1.2 %collective-permute-done.14 = f32[4,8,512]{2,1,0:T(8,128)S(1)} collective-permute-done((f32[4,8,512]{2,1,0:T(8,128)S(1)}, f32[4,8,512]{2,1,0:T(8,128)S(1)}, u32[]{:S(2)}, u32[]{:S(2)}) %collective-permute-start.14) | collective-permute-done | bytes 65568 | tf_op jit(solution)/shard_map/ppermute | solution.py:22
  61.0 0.7 node_terms.1
  61.6 1.6 %collective-permute-done.10.refs_1_ = bf16[16,32,256]{2,1,0:T(8,128)(2,1)S(1)} collective-permute-done((bf16[16,32,256]{2,1,0:T(8,128)(2,1)S(1)}, bf16[16,32,256]{2,1,0:T(8,128)(2,1)S(1)}, u32[]{:S(2)}, u32[]{:S(2)}) %collective-permute-start.10) | collective-permute-done | bytes 262176 | tf_op jit(solution)/shard_map/ppermute | solution.py:22
  63.2 1.1 %collective-permute-start.15 = (f32[8,128]{1,0:T(8,128)S(1)}, f32[8,128]{1,0:T(8,128)S(1)}, u32[]{:S(2)}, u32[]{:S(2)}) collective-permute-start(f32[8,128]{1,0:T(8,128)S(1)} %select_bitcast_fusion.2), channel_id=1, source_target_pairs={{0,14},{2,4},{4,2},{6,8},{8,6},{10,12},{12,10},{14,0},{1,15},{3,5}... | collective-permute-start | bytes 12296 | tf_op jit(solution)/shard_map/ppermute | solution.py:34
  64.3 5.2 %collective-permute-done.15 = f32[8,128]{1,0:T(8,128)S(1)} collective-permute-done((f32[8,128]{1,0:T(8,128)S(1)}, f32[8,128]{1,0:T(8,128)S(1)}, u32[]{:S(2)}, u32[]{:S(2)}) %collective-permute-start.15) | collective-permute-done | bytes 4128 | tf_op jit(solution)/shard_map/ppermute | solution.py:34
  69.5 0.8 %last_sums.1 = (bf16[16,32,256]{2,1,0:T(8,128)(2,1)}, f32[3,4096]{1,0:T(4,128)}) custom-call(f32[16,32,256]{2,1,0:T(8,128)S(1)} %slice.90.refs_0_, bf16[16,32,256]{2,1,0:T(8,128)(2,1)S(1)} %collective-permute-done.10.refs_1_, f32[3,4096]{1,0:T(4,128)S(1)} %get-tuple-element.42.refs_2_, f32[2,3,128]{2,1,0:T(4,128)S(1)} %pad_maximum_fusion.6.refs_3_), custom_call_target="tpu_custom_call" | custom-call | tf_op jit(solution)/shard_map/last_sums/pallas_call | solution.py:479
  (41 shorter events, 0.5 us)
Async XLA Ops:
  0.6 10.1 %copy-start = (s32[5,64]{1,0:T(8,128)S(1)}, s32[5,64]{1,0:T(8,128)}, u32[]{:S(2)}) copy-start(s32[5,64]{1,0:T(8,128)} %param.10) | copy-start | bytes 3844
  0.6 13.3 %collective-permute-start.4 = (bf16[16,32,256]{2,1,0:T(8,128)(2,1)}, bf16[16,32,256]{2,1,0:T(8,128)(2,1)S(1)}, u32[]{:S(2)}, u32[]{:S(2)}) collective-permute-start(bf16[16,32,256]{2,1,0:T(8,128)(2,1)} %refs_3_.5), channel_id=1, source_target_pairs={{0,2},{2,0},{1,3},{3,1},{4,6},{6,4},{5,7},{7,5},{8,10},{10,8},{9,1... | collective-permute-start | bytes 786440 | tf_op jit(solution)/shard_map/ppermute | solution.py:22
  3.6 13.0 %collective-permute-start.5 = (bf16[16,32,256]{2,1,0:T(8,128)(2,1)}, bf16[16,32,256]{2,1,0:T(8,128)(2,1)S(1)}, u32[]{:S(2)}, u32[]{:S(2)}) collective-permute-start(bf16[16,32,256]{2,1,0:T(8,128)(2,1)} %refs_3_.5), channel_id=1, source_target_pairs={{0,1},{1,0},{2,3},{3,2},{4,5},{5,4},{6,7},{7,6},{8,9},{9,8},{10,11... | collective-permute-start | bytes 786440 | tf_op jit(solution)/shard_map/ppermute | solution.py:22
  4.6 26.1 %copy-start.2 = (bf16[16,32,256]{2,1,0:T(8,128)(2,1)S(1)}, bf16[16,32,256]{2,1,0:T(8,128)(2,1)}, u32[]{:S(2)}) copy-start(bf16[16,32,256]{2,1,0:T(8,128)(2,1)} %refs_3_.5) | copy-start | bytes 786436
  5.5 8.5 %collective-permute-start = (bf16[576,128]{1,0:T(8,128)(2,1)S(1)}, bf16[576,128]{1,0:T(8,128)(2,1)S(1)}, u32[]{:S(2)}, u32[]{:S(2)}) collective-permute-start(bf16[576,128]{1,0:T(8,128)(2,1)S(1)} %pad_maximum_fusion), channel_id=1, source_target_pairs={{0,4},{4,8},{8,12},{12,0},{1,5},{5,9},{9,13},{13,1},{2,6},{6,10},{... | collective-permute-start | bytes 442376 | tf_op jit(solution)/shard_map/ppermute | solution.py:22
  7.1 9.0 %collective-permute-start.1 = (bf16[512,128]{1,0:T(8,128)(2,1)S(1)}, bf16[512,128]{1,0:T(8,128)(2,1)S(1)}, u32[]{:S(2)}, u32[]{:S(2)}) collective-permute-start(bf16[512,128]{1,0:T(8,128)(2,1)S(1)} %bitcast.48), channel_id=1, source_target_pairs={{0,5},{1,4},{4,9},{5,8},{8,13},{9,12},{12,1},{13,0},{2,7},{3,6},{6... | collective-permute-start | bytes 393224 | tf_op jit(solution)/shard_map/ppermute | solution.py:34
  10.2 6.3 %collective-permute-start.3 = (bf16[64,256]{1,0:T(8,128)(2,1)S(1)}, bf16[64,256]{1,0:T(8,128)(2,1)S(1)}, u32[]{:S(2)}, u32[]{:S(2)}) collective-permute-start(bf16[64,256]{1,0:T(8,128)(2,1)S(1)} %pad_maximum_fusion.3.refs_0_), channel_id=1, source_target_pairs={{0,2},{2,0},{1,3},{3,1},{4,6},{6,4},{5,7},{7,5},{8,10},{10,8},{9,1... | collective-permute-start | bytes 98312 | tf_op jit(solution)/shard_map/ppermute | solution.py:22
  14.0 2.7 %collective-permute-start.6 = (bf16[16,32,256]{2,1,0:T(8,128)(2,1)S(1)}, bf16[16,32,256]{2,1,0:T(8,128)(2,1)S(1)}, u32[]{:S(2)}, u32[]{:S(2)}) collective-permute-start(bf16[16,32,256]{2,1,0:T(8,128)(2,1)S(1)} %collective-permute-done.4.refs_4_), channel_id=1, source_target_pairs={{0,1},{1,0},{2,3},{3,2},{4,5},{5,4},{6,7},{7,6},{8,9},{9,8},{10,11... | collective-permute-start | bytes 786440 | tf_op jit(solution)/shard_map/ppermute | solution.py:22
  16.2 10.5 %collective-permute-start.2 = (bf16[1088,128]{1,0:T(8,128)(2,1)S(1)}, bf16[1088,128]{1,0:T(8,128)(2,1)S(1)}, u32[]{:S(2)}, u32[]{:S(2)}) collective-permute-start(bf16[1088,128]{1,0:T(8,128)(2,1)S(1)} %constant_dynamic-update-slice_fusion.refs_1_), channel_id=1, source_target_pairs={{0,4},{4,8},{8,12},{12,0},{1,5},{5,9},{9,13},{13,1},{2,6},{6,10},{... | collective-permute-start | bytes 835592 | tf_op jit(solution)/shard_map/ppermute | solution.py:22
  16.7 1.0 %copy-start.1 = (bf16[16,32,256]{2,1,0:T(8,128)(2,1)S(1)}, bf16[16,32,256]{2,1,0:T(8,128)(2,1)}, u32[]{:S(2)}) copy-start(bf16[16,32,256]{2,1,0:T(8,128)(2,1)} %refs_3_.5) | copy-start | bytes 786436
  26.7 12.2 %collective-permute-start.7 = (bf16[1088,128]{1,0:T(8,128)(2,1)S(1)}, bf16[1088,128]{1,0:T(8,128)(2,1)S(1)}, u32[]{:S(2)}, u32[]{:S(2)}) collective-permute-start(bf16[1088,128]{1,0:T(8,128)(2,1)S(1)} %collective-permute-done.2.refs_1_), channel_id=1, source_target_pairs={{0,4},{4,8},{8,12},{12,0},{1,5},{5,9},{9,13},{13,1},{2,6},{6,10},{... | collective-permute-start | bytes 835592 | tf_op jit(solution)/shard_map/ppermute | solution.py:22
  27.8 11.1 %collective-permute-start.8 = (f32[3,16,128]{2,0,1:T(4,128)S(1)}, f32[3,16,128]{2,0,1:T(4,128)S(1)}, u32[]{:S(2)}, u32[]{:S(2)}) collective-permute-start(f32[3,16,128]{2,0,1:T(4,128)S(1)} %copy.33), channel_id=1, source_target_pairs={{0,12},{4,0},{8,4},{12,8},{1,13},{5,1},{9,5},{13,9},{2,14},{6,2},{... | collective-permute-start | bytes 73736 | tf_op jit(solution)/shard_map/ppermute | solution.py:22
  47.7 6.3 %collective-permute-start.9 = (bf16[16,32,512]{2,1,0:T(8,128)(2,1)S(1)}, bf16[16,32,512]{2,1,0:T(8,128)(2,1)S(1)}, u32[]{:S(2)}, u32[]{:S(2)}) collective-permute-start(bf16[16,32,512]{2,1,0:T(8,128)(2,1)S(1)} %get-tuple-element.32), channel_id=1, source_target_pairs={{0,1},{1,0},{2,3},{3,2},{4,5},{5,4},{6,7},{7,6},{8,9},{9,8},{10,11... | collective-permute-start | bytes 1572872 | tf_op jit(solution)/shard_map/ppermute | solution.py:22
  47.8 4.9 %collective-permute-start.11 = (f32[3,16,128]{2,0,1:T(4,128)S(1)}, f32[3,16,128]{2,0,1:T(4,128)S(1)}, u32[]{:S(2)}, u32[]{:S(2)}) collective-permute-start(f32[3,16,128]{2,0,1:T(4,128)S(1)} %copy.36), channel_id=1, source_target_pairs={{0,8},{4,12},{8,0},{12,4},{1,9},{5,13},{9,1},{13,5},{2,10},{6,14},... | collective-permute-start | bytes 73736 | tf_op jit(solution)/shard_map/ppermute | solution.py:22
  48.2 5.8 %collective-permute-start.12 = (f32[3,16,128]{2,0,1:T(4,128)S(1)}, f32[3,16,128]{2,0,1:T(4,128)S(1)}, u32[]{:S(2)}, u32[]{:S(2)}) collective-permute-start(f32[3,16,128]{2,0,1:T(4,128)S(1)} %copy.37), channel_id=1, source_target_pairs={{0,4},{4,8},{8,12},{12,0},{1,5},{5,9},{9,13},{13,1},{2,6},{6,10},{... | collective-permute-start | bytes 73736 | tf_op jit(solution)/shard_map/ppermute | solution.py:22
  54.5 5.1 %collective-permute-start.13 = (f32[4,8,512]{2,1,0:T(8,128)S(1)}, f32[4,8,512]{2,1,0:T(8,128)S(1)}, u32[]{:S(2)}, u32[]{:S(2)}) collective-permute-start(f32[4,8,512]{2,1,0:T(8,128)S(1)} %pad_maximum_fusion.2), channel_id=1, source_target_pairs={{0,2},{2,0},{1,3},{3,1},{4,6},{6,4},{5,7},{7,5},{8,10},{10,8},{9,1... | collective-permute-start | bytes 196616 | tf_op jit(solution)/shard_map/ppermute | solution.py:22
  55.2 8.0 %collective-permute-start.10 = (bf16[16,32,256]{2,1,0:T(8,128)(2,1)S(1)}, bf16[16,32,256]{2,1,0:T(8,128)(2,1)S(1)}, u32[]{:S(2)}, u32[]{:S(2)}) collective-permute-start(bf16[16,32,256]{2,1,0:T(8,128)(2,1)S(1)} %slice.195), channel_id=1, source_target_pairs={{0,2},{2,0},{1,3},{3,1},{4,6},{6,4},{5,7},{7,5},{8,10},{10,8},{9,1... | collective-permute-start | bytes 786440 | tf_op jit(solution)/shard_map/ppermute | solution.py:22
  59.6 1.3 %collective-permute-start.14 = (f32[4,8,512]{2,1,0:T(8,128)S(1)}, f32[4,8,512]{2,1,0:T(8,128)S(1)}, u32[]{:S(2)}, u32[]{:S(2)}) collective-permute-start(f32[4,8,512]{2,1,0:T(8,128)S(1)} %copy_add_fusion), channel_id=1, source_target_pairs={{0,1},{1,0},{2,3},{3,2},{4,5},{5,4},{6,7},{7,6},{8,9},{9,8},{10,11... | collective-permute-start | bytes 196616 | tf_op jit(solution)/shard_map/ppermute | solution.py:22
  63.2 6.3 %collective-permute-start.15 = (f32[8,128]{1,0:T(8,128)S(1)}, f32[8,128]{1,0:T(8,128)S(1)}, u32[]{:S(2)}, u32[]{:S(2)}) collective-permute-start(f32[8,128]{1,0:T(8,128)S(1)} %select_bitcast_fusion.2), channel_id=1, source_target_pairs={{0,14},{2,4},{4,2},{6,8},{8,6},{10,12},{12,10},{14,0},{1,15},{3,5}... | collective-permute-start | bytes 12296 | tf_op jit(solution)/shard_map/ppermute | solution.py:34

commit v5 on v4

--- a/solution.py
+++ b/solution.py
@@ -48,6 +48,37 @@
     for place in range(1, len(choices)):
         out = jnp.where(index == place, choices[place], out)
     return out
+
+
+def prepare_kernel(places, density_ref, by_coord_ref, areas_ref, connect_ref, *out_refs):
+    part_refs, small_ref = out_refs[:-1], out_refs[-1]
+    clusters, rhs, row_count = density_ref.shape
+    quarter = part_refs[0].shape[1]
+    count = len(part_refs)
+    device, sub_place, core = places[0], places[1], places[2]
+
+    def part_of(array, place):
+        return pick(place, [array[:, at * quarter : (at + 1) * quarter] for at in range(count)])
+
+    first_id = places[3] * device + places[4] * sub_place
+    ids = lax.broadcasted_iota(jnp.int32, (clusters, row_count), 0) * places[5]
+    ids = ids + lax.broadcasted_iota(jnp.int32, (clusters, row_count), 1) + first_id
+    jitter = connect_ref[...] - ids
+    jitter = jnp.where(jitter > jitter_reach, jitter - places[6], jitter)
+    jitter = jnp.where(jitter < -jitter_reach, jitter + places[6], jitter)
+    jitter = jitter.astype(jnp.float32).astype(jnp.bfloat16)
+    rows = [by_coord_ref[coord] for coord in range(3)] + [areas_ref[...], jitter]
+    base = clusters * rhs
+    for cluster in range(clusters):
+        dens = density_ref[cluster]
+        for step, part_ref in enumerate(part_refs):
+            part_ref[cluster * rhs : (cluster + 1) * rhs, :] = part_of(dens, (core + step) % count)
+    for at, value in enumerate(rows):
+        span = slice(base + at * clusters, base + (at + 1) * clusters)
+        part_refs[0][span, :] = part_of(value, core)
+        if at != 3:
+            at = min(at, 3)
+            small_ref[at * clusters : (at + 1) * clusters, :] = value
 
 
 def own_kernel(*refs):
@@ -87,7 +118,7 @@
     clusters, _, panels = own_ref.shape
     quarter = source_ref.shape[1]
     base = clusters * rhs
-    starts = [0] + list(range(base + 4 * clusters, source_ref.shape[0], base))
+    starts = [0] + list(range(base + 5 * clusters, source_ref.shape[0], base))
 
     there = [
         source_ref[base + coord * clusters : base + (coord + 1) * clusters, :].astype(jnp.float32)
@@ -233,7 +264,7 @@
     )(*operands)
 
 
-def node_kernel(grad_ref, jitter_ref, edge_ref, edge_jitter_ref, main_ref, rims_ref):
+def node_kernel(grad_ref, jitter_ref, edge_ref, main_ref):
     clusters, panels = jitter_ref.shape
     wide = panels + 2 * LANES
 
@@ -250,8 +281,10 @@
 
     jitter = jitter_ref[...]
     row_at = lax.broadcasted_iota(jnp.int32, (clusters, LANES), 0)
-    rims_ref[...] = jnp.zeros(rims_ref.shape, jnp.float32)
-    edge = spread_of(edge_ref[...], edge_jitter_ref[...])
+    edge = edge_ref[...]
+    edge_at = lax.broadcasted_iota(jnp.int32, edge.shape, 0)
+    edge_jitter = jnp.where(edge_at < 3, edge[6:7], edge[7:8]).astype(jnp.int32)
+    edge = spread_of(edge, edge_jitter)
     for coord in range(3):
         spread = spread_of(grad_ref[coord], jitter)
         below = spread[:, :LANES]
@@ -273,19 +306,13 @@
             main_ref[coord : coord + 1, cluster * panels : (cluster + 1) * panels] = inner[
                 cluster : cluster + 1
             ]
-        rims_ref[0, coord : coord + 1, :] = below[:1]
-        rims_ref[1, coord : coord + 1, :] = above[clusters - 1 :]
-
-
-def last_kernel(*refs):
-    found, (main_ref, rim_ref, potential_ref, node_ref) = refs[:-4], refs[-4:]
-    total = found[0][...]
-    for ref in found[1:]:
+
+
+def sum_kernel(*refs):
+    total = refs[0][...]
+    for ref in refs[1:-1]:
         total = total + ref[...].astype(jnp.float32)
-    potential_ref[...] = total.astype(jnp.bfloat16)
-    node_ref[...] = main_ref[...]
-    node_ref[:, :LANES] += rim_ref[0]
-    node_ref[:, main_ref.shape[1] - LANES :] += rim_ref[1]
+    refs[-1][...] = total.astype(jnp.bfloat16)
 
 
 def on_device(positions, areas, density, cotangent, matching, connect):
@@ -301,26 +328,32 @@
     width = rhs * rhs_count
     vmem = pl.BlockSpec(memory_space=pltpu.VMEM)
 
-    def part_of(array, place):
-        return pick(
-            place % rhs_count,
-            [array[..., at * quarter : (at + 1) * quarter] for at in range(rhs_count)],
-        )
+    smem = pl.BlockSpec(memory_space=pltpu.SMEM)
+    nodes_total = clus_count * clusters * panels
+
+    cots = [cotangent] + [shifted(cotangent, "sub", step) for step in range(1, sub_count)]
+    for step in range(1, rhs_count):
+        cots += [shifted(block, "rhs", step) for block in cots[:sub_count]]
 
     by_coord = jnp.transpose(positions, (1, 0, 2))
-    placed = jnp.concatenate([by_coord, areas[None]], axis=0)
-    first_part = jnp.concatenate(
-        [
-            part_of(density, core).reshape(clusters * rhs, quarter),
-            part_of(placed, core).reshape(4 * clusters, quarter),
-        ],
-        axis=0,
-    )
-    arrived = [shifted(first_part, "clus", 1)]
+    places = [device, sub_place, core, clusters * panels, row_count, panels, nodes_total]
+    *parts, small = pl.pallas_call(
+        prepare_kernel,
+        out_shape=(
+            jax.ShapeDtypeStruct((clusters * (rhs + 5), quarter), jnp.bfloat16),
+            *[jax.ShapeDtypeStruct((clusters * rhs, quarter), jnp.bfloat16)] * (rhs_count - 1),
+            jax.ShapeDtypeStruct((clusters * 4, row_count), jnp.bfloat16),
+        ),
+        in_specs=[smem] + [vmem] * 4,
+        out_specs=(vmem,) * (rhs_count + 1),
+        compiler_params=pltpu.CompilerParams(vmem_limit_bytes=16 * 1024 * 1024),
+        name="prepare",
+    )(jnp.stack([jnp.asarray(place, jnp.int32) for place in places]), density, by_coord, areas,
+      connect[:, 0, :])
+    arrived = [shifted(parts[0], "clus", 1)]
     for step in range(1, rhs_count):
-        other_part = part_of(density, core + step).reshape(clusters * rhs, quarter)
         arrived.append(
-            moved(other_part, ("clus", "rhs"), lambda z, c, step=step: (z + 1, c + step))
+            moved(parts[step], ("clus", "rhs"), lambda z, c, step=step: (z + 1, c + step))
         )
     source = jnp.concatenate(arrived, axis=0)
 
@@ -346,20 +379,7 @@
     items = jnp.pad(listed, ((0, 0), (3, 3)), constant_values=clusters)
     items = jnp.concatenate([turns[:, None], items[:, 1:]], axis=1).reshape(-1)
 
-    cluster_at = jnp.arange(clusters, dtype=jnp.int32)
-    first_ids = (device * clusters + cluster_at) * panels
-    base_ids = first_ids[:, None] + (
-        sub_place * row_count + jnp.arange(row_count, dtype=jnp.int32)
-    )[None, :]
-    nodes_total = clus_count * clusters * panels
-    jitter = (connect[:, 0, :] - base_ids + jitter_reach) % nodes_total - jitter_reach
-    small = jnp.concatenate(
-        [by_coord.reshape(3 * clusters, row_count), jitter.astype(jnp.bfloat16)], axis=0
-    )
     smalls = [small] + [shifted(small, "sub", step) for step in range(1, sub_count)]
-    cots = [cotangent] + [shifted(cotangent, "sub", step) for step in range(1, sub_count)]
-    for step in range(1, rhs_count):
-        cots += [shifted(block, "rhs", step) for block in cots[:sub_count]]
 
     def in_order(blocks):
         return jnp.concatenate(
@@ -381,17 +401,12 @@
     )(*smalls)
 
     carried = None
-    backs = []
-    returned = jnp.zeros((3, clusters, quarter), jnp.float32)
+    backs, jitter_rows = [], []
     for step in range(1, clus_count):
         if step > 1:
             if step > 2:
                 source, backs[step - 3] = lax.optimization_barrier((source, backs[step - 3]))
             source = shifted(source, "clus", 1)
-            if step > 2:
-                home = shifted(backs[step - 3], "clus", 2 - step)
-                source, home = lax.optimization_barrier((source, home))
-                returned = returned + home
         last = step == clus_count - 1
         results = run_step(step - 1, length, items, source, cots, own, pos, carried, last)
         if last:
@@ -399,8 +414,28 @@
         else:
             carried, back = results
         backs.append(back)
-    for step in range(max(clus_count - 2, 1), clus_count):
-        returned = returned + shifted(backs[step - 1], "clus", -step)
+        at = clusters * (rhs + 4)
+        jitter_rows.append(source[at : at + clusters])
+
+    grad = in_order([grad[..., at * row_count : (at + 1) * row_count] for at in range(sub_count)])
+    low_part = (sub_place == 0) & (core == 0)
+    high_part = (sub_place == sub_count - 1) & (core == rhs_count - 1)
+    uppers = [grad[:, -1, -quarter:]] + [jnp.where(high_part, back[:, -1], 0.0) for back in backs]
+    lowers = [grad[:, 0, :quarter]] + [jnp.where(low_part, back[:, 0], 0.0) for back in backs]
+    returned = jnp.zeros((3, clusters, quarter), jnp.float32)
+    upper, lower = uppers[1], lowers[clus_count - 1]
+    nothing = jnp.zeros((2, quarter), jnp.float32)
+    for step in range(1, clus_count):
+        rows = [
+            backs[step - 1].reshape(3 * clusters, quarter),
+            uppers[(step + 1) % clus_count],
+            lowers[step - 1],
+            nothing,
+        ]
+        home = shifted(jnp.concatenate(rows, axis=0), "clus", -step)
+        returned = returned + home[: 3 * clusters].reshape(returned.shape)
+        upper = upper + home[3 * clusters : 3 * clusters + 3]
+        lower = lower + home[3 * clusters + 3 : 3 * clusters + 6]
 
     half = pot
     for step in range(1, rhs_count):
@@ -413,80 +448,70 @@
         sent = half[..., step * row_count : (step + 1) * row_count].astype(jnp.bfloat16)
         found.append(shifted(sent, "sub", -step))
 
-    grads = [grad[..., at * row_count : (at + 1) * row_count] for at in range(sub_count)]
-    grads[0] = grads[0] + jnp.concatenate(
-        [jnp.where(core == at, returned, 0.0) for at in range(rhs_count)], axis=-1
+    quarter_at = sub_place * rhs_count + core
+    grad = grad + jnp.concatenate(
+        [jnp.where(quarter_at == at, returned, 0.0) for at in range(sub_count * rhs_count)], axis=-1
     )
-    grad = in_order(grads)
     share = clusters // sub_count
 
-    def share_of(array, place):
-        own_rows, edges = [], []
-        for at in range(sub_count):
-            own_rows.append(array[:, at * share : (at + 1) * share])
-            none = jnp.zeros_like(array[:, 0])
-            edges.append(
-                [
-                    array[:, at * share - 1] if at > 0 else none,
-                    array[:, (at + 1) * share] if at < sub_count - 1 else none,
-                ]
-            )
-        place = place % sub_count
-        return (
-            pick(place, own_rows),
-            pick(place, [jnp.concatenate(edge, axis=0) for edge in edges]),
-        )
-
-    def packed(rows, edge):
-        edge = jnp.pad(edge, ((0, share - edge.shape[0] % share), (0, 0)))
-        return jnp.concatenate([rows, edge.reshape(-1, share, panels)], axis=0)
-
-    summed = packed(*share_of(grad, sub_place))
+    blank = jnp.zeros((3, panels - quarter), jnp.float32)
+    before = jnp.concatenate([blank, upper], axis=1)
+    after = jnp.concatenate([lower, blank], axis=1)
+    jitter_float = jitter_all.astype(jnp.float32)
+    jitter_before = jnp.concatenate(
+        [blank[:1], jitter_rows[0][clusters - 1 :].astype(jnp.float32)], axis=1
+    )
+    jitter_after = jnp.concatenate([jitter_rows[-1][:1].astype(jnp.float32), blank[:1]], axis=1)
+
+    def edge_rows(at):
+        first, end = at * share, (at + 1) * share
+        inside = at < sub_count - 1
+        return jnp.concatenate(
+            [
+                grad[:, first - 1] if at > 0 else before,
+                grad[:, end] if inside else after,
+                jnp.where(high_part, jitter_float[first - 1 : first] if at > 0 else jitter_before, 0.0),
+                jnp.where(low_part, jitter_float[end : end + 1] if inside else jitter_after, 0.0),
+            ],
+            axis=0,
+        ).reshape(-1, share, panels)
+
+    def packed(place):
+        return pick(
+            place % sub_count,
+            [
+                jnp.concatenate([grad[:, at * share : (at + 1) * share], edge_rows(at)], axis=0)
+                for at in range(sub_count)
+            ],
+        )
+
+    summed = packed(sub_place)
     for step in range(1, sub_count):
-        summed = summed + shifted(packed(*share_of(grad, sub_place + step)), "sub", step)
+        summed = summed + shifted(packed(sub_place + step), "sub", step)
     gathered = summed
     for step in range(1, rhs_count):
         gathered = gathered + shifted(summed, "rhs", step)
-    edge_terms = gathered[3:].reshape(-1, panels)[:6]
-    own_jitter, edge_jitter = share_of(jitter_all[None], sub_place)
-    edge_jitter = jnp.repeat(edge_jitter, 3, axis=0)
-    main, rims = pl.pallas_call(
+    own_jitter = pick(
+        sub_place, [jitter_all[at * share : (at + 1) * share] for at in range(sub_count)]
+    )
+    node_grad = pl.pallas_call(
         node_kernel,
-        out_shape=(
-            jax.ShapeDtypeStruct((3, share * panels), jnp.float32),
-            jax.ShapeDtypeStruct((2, 8, LANES), jnp.float32),
-        ),
-        in_specs=[vmem] * 4,
-        out_specs=(vmem, vmem),
+        out_shape=jax.ShapeDtypeStruct((3, share * panels), jnp.float32),
+        in_specs=[vmem] * 3,
+        out_specs=vmem,
         compiler_params=pltpu.CompilerParams(vmem_limit_bytes=16 * 1024 * 1024),
         cost_estimate=pl.CostEstimate(flops=2**20, bytes_accessed=2**18, transcendentals=0),
         name="node_terms",
-    )(gathered[:3], own_jitter[0], edge_terms, edge_jitter)
-
-    found, rims = lax.optimization_barrier((found, rims))
-
-    is_first, is_last = sub_place == 0, sub_place == sub_count - 1
-
-    def rim_goal(z, x):
-        if x == 0:
-            return (z - 1, sub_count - 1)
-        if x == sub_count - 1:
-            return (z + 1, 0)
-        return None
-
-    from_rim = moved(jnp.where(is_first, rims[0], rims[1]), ("clus", "sub"), rim_goal)[:3]
-    from_rim = jnp.where(is_first, from_rim, 0.0), jnp.where(is_last, from_rim, 0.0)
-    potential, node_grad = pl.pallas_call(
-        last_kernel,
-        out_shape=(
-            jax.ShapeDtypeStruct((clusters, rhs, row_count), jnp.bfloat16),
-            jax.ShapeDtypeStruct(main.shape, jnp.float32),
-        ),
-        in_specs=[vmem] * (sub_count + 2),
-        out_specs=(vmem, vmem),
+    )(gathered[:3], own_jitter, gathered[3:].reshape(8, panels))
+    potential = pl.pallas_call(
+        sum_kernel,
+        out_shape=jax.ShapeDtypeStruct((clusters, rhs, row_count), jnp.bfloat16),
+        in_specs=[vmem] * sub_count,
+        out_specs=vmem,
         compiler_params=pltpu.CompilerParams(vmem_limit_bytes=16 * 1024 * 1024),
-        name="last_sums",
-    )(*found, main, jnp.stack(from_rim))
+        cost_estimate=pl.CostEstimate(flops=2**20, bytes_accessed=2**18, transcendentals=0),
+        name="potential_sum",
+    )(*found)
     return (potential, node_grad)
 
 

time: 70.2 us -> 65.7 us (0.936)
  waiting for transfers between devices: 22.7 us -> 19 us
  other arithmetic: 3.78 us -> 1.14 us
  local copies, waits for them, and re-layouts: 2.58 us -> 5.22 us
  starting transfers between devices: 14.7 us -> 12.4 us
  Pallas kernels: 25.6 us -> 26.6 us
    ppermute x2 -> x1, waiting for transfers between devices: 7.25 us -> 2.02 us  [moved(): return lax.ppermute(value, axes, pairs)]
    unnamed x7 -> x14, local copies, waits for them, and re-layouts: 0.97 us -> 3.36 us
    select_n x6 -> x4, other arithmetic: 1.87 us -> 0.05 us  [pick(): out = jnp.where(index == place, choices[place], out)]
    ppermute x14, waiting for transfers between devices: 15.5 us -> 17 us  [shifted(): return lax.ppermute(value, axis, pairs)]
    ppermute x2 -> x1, starting transfers between devices: 2.54 us -> 1.13 us  [moved(): return lax.ppermute(value, axes, pairs)]
    pallas_call x2 -> x3, Pallas kernels: 1.49 us -> 2.67 us  [the longest x1 1.32 us: on_device(): pl.pallas_call(node_kernel, out_shape=jax.ShapeDtypeStruct((3, share * pa...]
    ppermute x14, starting transfers between devices: 12.1 us -> 11.3 us  [shifted(): return lax.ppermute(value, axis, pairs)]
    concatenate x4 -> x1, other arithmetic: 0.79 us -> 0.08 us  [on_device(): home = shifted(jnp.concatenate(rows, axis=0), 'clus', -step)]
  transfers between devices with their start and end apart: 16 -> 15, of which waited for: 9 -> 10; matrix products, arithmetic and copies ran while one was open for 7% -> 4% of each run, Pallas kernels for 23% -> 28%
where the time goes in v5:
time: 65.7 us; the launch traced here: 65.4 us
  Pallas kernels  26.6 us (40%)
  waiting for transfers between devices  19 us (29%)
  starting transfers between devices  12.4 us (19%)
  local copies, waits for them, and re-layouts  5.22 us (8%)
  other arithmetic  1.14 us (2%)
  between operations  1.03 us (2%)
    pallas_call x3, Pallas kernels, run_step(): pl.pallas_call(functools.partial(step_kernel, step, length, rhs, blocks,...  23.8 us
    ppermute x14, waiting for transfers between devices, shifted(): return lax.ppermute(value, axis, pairs)  17 us
    ppermute x14, starting transfers between devices, shifted(): return lax.ppermute(value, axis, pairs)  11.3 us
    unnamed x14, local copies, waits for them, and re-layouts  3.36 us
    ppermute x1, waiting for transfers between devices, moved(): return lax.ppermute(value, axes, pairs)  2.02 us
    pallas_call x1, Pallas kernels, on_device(): pl.pallas_call(node_kernel, out_shape=jax.ShapeDtypeStruct((3, share * pa...  1.32 us
  transfers between devices with their start and end apart: 15, of which 10 were waited for; matrix products, arithmetic and copies ran while one was open for 4% of the time, Pallas kernels for 28%

profile of v5, /device:TPU:0, one launch (start us, length us, event | category | flops | bytes accessed | tf_op | source)
XLA Modules:
  0.0 65.4 jit_solution(12492468622584214348)
XLA Ops:
  0.6 0.0 copy-start
  0.6 0.0 copy-start.2
  0.7 3.0 %collective-permute-start.4 = (bf16[16,32,256]{2,1,0:T(8,128)(2,1)}, bf16[16,32,256]{2,1,0:T(8,128)(2,1)S(1)}, u32[]{:S(2)}, u32[]{:S(2)}) collective-permute-start(bf16[16,32,256]{2,1,0:T(8,128)(2,1)} %refs_3_.5), channel_id=1, source_target_pairs={{0,2},{2,0},{1,3},{3,1},{4,6},{6,4},{5,7},{7,5},{8,10},{10,8},{9,1... | collective-permute-start | bytes 786440 | tf_op jit(solution)/shard_map/ppermute | solution.py:22
  3.7 0.0 collective-permute-start.5
  3.7 0.9 %slice.123 = s32[16,1,256]{2,1,0:T(1,128)S(1)} slice(s32[16,4,256]{2,1,0:T(4,128)} %param.11), slice={[0:16], [0:1], [0:256]} | slice | bytes 32768 | tf_op jit(solution)/shard_map/slice | solution.py:352
  4.5 0.1 stack.15.places
  4.6 0.0 copy-start.3
  4.6 0.9 %copy-done.3 = bf16[16,32,256]{2,1,0:T(8,128)(2,1)S(1)} copy-done((bf16[16,32,256]{2,1,0:T(8,128)(2,1)S(1)}, bf16[16,32,256]{2,1,0:T(8,128)(2,1)}, u32[]{:S(2)}) %copy-start.3) | copy-done | bytes 262168
  5.6 0.0 copy-start.4
  5.6 0.7 %copy-done.4 = bf16[16,3,256]{2,0,1:T(8,128)(2,1)S(1)} copy-done((bf16[16,3,256]{2,0,1:T(8,128)(2,1)S(1)}, bf16[16,3,256]{2,0,1:T(8,128)(2,1)}, u32[]{:S(2)}) %copy-start.4) | copy-done | bytes 24600
  6.3 0.0 copy-start.5
  6.3 0.7 %copy-done.5 = bf16[16,256]{1,0:T(8,128)(2,1)S(1)} copy-done((bf16[16,256]{1,0:T(8,128)(2,1)S(1)}, bf16[16,256]{1,0:T(8,128)(2,1)}, u32[]{:S(2)}) %copy-start.5) | copy-done | bytes 8216
  7.0 0.6 prepare.1
  7.6 0.2 collective-permute-start.3
  7.8 2.0 %collective-permute-start = (bf16[592,128]{1,0:T(8,128)(2,1)S(1)}, bf16[592,128]{1,0:T(8,128)(2,1)S(1)}, u32[]{:S(2)}, u32[]{:S(2)}) collective-permute-start(bf16[592,128]{1,0:T(8,128)(2,1)S(1)} %get-tuple-element.19), channel_id=1, source_target_pairs={{0,4},{4,8},{8,12},{12,0},{1,5},{5,9},{9,13},{13,1},{2,6},{6,10},{... | collective-permute-start | bytes 454664 | tf_op jit(solution)/shard_map/ppermute | solution.py:22
  9.8 1.1 %collective-permute-start.1 = (bf16[512,128]{1,0:T(8,128)(2,1)S(1)}, bf16[512,128]{1,0:T(8,128)(2,1)S(1)}, u32[]{:S(2)}, u32[]{:S(2)}) collective-permute-start(bf16[512,128]{1,0:T(8,128)(2,1)S(1)} %get-tuple-element.20), channel_id=1, source_target_pairs={{0,5},{1,4},{4,9},{5,8},{8,13},{9,12},{12,1},{13,0},{2,7},{3,6},{6... | collective-permute-start | bytes 393224 | tf_op jit(solution)/shard_map/ppermute | solution.py:34
  10.9 0.0 copy-done
  10.9 0.1 constant_dynamic-slice_fusion
  11.0 0.1 reshape.282
  11.1 0.1 mul.22
  11.2 0.2 convert_reduce_fusion
  11.4 0.2 convert_reduce_fusion.1
  11.6 0.2 select_reduce_fusion
  11.7 0.1 pad_slice_fusion
  11.8 0.1 copy.36
  11.9 0.1 pad_add_fusion
  12.0 0.1 reshape.283.refs_0_
  12.1 0.1 pad.40.clone
  12.2 0.0 collective-permute-done.3.refs_1_
  12.2 4.3 %collective-permute-done = bf16[592,128]{1,0:T(8,128)(2,1)S(1)} collective-permute-done((bf16[592,128]{1,0:T(8,128)(2,1)S(1)}, bf16[592,128]{1,0:T(8,128)(2,1)S(1)}, u32[]{:S(2)}, u32[]{:S(2)}) %collective-permute-start) | collective-permute-done | bytes 151584 | tf_op jit(solution)/shard_map/ppermute | solution.py:22
  16.5 2.0 %collective-permute-done.1 = bf16[512,128]{1,0:T(8,128)(2,1)S(1)} collective-permute-done((bf16[512,128]{1,0:T(8,128)(2,1)S(1)}, bf16[512,128]{1,0:T(8,128)(2,1)S(1)}, u32[]{:S(2)}, u32[]{:S(2)}) %collective-permute-start.1) | collective-permute-done | bytes 131104 | tf_op jit(solution)/shard_map/ppermute | solution.py:34
  18.6 0.1 collective-permute-start.2
  18.6 0.0 collective-permute-done.4.refs_4_
  18.7 0.3 collective-permute-start.6
  18.9 0.2 target_rows.1
  19.2 0.0 collective-permute-done.5.refs_5_
  19.2 1.1 %collective-permute-done.6.refs_6_ = bf16[16,32,256]{2,1,0:T(8,128)(2,1)S(1)} collective-permute-done((bf16[16,32,256]{2,1,0:T(8,128)(2,1)S(1)}, bf16[16,32,256]{2,1,0:T(8,128)(2,1)S(1)}, u32[]{:S(2)}, u32[]{:S(2)}) %collective-permute-start.6) | collective-permute-done | bytes 262176 | tf_op jit(solution)/shard_map/ppermute | solution.py:22
  20.3 0.9 %copy-done.1 = bf16[16,32,256]{2,1,0:T(8,128)(2,1)S(1)} copy-done((bf16[16,32,256]{2,1,0:T(8,128)(2,1)S(1)}, bf16[16,32,256]{2,1,0:T(8,128)(2,1)}, u32[]{:S(2)}) %copy-start.1) | copy-done | bytes 262168
  21.2 8.2 %near_field_0.1 = (f32[16,80,512]{2,1,0:T(8,128)S(1)}, f32[3,16,128]{2,1,0:T(8,128)S(1)}) custom-call(s32[108]{0:T(128)S(1)} %reshape.283.refs_0_, bf16[1104,128]{1,0:T(8,128)(2,1)S(1)} %constant_dynamic-update-slice_fusion.refs_1_, bf16[16,16,512]{2,1,0:T(8,128)(2,1)S(1)} %get-tuple-element.22.refs_2_, bf16[16,32,256]{2,1,0:T(8,128)(2,1)S(1)} %copy-done.1, ...), custom_call_target="tpu_custom_call" | custom-call | flops 692060160 | bytes 6291456 | tf_op jit(solution)/shard_map/near_field_0/pallas_call | solution.py:253
  29.5 0.0 collective-permute-done.2.refs_1_
  29.5 0.5 collective-permute-start.7
  30.0 0.0 copy-done.2
  30.0 7.7 %near_field_1.1 = (f32[16,80,512]{2,1,0:T(8,128)S(1)}, f32[3,16,128]{2,1,0:T(8,128)S(1)}) custom-call(s32[108]{0:T(128)S(1)} %reshape.283.refs_0_, bf16[1104,128]{1,0:T(8,128)(2,1)S(1)} %collective-permute-done.2.refs_1_, bf16[16,16,512]{2,1,0:T(8,128)(2,1)S(1)} %get-tuple-element.22.refs_2_, bf16[16,32,256]{2,1,0:T(8,128)(2,1)S(1)} %copy-done.2, ...), custom_call_target="tpu_custom_call" | custom-call | flops 692060160 | bytes 6291456 | tf_op jit(solution)/shard_map/near_field_1/pallas_call | solution.py:253
  37.7 2.4 %collective-permute-done.7.refs_1_ = bf16[1104,128]{1,0:T(8,128)(2,1)S(1)} collective-permute-done((bf16[1104,128]{1,0:T(8,128)(2,1)S(1)}, bf16[1104,128]{1,0:T(8,128)(2,1)S(1)}, u32[]{:S(2)}, u32[]{:S(2)}) %collective-permute-start.7) | collective-permute-done | bytes 282656 | tf_op jit(solution)/shard_map/ppermute | solution.py:22
  40.2 7.8 %near_field_2.1 = (f32[16,32,512]{2,1,0:T(8,128)S(1)}, bf16[16,32,512]{2,1,0:T(8,128)(2,1)S(1)}, f32[3,16,512]{2,1,0:T(8,128)S(1)}, f32[3,16,128]{2,1,0:T(8,128)S(1)}) custom-call(s32[108]{0:T(128)S(1)} %reshape.283.refs_0_, bf16[1104,128]{1,0:T(8,128)(2,1)S(1)} %collective-permute-done.7.refs_1_, bf16[16,16,512]{2,1,0:T(8,128)(2,1)S(1)} %get-tuple-element.22.refs_2_, ...), custom_call_target="tpu_custom_call" | custom-call | flops 692060160 | bytes 6291456 | tf_op jit(solution)/shard_map/near_field_2/pallas_call | solution.py:253
  48.0 0.1 copy.41
  48.2 0.1 maximum_maximum_fusion
  48.3 1.9 %collective-permute-start.10 = (f32[56,128]{1,0:T(8,128)S(1)}, f32[56,128]{1,0:T(8,128)S(1)}, u32[]{:S(2)}, u32[]{:S(2)}) collective-permute-start(f32[56,128]{1,0:T(8,128)S(1)} %get-tuple-element.59), channel_id=1, source_target_pairs={{0,12},{4,0},{8,4},{12,8},{1,13},{5,1},{9,5},{13,9},{2,14},{6,2},{... | collective-permute-start | bytes 86024 | tf_op jit(solution)/shard_map/ppermute | solution.py:22
  50.2 0.0 collective-permute-start.11
  50.2 1.1 %collective-permute-start.12 = (f32[56,128]{1,0:T(8,128)S(1)}, f32[56,128]{1,0:T(8,128)S(1)}, u32[]{:S(2)}, u32[]{:S(2)}) collective-permute-start(f32[56,128]{1,0:T(8,128)S(1)} %get-tuple-element.61), channel_id=1, source_target_pairs={{0,4},{4,8},{8,12},{12,0},{1,5},{5,9},{9,13},{13,1},{2,6},{6,10},{... | collective-permute-start | bytes 86024 | tf_op jit(solution)/shard_map/ppermute | solution.py:22
  51.3 0.0 collective-permute-start.8
  51.3 0.8 %collective-permute-done.10 = f32[56,128]{1,0:T(8,128)S(1)} collective-permute-done((f32[56,128]{1,0:T(8,128)S(1)}, f32[56,128]{1,0:T(8,128)S(1)}, u32[]{:S(2)}, u32[]{:S(2)}) %collective-permute-start.10) | collective-permute-done | bytes 28704 | tf_op jit(solution)/shard_map/ppermute | solution.py:22
  52.2 2.8 %collective-permute-done.11 = f32[56,128]{1,0:T(8,128)S(1)} collective-permute-done((f32[56,128]{1,0:T(8,128)S(1)}, f32[56,128]{1,0:T(8,128)S(1)}, u32[]{:S(2)}, u32[]{:S(2)}) %collective-permute-start.11) | collective-permute-done | bytes 28704 | tf_op jit(solution)/shard_map/ppermute | solution.py:22
  54.9 0.9 %collective-permute-done.12 = f32[56,128]{1,0:T(8,128)S(1)} collective-permute-done((f32[56,128]{1,0:T(8,128)S(1)}, f32[56,128]{1,0:T(8,128)S(1)}, u32[]{:S(2)}, u32[]{:S(2)}) %collective-permute-start.12) | collective-permute-done | bytes 28704 | tf_op jit(solution)/shard_map/ppermute | solution.py:22
  56.0 0.0 collective-permute-done.8
  56.0 0.2 convert_add_fusion
  56.4 1.4 %collective-permute-start.13 = (f32[4,8,512]{2,1,0:T(8,128)S(1)}, f32[4,8,512]{2,1,0:T(8,128)S(1)}, u32[]{:S(2)}, u32[]{:S(2)}) collective-permute-start(f32[4,8,512]{2,1,0:T(8,128)S(1)} %fusion), channel_id=1, source_target_pairs={{0,2},{2,0},{1,3},{3,1},{4,6},{6,4},{5,7},{7,5},{8,10},{10,8},{9,1... | collective-permute-start | bytes 196616 | tf_op jit(solution)/shard_map/ppermute | solution.py:22
  57.8 0.8 %collective-permute-start.9 = (bf16[16,32,256]{2,1,0:T(8,128)(2,1)S(1)}, bf16[16,32,256]{2,1,0:T(8,128)(2,1)S(1)}, u32[]{:S(2)}, u32[]{:S(2)}) collective-permute-start(bf16[16,32,256]{2,1,0:T(8,128)(2,1)S(1)} %slice.252), channel_id=1, source_target_pairs={{0,2},{2,0},{1,3},{3,1},{4,6},{6,4},{5,7},{7,5},{8,10},{10,8},{9,1... | collective-permute-start | bytes 786440 | tf_op jit(solution)/shard_map/ppermute | solution.py:22
  58.6 2.9 %collective-permute-done.13 = f32[4,8,512]{2,1,0:T(8,128)S(1)} collective-permute-done((f32[4,8,512]{2,1,0:T(8,128)S(1)}, f32[4,8,512]{2,1,0:T(8,128)S(1)}, u32[]{:S(2)}, u32[]{:S(2)}) %collective-permute-start.13) | collective-permute-done | bytes 65568 | tf_op jit(solution)/shard_map/ppermute | solution.py:22
  61.5 0.1 collective-permute-start.14
  61.6 1.2 %collective-permute-done.14 = f32[4,8,512]{2,1,0:T(8,128)S(1)} collective-permute-done((f32[4,8,512]{2,1,0:T(8,128)S(1)}, f32[4,8,512]{2,1,0:T(8,128)S(1)}, u32[]{:S(2)}, u32[]{:S(2)}) %collective-permute-start.14) | collective-permute-done | bytes 65568 | tf_op jit(solution)/shard_map/ppermute | solution.py:22
  62.8 1.3 %node_terms.1 = f32[3,4096]{1,0:T(4,128)} custom-call(f32[3,8,512]{2,1,0:T(8,128)S(1)} %slice.188.grad_ref, s32[8,512]{1,0:T(8,128)S(1)} %slice_select_fusion.2.jitter_ref, f32[8,512]{1,0:T(8,128)S(1)} %slice_bitcast_fusion.edge_ref), custom_call_target="tpu_custom_call" | custom-call | flops 1048576 | bytes 262144 | tf_op jit(solution)/shard_map/node_terms/pallas_call | solution.py:497
  64.2 0.5 collective-permute-done.9.refs_1_
  64.7 0.7 %potential_sum.1 = bf16[16,32,256]{2,1,0:T(8,128)(2,1)} custom-call(f32[16,32,256]{2,1,0:T(8,128)S(1)} %slice.126.refs_0_, bf16[16,32,256]{2,1,0:T(8,128)(2,1)S(1)} %collective-permute-done.9.refs_1_), custom_call_target="tpu_custom_call" | custom-call | flops 1048576 | bytes 262144 | tf_op jit(solution)/shard_map/potential_sum/pallas_call | solution.py:506
  (49 shorter events, 0.6 us)
Async XLA Ops:
  0.6 10.3 %copy-start = (s32[5,64]{1,0:T(8,128)S(1)}, s32[5,64]{1,0:T(8,128)}, u32[]{:S(2)}) copy-start(s32[5,64]{1,0:T(8,128)} %param.10) | copy-start | bytes 3844
  0.6 29.3 %copy-start.2 = (bf16[16,32,256]{2,1,0:T(8,128)(2,1)S(1)}, bf16[16,32,256]{2,1,0:T(8,128)(2,1)}, u32[]{:S(2)}) copy-start(bf16[16,32,256]{2,1,0:T(8,128)(2,1)} %refs_3_.5) | copy-start | bytes 786436
  0.7 18.0 %collective-permute-start.4 = (bf16[16,32,256]{2,1,0:T(8,128)(2,1)}, bf16[16,32,256]{2,1,0:T(8,128)(2,1)S(1)}, u32[]{:S(2)}, u32[]{:S(2)}) collective-permute-start(bf16[16,32,256]{2,1,0:T(8,128)(2,1)} %refs_3_.5), channel_id=1, source_target_pairs={{0,2},{2,0},{1,3},{3,1},{4,6},{6,4},{5,7},{7,5},{8,10},{10,8},{9,1... | collective-permute-start | bytes 786440 | tf_op jit(solution)/shard_map/ppermute | solution.py:22
  3.7 15.5 %collective-permute-start.5 = (bf16[16,32,256]{2,1,0:T(8,128)(2,1)}, bf16[16,32,256]{2,1,0:T(8,128)(2,1)S(1)}, u32[]{:S(2)}, u32[]{:S(2)}) collective-permute-start(bf16[16,32,256]{2,1,0:T(8,128)(2,1)} %refs_3_.5), channel_id=1, source_target_pairs={{0,1},{1,0},{2,3},{3,2},{4,5},{5,4},{6,7},{7,6},{8,9},{9,8},{10,11... | collective-permute-start | bytes 786440 | tf_op jit(solution)/shard_map/ppermute | solution.py:22
  4.6 1.0 %copy-start.3 = (bf16[16,32,256]{2,1,0:T(8,128)(2,1)S(1)}, bf16[16,32,256]{2,1,0:T(8,128)(2,1)}, u32[]{:S(2)}) copy-start(bf16[16,32,256]{2,1,0:T(8,128)(2,1)} %density_ref.1) | copy-start | bytes 786436
  5.6 0.7 %copy-start.4 = (bf16[16,3,256]{2,0,1:T(8,128)(2,1)S(1)}, bf16[16,3,256]{2,0,1:T(8,128)(2,1)}, u32[]{:S(2)}) copy-start(bf16[16,3,256]{2,0,1:T(8,128)(2,1)} %param.6) | copy-start | bytes 73732
  6.3 0.7 %copy-start.5 = (bf16[16,256]{1,0:T(8,128)(2,1)S(1)}, bf16[16,256]{1,0:T(8,128)(2,1)}, u32[]{:S(2)}) copy-start(bf16[16,256]{1,0:T(8,128)(2,1)} %areas_ref.1) | copy-start | bytes 24580
  7.6 4.5 %collective-permute-start.3 = (bf16[64,256]{1,0:T(8,128)(2,1)S(1)}, bf16[64,256]{1,0:T(8,128)(2,1)S(1)}, u32[]{:S(2)}, u32[]{:S(2)}) collective-permute-start(bf16[64,256]{1,0:T(8,128)(2,1)S(1)} %get-tuple-element.21.refs_0_), channel_id=1, source_target_pairs={{0,2},{2,0},{1,3},{3,1},{4,6},{6,4},{5,7},{7,5},{8,10},{10,8},{9,1... | collective-permute-start | bytes 98312 | tf_op jit(solution)/shard_map/ppermute | solution.py:22
  7.8 8.7 %collective-permute-start = (bf16[592,128]{1,0:T(8,128)(2,1)S(1)}, bf16[592,128]{1,0:T(8,128)(2,1)S(1)}, u32[]{:S(2)}, u32[]{:S(2)}) collective-permute-start(bf16[592,128]{1,0:T(8,128)(2,1)S(1)} %get-tuple-element.19), channel_id=1, source_target_pairs={{0,4},{4,8},{8,12},{12,0},{1,5},{5,9},{9,13},{13,1},{2,6},{6,10},{... | collective-permute-start | bytes 454664 | tf_op jit(solution)/shard_map/ppermute | solution.py:22
  9.8 8.8 %collective-permute-start.1 = (bf16[512,128]{1,0:T(8,128)(2,1)S(1)}, bf16[512,128]{1,0:T(8,128)(2,1)S(1)}, u32[]{:S(2)}, u32[]{:S(2)}) collective-permute-start(bf16[512,128]{1,0:T(8,128)(2,1)S(1)} %get-tuple-element.20), channel_id=1, source_target_pairs={{0,5},{1,4},{4,9},{5,8},{8,13},{9,12},{12,1},{13,0},{2,7},{3,6},{6... | collective-permute-start | bytes 393224 | tf_op jit(solution)/shard_map/ppermute | solution.py:34
  18.6 10.9 %collective-permute-start.2 = (bf16[1104,128]{1,0:T(8,128)(2,1)S(1)}, bf16[1104,128]{1,0:T(8,128)(2,1)S(1)}, u32[]{:S(2)}, u32[]{:S(2)}) collective-permute-start(bf16[1104,128]{1,0:T(8,128)(2,1)S(1)} %constant_dynamic-update-slice_fusion.refs_1_), channel_id=1, source_target_pairs={{0,4},{4,8},{8,12},{12,0},{1,5},{5,9},{9,13},{13,1},{2,6},{6,10},{... | collective-permute-start | bytes 847880 | tf_op jit(solution)/shard_map/ppermute | solution.py:22
  18.7 1.6 %collective-permute-start.6 = (bf16[16,32,256]{2,1,0:T(8,128)(2,1)S(1)}, bf16[16,32,256]{2,1,0:T(8,128)(2,1)S(1)}, u32[]{:S(2)}, u32[]{:S(2)}) collective-permute-start(bf16[16,32,256]{2,1,0:T(8,128)(2,1)S(1)} %collective-permute-done.4.refs_4_), channel_id=1, source_target_pairs={{0,1},{1,0},{2,3},{3,2},{4,5},{5,4},{6,7},{7,6},{8,9},{9,8},{10,11... | collective-permute-start | bytes 786440 | tf_op jit(solution)/shard_map/ppermute | solution.py:22
  20.3 1.0 %copy-start.1 = (bf16[16,32,256]{2,1,0:T(8,128)(2,1)S(1)}, bf16[16,32,256]{2,1,0:T(8,128)(2,1)}, u32[]{:S(2)}) copy-start(bf16[16,32,256]{2,1,0:T(8,128)(2,1)} %refs_3_.5) | copy-start | bytes 786436
  29.5 10.7 %collective-permute-start.7 = (bf16[1104,128]{1,0:T(8,128)(2,1)S(1)}, bf16[1104,128]{1,0:T(8,128)(2,1)S(1)}, u32[]{:S(2)}, u32[]{:S(2)}) collective-permute-start(bf16[1104,128]{1,0:T(8,128)(2,1)S(1)} %collective-permute-done.2.refs_1_), channel_id=1, source_target_pairs={{0,4},{4,8},{8,12},{12,0},{1,5},{5,9},{9,13},{13,1},{2,6},{6,10},{... | collective-permute-start | bytes 847880 | tf_op jit(solution)/shard_map/ppermute | solution.py:22
  48.3 3.9 %collective-permute-start.10 = (f32[56,128]{1,0:T(8,128)S(1)}, f32[56,128]{1,0:T(8,128)S(1)}, u32[]{:S(2)}, u32[]{:S(2)}) collective-permute-start(f32[56,128]{1,0:T(8,128)S(1)} %get-tuple-element.59), channel_id=1, source_target_pairs={{0,12},{4,0},{8,4},{12,8},{1,13},{5,1},{9,5},{13,9},{2,14},{6,2},{... | collective-permute-start | bytes 86024 | tf_op jit(solution)/shard_map/ppermute | solution.py:22
  50.2 4.8 %collective-permute-start.11 = (f32[56,128]{1,0:T(8,128)S(1)}, f32[56,128]{1,0:T(8,128)S(1)}, u32[]{:S(2)}, u32[]{:S(2)}) collective-permute-start(f32[56,128]{1,0:T(8,128)S(1)} %get-tuple-element.60), channel_id=1, source_target_pairs={{0,8},{4,12},{8,0},{12,4},{1,9},{5,13},{9,1},{13,5},{2,10},{6,14},... | collective-permute-start | bytes 86024 | tf_op jit(solution)/shard_map/ppermute | solution.py:22
  50.2 5.7 %collective-permute-start.12 = (f32[56,128]{1,0:T(8,128)S(1)}, f32[56,128]{1,0:T(8,128)S(1)}, u32[]{:S(2)}, u32[]{:S(2)}) collective-permute-start(f32[56,128]{1,0:T(8,128)S(1)} %get-tuple-element.61), channel_id=1, source_target_pairs={{0,4},{4,8},{8,12},{12,0},{1,5},{5,9},{9,13},{13,1},{2,6},{6,10},{... | collective-permute-start | bytes 86024 | tf_op jit(solution)/shard_map/ppermute | solution.py:22
  51.3 4.7 %collective-permute-start.8 = (bf16[16,32,512]{2,1,0:T(8,128)(2,1)S(1)}, bf16[16,32,512]{2,1,0:T(8,128)(2,1)S(1)}, u32[]{:S(2)}, u32[]{:S(2)}) collective-permute-start(bf16[16,32,512]{2,1,0:T(8,128)(2,1)S(1)} %get-tuple-element.29), channel_id=1, source_target_pairs={{0,1},{1,0},{2,3},{3,2},{4,5},{5,4},{6,7},{7,6},{8,9},{9,8},{10,11... | collective-permute-start | bytes 1572872 | tf_op jit(solution)/shard_map/ppermute | solution.py:22
  56.4 5.1 %collective-permute-start.13 = (f32[4,8,512]{2,1,0:T(8,128)S(1)}, f32[4,8,512]{2,1,0:T(8,128)S(1)}, u32[]{:S(2)}, u32[]{:S(2)}) collective-permute-start(f32[4,8,512]{2,1,0:T(8,128)S(1)} %fusion), channel_id=1, source_target_pairs={{0,2},{2,0},{1,3},{3,1},{4,6},{6,4},{5,7},{7,5},{8,10},{10,8},{9,1... | collective-permute-start | bytes 196616 | tf_op jit(solution)/shard_map/ppermute | solution.py:22
  57.8 6.9 %collective-permute-start.9 = (bf16[16,32,256]{2,1,0:T(8,128)(2,1)S(1)}, bf16[16,32,256]{2,1,0:T(8,128)(2,1)S(1)}, u32[]{:S(2)}, u32[]{:S(2)}) collective-permute-start(bf16[16,32,256]{2,1,0:T(8,128)(2,1)S(1)} %slice.252), channel_id=1, source_target_pairs={{0,2},{2,0},{1,3},{3,1},{4,6},{6,4},{5,7},{7,5},{8,10},{10,8},{9,1... | collective-permute-start | bytes 786440 | tf_op jit(solution)/shard_map/ppermute | solution.py:22
  61.5 1.3 %collective-permute-start.14 = (f32[4,8,512]{2,1,0:T(8,128)S(1)}, f32[4,8,512]{2,1,0:T(8,128)S(1)}, u32[]{:S(2)}, u32[]{:S(2)}) collective-permute-start(f32[4,8,512]{2,1,0:T(8,128)S(1)} %select_add_fusion), channel_id=1, source_target_pairs={{0,1},{1,0},{2,3},{3,2},{4,5},{5,4},{6,7},{7,6},{8,9},{9,8},{10,11... | collective-permute-start | bytes 196616 | tf_op jit(solution)/shard_map/ppermute | solution.py:22

commit v6 on v5

--- a/solution.py
+++ b/solution.py
@@ -50,7 +50,9 @@
     return out
 
 
-def prepare_kernel(places, density_ref, by_coord_ref, areas_ref, connect_ref, *out_refs):
+def prepare_kernel(
+    places, density_ref, by_coord_ref, areas_ref, connect_ref, cot_ref, cot_out_ref, *out_refs
+):
     part_refs, small_ref = out_refs[:-1], out_refs[-1]
     clusters, rhs, row_count = density_ref.shape
     quarter = part_refs[0].shape[1]
@@ -63,7 +65,8 @@
     first_id = places[3] * device + places[4] * sub_place
     ids = lax.broadcasted_iota(jnp.int32, (clusters, row_count), 0) * places[5]
     ids = ids + lax.broadcasted_iota(jnp.int32, (clusters, row_count), 1) + first_id
-    jitter = connect_ref[...] - ids
+    cot_out_ref[...] = cot_ref[...]
+    jitter = connect_ref[:, 0, :] - ids
     jitter = jnp.where(jitter > jitter_reach, jitter - places[6], jitter)
     jitter = jnp.where(jitter < -jitter_reach, jitter + places[6], jitter)
     jitter = jitter.astype(jnp.float32).astype(jnp.bfloat16)
@@ -82,7 +85,7 @@
 
 
 def own_kernel(*refs):
-    block_refs, (aug_ref, pos_ref, aug32) = refs[:-3], refs[-3:]
+    block_refs, (aug_ref, aug_t_ref, pos_ref, aug32) = refs[:-4], refs[-4:]
     clusters = aug_ref.shape[0]
     row_count = block_refs[0].shape[1]
     aug32[...] = jnp.zeros(aug32.shape, jnp.float32)
@@ -98,13 +101,15 @@
         for coord in range(3):
             pos_ref[coord, :, cols] = raw[coord]
     aug_ref[...] = aug32[...].astype(jnp.bfloat16)
+    for cluster in range(clusters):
+        aug_t_ref[cluster] = aug32[cluster].T.astype(jnp.bfloat16)
 
 
 def step_kernel(step, length, rhs, blocks, first, last, *refs):
-    items, source_ref, own_ref = refs[:3]
-    cot_refs = refs[3 : 3 + blocks[0] * blocks[1]]
+    items, source_ref, own_ref, own_t_ref = refs[:4]
+    cot_refs = refs[4 : 4 + blocks[0] * blocks[1]]
     width = rhs * blocks[1]
-    refs = refs[3 + len(cot_refs) :]
+    refs = refs[4 + len(cot_refs) :]
     if not first:
         acc_in = refs[0]
         refs = refs[1:]
@@ -184,12 +189,9 @@
         here, mate = decoded(place)
         mate = mate % clusters
         acc[here] += jnp.dot(left[mate], both[...], preferred_element_type=jnp.float32)
-        back[mate] += lax.dot_general(
-            own_ref[here],
-            both[quarter:, :],
-            (((1,), (1,)), ((), ())),
-            preferred_element_type=jnp.float32,
-        )[:8]
+        back[mate] += jnp.dot(
+            both[quarter:, :], own_t_ref[here], preferred_element_type=jnp.float32
+        )
 
     @pl.loop(0, items[step * length])
     def _(pair):
@@ -201,8 +203,10 @@
         pointwise(turn + 2, dist_a, prod_a, both_a)
         raw(turn + 3, dist_b, prod_b)
 
+    for cluster in range(clusters):
+        aug32[cluster] = back[cluster].T
     for coord in range(3):
-        back_ref[coord] = -0.5 * back[:, coord, :] - there[coord] * back[:, 6, :]
+        back_ref[coord] = -0.5 * aug32[:, coord, :] - there[coord] * aug32[:, 6, :]
     if last:
         for coord in range(3):
             grad_ref[coord] = (
@@ -213,7 +217,7 @@
         pot_out_ref[...] = acc[:, rhs:width, :].astype(jnp.bfloat16)
 
 
-def run_step(step, length, items, source, cots, own, pos, carried, last):
+def run_step(step, length, items, source, cots, own, own_t, pos, carried, last):
     clusters, _, panels = own.shape
     quarter = source.shape[1]
     rhs = cots[0].shape[1]
@@ -223,7 +227,7 @@
     first = carried is None
     vmem = pl.BlockSpec(memory_space=pltpu.VMEM)
     smem = pl.BlockSpec(memory_space=pltpu.SMEM)
-    operands = (items, source, own, *cots)
+    operands = (items, source, own, own_t, *cots)
     if not first:
         operands += (carried,)
     acc_shape = (clusters, width + AUG, panels)
@@ -234,7 +238,7 @@
         pltpu.VMEM((clusters, quarter, width), jnp.bfloat16),
         pltpu.VMEM((clusters, width + AUG, 2 * quarter), jnp.bfloat16),
         pltpu.VMEM((clusters + 1, quarter, LANES), jnp.float32),
-        pltpu.VMEM((clusters, 8, quarter), jnp.float32),
+        pltpu.VMEM((clusters, quarter, AUG), jnp.float32),
     ]
     scratch += [pltpu.VMEM((quarter, panels), jnp.float32)] * 4
     scratch += [pltpu.VMEM((2 * quarter, panels), jnp.bfloat16)] * 2
@@ -337,24 +341,27 @@
 
     by_coord = jnp.transpose(positions, (1, 0, 2))
     places = [device, sub_place, core, clusters * panels, row_count, panels, nodes_total]
-    *parts, small = pl.pallas_call(
+    own_cot, *parts, small = pl.pallas_call(
         prepare_kernel,
         out_shape=(
+            jax.ShapeDtypeStruct(cotangent.shape, jnp.bfloat16),
             jax.ShapeDtypeStruct((clusters * (rhs + 5), quarter), jnp.bfloat16),
             *[jax.ShapeDtypeStruct((clusters * rhs, quarter), jnp.bfloat16)] * (rhs_count - 1),
             jax.ShapeDtypeStruct((clusters * 4, row_count), jnp.bfloat16),
         ),
-        in_specs=[smem] + [vmem] * 4,
-        out_specs=(vmem,) * (rhs_count + 1),
-        compiler_params=pltpu.CompilerParams(vmem_limit_bytes=16 * 1024 * 1024),
+        in_specs=[smem] + [vmem] * 5,
+        out_specs=(vmem,) * (rhs_count + 2),
+        compiler_params=pltpu.CompilerParams(vmem_limit_bytes=56 * 1024 * 1024),
         name="prepare",
     )(jnp.stack([jnp.asarray(place, jnp.int32) for place in places]), density, by_coord, areas,
-      connect[:, 0, :])
+      connect, cotangent)
+    cots[0] = own_cot
     arrived = [shifted(parts[0], "clus", 1)]
     for step in range(1, rhs_count):
         arrived.append(
             moved(parts[step], ("clus", "rhs"), lambda z, c, step=step: (z + 1, c + step))
         )
+    arrived, cots = lax.optimization_barrier((arrived, cots))
     source = jnp.concatenate(arrived, axis=0)
 
     per_round = 2 * ((clusters // 2 + clus_count - 2) // (clus_count - 1))
@@ -387,14 +394,15 @@
         )
 
     jitter_all = in_order([block[3 * clusters :] for block in smalls]).astype(jnp.int32)
-    own, pos = pl.pallas_call(
+    own, own_t, pos = pl.pallas_call(
         own_kernel,
         out_shape=(
             jax.ShapeDtypeStruct((clusters, AUG, panels), jnp.bfloat16),
+            jax.ShapeDtypeStruct((clusters, panels, AUG), jnp.bfloat16),
             jax.ShapeDtypeStruct((3, clusters, panels), jnp.bfloat16),
         ),
         in_specs=[vmem] * sub_count,
-        out_specs=(vmem, vmem),
+        out_specs=(vmem, vmem, vmem),
         scratch_shapes=[pltpu.VMEM((clusters, AUG, panels), jnp.float32)],
         compiler_params=pltpu.CompilerParams(vmem_limit_bytes=16 * 1024 * 1024),
         name="target_rows",
@@ -408,7 +416,7 @@
                 source, backs[step - 3] = lax.optimization_barrier((source, backs[step - 3]))
             source = shifted(source, "clus", 1)
         last = step == clus_count - 1
-        results = run_step(step - 1, length, items, source, cots, own, pos, carried, last)
+        results = run_step(step - 1, length, items, source, cots, own, own_t, pos, carried, last)
         if last:
             pot, pot_out, grad, back = results
         else:

time: 65.7 us -> 64.6 us (0.983)
  waiting for transfers between devices: 19 us -> 15.2 us
  Pallas kernels: 26.6 us -> 29.1 us
  local copies, waits for them, and re-layouts: 5.22 us -> 3.3 us
  starting transfers between devices: 12.4 us -> 14.2 us
  other arithmetic: 1.14 us -> 1.83 us
    ppermute x14, waiting for transfers between devices: 17 us -> 12.1 us  [shifted(): return lax.ppermute(value, axis, pairs)]
    unnamed x14 -> x7, local copies, waits for them, and re-layouts: 3.36 us -> 1.72 us
    ppermute x14, starting transfers between devices: 11.3 us -> 12.8 us  [shifted(): return lax.ppermute(value, axis, pairs)]
    pallas_call x1, Pallas kernels: 0.6 us -> 1.95 us  [on_device(): pl.pallas_call(prepare_kernel, out_shape=(jax.ShapeDtypeStruct(cotangent....]
    ppermute x1, waiting for transfers between devices: 2.02 us -> 3.08 us  [moved(): return lax.ppermute(value, axes, pairs)]
    slice x1 -> x0, local copies, waits for them, and re-layouts: 0.85 us -> none  [on_device(): connect[:, 0, :]]
    select_n x4, other arithmetic: 0.05 us -> 0.75 us  [pick(): out = jnp.where(index == place, choices[place], out)]
  transfers between devices with their start and end apart: 15 -> 15, of which waited for: 10 -> 10; matrix products, arithmetic and copies ran while one was open for 4% -> 4% of each run, Pallas kernels for 28% -> 30%
where the time goes in v6:
time: 64.6 us; the launch traced here: 64.7 us
  Pallas kernels  29.1 us (45%)
  waiting for transfers between devices  15.2 us (24%)
  starting transfers between devices  14.2 us (22%)
  local copies, waits for them, and re-layouts  3.3 us (5%)
  other arithmetic  1.83 us (3%)
  between operations  1.02 us (2%)
    pallas_call x3, Pallas kernels, run_step(): pl.pallas_call(functools.partial(step_kernel, step, length, rhs, blocks,...  24.3 us
    ppermute x14, starting transfers between devices, shifted(): return lax.ppermute(value, axis, pairs)  12.8 us
    ppermute x14, waiting for transfers between devices, shifted(): return lax.ppermute(value, axis, pairs)  12.1 us
    ppermute x1, waiting for transfers between devices, moved(): return lax.ppermute(value, axes, pairs)  3.08 us
    pallas_call x1, Pallas kernels, on_device(): pl.pallas_call(prepare_kernel, out_shape=(jax.ShapeDtypeStruct(cotangent....  1.95 us
    unnamed x7, local copies, waits for them, and re-layouts  1.72 us
    ppermute x1, starting transfers between devices, moved(): return lax.ppermute(value, axes, pairs)  1.41 us
    pallas_call x1, Pallas kernels, on_device(): pl.pallas_call(node_kernel, out_shape=jax.ShapeDtypeStruct((3, share * pa...  1.32 us
  transfers between devices with their start and end apart: 15, of which 10 were waited for; matrix products, arithmetic and copies ran while one was open for 4% of the time, Pallas kernels for 30%

profile of v6, /device:TPU:0, one launch (start us, length us, event | category | flops | bytes accessed | tf_op | source)
XLA Modules:
  0.0 64.7 jit_solution(5977204021027446941)
XLA Ops:
  0.6 0.0 copy-start
  0.6 3.0 %collective-permute-start.2 = (bf16[16,32,256]{2,1,0:T(8,128)(2,1)}, bf16[16,32,256]{2,1,0:T(8,128)(2,1)S(1)}, u32[]{:S(2)}, u32[]{:S(2)}) collective-permute-start(bf16[16,32,256]{2,1,0:T(8,128)(2,1)} %cot_ref.1), channel_id=1, source_target_pairs={{0,2},{2,0},{1,3},{3,1},{4,6},{6,4},{5,7},{7,5},{8,10},{10,8},{9,1... | collective-permute-start | bytes 786440 | tf_op jit(solution)/shard_map/ppermute | solution.py:22
  3.6 0.0 collective-permute-start.3
  3.7 0.7 %stack.15.places = s32[7]{0:T(128)} concatenate(s32[1]{0:T(128)} %bitcast.1, s32[1]{0:T(128)} %bitcast.2, s32[1]{0:T(128)} %bitcast.3, s32[1]{0:T(128)} %constant.108.clone.1, s32[1]{0:T(128)} %constant.109.clone.1, s32[1]{0:T(128)} %constant.110.clone.1, s32[1]{0:T(128)} %constant.111.clone.1), dimensions={0} | concatenate | bytes 56 | tf_op jit(solution)/shard_map/stack | solution.py:356
  4.3 2.0 %prepare.1 = (bf16[16,32,256]{2,1,0:T(8,128)(2,1)}, bf16[592,128]{1,0:T(8,128)(2,1)}, bf16[512,128]{1,0:T(8,128)(2,1)}, bf16[64,256]{1,0:T(8,128)(2,1)}) custom-call(s32[7]{0:T(128)} %stack.15.places, bf16[16,32,256]{2,1,0:T(8,128)(2,1)} %density_ref.1, bf16[3,16,256]{2,1,0:T(8,128)(2,1)} %bitcast.50, bf16[16,256]{1,0:T(8,128)(2,1)} %areas_ref.1, ...), custom_call_target="tpu_custom_call" | custom-call | tf_op jit(solution)/shard_map/prepare/pallas_call | solution.py:344
  6.3 1.6 %collective-permute-start = (bf16[592,128]{1,0:T(8,128)(2,1)}, bf16[592,128]{1,0:T(8,128)(2,1)S(1)}, u32[]{:S(2)}, u32[]{:S(2)}) collective-permute-start(bf16[592,128]{1,0:T(8,128)(2,1)} %get-tuple-element.27), channel_id=1, source_target_pairs={{0,4},{4,8},{8,12},{12,0},{1,5},{5,9},{9,13},{13,1},{2,6},{6,10},{... | collective-permute-start | bytes 454664 | tf_op jit(solution)/shard_map/ppermute | solution.py:22
  7.8 1.4 %collective-permute-start.1 = (bf16[512,128]{1,0:T(8,128)(2,1)}, bf16[512,128]{1,0:T(8,128)(2,1)S(1)}, u32[]{:S(2)}, u32[]{:S(2)}) collective-permute-start(bf16[512,128]{1,0:T(8,128)(2,1)} %get-tuple-element.28), channel_id=1, source_target_pairs={{0,5},{1,4},{4,9},{5,8},{8,13},{9,12},{12,1},{13,0},{2,7},{3,6},{6... | collective-permute-start | bytes 393224 | tf_op jit(solution)/shard_map/ppermute | solution.py:34
  9.3 0.5 collective-permute-start.6
  9.8 0.0 copy-done
  9.8 0.1 constant_dynamic-slice_fusion
  9.9 0.1 reshape.282
  10.0 0.1 mul.22
  10.1 0.2 convert_reduce_fusion
  10.2 0.2 convert_reduce_fusion.1
  10.4 0.2 select_reduce_fusion
  10.6 0.1 copy.34
  10.7 0.1 pad_slice_fusion
  10.8 0.1 pad_add_fusion
  10.9 0.1 reshape.283.refs_0_
  10.9 0.1 pad.40.clone
  11.0 0.0 collective-permute-done.2.refs_5_
  11.0 0.0 collective-permute-start.4
  11.1 2.3 %collective-permute-done.6.refs_1_ = bf16[64,256]{1,0:T(8,128)(2,1)S(1)} collective-permute-done((bf16[64,256]{1,0:T(8,128)(2,1)}, bf16[64,256]{1,0:T(8,128)(2,1)S(1)}, u32[]{:S(2)}, u32[]{:S(2)}) %collective-permute-start.6) | collective-permute-done | bytes 32800 | tf_op jit(solution)/shard_map/ppermute | solution.py:22
  13.4 0.7 %broadcast_select_fusion.5 = (bf16[16,256]{1,0:T(8,128)(2,1)S(1)}, bf16[16,256]{1,0:T(8,128)(2,1)S(1)}) fusion(pred[]{:T(512)S(6)} %eq.104, bf16[64,256]{1,0:T(8,128)(2,1)S(1)} %collective-permute-done.6.refs_1_, bf16[64,256]{1,0:T(8,128)(2,1)} %get-tuple-element.32.refs_0_, pred[]{:T(512)S(6)} %eq.105), kind=kLoop, calls=%fused_computation.42 | loop fusion | flops 8192 | bytes 32770 | tf_op jit(solution)/shard_map/jit(_where)/select_n | solution.py:49
  14.1 3.1 %collective-permute-done.1 = bf16[512,128]{1,0:T(8,128)(2,1)S(1)} collective-permute-done((bf16[512,128]{1,0:T(8,128)(2,1)}, bf16[512,128]{1,0:T(8,128)(2,1)S(1)}, u32[]{:S(2)}, u32[]{:S(2)}) %collective-permute-start.1) | collective-permute-done | bytes 131104 | tf_op jit(solution)/shard_map/ppermute | solution.py:34
  17.2 0.0 collective-permute-done
  17.2 0.0 collective-permute-done.3.refs_6_
  17.2 0.0 collective-permute-done.4.refs_7_
  17.2 0.1 collective-permute-start.5
  17.3 0.0 copy-start.2
  17.3 0.7 %copy-done.2 = bf16[64,256]{1,0:T(8,128)(2,1)S(1)} copy-done((bf16[64,256]{1,0:T(8,128)(2,1)S(1)}, bf16[64,256]{1,0:T(8,128)(2,1)}, u32[]{:S(2)}) %copy-start.2) | copy-done | bytes 32792
  18.1 0.7 %target_rows.1 = (bf16[16,16,512]{2,1,0:T(8,128)(2,1)S(1)}, bf16[16,512,16]{2,1,0:T(8,128)(2,1)S(1)}, bf16[3,16,512]{2,1,0:T(8,128)(2,1)S(1)}) custom-call(bf16[64,256]{1,0:T(8,128)(2,1)S(1)} %copy-done.2, bf16[64,256]{1,0:T(8,128)(2,1)S(1)} %collective-permute-done.6.refs_1_), custom_call_target="tpu_custom_call" | custom-call | tf_op jit(solution)/shard_map/target_rows/pallas_call | solution.py:397
  18.8 0.0 copy-start.1
  18.9 0.9 %copy-done.1 = bf16[16,32,256]{2,1,0:T(8,128)(2,1)S(1)} copy-done((bf16[16,32,256]{2,1,0:T(8,128)(2,1)S(1)}, bf16[16,32,256]{2,1,0:T(8,128)(2,1)}, u32[]{:S(2)}) %copy-start.1) | copy-done | bytes 262168
  19.8 8.0 %near_field_0.1 = (f32[16,80,512]{2,1,0:T(8,128)S(1)}, f32[3,16,128]{2,1,0:T(8,128)S(1)}) custom-call(s32[108]{0:T(128)S(1)} %reshape.283.refs_0_, bf16[1104,128]{1,0:T(8,128)(2,1)S(1)} %constant_dynamic-update-slice_fusion.refs_1_, bf16[16,16,512]{2,1,0:T(8,128)(2,1)S(1)} %get-tuple-element.33.refs_2_, bf16[16,512,16]{2,1,0:T(8,128)(2,1)S(1)} %get-tuple-element.34.refs_3_, ...), custom_call_target="tpu_custom_call" | custom-call | flops 692060160 | bytes 6291456 | tf_op jit(solution)/shard_map/near_field_0/pallas_call | solution.py:257
  27.8 0.1 collective-permute-done.5.refs_1_
  27.9 2.0 %collective-permute-start.7 = (bf16[1104,128]{1,0:T(8,128)(2,1)S(1)}, bf16[1104,128]{1,0:T(8,128)(2,1)S(1)}, u32[]{:S(2)}, u32[]{:S(2)}) collective-permute-start(bf16[1104,128]{1,0:T(8,128)(2,1)S(1)} %collective-permute-done.5.refs_1_), channel_id=1, source_target_pairs={{0,4},{4,8},{8,12},{12,0},{1,5},{5,9},{9,13},{13,1},{2,6},{6,10},{... | collective-permute-start | bytes 847880 | tf_op jit(solution)/shard_map/ppermute | solution.py:22
  29.9 7.5 %near_field_1.1 = (f32[16,80,512]{2,1,0:T(8,128)S(1)}, f32[3,16,128]{2,1,0:T(8,128)S(1)}) custom-call(s32[108]{0:T(128)S(1)} %reshape.283.refs_0_, bf16[1104,128]{1,0:T(8,128)(2,1)S(1)} %collective-permute-done.5.refs_1_, bf16[16,16,512]{2,1,0:T(8,128)(2,1)S(1)} %get-tuple-element.33.refs_2_, bf16[16,512,16]{2,1,0:T(8,128)(2,1)S(1)} %get-tuple-element.34.refs_3_, ...), custom_call_target="tpu_custom_call" | custom-call | flops 692060160 | bytes 6291456 | tf_op jit(solution)/shard_map/near_field_1/pallas_call | solution.py:257
  37.4 1.8 %collective-permute-done.7.refs_1_ = bf16[1104,128]{1,0:T(8,128)(2,1)S(1)} collective-permute-done((bf16[1104,128]{1,0:T(8,128)(2,1)S(1)}, bf16[1104,128]{1,0:T(8,128)(2,1)S(1)}, u32[]{:S(2)}, u32[]{:S(2)}) %collective-permute-start.7) | collective-permute-done | bytes 282656 | tf_op jit(solution)/shard_map/ppermute | solution.py:22
  39.3 8.9 %near_field_2.1 = (f32[16,32,512]{2,1,0:T(8,128)S(1)}, bf16[16,32,512]{2,1,0:T(8,128)(2,1)S(1)}, f32[3,16,512]{2,1,0:T(8,128)S(1)}, f32[3,16,128]{2,1,0:T(8,128)S(1)}) custom-call(s32[108]{0:T(128)S(1)} %reshape.283.refs_0_, bf16[1104,128]{1,0:T(8,128)(2,1)S(1)} %collective-permute-done.7.refs_1_, bf16[16,16,512]{2,1,0:T(8,128)(2,1)S(1)} %get-tuple-element.33.refs_2_, ...), custom_call_target="tpu_custom_call" | custom-call | flops 692060160 | bytes 6291456 | tf_op jit(solution)/shard_map/near_field_2/pallas_call | solution.py:257
  48.2 0.1 copy.38
  48.3 0.1 maximum_maximum_fusion
  48.4 0.9 %collective-permute-start.10 = (f32[56,128]{1,0:T(8,128)S(1)}, f32[56,128]{1,0:T(8,128)S(1)}, u32[]{:S(2)}, u32[]{:S(2)}) collective-permute-start(f32[56,128]{1,0:T(8,128)S(1)} %get-tuple-element.75), channel_id=1, source_target_pairs={{0,12},{4,0},{8,4},{12,8},{1,13},{5,1},{9,5},{13,9},{2,14},{6,2},{... | collective-permute-start | bytes 86024 | tf_op jit(solution)/shard_map/ppermute | solution.py:22
  49.3 0.6 collective-permute-start.11
  49.9 1.9 %collective-permute-start.12 = (f32[56,128]{1,0:T(8,128)S(1)}, f32[56,128]{1,0:T(8,128)S(1)}, u32[]{:S(2)}, u32[]{:S(2)}) collective-permute-start(f32[56,128]{1,0:T(8,128)S(1)} %get-tuple-element.77), channel_id=1, source_target_pairs={{0,4},{4,8},{8,12},{12,0},{1,5},{5,9},{9,13},{13,1},{2,6},{6,10},{... | collective-permute-start | bytes 86024 | tf_op jit(solution)/shard_map/ppermute | solution.py:22
  51.8 0.0 collective-permute-start.8
  51.8 0.5 collective-permute-done.10
  52.3 1.9 %collective-permute-done.11 = f32[56,128]{1,0:T(8,128)S(1)} collective-permute-done((f32[56,128]{1,0:T(8,128)S(1)}, f32[56,128]{1,0:T(8,128)S(1)}, u32[]{:S(2)}, u32[]{:S(2)}) %collective-permute-start.11) | collective-permute-done | bytes 28704 | tf_op jit(solution)/shard_map/ppermute | solution.py:22
  54.2 1.4 %collective-permute-done.12 = f32[56,128]{1,0:T(8,128)S(1)} collective-permute-done((f32[56,128]{1,0:T(8,128)S(1)}, f32[56,128]{1,0:T(8,128)S(1)}, u32[]{:S(2)}, u32[]{:S(2)}) %collective-permute-start.12) | collective-permute-done | bytes 28704 | tf_op jit(solution)/shard_map/ppermute | solution.py:22
  55.7 0.0 collective-permute-done.8
  55.7 0.2 convert_add_fusion
  56.1 0.7 %collective-permute-start.13 = (f32[4,8,512]{2,1,0:T(8,128)S(1)}, f32[4,8,512]{2,1,0:T(8,128)S(1)}, u32[]{:S(2)}, u32[]{:S(2)}) collective-permute-start(f32[4,8,512]{2,1,0:T(8,128)S(1)} %fusion), channel_id=1, source_target_pairs={{0,2},{2,0},{1,3},{3,1},{4,6},{6,4},{5,7},{7,5},{8,10},{10,8},{9,1... | collective-permute-start | bytes 196616 | tf_op jit(solution)/shard_map/ppermute | solution.py:22
  56.8 1.4 %collective-permute-start.9 = (bf16[16,32,256]{2,1,0:T(8,128)(2,1)S(1)}, bf16[16,32,256]{2,1,0:T(8,128)(2,1)S(1)}, u32[]{:S(2)}, u32[]{:S(2)}) collective-permute-start(bf16[16,32,256]{2,1,0:T(8,128)(2,1)S(1)} %slice.247), channel_id=1, source_target_pairs={{0,2},{2,0},{1,3},{3,1},{4,6},{6,4},{5,7},{7,5},{8,10},{10,8},{9,1... | collective-permute-start | bytes 786440 | tf_op jit(solution)/shard_map/ppermute | solution.py:22
  58.3 2.9 %collective-permute-done.13 = f32[4,8,512]{2,1,0:T(8,128)S(1)} collective-permute-done((f32[4,8,512]{2,1,0:T(8,128)S(1)}, f32[4,8,512]{2,1,0:T(8,128)S(1)}, u32[]{:S(2)}, u32[]{:S(2)}) %collective-permute-start.13) | collective-permute-done | bytes 65568 | tf_op jit(solution)/shard_map/ppermute | solution.py:22
  61.1 0.1 collective-permute-start.14
  61.3 1.2 %collective-permute-done.14 = f32[4,8,512]{2,1,0:T(8,128)S(1)} collective-permute-done((f32[4,8,512]{2,1,0:T(8,128)S(1)}, f32[4,8,512]{2,1,0:T(8,128)S(1)}, u32[]{:S(2)}, u32[]{:S(2)}) %collective-permute-start.14) | collective-permute-done | bytes 65568 | tf_op jit(solution)/shard_map/ppermute | solution.py:22
  62.5 1.3 %node_terms.1 = f32[3,4096]{1,0:T(4,128)} custom-call(f32[3,8,512]{2,1,0:T(8,128)S(1)} %slice.183.grad_ref, s32[8,512]{1,0:T(8,128)S(1)} %slice_select_fusion.2.jitter_ref, f32[8,512]{1,0:T(8,128)S(1)} %slice_bitcast_fusion.edge_ref), custom_call_target="tpu_custom_call" | custom-call | flops 1048576 | bytes 262144 | tf_op jit(solution)/shard_map/node_terms/pallas_call | solution.py:505
  63.8 0.1 collective-permute-done.9.refs_1_
  63.9 0.7 %potential_sum.1 = bf16[16,32,256]{2,1,0:T(8,128)(2,1)} custom-call(f32[16,32,256]{2,1,0:T(8,128)S(1)} %slice.122.refs_0_, bf16[16,32,256]{2,1,0:T(8,128)(2,1)S(1)} %collective-permute-done.9.refs_1_), custom_call_target="tpu_custom_call" | custom-call | flops 1048576 | bytes 262144 | tf_op jit(solution)/shard_map/potential_sum/pallas_call | solution.py:514
  (46 shorter events, 0.6 us)
Async XLA Ops:
  0.6 9.2 %copy-start = (s32[5,64]{1,0:T(8,128)S(1)}, s32[5,64]{1,0:T(8,128)}, u32[]{:S(2)}) copy-start(s32[5,64]{1,0:T(8,128)} %param.10) | copy-start | bytes 3844
  0.6 10.4 %collective-permute-start.2 = (bf16[16,32,256]{2,1,0:T(8,128)(2,1)}, bf16[16,32,256]{2,1,0:T(8,128)(2,1)S(1)}, u32[]{:S(2)}, u32[]{:S(2)}) collective-permute-start(bf16[16,32,256]{2,1,0:T(8,128)(2,1)} %cot_ref.1), channel_id=1, source_target_pairs={{0,2},{2,0},{1,3},{3,1},{4,6},{6,4},{5,7},{7,5},{8,10},{10,8},{9,1... | collective-permute-start | bytes 786440 | tf_op jit(solution)/shard_map/ppermute | solution.py:22
  3.6 13.5 %collective-permute-start.3 = (bf16[16,32,256]{2,1,0:T(8,128)(2,1)}, bf16[16,32,256]{2,1,0:T(8,128)(2,1)S(1)}, u32[]{:S(2)}, u32[]{:S(2)}) collective-permute-start(bf16[16,32,256]{2,1,0:T(8,128)(2,1)} %cot_ref.1), channel_id=1, source_target_pairs={{0,1},{1,0},{2,3},{3,2},{4,5},{5,4},{6,7},{7,6},{8,9},{9,8},{10,11... | collective-permute-start | bytes 786440 | tf_op jit(solution)/shard_map/ppermute | solution.py:22
  6.3 10.9 %collective-permute-start = (bf16[592,128]{1,0:T(8,128)(2,1)}, bf16[592,128]{1,0:T(8,128)(2,1)S(1)}, u32[]{:S(2)}, u32[]{:S(2)}) collective-permute-start(bf16[592,128]{1,0:T(8,128)(2,1)} %get-tuple-element.27), channel_id=1, source_target_pairs={{0,4},{4,8},{8,12},{12,0},{1,5},{5,9},{9,13},{13,1},{2,6},{6,10},{... | collective-permute-start | bytes 454664 | tf_op jit(solution)/shard_map/ppermute | solution.py:22
  7.8 9.3 %collective-permute-start.1 = (bf16[512,128]{1,0:T(8,128)(2,1)}, bf16[512,128]{1,0:T(8,128)(2,1)S(1)}, u32[]{:S(2)}, u32[]{:S(2)}) collective-permute-start(bf16[512,128]{1,0:T(8,128)(2,1)} %get-tuple-element.28), channel_id=1, source_target_pairs={{0,5},{1,4},{4,9},{5,8},{8,13},{9,12},{12,1},{13,0},{2,7},{3,6},{6... | collective-permute-start | bytes 393224 | tf_op jit(solution)/shard_map/ppermute | solution.py:34
  9.3 4.1 %collective-permute-start.6 = (bf16[64,256]{1,0:T(8,128)(2,1)}, bf16[64,256]{1,0:T(8,128)(2,1)S(1)}, u32[]{:S(2)}, u32[]{:S(2)}) collective-permute-start(bf16[64,256]{1,0:T(8,128)(2,1)} %get-tuple-element.32.refs_0_), channel_id=1, source_target_pairs={{0,2},{2,0},{1,3},{3,1},{4,6},{6,4},{5,7},{7,5},{8,10},{10,8},{9,1... | collective-permute-start | bytes 98312 | tf_op jit(solution)/shard_map/ppermute | solution.py:22
  11.0 6.2 %collective-permute-start.4 = (bf16[16,32,256]{2,1,0:T(8,128)(2,1)S(1)}, bf16[16,32,256]{2,1,0:T(8,128)(2,1)S(1)}, u32[]{:S(2)}, u32[]{:S(2)}) collective-permute-start(bf16[16,32,256]{2,1,0:T(8,128)(2,1)S(1)} %collective-permute-done.2.refs_5_), channel_id=1, source_target_pairs={{0,1},{1,0},{2,3},{3,2},{4,5},{5,4},{6,7},{7,6},{8,9},{9,8},{10,11... | collective-permute-start | bytes 786440 | tf_op jit(solution)/shard_map/ppermute | solution.py:22
  17.2 10.6 %collective-permute-start.5 = (bf16[1104,128]{1,0:T(8,128)(2,1)S(1)}, bf16[1104,128]{1,0:T(8,128)(2,1)S(1)}, u32[]{:S(2)}, u32[]{:S(2)}) collective-permute-start(bf16[1104,128]{1,0:T(8,128)(2,1)S(1)} %constant_dynamic-update-slice_fusion.refs_1_), channel_id=1, source_target_pairs={{0,4},{4,8},{8,12},{12,0},{1,5},{5,9},{9,13},{13,1},{2,6},{6,10},{... | collective-permute-start | bytes 847880 | tf_op jit(solution)/shard_map/ppermute | solution.py:22
  17.3 0.8 %copy-start.2 = (bf16[64,256]{1,0:T(8,128)(2,1)S(1)}, bf16[64,256]{1,0:T(8,128)(2,1)}, u32[]{:S(2)}) copy-start(bf16[64,256]{1,0:T(8,128)(2,1)} %get-tuple-element.32.refs_0_) | copy-start | bytes 98308
  18.8 1.0 %copy-start.1 = (bf16[16,32,256]{2,1,0:T(8,128)(2,1)S(1)}, bf16[16,32,256]{2,1,0:T(8,128)(2,1)}, u32[]{:S(2)}) copy-start(bf16[16,32,256]{2,1,0:T(8,128)(2,1)} %get-tuple-element.35.refs_4_) | copy-start | bytes 786436
  27.9 11.4 %collective-permute-start.7 = (bf16[1104,128]{1,0:T(8,128)(2,1)S(1)}, bf16[1104,128]{1,0:T(8,128)(2,1)S(1)}, u32[]{:S(2)}, u32[]{:S(2)}) collective-permute-start(bf16[1104,128]{1,0:T(8,128)(2,1)S(1)} %collective-permute-done.5.refs_1_), channel_id=1, source_target_pairs={{0,4},{4,8},{8,12},{12,0},{1,5},{5,9},{9,13},{13,1},{2,6},{6,10},{... | collective-permute-start | bytes 847880 | tf_op jit(solution)/shard_map/ppermute | solution.py:22
  48.4 3.9 %collective-permute-start.10 = (f32[56,128]{1,0:T(8,128)S(1)}, f32[56,128]{1,0:T(8,128)S(1)}, u32[]{:S(2)}, u32[]{:S(2)}) collective-permute-start(f32[56,128]{1,0:T(8,128)S(1)} %get-tuple-element.75), channel_id=1, source_target_pairs={{0,12},{4,0},{8,4},{12,8},{1,13},{5,1},{9,5},{13,9},{2,14},{6,2},{... | collective-permute-start | bytes 86024 | tf_op jit(solution)/shard_map/ppermute | solution.py:22
  49.3 4.9 %collective-permute-start.11 = (f32[56,128]{1,0:T(8,128)S(1)}, f32[56,128]{1,0:T(8,128)S(1)}, u32[]{:S(2)}, u32[]{:S(2)}) collective-permute-start(f32[56,128]{1,0:T(8,128)S(1)} %get-tuple-element.76), channel_id=1, source_target_pairs={{0,8},{4,12},{8,0},{12,4},{1,9},{5,13},{9,1},{13,5},{2,10},{6,14},... | collective-permute-start | bytes 86024 | tf_op jit(solution)/shard_map/ppermute | solution.py:22
  49.9 5.7 %collective-permute-start.12 = (f32[56,128]{1,0:T(8,128)S(1)}, f32[56,128]{1,0:T(8,128)S(1)}, u32[]{:S(2)}, u32[]{:S(2)}) collective-permute-start(f32[56,128]{1,0:T(8,128)S(1)} %get-tuple-element.77), channel_id=1, source_target_pairs={{0,4},{4,8},{8,12},{12,0},{1,5},{5,9},{9,13},{13,1},{2,6},{6,10},{... | collective-permute-start | bytes 86024 | tf_op jit(solution)/shard_map/ppermute | solution.py:22
  51.8 3.9 %collective-permute-start.8 = (bf16[16,32,512]{2,1,0:T(8,128)(2,1)S(1)}, bf16[16,32,512]{2,1,0:T(8,128)(2,1)S(1)}, u32[]{:S(2)}, u32[]{:S(2)}) collective-permute-start(bf16[16,32,512]{2,1,0:T(8,128)(2,1)S(1)} %get-tuple-element.45), channel_id=1, source_target_pairs={{0,1},{1,0},{2,3},{3,2},{4,5},{5,4},{6,7},{7,6},{8,9},{9,8},{10,11... | collective-permute-start | bytes 1572872 | tf_op jit(solution)/shard_map/ppermute | solution.py:22
  56.1 5.1 %collective-permute-start.13 = (f32[4,8,512]{2,1,0:T(8,128)S(1)}, f32[4,8,512]{2,1,0:T(8,128)S(1)}, u32[]{:S(2)}, u32[]{:S(2)}) collective-permute-start(f32[4,8,512]{2,1,0:T(8,128)S(1)} %fusion), channel_id=1, source_target_pairs={{0,2},{2,0},{1,3},{3,1},{4,6},{6,4},{5,7},{7,5},{8,10},{10,8},{9,1... | collective-permute-start | bytes 196616 | tf_op jit(solution)/shard_map/ppermute | solution.py:22
  56.8 7.1 %collective-permute-start.9 = (bf16[16,32,256]{2,1,0:T(8,128)(2,1)S(1)}, bf16[16,32,256]{2,1,0:T(8,128)(2,1)S(1)}, u32[]{:S(2)}, u32[]{:S(2)}) collective-permute-start(bf16[16,32,256]{2,1,0:T(8,128)(2,1)S(1)} %slice.247), channel_id=1, source_target_pairs={{0,2},{2,0},{1,3},{3,1},{4,6},{6,4},{5,7},{7,5},{8,10},{10,8},{9,1... | collective-permute-start | bytes 786440 | tf_op jit(solution)/shard_map/ppermute | solution.py:22
  61.1 1.3 %collective-permute-start.14 = (f32[4,8,512]{2,1,0:T(8,128)S(1)}, f32[4,8,512]{2,1,0:T(8,128)S(1)}, u32[]{:S(2)}, u32[]{:S(2)}) collective-permute-start(f32[4,8,512]{2,1,0:T(8,128)S(1)} %select_add_fusion), channel_id=1, source_target_pairs={{0,1},{1,0},{2,3},{3,2},{4,5},{5,4},{6,7},{7,6},{8,9},{9,8},{10,11... | collective-permute-start | bytes 196616 | tf_op jit(solution)/shard_map/ppermute | solution.py:22

commit v7 on v5

--- a/solution.py
+++ b/solution.py
@@ -50,22 +50,35 @@
     return out
 
 
-def prepare_kernel(places, density_ref, by_coord_ref, areas_ref, connect_ref, *out_refs):
-    part_refs, small_ref = out_refs[:-1], out_refs[-1]
+def prepare_kernel(sizes, *refs):
+    arguments, refs = refs[:5], refs[5:]
+    cot_out_ref, part_refs, small_ref = refs[0], refs[1:-7], refs[-7]
+    density_ref, by_coord_ref, areas_ref, connect_ref, cot_ref, sems = refs[-6:]
+    copies = []
+    for at, (argument, place) in enumerate(
+        zip(arguments, (density_ref, by_coord_ref, areas_ref, connect_ref, cot_ref))
+    ):
+        copies.append(pltpu.make_async_copy(argument, place, sems.at[at]))
+        copies[-1].start()
+    for copy in copies:
+        copy.wait()
+
     clusters, rhs, row_count = density_ref.shape
     quarter = part_refs[0].shape[1]
     count = len(part_refs)
-    device, sub_place, core = places[0], places[1], places[2]
+    panels, nodes_total = sizes
+    device, sub_place, core = (lax.axis_index(axis) for axis in ("clus", "sub", "rhs"))
 
     def part_of(array, place):
         return pick(place, [array[:, at * quarter : (at + 1) * quarter] for at in range(count)])
 
-    first_id = places[3] * device + places[4] * sub_place
-    ids = lax.broadcasted_iota(jnp.int32, (clusters, row_count), 0) * places[5]
+    cot_out_ref[...] = cot_ref[...]
+    first_id = clusters * panels * device + row_count * sub_place
+    ids = lax.broadcasted_iota(jnp.int32, (clusters, row_count), 0) * panels
     ids = ids + lax.broadcasted_iota(jnp.int32, (clusters, row_count), 1) + first_id
-    jitter = connect_ref[...] - ids
-    jitter = jnp.where(jitter > jitter_reach, jitter - places[6], jitter)
-    jitter = jnp.where(jitter < -jitter_reach, jitter + places[6], jitter)
+    jitter = connect_ref[:, 0, :] - ids
+    jitter = jnp.where(jitter > jitter_reach, jitter - nodes_total, jitter)
+    jitter = jnp.where(jitter < -jitter_reach, jitter + nodes_total, jitter)
     jitter = jitter.astype(jnp.float32).astype(jnp.bfloat16)
     rows = [by_coord_ref[coord] for coord in range(3)] + [areas_ref[...], jitter]
     base = clusters * rhs
@@ -81,41 +94,43 @@
             small_ref[at * clusters : (at + 1) * clusters, :] = value
 
 
-def own_kernel(*refs):
-    block_refs, (aug_ref, pos_ref, aug32) = refs[:-3], refs[-3:]
-    clusters = aug_ref.shape[0]
-    row_count = block_refs[0].shape[1]
+def target_kernel(rhs_count, small_ref, *refs):
+    cot_refs, (lhs_ref, aug_ref, aug32) = refs[:rhs_count], refs[rhs_count:]
+    clusters, _, row_count = aug_ref.shape
+    pos = [
+        small_ref[coord * clusters : (coord + 1) * clusters, :].astype(jnp.float32)
+        for coord in range(3)
+    ]
+    square = pos[0] * pos[0] + pos[1] * pos[1] + pos[2] * pos[2] + core_radius * core_radius
+    ones = jnp.ones_like(square)
     aug32[...] = jnp.zeros(aug32.shape, jnp.float32)
-    for place, block_ref in enumerate(block_refs):
-        cols = slice(place * row_count, (place + 1) * row_count)
-        raw = [block_ref[coord * clusters : (coord + 1) * clusters, :] for coord in range(3)]
-        pos = [value.astype(jnp.float32) for value in raw]
-        square = pos[0] * pos[0] + pos[1] * pos[1] + pos[2] * pos[2] + core_radius * core_radius
-        ones = jnp.ones_like(square)
-        rows = [-2.0 * value for value in pos] + three_parts(square) + [ones] * 3
-        for row, value in enumerate(rows):
-            aug32[:, row, cols] = value
-        for coord in range(3):
-            pos_ref[coord, :, cols] = raw[coord]
-    aug_ref[...] = aug32[...].astype(jnp.bfloat16)
-
-
-def step_kernel(step, length, rhs, blocks, first, last, *refs):
-    items, source_ref, own_ref = refs[:3]
-    cot_refs = refs[3 : 3 + blocks[0] * blocks[1]]
-    width = rhs * blocks[1]
-    refs = refs[3 + len(cot_refs) :]
+    for row, value in enumerate([-2.0 * value for value in pos] + three_parts(square) + [ones] * 3):
+        aug32[:, row, :] = value
+    filled = AUG + sum(ref.shape[1] for ref in cot_refs)
+    blank = jnp.zeros((LANES - filled, row_count), jnp.bfloat16)
+    for cluster in range(clusters):
+        aug = aug32[cluster].astype(jnp.bfloat16)
+        aug_ref[cluster] = aug
+        rows = [ref[cluster] for ref in cot_refs] + [aug, blank]
+        lhs_ref[cluster] = jnp.concatenate(rows, axis=0).T
+
+
+def step_kernel(step, length, rhs, subs, first, last, *refs):
+    items, source_ref = refs[:2]
+    lhs_refs, aug_refs, refs = refs[2 : 2 + subs], refs[2 + subs : 2 + 2 * subs], refs[2 + 2 * subs :]
     if not first:
-        acc_in = refs[0]
-        refs = refs[1:]
+        acc_in, refs = refs[0], refs[1:]
     if last:
-        pos_ref, pot_ref, pot_out_ref, grad_ref, back_ref, acc = refs[:6]
-        refs = refs[6:]
+        small_refs, refs = refs[:subs], refs[subs:]
+        pot_ref, pot_out_ref, grad_ref, back_ref, acc = refs[:5]
+        refs = refs[5:]
     else:
         acc, back_ref = refs[:2]
         refs = refs[2:]
-    aug32, aug_t, dens_t, left, weight, back, dist_a, dist_b, prod_a, prod_b, both_a, both_b = refs
-    clusters, _, panels = own_ref.shape
+    aug32, left, weight, back, raw_a, raw_b, both_a, both_b = refs
+    clusters, rows, panels = acc.shape
+    width = rows - AUG
+    row_count = panels // subs
     quarter = source_ref.shape[1]
     base = clusters * rhs
     starts = [0] + list(range(base + 5 * clusters, source_ref.shape[0], base))
@@ -130,116 +145,101 @@
     aug32[...] = jnp.zeros(aug32.shape, jnp.float32)
     for row, value in enumerate(there + [ones] * 3 + three_parts(square)):
         aug32[:, row, :] = value
-    weight_t = (CP ** (-0.5) * area).T
+    weight[...] = jnp.zeros(weight.shape, jnp.float32)
+    weight[:clusters, :] = CP ** (-0.5) * area
     left[...] = jnp.zeros(left.shape, left.dtype)
     for cluster in range(clusters):
-        rows = aug32[cluster]
-        left[cluster, width:, quarter:] = rows.astype(jnp.bfloat16)
-        aug_t[cluster] = rows.T.astype(jnp.bfloat16)
-        dens = jnp.concatenate(
-            [source_ref[at + cluster * rhs : at + (cluster + 1) * rhs, :] for at in starts], axis=0
-        )
-        left[cluster, :width, :quarter] = dens
-        dens_t[cluster] = dens.T
-        weight[cluster] = jnp.broadcast_to(weight_t[:, cluster : cluster + 1], (quarter, LANES))
-    weight[clusters] = jnp.zeros((quarter, LANES), jnp.float32)
+        left[cluster, width:rows, quarter:] = aug32[cluster].astype(jnp.bfloat16)
+        for place, at in enumerate(starts):
+            left[cluster, place * rhs : (place + 1) * rhs, :quarter] = source_ref[
+                at + cluster * rhs : at + (cluster + 1) * rhs, :
+            ]
     back[...] = jnp.zeros(back.shape, jnp.float32)
     if first:
         acc[...] = jnp.zeros(acc.shape, jnp.float32)
     else:
         acc[...] = acc_in[...]
-    dist_b[...] = jnp.ones(dist_b.shape, jnp.float32)
-    prod_b[...] = jnp.zeros(prod_b.shape, jnp.float32)
+    raw_b[...] = jnp.ones(raw_b.shape, jnp.float32)
     both_a[...] = jnp.zeros(both_a.shape, both_a.dtype)
 
     def decoded(place):
         code = items[step * length + place]
         return code // (2 * clusters), code % (2 * clusters)
 
-    def raw(place, dist, prod):
+    def products(place, raw):
         here, mate = decoded(place)
         mate = mate % clusters
-        dist[...] = jnp.dot(aug_t[mate], own_ref[here], preferred_element_type=jnp.float32)
-        cot = [
-            jnp.concatenate(
-                [ref[here] for ref in cot_refs[at * blocks[0] : (at + 1) * blocks[0]]], axis=1
-            )
-            for at in range(blocks[1])
-        ]
-        prod[...] = jnp.dot(
-            dens_t[mate], jnp.concatenate(cot, axis=0), preferred_element_type=jnp.float32
-        )
-
-    def pointwise(place, dist, prod, both):
+        lhs = jnp.concatenate([ref[here] for ref in lhs_refs], axis=0)
+        raw[...] = jnp.dot(lhs, left[mate], preferred_element_type=jnp.float32)
+
+    def pointwise(place, raw, both):
         _, mate = decoded(place)
-        scale = weight[mate]
+        scale = weight[pl.ds(mate, 1), :]
         for start in range(0, panels, LANES):
-            cols = slice(start, start + LANES)
-            inverse = lax.rsqrt(dist[:, cols])
+            span = slice(start, start + LANES)
+            inverse = lax.rsqrt(raw[span, quarter:])
             kernel = scale * inverse
-            both[:quarter, cols] = kernel.astype(jnp.bfloat16)
-            both[quarter:, cols] = ((inverse * inverse) * (kernel * prod[:, cols])).astype(jnp.bfloat16)
+            both[span, :quarter] = kernel.astype(jnp.bfloat16)
+            weighted = (inverse * inverse) * (kernel * raw[span, :quarter])
+            both[span, quarter:] = weighted.astype(jnp.bfloat16)
 
     def summed(place, both):
         here, mate = decoded(place)
         mate = mate % clusters
-        acc[here] += jnp.dot(left[mate], both[...], preferred_element_type=jnp.float32)
-        back[mate] += lax.dot_general(
-            own_ref[here],
-            both[quarter:, :],
+        acc[here] += lax.dot_general(
+            left[mate, :rows, :],
+            both[...],
             (((1,), (1,)), ((), ())),
             preferred_element_type=jnp.float32,
-        )[:8]
+        )
+        aug = jnp.concatenate([ref[here] for ref in aug_refs], axis=1)
+        back[mate] += jnp.dot(aug, both[:, quarter:], preferred_element_type=jnp.float32)
 
     @pl.loop(0, items[step * length])
     def _(pair):
         turn = 2 * pair + 1
         summed(turn, both_a)
-        pointwise(turn + 1, dist_b, prod_b, both_b)
-        raw(turn + 2, dist_a, prod_a)
+        pointwise(turn + 1, raw_b, both_b)
+        products(turn + 2, raw_a)
         summed(turn + 1, both_b)
-        pointwise(turn + 2, dist_a, prod_a, both_a)
-        raw(turn + 3, dist_b, prod_b)
+        pointwise(turn + 2, raw_a, both_a)
+        products(turn + 3, raw_b)
 
     for coord in range(3):
         back_ref[coord] = -0.5 * back[:, coord, :] - there[coord] * back[:, 6, :]
     if last:
         for coord in range(3):
-            grad_ref[coord] = (
-                acc[:, width + coord, :]
-                - pos_ref[coord].astype(jnp.float32) * acc[:, width + 3, :]
-            )
+            pos = [ref[coord * clusters : (coord + 1) * clusters, :] for ref in small_refs]
+            pos = jnp.concatenate(pos, axis=1).astype(jnp.float32)
+            grad_ref[coord] = acc[:, width + coord, :] - pos * acc[:, width + 3, :]
         pot_ref[...] = acc[:, :rhs, :]
         pot_out_ref[...] = acc[:, rhs:width, :].astype(jnp.bfloat16)
 
 
-def run_step(step, length, items, source, cots, own, pos, carried, last):
-    clusters, _, panels = own.shape
+def run_step(step, length, items, source, targets, smalls, rhs, width, carried, last):
+    lhss, augs = zip(*targets)
+    clusters, _, row_count = augs[0].shape
+    subs = len(targets)
+    panels = subs * row_count
     quarter = source.shape[1]
-    rhs = cots[0].shape[1]
-    sub_blocks = panels // cots[0].shape[2]
-    blocks = (sub_blocks, len(cots) // sub_blocks)
-    width = rhs * blocks[1]
     first = carried is None
     vmem = pl.BlockSpec(memory_space=pltpu.VMEM)
     smem = pl.BlockSpec(memory_space=pltpu.SMEM)
-    operands = (items, source, own, *cots)
+    operands = (items, source, *lhss, *augs)
     if not first:
         operands += (carried,)
     acc_shape = (clusters, width + AUG, panels)
     back_shape = jax.ShapeDtypeStruct((3, clusters, quarter), jnp.float32)
     scratch = [
         pltpu.VMEM((clusters, AUG, quarter), jnp.float32),
-        pltpu.VMEM((clusters, quarter, AUG), jnp.bfloat16),
-        pltpu.VMEM((clusters, quarter, width), jnp.bfloat16),
-        pltpu.VMEM((clusters, width + AUG, 2 * quarter), jnp.bfloat16),
-        pltpu.VMEM((clusters + 1, quarter, LANES), jnp.float32),
-        pltpu.VMEM((clusters, 8, quarter), jnp.float32),
+        pltpu.VMEM((clusters, LANES, 2 * quarter), jnp.bfloat16),
+        pltpu.VMEM((clusters + 8, quarter), jnp.float32),
+        pltpu.VMEM((clusters, AUG, quarter), jnp.float32),
     ]
-    scratch += [pltpu.VMEM((quarter, panels), jnp.float32)] * 4
-    scratch += [pltpu.VMEM((2 * quarter, panels), jnp.bfloat16)] * 2
+    scratch += [pltpu.VMEM((panels, 2 * quarter), jnp.float32)] * 2
+    scratch += [pltpu.VMEM((panels, 2 * quarter), jnp.bfloat16)] * 2
     if last:
-        operands += (pos,)
+        operands += tuple(smalls)
         out_shape = (
             jax.ShapeDtypeStruct((clusters, rhs, panels), jnp.float32),
             jax.ShapeDtypeStruct((clusters, width - rhs, panels), jnp.bfloat16),
@@ -251,12 +251,12 @@
         out_shape = (jax.ShapeDtypeStruct(acc_shape, jnp.float32), back_shape)
     pairs = (length - 6) * panels * quarter
     return pl.pallas_call(
-        functools.partial(step_kernel, step, length, rhs, blocks, first, last),
+        functools.partial(step_kernel, step, length, rhs, subs, first, last),
         out_shape=out_shape,
         in_specs=[smem] + [vmem] * (len(operands) - 1),
         out_specs=(vmem,) * len(out_shape),
         scratch_shapes=scratch,
-        compiler_params=pltpu.CompilerParams(vmem_limit_bytes=16 * 1024 * 1024),
+        compiler_params=pltpu.CompilerParams(vmem_limit_bytes=20 * 1024 * 1024),
         cost_estimate=pl.CostEstimate(
             flops=2 * pairs * (2 * width + 3 * AUG), bytes_accessed=6 * 2**20, transcendentals=pairs
         ),
@@ -328,7 +328,6 @@
     width = rhs * rhs_count
     vmem = pl.BlockSpec(memory_space=pltpu.VMEM)
 
-    smem = pl.BlockSpec(memory_space=pltpu.SMEM)
     nodes_total = clus_count * clusters * panels
 
     cots = [cotangent] + [shifted(cotangent, "sub", step) for step in range(1, sub_count)]
@@ -336,26 +335,28 @@
         cots += [shifted(block, "rhs", step) for block in cots[:sub_count]]
 
     by_coord = jnp.transpose(positions, (1, 0, 2))
-    places = [device, sub_place, core, clusters * panels, row_count, panels, nodes_total]
-    *parts, small = pl.pallas_call(
-        prepare_kernel,
+    arguments = (density, by_coord, areas, connect, cotangent)
+    own_cot, *parts, small = pl.pallas_call(
+        functools.partial(prepare_kernel, (panels, nodes_total)),
         out_shape=(
+            jax.ShapeDtypeStruct(cotangent.shape, jnp.bfloat16),
             jax.ShapeDtypeStruct((clusters * (rhs + 5), quarter), jnp.bfloat16),
             *[jax.ShapeDtypeStruct((clusters * rhs, quarter), jnp.bfloat16)] * (rhs_count - 1),
             jax.ShapeDtypeStruct((clusters * 4, row_count), jnp.bfloat16),
         ),
-        in_specs=[smem] + [vmem] * 4,
-        out_specs=(vmem,) * (rhs_count + 1),
+        in_specs=[pl.BlockSpec(memory_space=pltpu.HBM)] * len(arguments),
+        out_specs=(vmem,) * (rhs_count + 2),
+        scratch_shapes=[pltpu.VMEM(array.shape, array.dtype) for array in arguments]
+        + [pltpu.SemaphoreType.DMA((len(arguments),))],
         compiler_params=pltpu.CompilerParams(vmem_limit_bytes=16 * 1024 * 1024),
         name="prepare",
-    )(jnp.stack([jnp.asarray(place, jnp.int32) for place in places]), density, by_coord, areas,
-      connect[:, 0, :])
+    )(*arguments)
+    cots[0] = own_cot
     arrived = [shifted(parts[0], "clus", 1)]
     for step in range(1, rhs_count):
         arrived.append(
             moved(parts[step], ("clus", "rhs"), lambda z, c, step=step: (z + 1, c + step))
         )
-    source = jnp.concatenate(arrived, axis=0)
 
     per_round = 2 * ((clusters // 2 + clus_count - 2) // (clus_count - 1))
     cap = ROUNDS * per_round
@@ -387,19 +388,24 @@
         )
 
     jitter_all = in_order([block[3 * clusters :] for block in smalls]).astype(jnp.int32)
-    own, pos = pl.pallas_call(
-        own_kernel,
-        out_shape=(
-            jax.ShapeDtypeStruct((clusters, AUG, panels), jnp.bfloat16),
-            jax.ShapeDtypeStruct((3, clusters, panels), jnp.bfloat16),
-        ),
-        in_specs=[vmem] * sub_count,
-        out_specs=(vmem, vmem),
-        scratch_shapes=[pltpu.VMEM((clusters, AUG, panels), jnp.float32)],
-        compiler_params=pltpu.CompilerParams(vmem_limit_bytes=16 * 1024 * 1024),
-        name="target_rows",
-    )(*smalls)
-
+    targets = [
+        pl.pallas_call(
+            functools.partial(target_kernel, rhs_count),
+            out_shape=(
+                jax.ShapeDtypeStruct((clusters, row_count, LANES), jnp.bfloat16),
+                jax.ShapeDtypeStruct((clusters, AUG, row_count), jnp.bfloat16),
+            ),
+            in_specs=[vmem] * (1 + rhs_count),
+            out_specs=(vmem, vmem),
+            scratch_shapes=[pltpu.VMEM((clusters, AUG, row_count), jnp.float32)],
+            compiler_params=pltpu.CompilerParams(vmem_limit_bytes=16 * 1024 * 1024),
+            name=f"targets_{place}",
+        )(smalls[place], *cots[place::sub_count])
+        for place in range(sub_count)
+    ]
+
+    arrived, targets = lax.optimization_barrier((arrived, targets))
+    source = jnp.concatenate(arrived, axis=0)
     carried = None
     backs, jitter_rows = [], []
     for step in range(1, clus_count):
@@ -408,7 +414,9 @@
                 source, backs[step - 3] = lax.optimization_barrier((source, backs[step - 3]))
             source = shifted(source, "clus", 1)
         last = step == clus_count - 1
-        results = run_step(step - 1, length, items, source, cots, own, pos, carried, last)
+        results = run_step(
+            step - 1, length, items, source, targets, smalls, rhs, width, carried, last
+        )
         if last:
             pot, pot_out, grad, back = results
         else:

time: 65.7 us -> 64.8 us (0.986)
  Pallas kernels: 26.6 us -> 25.8 us
  waiting for transfers between devices: 19 us -> 19.8 us
  starting transfers between devices: 12.4 us -> 11.7 us
    ppermute x1, waiting for transfers between devices: 2.02 us -> 4.27 us  [moved(): return lax.ppermute(value, axes, pairs)]
    ppermute x14, waiting for transfers between devices: 17 us -> 15.5 us  [shifted(): return lax.ppermute(value, axis, pairs)]
    slice x1 -> x0, local copies, waits for them, and re-layouts: 0.85 us -> none  [on_device(): connect[:, 0, :]]
    pallas_call x5 -> x6, Pallas kernels: 24.5 us -> 23.7 us  [the longest x3 22.6 us: run_step(): pl.pallas_call(functools.partial(step_kernel, step, length, rhs, subs, fi...]
    unnamed x14 -> x13, local copies, waits for them, and re-layouts: 3.36 us -> 4.19 us
    ppermute x14, starting transfers between devices: 11.3 us -> 10.6 us  [shifted(): return lax.ppermute(value, axis, pairs)]
  transfers between devices with their start and end apart: 15 -> 15, of which waited for: 10 -> 10; matrix products, arithmetic and copies ran while one was open for 4% -> 2% of each run, Pallas kernels for 28% -> 27%
where the time goes in v7:
time: 64.8 us; the launch traced here: 64.5 us
  Pallas kernels  25.8 us (40%)
  waiting for transfers between devices  19.8 us (31%)
  starting transfers between devices  11.7 us (18%)
  local copies, waits for them, and re-layouts  5.11 us (8%)
  other arithmetic  1.15 us (2%)
  between operations  1.02 us (2%)
    pallas_call x3, Pallas kernels, run_step(): pl.pallas_call(functools.partial(step_kernel, step, length, rhs, subs, fi...  22.6 us
    ppermute x14, waiting for transfers between devices, shifted(): return lax.ppermute(value, axis, pairs)  15.5 us
    ppermute x14, starting transfers between devices, shifted(): return lax.ppermute(value, axis, pairs)  10.6 us
    ppermute x1, waiting for transfers between devices, moved(): return lax.ppermute(value, axes, pairs)  4.27 us
    unnamed x13, local copies, waits for them, and re-layouts  4.19 us
    pallas_call x1, Pallas kernels, on_device(): pl.pallas_call(node_kernel, out_shape=jax.ShapeDtypeStruct((3, share * pa...  1.32 us
  transfers between devices with their start and end apart: 15, of which 10 were waited for; matrix products, arithmetic and copies ran while one was open for 2% of the time, Pallas kernels for 27%

profile of v7, /device:TPU:0, one launch (start us, length us, event | category | flops | bytes accessed | tf_op | source)
XLA Modules:
  0.0 64.5 jit_solution(3001614600968806199)
XLA Ops:
  0.6 0.0 copy-start
  0.6 3.0 %collective-permute-start.4 = (bf16[16,32,256]{2,1,0:T(8,128)(2,1)}, bf16[16,32,256]{2,1,0:T(8,128)(2,1)S(1)}, u32[]{:S(2)}, u32[]{:S(2)}) collective-permute-start(bf16[16,32,256]{2,1,0:T(8,128)(2,1)} %refs_4_.1), channel_id=1, source_target_pairs={{0,2},{2,0},{1,3},{3,1},{4,6},{6,4},{5,7},{7,5},{8,10},{10,8},{9,1... | collective-permute-start | bytes 786440 | tf_op jit(solution)/shard_map/ppermute | solution.py:22
  3.7 0.0 collective-permute-start.2
  3.7 0.0 copy-start.1
  3.7 0.9 %copy-done.1 = bf16[16,32,256]{2,1,0:T(8,128)(2,1)S(1)} copy-done((bf16[16,32,256]{2,1,0:T(8,128)(2,1)S(1)}, bf16[16,32,256]{2,1,0:T(8,128)(2,1)}, u32[]{:S(2)}) %copy-start.1) | copy-done | bytes 262168
  4.6 0.0 copy-start.2
  4.6 0.9 %copy-done.2 = bf16[16,32,256]{2,1,0:T(8,128)(2,1)S(1)} copy-done((bf16[16,32,256]{2,1,0:T(8,128)(2,1)S(1)}, bf16[16,32,256]{2,1,0:T(8,128)(2,1)}, u32[]{:S(2)}) %copy-start.2) | copy-done | bytes 262168
  5.6 0.0 copy-start.3
  5.6 0.8 %copy-done.3 = s32[16,4,256]{2,1,0:T(4,128)S(1)} copy-done((s32[16,4,256]{2,1,0:T(4,128)S(1)}, s32[16,4,256]{2,1,0:T(4,128)}, u32[]{:S(2)}) %copy-start.3) | copy-done | bytes 65560
  6.4 0.0 copy-start.4
  6.4 0.7 %copy-done.4 = bf16[16,3,256]{2,0,1:T(8,128)(2,1)S(1)} copy-done((bf16[16,3,256]{2,0,1:T(8,128)(2,1)S(1)}, bf16[16,3,256]{2,0,1:T(8,128)(2,1)}, u32[]{:S(2)}) %copy-start.4) | copy-done | bytes 24600
  7.1 0.0 copy-start.5
  7.1 0.7 %copy-done.5 = bf16[16,256]{1,0:T(8,128)(2,1)S(1)} copy-done((bf16[16,256]{1,0:T(8,128)(2,1)S(1)}, bf16[16,256]{1,0:T(8,128)(2,1)}, u32[]{:S(2)}) %copy-start.5) | copy-done | bytes 8216
  7.8 0.3 prepare.1
  8.1 0.2 collective-permute-start.3
  8.3 2.0 %collective-permute-start = (bf16[592,128]{1,0:T(8,128)(2,1)S(1)}, bf16[592,128]{1,0:T(8,128)(2,1)S(1)}, u32[]{:S(2)}, u32[]{:S(2)}) collective-permute-start(bf16[592,128]{1,0:T(8,128)(2,1)S(1)} %get-tuple-element.28), channel_id=1, source_target_pairs={{0,4},{4,8},{8,12},{12,0},{1,5},{5,9},{9,13},{13,1},{2,6},{6,10},{... | collective-permute-start | bytes 454664 | tf_op jit(solution)/shard_map/ppermute | solution.py:22
  10.3 1.1 %collective-permute-start.1 = (bf16[512,128]{1,0:T(8,128)(2,1)S(1)}, bf16[512,128]{1,0:T(8,128)(2,1)S(1)}, u32[]{:S(2)}, u32[]{:S(2)}) collective-permute-start(bf16[512,128]{1,0:T(8,128)(2,1)S(1)} %get-tuple-element.29), channel_id=1, source_target_pairs={{0,5},{1,4},{4,9},{5,8},{8,13},{9,12},{12,1},{13,0},{2,7},{3,6},{6... | collective-permute-start | bytes 393224 | tf_op jit(solution)/shard_map/ppermute | solution.py:34
  11.4 0.0 copy-done
  11.4 0.1 constant_dynamic-slice_fusion
  11.5 0.1 reshape.282
  11.6 0.1 mul.22
  11.7 0.2 convert_reduce_fusion
  11.9 0.2 convert_reduce_fusion.1
  12.1 0.2 select_reduce_fusion
  12.2 0.1 copy.34
  12.3 0.1 pad_slice_fusion
  12.4 0.1 pad_add_fusion
  12.5 0.1 reshape.283.refs_0_
  12.6 0.1 pad.40.clone
  12.7 0.0 collective-permute-done.4.refs_0_
  12.7 0.6 collective-permute-start.5
  13.2 0.0 collective-permute-done.3.small_ref.refs_8_
  13.3 0.0 collective-permute-done.2.refs_1_
  13.3 0.4 targets_0.1
  13.7 0.7 %collective-permute-done.5.refs_1_ = bf16[16,32,256]{2,1,0:T(8,128)(2,1)S(1)} collective-permute-done((bf16[16,32,256]{2,1,0:T(8,128)(2,1)S(1)}, bf16[16,32,256]{2,1,0:T(8,128)(2,1)S(1)}, u32[]{:S(2)}, u32[]{:S(2)}) %collective-permute-start.5) | collective-permute-done | bytes 262176 | tf_op jit(solution)/shard_map/ppermute | solution.py:22
  14.4 0.4 targets_1.1
  14.8 4.3 %collective-permute-done.1 = bf16[512,128]{1,0:T(8,128)(2,1)S(1)} collective-permute-done((bf16[512,128]{1,0:T(8,128)(2,1)S(1)}, bf16[512,128]{1,0:T(8,128)(2,1)S(1)}, u32[]{:S(2)}, u32[]{:S(2)}) %collective-permute-start.1) | collective-permute-done | bytes 131104 | tf_op jit(solution)/shard_map/ppermute | solution.py:34
  19.1 0.0 collective-permute-done
  19.1 0.1 collective-permute-start.6
  19.2 7.8 %near_field_0.1 = (f32[16,80,512]{2,1,0:T(8,128)S(1)}, f32[3,16,128]{2,1,0:T(8,128)S(1)}) custom-call(s32[108]{0:T(128)S(1)} %reshape.283.refs_0_, bf16[1104,128]{1,0:T(8,128)(2,1)S(1)} %constant_dynamic-update-slice_fusion.refs_1_, bf16[16,256,128]{2,1,0:T(8,128)(2,1)S(1)} %get-tuple-element.38.refs_2_, ...), custom_call_target="tpu_custom_call" | custom-call | flops 692060160 | bytes 6291456 | tf_op jit(solution)/shard_map/near_field_0/pallas_call | solution.py:253
  27.0 2.8 %collective-permute-done.6.refs_1_ = bf16[1104,128]{1,0:T(8,128)(2,1)S(1)} collective-permute-done((bf16[1104,128]{1,0:T(8,128)(2,1)S(1)}, bf16[1104,128]{1,0:T(8,128)(2,1)S(1)}, u32[]{:S(2)}, u32[]{:S(2)}) %collective-permute-start.6) | collective-permute-done | bytes 282656 | tf_op jit(solution)/shard_map/ppermute | solution.py:22
  29.8 0.0 collective-permute-start.7
  29.8 7.3 %near_field_1.1 = (f32[16,80,512]{2,1,0:T(8,128)S(1)}, f32[3,16,128]{2,1,0:T(8,128)S(1)}) custom-call(s32[108]{0:T(128)S(1)} %reshape.283.refs_0_, bf16[1104,128]{1,0:T(8,128)(2,1)S(1)} %collective-permute-done.6.refs_1_, bf16[16,256,128]{2,1,0:T(8,128)(2,1)S(1)} %get-tuple-element.38.refs_2_, bf16[16,256,128]{2,1,0:T(8,128)(2,1)S(1)} %get-tuple-element.39.refs_3_, ...), custom_call_target="tpu_custom_call" | custom-call | flops 692060160 | bytes 6291456 | tf_op jit(solution)/shard_map/near_field_1/pallas_call | solution.py:253
  37.2 2.4 %collective-permute-done.7.refs_1_ = bf16[1104,128]{1,0:T(8,128)(2,1)S(1)} collective-permute-done((bf16[1104,128]{1,0:T(8,128)(2,1)S(1)}, bf16[1104,128]{1,0:T(8,128)(2,1)S(1)}, u32[]{:S(2)}, u32[]{:S(2)}) %collective-permute-start.7) | collective-permute-done | bytes 282656 | tf_op jit(solution)/shard_map/ppermute | solution.py:22
  39.7 7.5 %near_field_2.1 = (f32[16,32,512]{2,1,0:T(8,128)S(1)}, bf16[16,32,512]{2,1,0:T(8,128)(2,1)S(1)}, f32[3,16,512]{2,1,0:T(8,128)S(1)}, f32[3,16,128]{2,1,0:T(8,128)S(1)}) custom-call(s32[108]{0:T(128)S(1)} %reshape.283.refs_0_, bf16[1104,128]{1,0:T(8,128)(2,1)S(1)} %collective-permute-done.7.refs_1_, bf16[16,256,128]{2,1,0:T(8,128)(2,1)S(1)} %get-tuple-element.38.refs_2_, ...), custom_call_target="tpu_custom_call" | custom-call | flops 692060160 | bytes 6291456 | tf_op jit(solution)/shard_map/near_field_2/pallas_call | solution.py:253
  47.2 0.1 copy.38
  47.4 0.1 maximum_maximum_fusion
  47.4 1.9 %collective-permute-start.10 = (f32[56,128]{1,0:T(8,128)S(1)}, f32[56,128]{1,0:T(8,128)S(1)}, u32[]{:S(2)}, u32[]{:S(2)}) collective-permute-start(f32[56,128]{1,0:T(8,128)S(1)} %get-tuple-element.77), channel_id=1, source_target_pairs={{0,12},{4,0},{8,4},{12,8},{1,13},{5,1},{9,5},{13,9},{2,14},{6,2},{... | collective-permute-start | bytes 86024 | tf_op jit(solution)/shard_map/ppermute | solution.py:22
  49.3 0.0 collective-permute-start.11
  49.3 0.6 collective-permute-start.12
  49.9 0.0 collective-permute-start.8
  50.0 1.4 %collective-permute-done.10 = f32[56,128]{1,0:T(8,128)S(1)} collective-permute-done((f32[56,128]{1,0:T(8,128)S(1)}, f32[56,128]{1,0:T(8,128)S(1)}, u32[]{:S(2)}, u32[]{:S(2)}) %collective-permute-start.10) | collective-permute-done | bytes 28704 | tf_op jit(solution)/shard_map/ppermute | solution.py:22
  51.3 2.7 %collective-permute-done.11 = f32[56,128]{1,0:T(8,128)S(1)} collective-permute-done((f32[56,128]{1,0:T(8,128)S(1)}, f32[56,128]{1,0:T(8,128)S(1)}, u32[]{:S(2)}, u32[]{:S(2)}) %collective-permute-start.11) | collective-permute-done | bytes 28704 | tf_op jit(solution)/shard_map/ppermute | solution.py:22
  54.1 0.9 %collective-permute-done.12 = f32[56,128]{1,0:T(8,128)S(1)} collective-permute-done((f32[56,128]{1,0:T(8,128)S(1)}, f32[56,128]{1,0:T(8,128)S(1)}, u32[]{:S(2)}, u32[]{:S(2)}) %collective-permute-start.12) | collective-permute-done | bytes 28704 | tf_op jit(solution)/shard_map/ppermute | solution.py:22
  55.1 0.0 collective-permute-done.8
  55.1 0.2 convert_add_fusion
  55.5 1.6 %collective-permute-start.13 = (f32[4,8,512]{2,1,0:T(8,128)S(1)}, f32[4,8,512]{2,1,0:T(8,128)S(1)}, u32[]{:S(2)}, u32[]{:S(2)}) collective-permute-start(f32[4,8,512]{2,1,0:T(8,128)S(1)} %fusion), channel_id=1, source_target_pairs={{0,2},{2,0},{1,3},{3,1},{4,6},{6,4},{5,7},{7,5},{8,10},{10,8},{9,1... | collective-permute-start | bytes 196616 | tf_op jit(solution)/shard_map/ppermute | solution.py:22
  57.1 0.6 collective-permute-start.9
  57.7 2.9 %collective-permute-done.13 = f32[4,8,512]{2,1,0:T(8,128)S(1)} collective-permute-done((f32[4,8,512]{2,1,0:T(8,128)S(1)}, f32[4,8,512]{2,1,0:T(8,128)S(1)}, u32[]{:S(2)}, u32[]{:S(2)}) %collective-permute-start.13) | collective-permute-done | bytes 65568 | tf_op jit(solution)/shard_map/ppermute | solution.py:22
  60.6 0.1 collective-permute-start.14
  60.8 1.2 %collective-permute-done.14 = f32[4,8,512]{2,1,0:T(8,128)S(1)} collective-permute-done((f32[4,8,512]{2,1,0:T(8,128)S(1)}, f32[4,8,512]{2,1,0:T(8,128)S(1)}, u32[]{:S(2)}, u32[]{:S(2)}) %collective-permute-start.14) | collective-permute-done | bytes 65568 | tf_op jit(solution)/shard_map/ppermute | solution.py:22
  62.0 1.3 %node_terms.1 = f32[3,4096]{1,0:T(4,128)} custom-call(f32[3,8,512]{2,1,0:T(8,128)S(1)} %slice.183.grad_ref, s32[8,512]{1,0:T(8,128)S(1)} %slice_select_fusion.2.jitter_ref, f32[8,512]{1,0:T(8,128)S(1)} %slice_bitcast_fusion.edge_ref), custom_call_target="tpu_custom_call" | custom-call | flops 1048576 | bytes 262144 | tf_op jit(solution)/shard_map/node_terms/pallas_call | solution.py:505
  63.3 0.5 collective-permute-done.9.refs_1_
  63.8 0.7 %potential_sum.1 = bf16[16,32,256]{2,1,0:T(8,128)(2,1)} custom-call(f32[16,32,256]{2,1,0:T(8,128)S(1)} %slice.122.refs_0_, bf16[16,32,256]{2,1,0:T(8,128)(2,1)S(1)} %collective-permute-done.9.refs_1_), custom_call_target="tpu_custom_call" | custom-call | flops 1048576 | bytes 262144 | tf_op jit(solution)/shard_map/potential_sum/pallas_call | solution.py:514
  (47 shorter events, 0.6 us)
Async XLA Ops:
  0.6 10.8 %copy-start = (s32[5,64]{1,0:T(8,128)S(1)}, s32[5,64]{1,0:T(8,128)}, u32[]{:S(2)}) copy-start(s32[5,64]{1,0:T(8,128)} %param.10) | copy-start | bytes 3844
  0.6 12.0 %collective-permute-start.4 = (bf16[16,32,256]{2,1,0:T(8,128)(2,1)}, bf16[16,32,256]{2,1,0:T(8,128)(2,1)S(1)}, u32[]{:S(2)}, u32[]{:S(2)}) collective-permute-start(bf16[16,32,256]{2,1,0:T(8,128)(2,1)} %refs_4_.1), channel_id=1, source_target_pairs={{0,2},{2,0},{1,3},{3,1},{4,6},{6,4},{5,7},{7,5},{8,10},{10,8},{9,1... | collective-permute-start | bytes 786440 | tf_op jit(solution)/shard_map/ppermute | solution.py:22
  3.7 9.6 %collective-permute-start.2 = (bf16[16,32,256]{2,1,0:T(8,128)(2,1)}, bf16[16,32,256]{2,1,0:T(8,128)(2,1)S(1)}, u32[]{:S(2)}, u32[]{:S(2)}) collective-permute-start(bf16[16,32,256]{2,1,0:T(8,128)(2,1)} %refs_4_.1), channel_id=1, source_target_pairs={{0,1},{1,0},{2,3},{3,2},{4,5},{5,4},{6,7},{7,6},{8,9},{9,8},{10,11... | collective-permute-start | bytes 786440 | tf_op jit(solution)/shard_map/ppermute | solution.py:22
  3.7 1.0 %copy-start.1 = (bf16[16,32,256]{2,1,0:T(8,128)(2,1)S(1)}, bf16[16,32,256]{2,1,0:T(8,128)(2,1)}, u32[]{:S(2)}) copy-start(bf16[16,32,256]{2,1,0:T(8,128)(2,1)} %refs_0_.1) | copy-start | bytes 786436
  4.6 0.9 %copy-start.2 = (bf16[16,32,256]{2,1,0:T(8,128)(2,1)S(1)}, bf16[16,32,256]{2,1,0:T(8,128)(2,1)}, u32[]{:S(2)}) copy-start(bf16[16,32,256]{2,1,0:T(8,128)(2,1)} %refs_4_.1) | copy-start | bytes 786436
  5.6 0.8 %copy-start.3 = (s32[16,4,256]{2,1,0:T(4,128)S(1)}, s32[16,4,256]{2,1,0:T(4,128)}, u32[]{:S(2)}) copy-start(s32[16,4,256]{2,1,0:T(4,128)} %refs_3_.1) | copy-start | bytes 196612
  6.4 0.7 %copy-start.4 = (bf16[16,3,256]{2,0,1:T(8,128)(2,1)S(1)}, bf16[16,3,256]{2,0,1:T(8,128)(2,1)}, u32[]{:S(2)}) copy-start(bf16[16,3,256]{2,0,1:T(8,128)(2,1)} %param.6) | copy-start | bytes 73732
  7.1 0.7 %copy-start.5 = (bf16[16,256]{1,0:T(8,128)(2,1)S(1)}, bf16[16,256]{1,0:T(8,128)(2,1)}, u32[]{:S(2)}) copy-start(bf16[16,256]{1,0:T(8,128)(2,1)} %refs_2_.1) | copy-start | bytes 24580
  8.1 5.1 %collective-permute-start.3 = (bf16[64,256]{1,0:T(8,128)(2,1)S(1)}, bf16[64,256]{1,0:T(8,128)(2,1)S(1)}, u32[]{:S(2)}, u32[]{:S(2)}) collective-permute-start(bf16[64,256]{1,0:T(8,128)(2,1)S(1)} %get-tuple-element.30.small_ref.refs_7_), channel_id=1, source_target_pairs={{0,2},{2,0},{1,3},{3,1},{4,6},{6,4},{5,7},{7,5},{8,10},{10,8},{9,1... | collective-permute-start | bytes 98312 | tf_op jit(solution)/shard_map/ppermute | solution.py:22
  8.3 10.8 %collective-permute-start = (bf16[592,128]{1,0:T(8,128)(2,1)S(1)}, bf16[592,128]{1,0:T(8,128)(2,1)S(1)}, u32[]{:S(2)}, u32[]{:S(2)}) collective-permute-start(bf16[592,128]{1,0:T(8,128)(2,1)S(1)} %get-tuple-element.28), channel_id=1, source_target_pairs={{0,4},{4,8},{8,12},{12,0},{1,5},{5,9},{9,13},{13,1},{2,6},{6,10},{... | collective-permute-start | bytes 454664 | tf_op jit(solution)/shard_map/ppermute | solution.py:22
  10.3 8.8 %collective-permute-start.1 = (bf16[512,128]{1,0:T(8,128)(2,1)S(1)}, bf16[512,128]{1,0:T(8,128)(2,1)S(1)}, u32[]{:S(2)}, u32[]{:S(2)}) collective-permute-start(bf16[512,128]{1,0:T(8,128)(2,1)S(1)} %get-tuple-element.29), channel_id=1, source_target_pairs={{0,5},{1,4},{4,9},{5,8},{8,13},{9,12},{12,1},{13,0},{2,7},{3,6},{6... | collective-permute-start | bytes 393224 | tf_op jit(solution)/shard_map/ppermute | solution.py:34
  12.7 1.7 %collective-permute-start.5 = (bf16[16,32,256]{2,1,0:T(8,128)(2,1)S(1)}, bf16[16,32,256]{2,1,0:T(8,128)(2,1)S(1)}, u32[]{:S(2)}, u32[]{:S(2)}) collective-permute-start(bf16[16,32,256]{2,1,0:T(8,128)(2,1)S(1)} %collective-permute-done.4.refs_0_), channel_id=1, source_target_pairs={{0,1},{1,0},{2,3},{3,2},{4,5},{5,4},{6,7},{7,6},{8,9},{9,8},{10,11... | collective-permute-start | bytes 786440 | tf_op jit(solution)/shard_map/ppermute | solution.py:22
  19.1 10.7 %collective-permute-start.6 = (bf16[1104,128]{1,0:T(8,128)(2,1)S(1)}, bf16[1104,128]{1,0:T(8,128)(2,1)S(1)}, u32[]{:S(2)}, u32[]{:S(2)}) collective-permute-start(bf16[1104,128]{1,0:T(8,128)(2,1)S(1)} %constant_dynamic-update-slice_fusion.refs_1_), channel_id=1, source_target_pairs={{0,4},{4,8},{8,12},{12,0},{1,5},{5,9},{9,13},{13,1},{2,6},{6,10},{... | collective-permute-start | bytes 847880 | tf_op jit(solution)/shard_map/ppermute | solution.py:22
  29.8 9.8 %collective-permute-start.7 = (bf16[1104,128]{1,0:T(8,128)(2,1)S(1)}, bf16[1104,128]{1,0:T(8,128)(2,1)S(1)}, u32[]{:S(2)}, u32[]{:S(2)}) collective-permute-start(bf16[1104,128]{1,0:T(8,128)(2,1)S(1)} %collective-permute-done.6.refs_1_), channel_id=1, source_target_pairs={{0,4},{4,8},{8,12},{12,0},{1,5},{5,9},{9,13},{13,1},{2,6},{6,10},{... | collective-permute-start | bytes 847880 | tf_op jit(solution)/shard_map/ppermute | solution.py:22
  47.4 3.9 %collective-permute-start.10 = (f32[56,128]{1,0:T(8,128)S(1)}, f32[56,128]{1,0:T(8,128)S(1)}, u32[]{:S(2)}, u32[]{:S(2)}) collective-permute-start(f32[56,128]{1,0:T(8,128)S(1)} %get-tuple-element.77), channel_id=1, source_target_pairs={{0,12},{4,0},{8,4},{12,8},{1,13},{5,1},{9,5},{13,9},{2,14},{6,2},{... | collective-permute-start | bytes 86024 | tf_op jit(solution)/shard_map/ppermute | solution.py:22
  49.3 4.8 %collective-permute-start.11 = (f32[56,128]{1,0:T(8,128)S(1)}, f32[56,128]{1,0:T(8,128)S(1)}, u32[]{:S(2)}, u32[]{:S(2)}) collective-permute-start(f32[56,128]{1,0:T(8,128)S(1)} %get-tuple-element.78), channel_id=1, source_target_pairs={{0,8},{4,12},{8,0},{12,4},{1,9},{5,13},{9,1},{13,5},{2,10},{6,14},... | collective-permute-start | bytes 86024 | tf_op jit(solution)/shard_map/ppermute | solution.py:22
  49.3 5.7 %collective-permute-start.12 = (f32[56,128]{1,0:T(8,128)S(1)}, f32[56,128]{1,0:T(8,128)S(1)}, u32[]{:S(2)}, u32[]{:S(2)}) collective-permute-start(f32[56,128]{1,0:T(8,128)S(1)} %get-tuple-element.79), channel_id=1, source_target_pairs={{0,4},{4,8},{8,12},{12,0},{1,5},{5,9},{9,13},{13,1},{2,6},{6,10},{... | collective-permute-start | bytes 86024 | tf_op jit(solution)/shard_map/ppermute | solution.py:22
  49.9 5.2 %collective-permute-start.8 = (bf16[16,32,512]{2,1,0:T(8,128)(2,1)S(1)}, bf16[16,32,512]{2,1,0:T(8,128)(2,1)S(1)}, u32[]{:S(2)}, u32[]{:S(2)}) collective-permute-start(bf16[16,32,512]{2,1,0:T(8,128)(2,1)S(1)} %get-tuple-element.47), channel_id=1, source_target_pairs={{0,1},{1,0},{2,3},{3,2},{4,5},{5,4},{6,7},{7,6},{8,9},{9,8},{10,11... | collective-permute-start | bytes 1572872 | tf_op jit(solution)/shard_map/ppermute | solution.py:22
  55.5 5.1 %collective-permute-start.13 = (f32[4,8,512]{2,1,0:T(8,128)S(1)}, f32[4,8,512]{2,1,0:T(8,128)S(1)}, u32[]{:S(2)}, u32[]{:S(2)}) collective-permute-start(f32[4,8,512]{2,1,0:T(8,128)S(1)} %fusion), channel_id=1, source_target_pairs={{0,2},{2,0},{1,3},{3,1},{4,6},{6,4},{5,7},{7,5},{8,10},{10,8},{9,1... | collective-permute-start | bytes 196616 | tf_op jit(solution)/shard_map/ppermute | solution.py:22
  57.1 6.7 %collective-permute-start.9 = (bf16[16,32,256]{2,1,0:T(8,128)(2,1)S(1)}, bf16[16,32,256]{2,1,0:T(8,128)(2,1)S(1)}, u32[]{:S(2)}, u32[]{:S(2)}) collective-permute-start(bf16[16,32,256]{2,1,0:T(8,128)(2,1)S(1)} %slice.247), channel_id=1, source_target_pairs={{0,2},{2,0},{1,3},{3,1},{4,6},{6,4},{5,7},{7,5},{8,10},{10,8},{9,1... | collective-permute-start | bytes 786440 | tf_op jit(solution)/shard_map/ppermute | solution.py:22
  60.6 1.3 %collective-permute-start.14 = (f32[4,8,512]{2,1,0:T(8,128)S(1)}, f32[4,8,512]{2,1,0:T(8,128)S(1)}, u32[]{:S(2)}, u32[]{:S(2)}) collective-permute-start(f32[4,8,512]{2,1,0:T(8,128)S(1)} %select_add_fusion), channel_id=1, source_target_pairs={{0,1},{1,0},{2,3},{3,2},{4,5},{5,4},{6,7},{7,6},{8,9},{9,8},{10,11... | collective-permute-start | bytes 196616 | tf_op jit(solution)/shard_map/ppermute | solution.py:22

commit v8 on v7

--- a/solution.py
+++ b/solution.py
@@ -335,7 +335,10 @@
         cots += [shifted(block, "rhs", step) for block in cots[:sub_count]]
 
     by_coord = jnp.transpose(positions, (1, 0, 2))
-    arguments = (density, by_coord, areas, connect, cotangent)
+    arguments = [
+        pltpu.with_memory_space_constraint(array, pltpu.HBM)
+        for array in (density, by_coord, areas, connect, cotangent)
+    ]
     own_cot, *parts, small = pl.pallas_call(
         functools.partial(prepare_kernel, (panels, nodes_total)),
         out_shape=(
@@ -399,6 +402,7 @@
             out_specs=(vmem, vmem),
             scratch_shapes=[pltpu.VMEM((clusters, AUG, row_count), jnp.float32)],
             compiler_params=pltpu.CompilerParams(vmem_limit_bytes=16 * 1024 * 1024),
+            cost_estimate=pl.CostEstimate(flops=2**20, bytes_accessed=2**18, transcendentals=0),
             name=f"targets_{place}",
         )(smalls[place], *cots[place::sub_count])
         for place in range(sub_count)
@@ -430,20 +434,25 @@
     high_part = (sub_place == sub_count - 1) & (core == rhs_count - 1)
     uppers = [grad[:, -1, -quarter:]] + [jnp.where(high_part, back[:, -1], 0.0) for back in backs]
     lowers = [grad[:, 0, :quarter]] + [jnp.where(low_part, back[:, 0], 0.0) for back in backs]
-    returned = jnp.zeros((3, clusters, quarter), jnp.float32)
-    upper, lower = uppers[1], lowers[clus_count - 1]
     nothing = jnp.zeros((2, quarter), jnp.float32)
-    for step in range(1, clus_count):
-        rows = [
-            backs[step - 1].reshape(3 * clusters, quarter),
+    parcels = []
+    for step in range(clus_count):
+        back = backs[step - 1] if step > 0 else jnp.zeros_like(backs[0])
+        parcels += [
+            back.reshape(3 * clusters, quarter),
             uppers[(step + 1) % clus_count],
-            lowers[step - 1],
+            lowers[(step - 1) % clus_count],
             nothing,
         ]
-        home = shifted(jnp.concatenate(rows, axis=0), "clus", -step)
-        returned = returned + home[: 3 * clusters].reshape(returned.shape)
-        upper = upper + home[3 * clusters : 3 * clusters + 3]
-        lower = lower + home[3 * clusters + 3 : 3 * clusters + 6]
+    rows = 3 * clusters + 8
+    parcels = jnp.concatenate(parcels, axis=0).reshape(clus_count, rows, quarter)[::-1]
+    parcels = jnp.concatenate([parcels, parcels], axis=0)
+    parcels = lax.dynamic_slice_in_dim(parcels, clus_count - 1 - device, clus_count, 0)
+    home = lax.all_to_all(parcels, "clus", split_axis=0, concat_axis=0, tiled=True)
+    home = jnp.sum(home, axis=0)
+    returned = home[: 3 * clusters].reshape(3, clusters, quarter)
+    upper = home[3 * clusters : 3 * clusters + 3]
+    lower = home[3 * clusters + 3 : 3 * clusters + 6]
 
     half = pot
     for step in range(1, rhs_count):

time: 64.8 us -> 64.5 us (level)
  local copies, waits for them, and re-layouts: 5.11 us -> 0.97 us
  starting transfers between devices: 11.7 us -> 13.5 us
  Pallas kernels: 25.8 us -> 26.7 us
    all_to_all x0 -> x1, waiting for transfers between devices: none -> 5.82 us  [on_device(): lax.all_to_all(parcels, 'clus', split_axis=0, concat_axis=0, tiled=True)]
    all_to_all x0 -> x1, starting transfers between devices: none -> 4.94 us  [on_device(): lax.all_to_all(parcels, 'clus', split_axis=0, concat_axis=0, tiled=True)]
    ppermute x14 -> x11, waiting for transfers between devices: 15.5 us -> 11.2 us  [shifted(): return lax.ppermute(value, axis, pairs)]
    unnamed x13 -> x3, local copies, waits for them, and re-layouts: 4.19 us -> 0.02 us
    ppermute x14 -> x11, starting transfers between devices: 10.6 us -> 7.48 us  [shifted(): return lax.ppermute(value, axis, pairs)]
    pallas_call x1, Pallas kernels: 0.28 us -> 1.21 us  [on_device(): pl.pallas_call(functools.partial(prepare_kernel, (panels, nodes_total)),...]
    ppermute x1, waiting for transfers between devices: 4.27 us -> 3.37 us  [moved(): return lax.ppermute(value, axes, pairs)]
  transfers between devices with their start and end apart: 15 -> 13, of which waited for: 10 -> 10; matrix products, arithmetic and copies ran while one was open for 2% -> 2% of each run, Pallas kernels for 27% -> 30%
where the time goes in v8:
time: 64.5 us; the launch traced here: 64.3 us
  Pallas kernels  26.7 us (41%)
  waiting for transfers between devices  20.3 us (31%)
  starting transfers between devices  13.5 us (21%)
  other arithmetic  1.72 us (3%)
  between operations  1.04 us (2%)
  local copies, waits for them, and re-layouts  0.97 us (2%)
    pallas_call x3, Pallas kernels, run_step(): pl.pallas_call(functools.partial(step_kernel, step, length, rhs, subs, fi...  22.6 us
    ppermute x11, waiting for transfers between devices, shifted(): return lax.ppermute(value, axis, pairs)  11.2 us
    ppermute x11, starting transfers between devices, shifted(): return lax.ppermute(value, axis, pairs)  7.48 us
    all_to_all x1, waiting for transfers between devices, on_device(): lax.all_to_all(parcels, 'clus', split_axis=0, concat_axis=0, tiled=True)  5.82 us
    all_to_all x1, starting transfers between devices, on_device(): lax.all_to_all(parcels, 'clus', split_axis=0, concat_axis=0, tiled=True)  4.94 us
    ppermute x1, waiting for transfers between devices, moved(): return lax.ppermute(value, axes, pairs)  3.37 us
    pallas_call x1, Pallas kernels, on_device(): pl.pallas_call(node_kernel, out_shape=jax.ShapeDtypeStruct((3, share * pa...  1.32 us
  transfers between devices with their start and end apart: 13, of which 10 were waited for; matrix products, arithmetic and copies ran while one was open for 2% of the time, Pallas kernels for 30%

profile of v8, /device:TPU:0, one launch (start us, length us, event | category | flops | bytes accessed | tf_op | source)
XLA Modules:
  0.0 64.3 jit_solution(2331991952511921522)
XLA Ops:
  0.6 0.0 copy-start
  0.6 3.0 %collective-permute-start.4 = (bf16[16,32,256]{2,1,0:T(8,128)(2,1)}, bf16[16,32,256]{2,1,0:T(8,128)(2,1)S(1)}, u32[]{:S(2)}, u32[]{:S(2)}) collective-permute-start(bf16[16,32,256]{2,1,0:T(8,128)(2,1)} %refs_4_.1), channel_id=1, source_target_pairs={{0,2},{2,0},{1,3},{3,1},{4,6},{6,4},{5,7},{7,5},{8,10},{10,8},{9,1... | collective-permute-start | bytes 786440 | tf_op jit(solution)/shard_map/ppermute | solution.py:22
  3.7 0.0 collective-permute-start.2
  3.7 1.2 %prepare.1 = (bf16[16,32,256]{2,1,0:T(8,128)(2,1)S(1)}, bf16[592,128]{1,0:T(8,128)(2,1)S(1)}, bf16[512,128]{1,0:T(8,128)(2,1)S(1)}, bf16[64,256]{1,0:T(8,128)(2,1)S(1)}) custom-call(bf16[16,32,256]{2,1,0:T(8,128)(2,1)} %refs_0_.1, bf16[3,16,256]{2,1,0:T(8,128)(2,1)} %bitcast.45, bf16[16,256]{1,0:T(8,128)(2,1)} %refs_2_.1, s32[16,4,256]{2,1,0:T(4,128)} %refs_3_.1, ...), custom_call_target="tpu_custom_call" | custom-call | tf_op jit(solution)/shard_map/prepare/pallas_call | solution.py:342
  4.9 0.2 collective-permute-start.3
  5.0 2.0 %collective-permute-start = (bf16[592,128]{1,0:T(8,128)(2,1)S(1)}, bf16[592,128]{1,0:T(8,128)(2,1)S(1)}, u32[]{:S(2)}, u32[]{:S(2)}) collective-permute-start(bf16[592,128]{1,0:T(8,128)(2,1)S(1)} %get-tuple-element.28), channel_id=1, source_target_pairs={{0,4},{4,8},{8,12},{12,0},{1,5},{5,9},{9,13},{13,1},{2,6},{6,10},{... | collective-permute-start | bytes 454664 | tf_op jit(solution)/shard_map/ppermute | solution.py:22
  7.0 1.1 %collective-permute-start.1 = (bf16[512,128]{1,0:T(8,128)(2,1)S(1)}, bf16[512,128]{1,0:T(8,128)(2,1)S(1)}, u32[]{:S(2)}, u32[]{:S(2)}) collective-permute-start(bf16[512,128]{1,0:T(8,128)(2,1)S(1)} %get-tuple-element.29), channel_id=1, source_target_pairs={{0,5},{1,4},{4,9},{5,8},{8,13},{9,12},{12,1},{13,0},{2,7},{3,6},{6... | collective-permute-start | bytes 393224 | tf_op jit(solution)/shard_map/ppermute | solution.py:34
  8.2 0.0 copy-done
  8.2 0.1 constant_dynamic-slice_fusion
  8.3 0.1 reshape.284
  8.3 0.1 mul.22
  8.4 0.2 convert_reduce_fusion
  8.6 0.2 convert_reduce_fusion.1
  8.8 0.2 select_reduce_fusion
  9.0 0.1 copy.34
  9.1 0.1 pad_slice_fusion
  9.2 0.1 pad_add_fusion
  9.3 0.1 reshape.285.refs_0_
  9.3 1.2 %collective-permute-done.4.refs_0_ = bf16[16,32,256]{2,1,0:T(8,128)(2,1)S(1)} collective-permute-done((bf16[16,32,256]{2,1,0:T(8,128)(2,1)}, bf16[16,32,256]{2,1,0:T(8,128)(2,1)S(1)}, u32[]{:S(2)}, u32[]{:S(2)}) %collective-permute-start.4) | collective-permute-done | bytes 262176 | tf_op jit(solution)/shard_map/ppermute | solution.py:22
  10.5 0.0 collective-permute-start.5
  10.5 0.3 collective-permute-done.3.small_ref.refs_8_
  10.9 0.0 collective-permute-done.2.refs_1_
  10.9 0.4 targets_0.1
  11.3 0.8 %collective-permute-done.5.refs_1_ = bf16[16,32,256]{2,1,0:T(8,128)(2,1)S(1)} collective-permute-done((bf16[16,32,256]{2,1,0:T(8,128)(2,1)S(1)}, bf16[16,32,256]{2,1,0:T(8,128)(2,1)S(1)}, u32[]{:S(2)}, u32[]{:S(2)}) %collective-permute-start.5) | collective-permute-done | bytes 262176 | tf_op jit(solution)/shard_map/ppermute | solution.py:22
  12.1 0.4 targets_1.1
  12.4 3.4 %collective-permute-done.1 = bf16[512,128]{1,0:T(8,128)(2,1)S(1)} collective-permute-done((bf16[512,128]{1,0:T(8,128)(2,1)S(1)}, bf16[512,128]{1,0:T(8,128)(2,1)S(1)}, u32[]{:S(2)}, u32[]{:S(2)}) %collective-permute-start.1) | collective-permute-done | bytes 131104 | tf_op jit(solution)/shard_map/ppermute | solution.py:34
  15.8 0.0 collective-permute-done
  15.9 0.1 collective-permute-start.6
  16.0 7.8 %near_field_0.1 = (f32[16,80,512]{2,1,0:T(8,128)S(1)}, f32[3,16,128]{2,1,0:T(8,128)S(1)}) custom-call(s32[108]{0:T(128)S(1)} %reshape.285.refs_0_, bf16[1104,128]{1,0:T(8,128)(2,1)S(1)} %constant_dynamic-update-slice_fusion.refs_1_, bf16[16,256,128]{2,1,0:T(8,128)(2,1)S(1)} %get-tuple-element.38.refs_2_, ...), custom_call_target="tpu_custom_call" | custom-call | flops 692060160 | bytes 6291456 | tf_op jit(solution)/shard_map/near_field_0/pallas_call | solution.py:253
  23.8 2.8 %collective-permute-done.6.refs_1_ = bf16[1104,128]{1,0:T(8,128)(2,1)S(1)} collective-permute-done((bf16[1104,128]{1,0:T(8,128)(2,1)S(1)}, bf16[1104,128]{1,0:T(8,128)(2,1)S(1)}, u32[]{:S(2)}, u32[]{:S(2)}) %collective-permute-start.6) | collective-permute-done | bytes 282656 | tf_op jit(solution)/shard_map/ppermute | solution.py:22
  26.6 0.0 collective-permute-start.7
  26.6 8.3 %near_field_1.1 = (f32[16,80,512]{2,1,0:T(8,128)S(1)}, f32[3,16,128]{2,1,0:T(8,128)S(1)}) custom-call(s32[108]{0:T(128)S(1)} %reshape.285.refs_0_, bf16[1104,128]{1,0:T(8,128)(2,1)S(1)} %collective-permute-done.6.refs_1_, bf16[16,256,128]{2,1,0:T(8,128)(2,1)S(1)} %get-tuple-element.38.refs_2_, bf16[16,256,128]{2,1,0:T(8,128)(2,1)S(1)} %get-tuple-element.39.refs_3_, ...), custom_call_target="tpu_custom_call" | custom-call | flops 692060160 | bytes 6291456 | tf_op jit(solution)/shard_map/near_field_1/pallas_call | solution.py:253
  34.9 1.5 %collective-permute-done.7.refs_1_ = bf16[1104,128]{1,0:T(8,128)(2,1)S(1)} collective-permute-done((bf16[1104,128]{1,0:T(8,128)(2,1)S(1)}, bf16[1104,128]{1,0:T(8,128)(2,1)S(1)}, u32[]{:S(2)}, u32[]{:S(2)}) %collective-permute-start.7) | collective-permute-done | bytes 282656 | tf_op jit(solution)/shard_map/ppermute | solution.py:22
  36.4 6.6 %near_field_2.1 = (f32[16,32,512]{2,1,0:T(8,128)S(1)}, bf16[16,32,512]{2,1,0:T(8,128)(2,1)S(1)}, f32[3,16,512]{2,1,0:T(8,128)S(1)}, f32[3,16,128]{2,1,0:T(8,128)S(1)}) custom-call(s32[108]{0:T(128)S(1)} %reshape.285.refs_0_, bf16[1104,128]{1,0:T(8,128)(2,1)S(1)} %collective-permute-done.7.refs_1_, bf16[16,256,128]{2,1,0:T(8,128)(2,1)S(1)} %get-tuple-element.38.refs_2_, ...), custom_call_target="tpu_custom_call" | custom-call | flops 692060160 | bytes 6291456 | tf_op jit(solution)/shard_map/near_field_2/pallas_call | solution.py:253
  43.0 0.1 copy.38
  43.2 0.1 concatenate.56
  43.3 0.7 %fusion = f32[4,56,128]{2,1,0:T(8,128)} fusion(s32[]{:T(128)S(6)} %select_n.272, f32[4,56,128]{2,1,0:T(8,128)S(1)} %rev.3), kind=kLoop, calls=%fused_computation.6 | loop fusion | flops 28672 | bytes 229380 | tf_op jit(solution)/shard_map/concatenate | solution.py:449
  44.0 4.9 %all-to-all-start = ((f32[4,56,128]{2,1,0:T(8,128)}), f32[4,56,128]{2,1,0:T(8,128)S(1)}, u32[]{:S(2)}, u32[]{:S(2)}) async-start(f32[4,56,128]{2,1,0:T(8,128)} %fusion), calls=%async_computation | async-start | bytes 229376 | tf_op jit(solution)/shard_map/all_to_all | solution.py:451
  48.9 0.0 collective-permute-start.8
  48.9 5.8 %all-to-all-done = f32[4,56,128]{2,1,0:T(8,128)S(1)} async-done(((f32[4,56,128]{2,1,0:T(8,128)}), f32[4,56,128]{2,1,0:T(8,128)S(1)}, u32[]{:S(2)}, u32[]{:S(2)}) %all-to-all-start) | async-done | bytes 114720 | tf_op jit(solution)/shard_map/all_to_all | solution.py:451
  54.9 0.0 collective-permute-done.8
  54.9 0.2 convert_add_fusion
  55.3 1.6 %collective-permute-start.10 = (f32[4,8,512]{2,1,0:T(8,128)S(1)}, f32[4,8,512]{2,1,0:T(8,128)S(1)}, u32[]{:S(2)}, u32[]{:S(2)}) collective-permute-start(f32[4,8,512]{2,1,0:T(8,128)S(1)} %fusion.1), channel_id=1, source_target_pairs={{0,2},{2,0},{1,3},{3,1},{4,6},{6,4},{5,7},{7,5},{8,10},{10,8},{9,1... | collective-permute-start | bytes 196616 | tf_op jit(solution)/shard_map/ppermute | solution.py:22
  56.9 0.6 collective-permute-start.9
  57.5 2.9 %collective-permute-done.10 = f32[4,8,512]{2,1,0:T(8,128)S(1)} collective-permute-done((f32[4,8,512]{2,1,0:T(8,128)S(1)}, f32[4,8,512]{2,1,0:T(8,128)S(1)}, u32[]{:S(2)}, u32[]{:S(2)}) %collective-permute-start.10) | collective-permute-done | bytes 65568 | tf_op jit(solution)/shard_map/ppermute | solution.py:22
  60.4 0.1 collective-permute-start.11
  60.5 1.2 %collective-permute-done.11 = f32[4,8,512]{2,1,0:T(8,128)S(1)} collective-permute-done((f32[4,8,512]{2,1,0:T(8,128)S(1)}, f32[4,8,512]{2,1,0:T(8,128)S(1)}, u32[]{:S(2)}, u32[]{:S(2)}) %collective-permute-start.11) | collective-permute-done | bytes 65568 | tf_op jit(solution)/shard_map/ppermute | solution.py:22
  61.8 1.3 %node_terms.1 = f32[3,4096]{1,0:T(4,128)} custom-call(f32[3,8,512]{2,1,0:T(8,128)S(1)} %slice.153.grad_ref, s32[8,512]{1,0:T(8,128)S(1)} %slice_select_fusion.6.jitter_ref, f32[8,512]{1,0:T(8,128)S(1)} %slice_bitcast_fusion.edge_ref), custom_call_target="tpu_custom_call" | custom-call | flops 1048576 | bytes 262144 | tf_op jit(solution)/shard_map/node_terms/pallas_call | solution.py:514
  63.1 0.5 collective-permute-done.9.refs_1_
  63.6 0.7 %potential_sum.1 = bf16[16,32,256]{2,1,0:T(8,128)(2,1)} custom-call(f32[16,32,256]{2,1,0:T(8,128)S(1)} %slice.104.refs_0_, bf16[16,32,256]{2,1,0:T(8,128)(2,1)S(1)} %collective-permute-done.9.refs_1_), custom_call_target="tpu_custom_call" | custom-call | flops 1048576 | bytes 262144 | tf_op jit(solution)/shard_map/potential_sum/pallas_call | solution.py:523
  (49 shorter events, 0.6 us)
Async XLA Ops:
  0.6 7.6 %copy-start = (s32[5,64]{1,0:T(8,128)S(1)}, s32[5,64]{1,0:T(8,128)}, u32[]{:S(2)}) copy-start(s32[5,64]{1,0:T(8,128)} %param.10) | copy-start | bytes 3844
  0.6 9.9 %collective-permute-start.4 = (bf16[16,32,256]{2,1,0:T(8,128)(2,1)}, bf16[16,32,256]{2,1,0:T(8,128)(2,1)S(1)}, u32[]{:S(2)}, u32[]{:S(2)}) collective-permute-start(bf16[16,32,256]{2,1,0:T(8,128)(2,1)} %refs_4_.1), channel_id=1, source_target_pairs={{0,2},{2,0},{1,3},{3,1},{4,6},{6,4},{5,7},{7,5},{8,10},{10,8},{9,1... | collective-permute-start | bytes 786440 | tf_op jit(solution)/shard_map/ppermute | solution.py:22
  3.7 7.2 %collective-permute-start.2 = (bf16[16,32,256]{2,1,0:T(8,128)(2,1)}, bf16[16,32,256]{2,1,0:T(8,128)(2,1)S(1)}, u32[]{:S(2)}, u32[]{:S(2)}) collective-permute-start(bf16[16,32,256]{2,1,0:T(8,128)(2,1)} %refs_4_.1), channel_id=1, source_target_pairs={{0,1},{1,0},{2,3},{3,2},{4,5},{5,4},{6,7},{7,6},{8,9},{9,8},{10,11... | collective-permute-start | bytes 786440 | tf_op jit(solution)/shard_map/ppermute | solution.py:22
  4.9 6.0 %collective-permute-start.3 = (bf16[64,256]{1,0:T(8,128)(2,1)S(1)}, bf16[64,256]{1,0:T(8,128)(2,1)S(1)}, u32[]{:S(2)}, u32[]{:S(2)}) collective-permute-start(bf16[64,256]{1,0:T(8,128)(2,1)S(1)} %get-tuple-element.30.small_ref.refs_7_), channel_id=1, source_target_pairs={{0,2},{2,0},{1,3},{3,1},{4,6},{6,4},{5,7},{7,5},{8,10},{10,8},{9,1... | collective-permute-start | bytes 98312 | tf_op jit(solution)/shard_map/ppermute | solution.py:22
  5.0 10.8 %collective-permute-start = (bf16[592,128]{1,0:T(8,128)(2,1)S(1)}, bf16[592,128]{1,0:T(8,128)(2,1)S(1)}, u32[]{:S(2)}, u32[]{:S(2)}) collective-permute-start(bf16[592,128]{1,0:T(8,128)(2,1)S(1)} %get-tuple-element.28), channel_id=1, source_target_pairs={{0,4},{4,8},{8,12},{12,0},{1,5},{5,9},{9,13},{13,1},{2,6},{6,10},{... | collective-permute-start | bytes 454664 | tf_op jit(solution)/shard_map/ppermute | solution.py:22
  7.0 8.8 %collective-permute-start.1 = (bf16[512,128]{1,0:T(8,128)(2,1)S(1)}, bf16[512,128]{1,0:T(8,128)(2,1)S(1)}, u32[]{:S(2)}, u32[]{:S(2)}) collective-permute-start(bf16[512,128]{1,0:T(8,128)(2,1)S(1)} %get-tuple-element.29), channel_id=1, source_target_pairs={{0,5},{1,4},{4,9},{5,8},{8,13},{9,12},{12,1},{13,0},{2,7},{3,6},{6... | collective-permute-start | bytes 393224 | tf_op jit(solution)/shard_map/ppermute | solution.py:34
  10.5 1.5 %collective-permute-start.5 = (bf16[16,32,256]{2,1,0:T(8,128)(2,1)S(1)}, bf16[16,32,256]{2,1,0:T(8,128)(2,1)S(1)}, u32[]{:S(2)}, u32[]{:S(2)}) collective-permute-start(bf16[16,32,256]{2,1,0:T(8,128)(2,1)S(1)} %collective-permute-done.4.refs_0_), channel_id=1, source_target_pairs={{0,1},{1,0},{2,3},{3,2},{4,5},{5,4},{6,7},{7,6},{8,9},{9,8},{10,11... | collective-permute-start | bytes 786440 | tf_op jit(solution)/shard_map/ppermute | solution.py:22
  15.9 10.7 %collective-permute-start.6 = (bf16[1104,128]{1,0:T(8,128)(2,1)S(1)}, bf16[1104,128]{1,0:T(8,128)(2,1)S(1)}, u32[]{:S(2)}, u32[]{:S(2)}) collective-permute-start(bf16[1104,128]{1,0:T(8,128)(2,1)S(1)} %constant_dynamic-update-slice_fusion.refs_1_), channel_id=1, source_target_pairs={{0,4},{4,8},{8,12},{12,0},{1,5},{5,9},{9,13},{13,1},{2,6},{6,10},{... | collective-permute-start | bytes 847880 | tf_op jit(solution)/shard_map/ppermute | solution.py:22
  26.6 9.8 %collective-permute-start.7 = (bf16[1104,128]{1,0:T(8,128)(2,1)S(1)}, bf16[1104,128]{1,0:T(8,128)(2,1)S(1)}, u32[]{:S(2)}, u32[]{:S(2)}) collective-permute-start(bf16[1104,128]{1,0:T(8,128)(2,1)S(1)} %collective-permute-done.6.refs_1_), channel_id=1, source_target_pairs={{0,4},{4,8},{8,12},{12,0},{1,5},{5,9},{9,13},{13,1},{2,6},{6,10},{... | collective-permute-start | bytes 847880 | tf_op jit(solution)/shard_map/ppermute | solution.py:22
  44.0 10.8 %all-to-all-start = ((f32[4,56,128]{2,1,0:T(8,128)}), f32[4,56,128]{2,1,0:T(8,128)S(1)}, u32[]{:S(2)}, u32[]{:S(2)}) async-start(f32[4,56,128]{2,1,0:T(8,128)} %fusion), calls=%async_computation | async-start | bytes 229376 | tf_op jit(solution)/shard_map/all_to_all | solution.py:451
  48.9 6.0 %collective-permute-start.8 = (bf16[16,32,512]{2,1,0:T(8,128)(2,1)S(1)}, bf16[16,32,512]{2,1,0:T(8,128)(2,1)S(1)}, u32[]{:S(2)}, u32[]{:S(2)}) collective-permute-start(bf16[16,32,512]{2,1,0:T(8,128)(2,1)S(1)} %get-tuple-element.47), channel_id=1, source_target_pairs={{0,1},{1,0},{2,3},{3,2},{4,5},{5,4},{6,7},{7,6},{8,9},{9,8},{10,11... | collective-permute-start | bytes 1572872 | tf_op jit(solution)/shard_map/ppermute | solution.py:22
  55.3 5.1 %collective-permute-start.10 = (f32[4,8,512]{2,1,0:T(8,128)S(1)}, f32[4,8,512]{2,1,0:T(8,128)S(1)}, u32[]{:S(2)}, u32[]{:S(2)}) collective-permute-start(f32[4,8,512]{2,1,0:T(8,128)S(1)} %fusion.1), channel_id=1, source_target_pairs={{0,2},{2,0},{1,3},{3,1},{4,6},{6,4},{5,7},{7,5},{8,10},{10,8},{9,1... | collective-permute-start | bytes 196616 | tf_op jit(solution)/shard_map/ppermute | solution.py:22
  56.9 6.7 %collective-permute-start.9 = (bf16[16,32,256]{2,1,0:T(8,128)(2,1)S(1)}, bf16[16,32,256]{2,1,0:T(8,128)(2,1)S(1)}, u32[]{:S(2)}, u32[]{:S(2)}) collective-permute-start(bf16[16,32,256]{2,1,0:T(8,128)(2,1)S(1)} %slice.198), channel_id=1, source_target_pairs={{0,2},{2,0},{1,3},{3,1},{4,6},{6,4},{5,7},{7,5},{8,10},{10,8},{9,1... | collective-permute-start | bytes 786440 | tf_op jit(solution)/shard_map/ppermute | solution.py:22
  60.4 1.3 %collective-permute-start.11 = (f32[4,8,512]{2,1,0:T(8,128)S(1)}, f32[4,8,512]{2,1,0:T(8,128)S(1)}, u32[]{:S(2)}, u32[]{:S(2)}) collective-permute-start(f32[4,8,512]{2,1,0:T(8,128)S(1)} %select_add_fusion), channel_id=1, source_target_pairs={{0,1},{1,0},{2,3},{3,2},{4,5},{5,4},{6,7},{7,6},{8,9},{9,8},{10,11... | collective-permute-start | bytes 196616 | tf_op jit(solution)/shard_map/ppermute | solution.py:22

commit v9 on v7

--- a/solution.py
+++ b/solution.py
@@ -20,6 +20,16 @@
     count = lax.axis_size(axis)
     pairs = [(source, (source + steps) % count) for source in range(count)]
     return lax.ppermute(value, axis, pairs)
+
+
+def ring_order(count):
+    return [*range(0, count, 2), *reversed(range(1, count, 2))]
+
+
+def round_ring(value, steps):
+    order = ring_order(lax.axis_size("clus"))
+    pairs = [(source, order[(at + steps) % len(order)]) for at, source in enumerate(order)]
+    return lax.ppermute(value, "clus", pairs)
 
 
 def moved(value, axes, target):
@@ -335,7 +345,10 @@
         cots += [shifted(block, "rhs", step) for block in cots[:sub_count]]
 
     by_coord = jnp.transpose(positions, (1, 0, 2))
-    arguments = (density, by_coord, areas, connect, cotangent)
+    arguments = [
+        pltpu.with_memory_space_constraint(array, pltpu.HBM)
+        for array in (density, by_coord, areas, connect, cotangent)
+    ]
     own_cot, *parts, small = pl.pallas_call(
         functools.partial(prepare_kernel, (panels, nodes_total)),
         out_shape=(
@@ -352,18 +365,23 @@
         name="prepare",
     )(*arguments)
     cots[0] = own_cot
-    arrived = [shifted(parts[0], "clus", 1)]
+    ring = ring_order(clus_count)
+    at_place = [ring.index(index) for index in range(clus_count)]
+    ring_place = pick(device, at_place)
+    arrived = [round_ring(parts[0], 1)]
     for step in range(1, rhs_count):
-        arrived.append(
-            moved(parts[step], ("clus", "rhs"), lambda z, c, step=step: (z + 1, c + step))
-        )
+
+        def goal(z, c, step=step):
+            return (ring[(at_place[z] + 1) % clus_count], c + step)
+
+        arrived.append(moved(parts[step], ("clus", "rhs"), goal))
 
     per_round = 2 * ((clusters // 2 + clus_count - 2) // (clus_count - 1))
     cap = ROUNDS * per_round
     partners = lax.dynamic_slice_in_dim(matching, device * clusters, clusters, 1).reshape(-1)
     here = jnp.tile(jnp.arange(clusters, dtype=jnp.int32), ROUNDS)
     code = here * (2 * clusters) + partners % clusters
-    behind = (device - partners // clusters) % clus_count
+    behind = (ring_place - pick(partners // clusters, at_place)) % clus_count
     total_items = ROUNDS * clusters
     order = jnp.arange(total_items, dtype=jnp.int32)
     rank = jnp.sum(
@@ -399,6 +417,7 @@
             out_specs=(vmem, vmem),
             scratch_shapes=[pltpu.VMEM((clusters, AUG, row_count), jnp.float32)],
             compiler_params=pltpu.CompilerParams(vmem_limit_bytes=16 * 1024 * 1024),
+            cost_estimate=pl.CostEstimate(flops=2**20, bytes_accessed=2**18, transcendentals=0),
             name=f"targets_{place}",
         )(smalls[place], *cots[place::sub_count])
         for place in range(sub_count)
@@ -407,12 +426,12 @@
     arrived, targets = lax.optimization_barrier((arrived, targets))
     source = jnp.concatenate(arrived, axis=0)
     carried = None
-    backs, jitter_rows = [], []
+    backs, jitter_rows = [], [None]
     for step in range(1, clus_count):
         if step > 1:
             if step > 2:
                 source, backs[step - 3] = lax.optimization_barrier((source, backs[step - 3]))
-            source = shifted(source, "clus", 1)
+            source = round_ring(source, 1)
         last = step == clus_count - 1
         results = run_step(
             step - 1, length, items, source, targets, smalls, rhs, width, carried, last
@@ -430,17 +449,28 @@
     high_part = (sub_place == sub_count - 1) & (core == rhs_count - 1)
     uppers = [grad[:, -1, -quarter:]] + [jnp.where(high_part, back[:, -1], 0.0) for back in backs]
     lowers = [grad[:, 0, :quarter]] + [jnp.where(low_part, back[:, 0], 0.0) for back in backs]
+
+    def step_between(index, owner):
+        return (at_place[index] - at_place[owner % clus_count]) % clus_count
+
+    def needed(parts, step, offset):
+        choices = []
+        for index in range(clus_count):
+            goal = ring[(at_place[index] - step) % clus_count]
+            choices.append(parts[step_between(index, goal + offset)])
+        return pick(device, choices)
+
+    nothing = jnp.zeros((2, quarter), jnp.float32)
     returned = jnp.zeros((3, clusters, quarter), jnp.float32)
-    upper, lower = uppers[1], lowers[clus_count - 1]
-    nothing = jnp.zeros((2, quarter), jnp.float32)
+    upper, lower = needed(uppers, 0, -1), needed(lowers, 0, 1)
     for step in range(1, clus_count):
         rows = [
             backs[step - 1].reshape(3 * clusters, quarter),
-            uppers[(step + 1) % clus_count],
-            lowers[step - 1],
+            needed(uppers, step, -1),
+            needed(lowers, step, 1),
             nothing,
         ]
-        home = shifted(jnp.concatenate(rows, axis=0), "clus", -step)
+        home = round_ring(jnp.concatenate(rows, axis=0), -step)
         returned = returned + home[: 3 * clusters].reshape(returned.shape)
         upper = upper + home[3 * clusters : 3 * clusters + 3]
         lower = lower + home[3 * clusters + 3 : 3 * clusters + 6]
@@ -467,9 +497,11 @@
     after = jnp.concatenate([lower, blank], axis=1)
     jitter_float = jitter_all.astype(jnp.float32)
     jitter_before = jnp.concatenate(
-        [blank[:1], jitter_rows[0][clusters - 1 :].astype(jnp.float32)], axis=1
-    )
-    jitter_after = jnp.concatenate([jitter_rows[-1][:1].astype(jnp.float32), blank[:1]], axis=1)
+        [blank[:1], needed(jitter_rows, 0, -1)[clusters - 1 :].astype(jnp.float32)], axis=1
+    )
+    jitter_after = jnp.concatenate(
+        [needed(jitter_rows, 0, 1)[:1].astype(jnp.float32), blank[:1]], axis=1
+    )
 
     def edge_rows(at):
         first, end = at * share, (at + 1) * share

time: 64.8 us -> 60.2 us (0.929)
  waiting for transfers between devices: 19.8 us -> 11.8 us
  starting transfers between devices: 11.7 us -> 18.2 us
  local copies, waits for them, and re-layouts: 5.11 us -> 0.94 us
  Pallas kernels: 25.8 us -> 26.7 us
    ppermute x0 -> x6, starting transfers between devices: none -> 11.6 us  [round_ring(): return lax.ppermute(value, 'clus', pairs)]
    ppermute x14 -> x8, waiting for transfers between devices: 15.5 us -> 6.5 us  [shifted(): return lax.ppermute(value, axis, pairs)]
    ppermute x14 -> x8, starting transfers between devices: 10.6 us -> 5.51 us  [shifted(): return lax.ppermute(value, axis, pairs)]
    unnamed x13 -> x5, local copies, waits for them, and re-layouts: 4.19 us -> 0.02 us
    ppermute x0 -> x6, waiting for transfers between devices: none -> 3.32 us  [round_ring(): return lax.ppermute(value, 'clus', pairs)]
    ppermute x1, waiting for transfers between devices: 4.27 us -> 2.01 us  [moved(): return lax.ppermute(value, axes, pairs)]
    pallas_call x1, Pallas kernels: 0.28 us -> 1.21 us  [on_device(): pl.pallas_call(functools.partial(prepare_kernel, (panels, nodes_total)),...]
  transfers between devices with their start and end apart: 15 -> 15, of which waited for: 10 -> 9; matrix products, arithmetic and copies ran while one was open for 2% -> 2% of each run, Pallas kernels for 27% -> 30%
where the time goes in v9:
time: 60.2 us; the launch traced here: 59.9 us
  Pallas kernels  26.7 us (44%)
  starting transfers between devices  18.2 us (30%)
  waiting for transfers between devices  11.8 us (20%)
  other arithmetic  1.17 us (2%)
  between operations  1.07 us (2%)
  local copies, waits for them, and re-layouts  0.94 us (2%)
    pallas_call x3, Pallas kernels, run_step(): pl.pallas_call(functools.partial(step_kernel, step, length, rhs, subs, fi...  22.6 us
    ppermute x6, starting transfers between devices, round_ring(): return lax.ppermute(value, 'clus', pairs)  11.6 us
    ppermute x8, waiting for transfers between devices, shifted(): return lax.ppermute(value, axis, pairs)  6.5 us
    ppermute x8, starting transfers between devices, shifted(): return lax.ppermute(value, axis, pairs)  5.51 us
    ppermute x6, waiting for transfers between devices, round_ring(): return lax.ppermute(value, 'clus', pairs)  3.32 us
    ppermute x1, waiting for transfers between devices, moved(): return lax.ppermute(value, axes, pairs)  2.01 us
    pallas_call x1, Pallas kernels, on_device(): pl.pallas_call(node_kernel, out_shape=jax.ShapeDtypeStruct((3, share * pa...  1.32 us
    pallas_call x1, Pallas kernels, on_device(): pl.pallas_call(functools.partial(prepare_kernel, (panels, nodes_total)),...  1.21 us
  transfers between devices with their start and end apart: 15, of which 9 were waited for; matrix products, arithmetic and copies ran while one was open for 2% of the time, Pallas kernels for 30%

profile of v9, /device:TPU:0, one launch (start us, length us, event | category | flops | bytes accessed | tf_op | source)
XLA Modules:
  0.0 59.9 jit_solution(294261457824714496)
XLA Ops:
  0.6 0.0 copy-start
  0.6 3.0 %collective-permute-start.4 = (bf16[16,32,256]{2,1,0:T(8,128)(2,1)}, bf16[16,32,256]{2,1,0:T(8,128)(2,1)S(1)}, u32[]{:S(2)}, u32[]{:S(2)}) collective-permute-start(bf16[16,32,256]{2,1,0:T(8,128)(2,1)} %refs_4_.1), channel_id=1, source_target_pairs={{0,2},{2,0},{1,3},{3,1},{4,6},{6,4},{5,7},{7,5},{8,10},{10,8},{9,1... | collective-permute-start | bytes 786440 | tf_op jit(solution)/shard_map/ppermute | solution.py:22
  3.7 0.0 collective-permute-start.2
  3.7 1.2 %prepare.1 = (bf16[16,32,256]{2,1,0:T(8,128)(2,1)S(1)}, bf16[592,128]{1,0:T(8,128)(2,1)S(1)}, bf16[512,128]{1,0:T(8,128)(2,1)S(1)}, bf16[64,256]{1,0:T(8,128)(2,1)S(1)}) custom-call(bf16[16,32,256]{2,1,0:T(8,128)(2,1)} %refs_0_.1, bf16[3,16,256]{2,1,0:T(8,128)(2,1)} %bitcast.91, bf16[16,256]{1,0:T(8,128)(2,1)} %refs_2_.1, s32[16,4,256]{2,1,0:T(4,128)} %refs_3_.1, ...), custom_call_target="tpu_custom_call" | custom-call | tf_op jit(solution)/shard_map/prepare/pallas_call | solution.py:352
  4.9 0.2 collective-permute-start.3
  5.0 3.0 %collective-permute-start = (bf16[592,128]{1,0:T(8,128)(2,1)S(1)}, bf16[592,128]{1,0:T(8,128)(2,1)S(1)}, u32[]{:S(2)}, u32[]{:S(2)}) collective-permute-start(bf16[592,128]{1,0:T(8,128)(2,1)S(1)} %get-tuple-element.28), channel_id=1, source_target_pairs={{0,8},{8,12},{12,4},{4,0},{1,9},{9,13},{13,5},{5,1},{2,10},{10,14}... | collective-permute-start | bytes 454664 | tf_op jit(solution)/shard_map/ppermute | solution.py:32
  8.1 1.1 %collective-permute-start.1 = (bf16[512,128]{1,0:T(8,128)(2,1)S(1)}, bf16[512,128]{1,0:T(8,128)(2,1)S(1)}, u32[]{:S(2)}, u32[]{:S(2)}) collective-permute-start(bf16[512,128]{1,0:T(8,128)(2,1)S(1)} %get-tuple-element.29), channel_id=1, source_target_pairs={{0,9},{1,8},{4,1},{5,0},{8,13},{9,12},{12,5},{13,4},{2,11},{3,10},... | collective-permute-start | bytes 393224 | tf_op jit(solution)/shard_map/ppermute | solution.py:44
  9.2 0.0 copy-done
  9.2 0.1 constant_dynamic-slice_fusion
  9.3 0.1 reshape.294
  9.4 0.1 mul.22
  9.5 0.2 convert_reduce_fusion
  9.6 0.2 convert_reduce_fusion.1
  9.8 0.2 select_reduce_fusion
  10.0 0.5 collective-permute-done.4.refs_0_
  10.5 0.1 collective-permute-start.5
  10.6 0.1 copy.34
  10.8 0.0 collective-permute-done.2.refs_1_
  10.8 0.4 targets_0.1
  11.2 0.0 collective-permute-done.3.small_ref.refs_8_
  11.2 0.9 %collective-permute-done.5.refs_1_ = bf16[16,32,256]{2,1,0:T(8,128)(2,1)S(1)} collective-permute-done((bf16[16,32,256]{2,1,0:T(8,128)(2,1)S(1)}, bf16[16,32,256]{2,1,0:T(8,128)(2,1)S(1)}, u32[]{:S(2)}, u32[]{:S(2)}) %collective-permute-start.5) | collective-permute-done | bytes 262176 | tf_op jit(solution)/shard_map/ppermute | solution.py:22
  12.1 0.4 targets_1.1
  12.4 2.0 %collective-permute-done.1 = bf16[512,128]{1,0:T(8,128)(2,1)S(1)} collective-permute-done((bf16[512,128]{1,0:T(8,128)(2,1)S(1)}, bf16[512,128]{1,0:T(8,128)(2,1)S(1)}, u32[]{:S(2)}, u32[]{:S(2)}) %collective-permute-start.1) | collective-permute-done | bytes 131104 | tf_op jit(solution)/shard_map/ppermute | solution.py:44
  14.5 0.0 collective-permute-done
  14.5 0.0 copy-start.1
  14.5 2.7 %collective-permute-start.6 = (bf16[1104,128]{1,0:T(8,128)(2,1)S(1)}, bf16[1104,128]{1,0:T(8,128)(2,1)S(1)}, u32[]{:S(2)}, u32[]{:S(2)}) collective-permute-start(bf16[1104,128]{1,0:T(8,128)(2,1)S(1)} %constant_dynamic-update-slice_fusion.refs_1_), channel_id=1, source_target_pairs={{0,8},{8,12},{12,4},{4,0},{1,9},{9,13},{13,5},{5,1},{2,10},{10,14}... | collective-permute-start | bytes 847880 | tf_op jit(solution)/shard_map/ppermute | solution.py:32
  17.2 0.1 pad_slice_fusion
  17.3 0.1 pad_add_fusion
  17.4 0.1 reshape.295.refs_0_
  17.5 0.1 pad.40.clone
  17.5 7.3 %near_field_0.1 = (f32[16,80,512]{2,1,0:T(8,128)S(1)}, f32[3,16,128]{2,1,0:T(8,128)S(1)}) custom-call(s32[108]{0:T(128)S(1)} %reshape.295.refs_0_, bf16[1104,128]{1,0:T(8,128)(2,1)S(1)} %constant_dynamic-update-slice_fusion.refs_1_, bf16[16,256,128]{2,1,0:T(8,128)(2,1)S(1)} %get-tuple-element.38.refs_2_, ...), custom_call_target="tpu_custom_call" | custom-call | flops 692060160 | bytes 6291456 | tf_op jit(solution)/shard_map/near_field_0/pallas_call | solution.py:263
  24.9 0.0 collective-permute-done.6.refs_1_
  24.9 2.4 %collective-permute-start.7 = (bf16[1104,128]{1,0:T(8,128)(2,1)S(1)}, bf16[1104,128]{1,0:T(8,128)(2,1)S(1)}, u32[]{:S(2)}, u32[]{:S(2)}) collective-permute-start(bf16[1104,128]{1,0:T(8,128)(2,1)S(1)} %collective-permute-done.6.refs_1_), channel_id=1, source_target_pairs={{0,8},{8,12},{12,4},{4,0},{1,9},{9,13},{13,5},{5,1},{2,10},{10,14}... | collective-permute-start | bytes 847880 | tf_op jit(solution)/shard_map/ppermute | solution.py:32
  27.3 7.3 %near_field_1.1 = (f32[16,80,512]{2,1,0:T(8,128)S(1)}, f32[3,16,128]{2,1,0:T(8,128)S(1)}) custom-call(s32[108]{0:T(128)S(1)} %reshape.295.refs_0_, bf16[1104,128]{1,0:T(8,128)(2,1)S(1)} %collective-permute-done.6.refs_1_, bf16[16,256,128]{2,1,0:T(8,128)(2,1)S(1)} %get-tuple-element.38.refs_2_, bf16[16,256,128]{2,1,0:T(8,128)(2,1)S(1)} %get-tuple-element.39.refs_3_, ...), custom_call_target="tpu_custom_call" | custom-call | flops 692060160 | bytes 6291456 | tf_op jit(solution)/shard_map/near_field_1/pallas_call | solution.py:263
  34.7 0.0 copy-done.1
  34.7 0.0 collective-permute-done.7.refs_1_
  34.7 0.0 slice-start
  34.8 7.9 %near_field_2.1 = (f32[16,32,512]{2,1,0:T(8,128)S(1)}, bf16[16,32,512]{2,1,0:T(8,128)(2,1)S(1)}, f32[3,16,512]{2,1,0:T(8,128)S(1)}, f32[3,16,128]{2,1,0:T(8,128)S(1)}) custom-call(s32[108]{0:T(128)S(1)} %reshape.295.refs_0_, bf16[1104,128]{1,0:T(8,128)(2,1)S(1)} %collective-permute-done.7.refs_1_, bf16[16,256,128]{2,1,0:T(8,128)(2,1)S(1)} %get-tuple-element.38.refs_2_, ...), custom_call_target="tpu_custom_call" | custom-call | flops 692060160 | bytes 6291456 | tf_op jit(solution)/shard_map/near_field_2/pallas_call | solution.py:263
  42.7 0.1 copy.38
  42.9 0.1 maximum_maximum_fusion
  43.0 0.4 collective-permute-start.10
  43.4 2.5 %collective-permute-start.11 = (f32[56,128]{1,0:T(8,128)S(1)}, f32[56,128]{1,0:T(8,128)S(1)}, u32[]{:S(2)}, u32[]{:S(2)}) collective-permute-start(f32[56,128]{1,0:T(8,128)S(1)} %get-tuple-element.84), channel_id=1, source_target_pairs={{0,12},{8,4},{12,0},{4,8},{1,13},{9,5},{13,1},{5,9},{2,14},{10,6},... | collective-permute-start | bytes 86024 | tf_op jit(solution)/shard_map/ppermute | solution.py:32
  45.9 0.5 collective-permute-start.12
  46.4 0.0 collective-permute-start.8
  46.4 0.0 slice-done
  46.4 1.4 %collective-permute-done.10 = f32[56,128]{1,0:T(8,128)S(1)} collective-permute-done((f32[56,128]{1,0:T(8,128)S(1)}, f32[56,128]{1,0:T(8,128)S(1)}, u32[]{:S(2)}, u32[]{:S(2)}) %collective-permute-start.10) | collective-permute-done | bytes 28704 | tf_op jit(solution)/shard_map/ppermute | solution.py:32
  47.8 1.3 %collective-permute-done.11 = f32[56,128]{1,0:T(8,128)S(1)} collective-permute-done((f32[56,128]{1,0:T(8,128)S(1)}, f32[56,128]{1,0:T(8,128)S(1)}, u32[]{:S(2)}, u32[]{:S(2)}) %collective-permute-start.11) | collective-permute-done | bytes 28704 | tf_op jit(solution)/shard_map/ppermute | solution.py:32
  49.1 0.7 %collective-permute-done.12 = f32[56,128]{1,0:T(8,128)S(1)} collective-permute-done((f32[56,128]{1,0:T(8,128)S(1)}, f32[56,128]{1,0:T(8,128)S(1)}, u32[]{:S(2)}, u32[]{:S(2)}) %collective-permute-start.12) | collective-permute-done | bytes 28704 | tf_op jit(solution)/shard_map/ppermute | solution.py:32
  49.9 0.0 collective-permute-done.8
  49.9 0.2 convert_add_fusion
  50.3 1.6 %collective-permute-start.13 = (f32[4,8,512]{2,1,0:T(8,128)S(1)}, f32[4,8,512]{2,1,0:T(8,128)S(1)}, u32[]{:S(2)}, u32[]{:S(2)}) collective-permute-start(f32[4,8,512]{2,1,0:T(8,128)S(1)} %fusion), channel_id=1, source_target_pairs={{0,2},{2,0},{1,3},{3,1},{4,6},{6,4},{5,7},{7,5},{8,10},{10,8},{9,1... | collective-permute-start | bytes 196616 | tf_op jit(solution)/shard_map/ppermute | solution.py:22
  51.9 0.6 %collective-permute-start.9 = (bf16[16,32,256]{2,1,0:T(8,128)(2,1)S(1)}, bf16[16,32,256]{2,1,0:T(8,128)(2,1)S(1)}, u32[]{:S(2)}, u32[]{:S(2)}) collective-permute-start(bf16[16,32,256]{2,1,0:T(8,128)(2,1)S(1)} %slice.308), channel_id=1, source_target_pairs={{0,2},{2,0},{1,3},{3,1},{4,6},{6,4},{5,7},{7,5},{8,10},{10,8},{9,1... | collective-permute-start | bytes 786440 | tf_op jit(solution)/shard_map/ppermute | solution.py:22
  52.5 2.8 %collective-permute-done.13 = f32[4,8,512]{2,1,0:T(8,128)S(1)} collective-permute-done((f32[4,8,512]{2,1,0:T(8,128)S(1)}, f32[4,8,512]{2,1,0:T(8,128)S(1)}, u32[]{:S(2)}, u32[]{:S(2)}) %collective-permute-start.13) | collective-permute-done | bytes 65568 | tf_op jit(solution)/shard_map/ppermute | solution.py:22
  55.3 0.1 collective-permute-start.14
  55.5 1.2 %collective-permute-done.14 = f32[4,8,512]{2,1,0:T(8,128)S(1)} collective-permute-done((f32[4,8,512]{2,1,0:T(8,128)S(1)}, f32[4,8,512]{2,1,0:T(8,128)S(1)}, u32[]{:S(2)}, u32[]{:S(2)}) %collective-permute-start.14) | collective-permute-done | bytes 65568 | tf_op jit(solution)/shard_map/ppermute | solution.py:22
  56.7 1.3 %node_terms.1 = f32[3,4096]{1,0:T(4,128)} custom-call(f32[3,8,512]{2,1,0:T(8,128)S(1)} %slice.198.grad_ref, s32[8,512]{1,0:T(8,128)S(1)} %slice_select_fusion.2.jitter_ref, f32[8,512]{1,0:T(8,128)S(1)} %slice_bitcast_fusion.edge_ref), custom_call_target="tpu_custom_call" | custom-call | flops 1048576 | bytes 262144 | tf_op jit(solution)/shard_map/node_terms/pallas_call | solution.py:537
  58.0 1.1 %collective-permute-done.9.refs_1_ = bf16[16,32,256]{2,1,0:T(8,128)(2,1)S(1)} collective-permute-done((bf16[16,32,256]{2,1,0:T(8,128)(2,1)S(1)}, bf16[16,32,256]{2,1,0:T(8,128)(2,1)S(1)}, u32[]{:S(2)}, u32[]{:S(2)}) %collective-permute-start.9) | collective-permute-done | bytes 262176 | tf_op jit(solution)/shard_map/ppermute | solution.py:22
  59.1 0.7 %potential_sum.1 = bf16[16,32,256]{2,1,0:T(8,128)(2,1)} custom-call(f32[16,32,256]{2,1,0:T(8,128)S(1)} %slice.127.refs_0_, bf16[16,32,256]{2,1,0:T(8,128)(2,1)S(1)} %collective-permute-done.9.refs_1_), custom_call_target="tpu_custom_call" | custom-call | flops 1048576 | bytes 262144 | tf_op jit(solution)/shard_map/potential_sum/pallas_call | solution.py:546
  (46 shorter events, 0.6 us)
Async XLA Ops:
  0.6 8.6 %copy-start = (s32[5,64]{1,0:T(8,128)S(1)}, s32[5,64]{1,0:T(8,128)}, u32[]{:S(2)}) copy-start(s32[5,64]{1,0:T(8,128)} %param.10) | copy-start | bytes 3844
  0.6 9.9 %collective-permute-start.4 = (bf16[16,32,256]{2,1,0:T(8,128)(2,1)}, bf16[16,32,256]{2,1,0:T(8,128)(2,1)S(1)}, u32[]{:S(2)}, u32[]{:S(2)}) collective-permute-start(bf16[16,32,256]{2,1,0:T(8,128)(2,1)} %refs_4_.1), channel_id=1, source_target_pairs={{0,2},{2,0},{1,3},{3,1},{4,6},{6,4},{5,7},{7,5},{8,10},{10,8},{9,1... | collective-permute-start | bytes 786440 | tf_op jit(solution)/shard_map/ppermute | solution.py:22
  3.7 7.1 %collective-permute-start.2 = (bf16[16,32,256]{2,1,0:T(8,128)(2,1)}, bf16[16,32,256]{2,1,0:T(8,128)(2,1)S(1)}, u32[]{:S(2)}, u32[]{:S(2)}) collective-permute-start(bf16[16,32,256]{2,1,0:T(8,128)(2,1)} %refs_4_.1), channel_id=1, source_target_pairs={{0,1},{1,0},{2,3},{3,2},{4,5},{5,4},{6,7},{7,6},{8,9},{9,8},{10,11... | collective-permute-start | bytes 786440 | tf_op jit(solution)/shard_map/ppermute | solution.py:22
  4.9 6.3 %collective-permute-start.3 = (bf16[64,256]{1,0:T(8,128)(2,1)S(1)}, bf16[64,256]{1,0:T(8,128)(2,1)S(1)}, u32[]{:S(2)}, u32[]{:S(2)}) collective-permute-start(bf16[64,256]{1,0:T(8,128)(2,1)S(1)} %get-tuple-element.30.small_ref.refs_7_), channel_id=1, source_target_pairs={{0,2},{2,0},{1,3},{3,1},{4,6},{6,4},{5,7},{7,5},{8,10},{10,8},{9,1... | collective-permute-start | bytes 98312 | tf_op jit(solution)/shard_map/ppermute | solution.py:22
  5.0 9.4 %collective-permute-start = (bf16[592,128]{1,0:T(8,128)(2,1)S(1)}, bf16[592,128]{1,0:T(8,128)(2,1)S(1)}, u32[]{:S(2)}, u32[]{:S(2)}) collective-permute-start(bf16[592,128]{1,0:T(8,128)(2,1)S(1)} %get-tuple-element.28), channel_id=1, source_target_pairs={{0,8},{8,12},{12,4},{4,0},{1,9},{9,13},{13,5},{5,1},{2,10},{10,14}... | collective-permute-start | bytes 454664 | tf_op jit(solution)/shard_map/ppermute | solution.py:32
  8.1 6.4 %collective-permute-start.1 = (bf16[512,128]{1,0:T(8,128)(2,1)S(1)}, bf16[512,128]{1,0:T(8,128)(2,1)S(1)}, u32[]{:S(2)}, u32[]{:S(2)}) collective-permute-start(bf16[512,128]{1,0:T(8,128)(2,1)S(1)} %get-tuple-element.29), channel_id=1, source_target_pairs={{0,9},{1,8},{4,1},{5,0},{8,13},{9,12},{12,5},{13,4},{2,11},{3,10},... | collective-permute-start | bytes 393224 | tf_op jit(solution)/shard_map/ppermute | solution.py:44
  10.5 1.5 %collective-permute-start.5 = (bf16[16,32,256]{2,1,0:T(8,128)(2,1)S(1)}, bf16[16,32,256]{2,1,0:T(8,128)(2,1)S(1)}, u32[]{:S(2)}, u32[]{:S(2)}) collective-permute-start(bf16[16,32,256]{2,1,0:T(8,128)(2,1)S(1)} %collective-permute-done.4.refs_0_), channel_id=1, source_target_pairs={{0,1},{1,0},{2,3},{3,2},{4,5},{5,4},{6,7},{7,6},{8,9},{9,8},{10,11... | collective-permute-start | bytes 786440 | tf_op jit(solution)/shard_map/ppermute | solution.py:22
  14.5 20.2 %copy-start.1 = (bf16[592,128]{1,0:T(8,128)(2,1)}, bf16[592,128]{1,0:T(8,128)(2,1)S(1)}, u32[]{:S(2)}) copy-start(bf16[592,128]{1,0:T(8,128)(2,1)S(1)} %collective-permute-done) | copy-start | bytes 454660
  14.5 10.4 %collective-permute-start.6 = (bf16[1104,128]{1,0:T(8,128)(2,1)S(1)}, bf16[1104,128]{1,0:T(8,128)(2,1)S(1)}, u32[]{:S(2)}, u32[]{:S(2)}) collective-permute-start(bf16[1104,128]{1,0:T(8,128)(2,1)S(1)} %constant_dynamic-update-slice_fusion.refs_1_), channel_id=1, source_target_pairs={{0,8},{8,12},{12,4},{4,0},{1,9},{9,13},{13,5},{5,1},{2,10},{10,14}... | collective-permute-start | bytes 847880 | tf_op jit(solution)/shard_map/ppermute | solution.py:32
  24.9 9.8 %collective-permute-start.7 = (bf16[1104,128]{1,0:T(8,128)(2,1)S(1)}, bf16[1104,128]{1,0:T(8,128)(2,1)S(1)}, u32[]{:S(2)}, u32[]{:S(2)}) collective-permute-start(bf16[1104,128]{1,0:T(8,128)(2,1)S(1)} %collective-permute-done.6.refs_1_), channel_id=1, source_target_pairs={{0,8},{8,12},{12,4},{4,0},{1,9},{9,13},{13,5},{5,1},{2,10},{10,14}... | collective-permute-start | bytes 847880 | tf_op jit(solution)/shard_map/ppermute | solution.py:32
  34.7 11.6 %slice-start = ((bf16[592,128]{1,0:T(8,128)(2,1)}), bf16[16,128]{1,0:T(8,128)(2,1)S(1)}, s32[]{:S(2)}) async-start(bf16[592,128]{1,0:T(8,128)(2,1)} %copy-done.1), calls=%async_computation | async-start | bytes 8192 | tf_op jit(solution)/shard_map/slice | solution.py:445
  43.0 4.8 %collective-permute-start.10 = (f32[56,128]{1,0:T(8,128)S(1)}, f32[56,128]{1,0:T(8,128)S(1)}, u32[]{:S(2)}, u32[]{:S(2)}) collective-permute-start(f32[56,128]{1,0:T(8,128)S(1)} %get-tuple-element.83), channel_id=1, source_target_pairs={{0,4},{8,0},{12,8},{4,12},{1,5},{9,1},{13,9},{5,13},{2,6},{10,2},{... | collective-permute-start | bytes 86024 | tf_op jit(solution)/shard_map/ppermute | solution.py:32
  43.4 5.7 %collective-permute-start.11 = (f32[56,128]{1,0:T(8,128)S(1)}, f32[56,128]{1,0:T(8,128)S(1)}, u32[]{:S(2)}, u32[]{:S(2)}) collective-permute-start(f32[56,128]{1,0:T(8,128)S(1)} %get-tuple-element.84), channel_id=1, source_target_pairs={{0,12},{8,4},{12,0},{4,8},{1,13},{9,5},{13,1},{5,9},{2,14},{10,6},... | collective-permute-start | bytes 86024 | tf_op jit(solution)/shard_map/ppermute | solution.py:32
  45.9 3.9 %collective-permute-start.12 = (f32[56,128]{1,0:T(8,128)S(1)}, f32[56,128]{1,0:T(8,128)S(1)}, u32[]{:S(2)}, u32[]{:S(2)}) collective-permute-start(f32[56,128]{1,0:T(8,128)S(1)} %get-tuple-element.85), channel_id=1, source_target_pairs={{0,8},{8,12},{12,4},{4,0},{1,9},{9,13},{13,5},{5,1},{2,10},{10,14}... | collective-permute-start | bytes 86024 | tf_op jit(solution)/shard_map/ppermute | solution.py:32
  46.4 3.5 %collective-permute-start.8 = (bf16[16,32,512]{2,1,0:T(8,128)(2,1)S(1)}, bf16[16,32,512]{2,1,0:T(8,128)(2,1)S(1)}, u32[]{:S(2)}, u32[]{:S(2)}) collective-permute-start(bf16[16,32,512]{2,1,0:T(8,128)(2,1)S(1)} %get-tuple-element.47), channel_id=1, source_target_pairs={{0,1},{1,0},{2,3},{3,2},{4,5},{5,4},{6,7},{7,6},{8,9},{9,8},{10,11... | collective-permute-start | bytes 1572872 | tf_op jit(solution)/shard_map/ppermute | solution.py:22
  50.3 5.0 %collective-permute-start.13 = (f32[4,8,512]{2,1,0:T(8,128)S(1)}, f32[4,8,512]{2,1,0:T(8,128)S(1)}, u32[]{:S(2)}, u32[]{:S(2)}) collective-permute-start(f32[4,8,512]{2,1,0:T(8,128)S(1)} %fusion), channel_id=1, source_target_pairs={{0,2},{2,0},{1,3},{3,1},{4,6},{6,4},{5,7},{7,5},{8,10},{10,8},{9,1... | collective-permute-start | bytes 196616 | tf_op jit(solution)/shard_map/ppermute | solution.py:22
  51.9 7.2 %collective-permute-start.9 = (bf16[16,32,256]{2,1,0:T(8,128)(2,1)S(1)}, bf16[16,32,256]{2,1,0:T(8,128)(2,1)S(1)}, u32[]{:S(2)}, u32[]{:S(2)}) collective-permute-start(bf16[16,32,256]{2,1,0:T(8,128)(2,1)S(1)} %slice.308), channel_id=1, source_target_pairs={{0,2},{2,0},{1,3},{3,1},{4,6},{6,4},{5,7},{7,5},{8,10},{10,8},{9,1... | collective-permute-start | bytes 786440 | tf_op jit(solution)/shard_map/ppermute | solution.py:22
  55.3 1.3 %collective-permute-start.14 = (f32[4,8,512]{2,1,0:T(8,128)S(1)}, f32[4,8,512]{2,1,0:T(8,128)S(1)}, u32[]{:S(2)}, u32[]{:S(2)}) collective-permute-start(f32[4,8,512]{2,1,0:T(8,128)S(1)} %select_add_fusion), channel_id=1, source_target_pairs={{0,1},{1,0},{2,3},{3,2},{4,5},{5,4},{6,7},{7,6},{8,9},{9,8},{10,11... | collective-permute-start | bytes 196616 | tf_op jit(solution)/shard_map/ppermute | solution.py:22

commit v10 on v9

--- a/solution.py
+++ b/solution.py
@@ -60,55 +60,61 @@
     return out
 
 
-def prepare_kernel(sizes, *refs):
-    arguments, refs = refs[:5], refs[5:]
-    cot_out_ref, part_refs, small_ref = refs[0], refs[1:-7], refs[-7]
-    density_ref, by_coord_ref, areas_ref, connect_ref, cot_ref, sems = refs[-6:]
+def fetched(arguments, places, sems):
     copies = []
-    for at, (argument, place) in enumerate(
-        zip(arguments, (density_ref, by_coord_ref, areas_ref, connect_ref, cot_ref))
-    ):
+    for at, (argument, place) in enumerate(zip(arguments, places)):
         copies.append(pltpu.make_async_copy(argument, place, sems.at[at]))
         copies[-1].start()
     for copy in copies:
         copy.wait()
 
-    clusters, rhs, row_count = density_ref.shape
-    quarter = part_refs[0].shape[1]
-    count = len(part_refs)
+
+def jitter_of(connect_ref, sizes):
+    clusters, _, row_count = connect_ref.shape
     panels, nodes_total = sizes
-    device, sub_place, core = (lax.axis_index(axis) for axis in ("clus", "sub", "rhs"))
-
-    def part_of(array, place):
-        return pick(place, [array[:, at * quarter : (at + 1) * quarter] for at in range(count)])
-
-    cot_out_ref[...] = cot_ref[...]
-    first_id = clusters * panels * device + row_count * sub_place
+    first_id = clusters * panels * lax.axis_index("clus") + row_count * lax.axis_index("sub")
     ids = lax.broadcasted_iota(jnp.int32, (clusters, row_count), 0) * panels
     ids = ids + lax.broadcasted_iota(jnp.int32, (clusters, row_count), 1) + first_id
     jitter = connect_ref[:, 0, :] - ids
     jitter = jnp.where(jitter > jitter_reach, jitter - nodes_total, jitter)
     jitter = jnp.where(jitter < -jitter_reach, jitter + nodes_total, jitter)
-    jitter = jitter.astype(jnp.float32).astype(jnp.bfloat16)
-    rows = [by_coord_ref[coord] for coord in range(3)] + [areas_ref[...], jitter]
+    return jitter.astype(jnp.float32).astype(jnp.bfloat16)
+
+
+def prepare_kernel(sizes, *refs):
+    arguments, part_refs, local_ref, scratch = refs[:5], refs[5:-7], refs[-7], refs[-6:]
+    fetched(arguments, scratch[:5], scratch[5])
+    density_ref, by_coord_ref, areas_ref, connect_ref, cot_ref = scratch[:5]
+    clusters, rhs, _ = density_ref.shape
+    quarter = part_refs[0].shape[1]
+    count = len(part_refs)
+    core = lax.axis_index("rhs")
+
+    def part_of(array, place):
+        return pick(place, [array[:, at * quarter : (at + 1) * quarter] for at in range(count)])
+
+    pos = [by_coord_ref[coord] for coord in range(3)]
+    jitter = jitter_of(connect_ref, sizes)
     base = clusters * rhs
     for cluster in range(clusters):
         dens = density_ref[cluster]
+        span = slice(cluster * rhs, (cluster + 1) * rhs)
+        local_ref[span, :] = cot_ref[cluster]
         for step, part_ref in enumerate(part_refs):
-            part_ref[cluster * rhs : (cluster + 1) * rhs, :] = part_of(dens, (core + step) % count)
-    for at, value in enumerate(rows):
-        span = slice(base + at * clusters, base + (at + 1) * clusters)
-        part_refs[0][span, :] = part_of(value, core)
-        if at != 3:
-            at = min(at, 3)
-            small_ref[at * clusters : (at + 1) * clusters, :] = value
-
-
-def target_kernel(rhs_count, small_ref, *refs):
-    cot_refs, (lhs_ref, aug_ref, aug32) = refs[:rhs_count], refs[rhs_count:]
+            part_ref[span, :] = part_of(dens, (core + step) % count)
+    for at, value in enumerate([*pos, areas_ref[...], jitter]):
+        part_refs[0][base + at * clusters : base + (at + 1) * clusters, :] = part_of(value, core)
+    for at, value in enumerate([*pos, jitter]):
+        local_ref[base + at * clusters : base + (at + 1) * clusters, :] = value
+
+
+def target_kernel(*refs):
+    local_refs, (lhs_ref, aug_ref, aug32) = refs[:-3], refs[-3:]
     clusters, _, row_count = aug_ref.shape
+    rhs = local_refs[0].shape[0] // clusters - 4
+    base = clusters * rhs
     pos = [
-        small_ref[coord * clusters : (coord + 1) * clusters, :].astype(jnp.float32)
+        local_refs[0][base + coord * clusters : base + (coord + 1) * clusters, :].astype(jnp.float32)
         for coord in range(3)
     ]
     square = pos[0] * pos[0] + pos[1] * pos[1] + pos[2] * pos[2] + core_radius * core_radius
@@ -116,22 +122,23 @@
     aug32[...] = jnp.zeros(aug32.shape, jnp.float32)
     for row, value in enumerate([-2.0 * value for value in pos] + three_parts(square) + [ones] * 3):
         aug32[:, row, :] = value
-    filled = AUG + sum(ref.shape[1] for ref in cot_refs)
-    blank = jnp.zeros((LANES - filled, row_count), jnp.bfloat16)
+    blank = jnp.zeros((LANES - AUG - rhs * len(local_refs), row_count), jnp.bfloat16)
     for cluster in range(clusters):
         aug = aug32[cluster].astype(jnp.bfloat16)
         aug_ref[cluster] = aug
-        rows = [ref[cluster] for ref in cot_refs] + [aug, blank]
-        lhs_ref[cluster] = jnp.concatenate(rows, axis=0).T
-
-
-def step_kernel(step, length, rhs, subs, first, last, *refs):
-    items, source_ref = refs[:2]
-    lhs_refs, aug_refs, refs = refs[2 : 2 + subs], refs[2 + subs : 2 + 2 * subs], refs[2 + 2 * subs :]
+        rows = [ref[cluster * rhs : (cluster + 1) * rhs, :] for ref in local_refs]
+        lhs_ref[cluster] = jnp.concatenate([*rows, aug, blank], axis=0).T
+
+
+def step_kernel(step, length, rhs, subs, cores, first, last, *refs):
+    items, refs = refs[0], refs[1:]
+    source_refs, refs = refs[:cores], refs[cores:]
+    source_ref = source_refs[0]
+    lhs_refs, aug_refs, refs = refs[:subs], refs[subs : 2 * subs], refs[2 * subs :]
     if not first:
         acc_in, refs = refs[0], refs[1:]
     if last:
-        small_refs, refs = refs[:subs], refs[subs:]
+        local_refs, refs = refs[:subs], refs[subs:]
         pot_ref, pot_out_ref, grad_ref, back_ref, acc = refs[:5]
         refs = refs[5:]
     else:
@@ -143,7 +150,6 @@
     row_count = panels // subs
     quarter = source_ref.shape[1]
     base = clusters * rhs
-    starts = [0] + list(range(base + 5 * clusters, source_ref.shape[0], base))
 
     there = [
         source_ref[base + coord * clusters : base + (coord + 1) * clusters, :].astype(jnp.float32)
@@ -160,9 +166,9 @@
     left[...] = jnp.zeros(left.shape, left.dtype)
     for cluster in range(clusters):
         left[cluster, width:rows, quarter:] = aug32[cluster].astype(jnp.bfloat16)
-        for place, at in enumerate(starts):
-            left[cluster, place * rhs : (place + 1) * rhs, :quarter] = source_ref[
-                at + cluster * rhs : at + (cluster + 1) * rhs, :
+        for place, ref in enumerate(source_refs):
+            left[cluster, place * rhs : (place + 1) * rhs, :quarter] = ref[
+                cluster * rhs : (cluster + 1) * rhs, :
             ]
     back[...] = jnp.zeros(back.shape, jnp.float32)
     if first:
@@ -219,23 +225,24 @@
         back_ref[coord] = -0.5 * back[:, coord, :] - there[coord] * back[:, 6, :]
     if last:
         for coord in range(3):
-            pos = [ref[coord * clusters : (coord + 1) * clusters, :] for ref in small_refs]
+            span = slice(base + coord * clusters, base + (coord + 1) * clusters)
+            pos = [ref[span, :] for ref in local_refs]
             pos = jnp.concatenate(pos, axis=1).astype(jnp.float32)
             grad_ref[coord] = acc[:, width + coord, :] - pos * acc[:, width + 3, :]
         pot_ref[...] = acc[:, :rhs, :]
         pot_out_ref[...] = acc[:, rhs:width, :].astype(jnp.bfloat16)
 
 
-def run_step(step, length, items, source, targets, smalls, rhs, width, carried, last):
+def run_step(step, length, items, sources, targets, locals_, rhs, width, carried, last):
     lhss, augs = zip(*targets)
     clusters, _, row_count = augs[0].shape
     subs = len(targets)
     panels = subs * row_count
-    quarter = source.shape[1]
+    quarter = sources[0].shape[1]
     first = carried is None
     vmem = pl.BlockSpec(memory_space=pltpu.VMEM)
     smem = pl.BlockSpec(memory_space=pltpu.SMEM)
-    operands = (items, source, *lhss, *augs)
+    operands = (items, *sources, *lhss, *augs)
     if not first:
         operands += (carried,)
     acc_shape = (clusters, width + AUG, panels)
@@ -249,7 +256,7 @@
     scratch += [pltpu.VMEM((panels, 2 * quarter), jnp.float32)] * 2
     scratch += [pltpu.VMEM((panels, 2 * quarter), jnp.bfloat16)] * 2
     if last:
-        operands += tuple(smalls)
+        operands += tuple(locals_)
         out_shape = (
             jax.ShapeDtypeStruct((clusters, rhs, panels), jnp.float32),
             jax.ShapeDtypeStruct((clusters, width - rhs, panels), jnp.bfloat16),
@@ -261,7 +268,7 @@
         out_shape = (jax.ShapeDtypeStruct(acc_shape, jnp.float32), back_shape)
     pairs = (length - 6) * panels * quarter
     return pl.pallas_call(
-        functools.partial(step_kernel, step, length, rhs, subs, first, last),
+        functools.partial(step_kernel, step, length, rhs, subs, len(sources), first, last),
         out_shape=out_shape,
         in_specs=[smem] + [vmem] * (len(operands) - 1),
         out_specs=(vmem,) * len(out_shape),
@@ -340,31 +347,23 @@
 
     nodes_total = clus_count * clusters * panels
 
-    cots = [cotangent] + [shifted(cotangent, "sub", step) for step in range(1, sub_count)]
-    for step in range(1, rhs_count):
-        cots += [shifted(block, "rhs", step) for block in cots[:sub_count]]
-
     by_coord = jnp.transpose(positions, (1, 0, 2))
     arguments = [
         pltpu.with_memory_space_constraint(array, pltpu.HBM)
         for array in (density, by_coord, areas, connect, cotangent)
     ]
-    own_cot, *parts, small = pl.pallas_call(
+    shapes = [(clusters * (rhs + 5), quarter)] + [(clusters * rhs, quarter)] * (rhs_count - 1)
+    shapes.append((clusters * (rhs + 4), row_count))
+    *parts, local = pl.pallas_call(
         functools.partial(prepare_kernel, (panels, nodes_total)),
-        out_shape=(
-            jax.ShapeDtypeStruct(cotangent.shape, jnp.bfloat16),
-            jax.ShapeDtypeStruct((clusters * (rhs + 5), quarter), jnp.bfloat16),
-            *[jax.ShapeDtypeStruct((clusters * rhs, quarter), jnp.bfloat16)] * (rhs_count - 1),
-            jax.ShapeDtypeStruct((clusters * 4, row_count), jnp.bfloat16),
-        ),
+        out_shape=[jax.ShapeDtypeStruct(shape, jnp.bfloat16) for shape in shapes],
         in_specs=[pl.BlockSpec(memory_space=pltpu.HBM)] * len(arguments),
-        out_specs=(vmem,) * (rhs_count + 2),
+        out_specs=[vmem] * len(shapes),
         scratch_shapes=[pltpu.VMEM(array.shape, array.dtype) for array in arguments]
         + [pltpu.SemaphoreType.DMA((len(arguments),))],
         compiler_params=pltpu.CompilerParams(vmem_limit_bytes=16 * 1024 * 1024),
         name="prepare",
     )(*arguments)
-    cots[0] = own_cot
     ring = ring_order(clus_count)
     at_place = [ring.index(index) for index in range(clus_count)]
     ring_place = pick(device, at_place)
@@ -398,43 +397,46 @@
     items = jnp.pad(listed, ((0, 0), (3, 3)), constant_values=clusters)
     items = jnp.concatenate([turns[:, None], items[:, 1:]], axis=1).reshape(-1)
 
-    smalls = [small] + [shifted(small, "sub", step) for step in range(1, sub_count)]
+    locals_ = [local] + [shifted(local, "sub", step) for step in range(1, sub_count)]
+    blocks = [
+        [block] + [shifted(block, "rhs", step) for step in range(1, rhs_count)] for block in locals_
+    ]
 
     def in_order(blocks):
         return jnp.concatenate(
             [pick((sub_place - place) % sub_count, blocks) for place in range(sub_count)], axis=-1
         )
 
-    jitter_all = in_order([block[3 * clusters :] for block in smalls]).astype(jnp.int32)
+    jitter_all = in_order([block[clusters * (rhs + 3) :] for block in locals_]).astype(jnp.int32)
     targets = [
         pl.pallas_call(
-            functools.partial(target_kernel, rhs_count),
+            target_kernel,
             out_shape=(
                 jax.ShapeDtypeStruct((clusters, row_count, LANES), jnp.bfloat16),
                 jax.ShapeDtypeStruct((clusters, AUG, row_count), jnp.bfloat16),
             ),
-            in_specs=[vmem] * (1 + rhs_count),
+            in_specs=[vmem] * rhs_count,
             out_specs=(vmem, vmem),
             scratch_shapes=[pltpu.VMEM((clusters, AUG, row_count), jnp.float32)],
             compiler_params=pltpu.CompilerParams(vmem_limit_bytes=16 * 1024 * 1024),
             cost_estimate=pl.CostEstimate(flops=2**20, bytes_accessed=2**18, transcendentals=0),
             name=f"targets_{place}",
-        )(smalls[place], *cots[place::sub_count])
+        )(*blocks[place])
         for place in range(sub_count)
     ]
 
     arrived, targets = lax.optimization_barrier((arrived, targets))
-    source = jnp.concatenate(arrived, axis=0)
+    sources = arrived
     carried = None
     backs, jitter_rows = [], [None]
     for step in range(1, clus_count):
         if step > 1:
             if step > 2:
-                source, backs[step - 3] = lax.optimization_barrier((source, backs[step - 3]))
-            source = round_ring(source, 1)
+                sources, backs[step - 3] = lax.optimization_barrier((sources, backs[step - 3]))
+            sources = [round_ring(source, 1) for source in sources]
         last = step == clus_count - 1
         results = run_step(
-            step - 1, length, items, source, targets, smalls, rhs, width, carried, last
+            step - 1, length, items, sources, targets, locals_, rhs, width, carried, last
         )
         if last:
             pot, pot_out, grad, back = results
@@ -442,7 +444,7 @@
             carried, back = results
         backs.append(back)
         at = clusters * (rhs + 4)
-        jitter_rows.append(source[at : at + clusters])
+        jitter_rows.append(sources[0][at : at + clusters])
 
     grad = in_order([grad[..., at * row_count : (at + 1) * row_count] for at in range(sub_count)])
     low_part = (sub_place == 0) & (core == 0)

time: 60.2 us -> 61.5 us (1.022)
  starting transfers between devices: 18.2 us -> 19.9 us
    ppermute x8 -> x7, waiting for transfers between devices: 6.5 us -> 8.75 us  [shifted(): return lax.ppermute(value, axis, pairs)]
    ppermute x6 -> x8, starting transfers between devices: 11.6 us -> 13.3 us  [round_ring(): return lax.ppermute(value, 'clus', pairs)]
    ppermute x1, waiting for transfers between devices: 2.01 us -> 0.28 us  [moved(): return lax.ppermute(value, axes, pairs)]
    ppermute x6 -> x8, waiting for transfers between devices: 3.32 us -> 2.65 us  [round_ring(): return lax.ppermute(value, 'clus', pairs)]
    ppermute x8 -> x7, starting transfers between devices: 5.51 us -> 5.24 us  [shifted(): return lax.ppermute(value, axis, pairs)]
  transfers between devices with their start and end apart: 15 -> 16, of which waited for: 9 -> 8; matrix products, arithmetic and copies ran while one was open for 2% -> 2% of each run, Pallas kernels for 30% -> 28%
where the time goes in v10:
time: 61.5 us; the launch traced here: 61.4 us
  Pallas kernels  26.7 us (43%)
  starting transfers between devices  19.9 us (32%)
  waiting for transfers between devices  11.7 us (19%)
  other arithmetic  1.15 us (2%)
  between operations  1.03 us (2%)
  local copies, waits for them, and re-layouts  0.9 us (1%)
    pallas_call x3, Pallas kernels, run_step(): pl.pallas_call(functools.partial(step_kernel, step, length, rhs, subs, le...  22.6 us
    ppermute x8, starting transfers between devices, round_ring(): return lax.ppermute(value, 'clus', pairs)  13.3 us
    ppermute x7, waiting for transfers between devices, shifted(): return lax.ppermute(value, axis, pairs)  8.75 us
    ppermute x7, starting transfers between devices, shifted(): return lax.ppermute(value, axis, pairs)  5.24 us
    ppermute x8, waiting for transfers between devices, round_ring(): return lax.ppermute(value, 'clus', pairs)  2.65 us
    ppermute x1, starting transfers between devices, moved(): return lax.ppermute(value, axes, pairs)  1.41 us
    pallas_call x1, Pallas kernels, on_device(): pl.pallas_call(node_kernel, out_shape=jax.ShapeDtypeStruct((3, share * pa...  1.32 us
  transfers between devices with their start and end apart: 16, of which 8 were waited for; matrix products, arithmetic and copies ran while one was open for 2% of the time, Pallas kernels for 28%

profile of v10, /device:TPU:0, one launch (start us, length us, event | category | flops | bytes accessed | tf_op | source)
XLA Modules:
  0.0 61.4 jit_solution(4607952078680927942)
XLA Ops:
  0.6 0.0 copy-start
  0.6 1.2 %prepare.1 = (bf16[592,128]{1,0:T(8,128)(2,1)S(1)}, bf16[512,128]{1,0:T(8,128)(2,1)S(1)}, bf16[576,256]{1,0:T(8,128)(2,1)S(1)}) custom-call(bf16[16,32,256]{2,1,0:T(8,128)(2,1)} %refs_0_.1, bf16[3,16,256]{2,1,0:T(8,128)(2,1)} %bitcast.91, bf16[16,256]{1,0:T(8,128)(2,1)} %refs_2_.1, s32[16,4,256]{2,1,0:T(4,128)} %refs_3_.1, bf16[16,32,256]{2,1,0:T(8,128)(2,1)} %refs_4_.1), custom_call_target="tpu_custom_call" | custom-call | tf_op jit(solution)/shard_map/prepare/pallas_call | solution.py:357
  1.9 3.0 %collective-permute-start.3 = (bf16[576,256]{1,0:T(8,128)(2,1)S(1)}, bf16[576,256]{1,0:T(8,128)(2,1)S(1)}, u32[]{:S(2)}, u32[]{:S(2)}) collective-permute-start(bf16[576,256]{1,0:T(8,128)(2,1)S(1)} %get-tuple-element.30.refs_0_.refs_8_), channel_id=1, source_target_pairs={{0,2},{2,0},{1,3},{3,1},{4,6},{6,4},{5,7},{7,5},{8,10},{10,8},{9,1... | collective-permute-start | bytes 884744 | tf_op jit(solution)/shard_map/ppermute | solution.py:22
  4.9 0.0 collective-permute-start.2
  4.9 2.6 %collective-permute-start = (bf16[592,128]{1,0:T(8,128)(2,1)S(1)}, bf16[592,128]{1,0:T(8,128)(2,1)S(1)}, u32[]{:S(2)}, u32[]{:S(2)}) collective-permute-start(bf16[592,128]{1,0:T(8,128)(2,1)S(1)} %get-tuple-element.28), channel_id=1, source_target_pairs={{0,8},{8,12},{12,4},{4,0},{1,9},{9,13},{13,5},{5,1},{2,10},{10,14}... | collective-permute-start | bytes 454664 | tf_op jit(solution)/shard_map/ppermute | solution.py:32
  7.5 1.4 %collective-permute-start.1 = (bf16[512,128]{1,0:T(8,128)(2,1)S(1)}, bf16[512,128]{1,0:T(8,128)(2,1)S(1)}, u32[]{:S(2)}, u32[]{:S(2)}) collective-permute-start(bf16[512,128]{1,0:T(8,128)(2,1)S(1)} %get-tuple-element.29), channel_id=1, source_target_pairs={{0,9},{1,8},{4,1},{5,0},{8,13},{9,12},{12,5},{13,4},{2,11},{3,10},... | collective-permute-start | bytes 393224 | tf_op jit(solution)/shard_map/ppermute | solution.py:44
  8.9 0.0 copy-done
  8.9 0.1 constant_dynamic-slice_fusion
  9.0 0.1 reshape.294
  9.0 0.1 mul.22
  9.2 0.2 convert_reduce_fusion
  9.3 0.2 convert_reduce_fusion.1
  9.5 0.1 copy.34
  9.6 0.1 select_reduce_fusion
  9.8 2.1 %collective-permute-done.3.refs_0_.refs_9_ = bf16[576,256]{1,0:T(8,128)(2,1)S(1)} collective-permute-done((bf16[576,256]{1,0:T(8,128)(2,1)S(1)}, bf16[576,256]{1,0:T(8,128)(2,1)S(1)}, u32[]{:S(2)}, u32[]{:S(2)}) %collective-permute-start.3) | collective-permute-done | bytes 294944 | tf_op jit(solution)/shard_map/ppermute | solution.py:22
  11.9 0.0 collective-permute-start.4
  11.9 0.1 pad_slice_fusion
  12.0 0.1 pad_add_fusion
  12.1 0.1 reshape.295.refs_0_
  12.1 0.1 pad.40.clone
  12.2 0.0 collective-permute-done.2.refs_1_
  12.2 0.4 targets_0.1
  12.6 0.9 %collective-permute-done.4.refs_1_ = bf16[576,256]{1,0:T(8,128)(2,1)S(1)} collective-permute-done((bf16[576,256]{1,0:T(8,128)(2,1)S(1)}, bf16[576,256]{1,0:T(8,128)(2,1)S(1)}, u32[]{:S(2)}, u32[]{:S(2)}) %collective-permute-start.4) | collective-permute-done | bytes 294944 | tf_op jit(solution)/shard_map/ppermute | solution.py:22
  13.5 0.4 targets_1.1
  13.9 0.3 collective-permute-done.1.refs_2_
  14.1 0.0 collective-permute-done.refs_1_
  14.2 3.0 %collective-permute-start.5 = (bf16[592,128]{1,0:T(8,128)(2,1)S(1)}, bf16[592,128]{1,0:T(8,128)(2,1)S(1)}, u32[]{:S(2)}, u32[]{:S(2)}) collective-permute-start(bf16[592,128]{1,0:T(8,128)(2,1)S(1)} %collective-permute-done.refs_1_), channel_id=1, source_target_pairs={{0,8},{8,12},{12,4},{4,0},{1,9},{9,13},{13,5},{5,1},{2,10},{10,14}... | collective-permute-start | bytes 454664 | tf_op jit(solution)/shard_map/ppermute | solution.py:32
  17.1 1.2 %collective-permute-start.6 = (bf16[512,128]{1,0:T(8,128)(2,1)S(1)}, bf16[512,128]{1,0:T(8,128)(2,1)S(1)}, u32[]{:S(2)}, u32[]{:S(2)}) collective-permute-start(bf16[512,128]{1,0:T(8,128)(2,1)S(1)} %collective-permute-done.1.refs_2_), channel_id=1, source_target_pairs={{0,8},{8,12},{12,4},{4,0},{1,9},{9,13},{13,5},{5,1},{2,10},{10,14}... | collective-permute-start | bytes 393224 | tf_op jit(solution)/shard_map/ppermute | solution.py:32
  18.4 7.8 %near_field_0.1 = (f32[16,80,512]{2,1,0:T(8,128)S(1)}, f32[3,16,128]{2,1,0:T(8,128)S(1)}) custom-call(s32[108]{0:T(128)S(1)} %reshape.295.refs_0_, bf16[592,128]{1,0:T(8,128)(2,1)S(1)} %collective-permute-done.refs_1_, bf16[512,128]{1,0:T(8,128)(2,1)S(1)} %collective-permute-done.1.refs_2_, bf16[16,256,128]{2,1,0:T(8,128)(2,1)S(1)} %get-tuple-element.37.refs_3_, ...), custom_call_target="tpu_custom_call" | custom-call | flops 692060160 | bytes 6291456 | tf_op jit(solution)/shard_map/near_field_0/pallas_call | solution.py:270
  26.2 0.0 collective-permute-done.6.refs_2_
  26.2 0.0 collective-permute-done.5.refs_1_
  26.2 0.7 %collective-permute-start.7 = (bf16[592,128]{1,0:T(8,128)(2,1)S(1)}, bf16[592,128]{1,0:T(8,128)(2,1)S(1)}, u32[]{:S(2)}, u32[]{:S(2)}) collective-permute-start(bf16[592,128]{1,0:T(8,128)(2,1)S(1)} %collective-permute-done.5.refs_1_), channel_id=1, source_target_pairs={{0,8},{8,12},{12,4},{4,0},{1,9},{9,13},{13,5},{5,1},{2,10},{10,14}... | collective-permute-start | bytes 454664 | tf_op jit(solution)/shard_map/ppermute | solution.py:32
  26.9 0.2 collective-permute-start.8
  27.2 7.3 %near_field_1.1 = (f32[16,80,512]{2,1,0:T(8,128)S(1)}, f32[3,16,128]{2,1,0:T(8,128)S(1)}) custom-call(s32[108]{0:T(128)S(1)} %reshape.295.refs_0_, bf16[592,128]{1,0:T(8,128)(2,1)S(1)} %collective-permute-done.5.refs_1_, bf16[512,128]{1,0:T(8,128)(2,1)S(1)} %collective-permute-done.6.refs_2_, bf16[16,256,128]{2,1,0:T(8,128)(2,1)S(1)} %get-tuple-element.37.refs_3_, ...), custom_call_target="tpu_custom_call" | custom-call | flops 692060160 | bytes 6291456 | tf_op jit(solution)/shard_map/near_field_1/pallas_call | solution.py:270
  34.6 0.0 collective-permute-done.8.refs_2_
  34.6 0.0 collective-permute-done.7.refs_1_
  34.6 7.5 %near_field_2.1 = (f32[16,32,512]{2,1,0:T(8,128)S(1)}, bf16[16,32,512]{2,1,0:T(8,128)(2,1)S(1)}, f32[3,16,512]{2,1,0:T(8,128)S(1)}, f32[3,16,128]{2,1,0:T(8,128)S(1)}) custom-call(s32[108]{0:T(128)S(1)} %reshape.295.refs_0_, bf16[592,128]{1,0:T(8,128)(2,1)S(1)} %collective-permute-done.7.refs_1_, bf16[512,128]{1,0:T(8,128)(2,1)S(1)} %collective-permute-done.8.refs_2_, ...), custom_call_target="tpu_custom_call" | custom-call | flops 692060160 | bytes 6291456 | tf_op jit(solution)/shard_map/near_field_2/pallas_call | solution.py:270
  42.1 0.1 copy.38
  42.3 0.1 maximum_maximum_fusion
  42.4 2.3 %collective-permute-start.11 = (f32[56,128]{1,0:T(8,128)S(1)}, f32[56,128]{1,0:T(8,128)S(1)}, u32[]{:S(2)}, u32[]{:S(2)}) collective-permute-start(f32[56,128]{1,0:T(8,128)S(1)} %get-tuple-element.83), channel_id=1, source_target_pairs={{0,4},{8,0},{12,8},{4,12},{1,5},{9,1},{13,9},{5,13},{2,6},{10,2},{... | collective-permute-start | bytes 86024 | tf_op jit(solution)/shard_map/ppermute | solution.py:32
  44.6 2.1 %collective-permute-start.12 = (f32[56,128]{1,0:T(8,128)S(1)}, f32[56,128]{1,0:T(8,128)S(1)}, u32[]{:S(2)}, u32[]{:S(2)}) collective-permute-start(f32[56,128]{1,0:T(8,128)S(1)} %get-tuple-element.84), channel_id=1, source_target_pairs={{0,12},{8,4},{12,0},{4,8},{1,13},{9,5},{13,1},{5,9},{2,14},{10,6},... | collective-permute-start | bytes 86024 | tf_op jit(solution)/shard_map/ppermute | solution.py:32
  46.7 1.2 %collective-permute-start.13 = (f32[56,128]{1,0:T(8,128)S(1)}, f32[56,128]{1,0:T(8,128)S(1)}, u32[]{:S(2)}, u32[]{:S(2)}) collective-permute-start(f32[56,128]{1,0:T(8,128)S(1)} %get-tuple-element.85), channel_id=1, source_target_pairs={{0,8},{8,12},{12,4},{4,0},{1,9},{9,13},{13,5},{5,1},{2,10},{10,14}... | collective-permute-start | bytes 86024 | tf_op jit(solution)/shard_map/ppermute | solution.py:32
  47.9 0.0 collective-permute-start.9
  48.0 0.0 collective-permute-done.11
  48.0 2.3 %collective-permute-done.12 = f32[56,128]{1,0:T(8,128)S(1)} collective-permute-done((f32[56,128]{1,0:T(8,128)S(1)}, f32[56,128]{1,0:T(8,128)S(1)}, u32[]{:S(2)}, u32[]{:S(2)}) %collective-permute-start.12) | collective-permute-done | bytes 28704 | tf_op jit(solution)/shard_map/ppermute | solution.py:32
  50.3 0.3 collective-permute-done.13
  50.8 0.0 collective-permute-done.9
  50.8 0.2 convert_add_fusion
  51.1 1.2 %collective-permute-start.14 = (f32[4,8,512]{2,1,0:T(8,128)S(1)}, f32[4,8,512]{2,1,0:T(8,128)S(1)}, u32[]{:S(2)}, u32[]{:S(2)}) collective-permute-start(f32[4,8,512]{2,1,0:T(8,128)S(1)} %fusion), channel_id=1, source_target_pairs={{0,2},{2,0},{1,3},{3,1},{4,6},{6,4},{5,7},{7,5},{8,10},{10,8},{9,1... | collective-permute-start | bytes 196616 | tf_op jit(solution)/shard_map/ppermute | solution.py:22
  52.4 0.9 %collective-permute-start.10 = (bf16[16,32,256]{2,1,0:T(8,128)(2,1)S(1)}, bf16[16,32,256]{2,1,0:T(8,128)(2,1)S(1)}, u32[]{:S(2)}, u32[]{:S(2)}) collective-permute-start(bf16[16,32,256]{2,1,0:T(8,128)(2,1)S(1)} %slice.308), channel_id=1, source_target_pairs={{0,2},{2,0},{1,3},{3,1},{4,6},{6,4},{5,7},{7,5},{8,10},{10,8},{9,1... | collective-permute-start | bytes 786440 | tf_op jit(solution)/shard_map/ppermute | solution.py:22
  53.3 2.8 %collective-permute-done.14 = f32[4,8,512]{2,1,0:T(8,128)S(1)} collective-permute-done((f32[4,8,512]{2,1,0:T(8,128)S(1)}, f32[4,8,512]{2,1,0:T(8,128)S(1)}, u32[]{:S(2)}, u32[]{:S(2)}) %collective-permute-start.14) | collective-permute-done | bytes 65568 | tf_op jit(solution)/shard_map/ppermute | solution.py:22
  56.1 0.1 collective-permute-start.15
  56.2 1.2 %collective-permute-done.15 = f32[4,8,512]{2,1,0:T(8,128)S(1)} collective-permute-done((f32[4,8,512]{2,1,0:T(8,128)S(1)}, f32[4,8,512]{2,1,0:T(8,128)S(1)}, u32[]{:S(2)}, u32[]{:S(2)}) %collective-permute-start.15) | collective-permute-done | bytes 65568 | tf_op jit(solution)/shard_map/ppermute | solution.py:22
  57.5 1.3 %node_terms.1 = f32[3,4096]{1,0:T(4,128)} custom-call(f32[3,8,512]{2,1,0:T(8,128)S(1)} %slice.198.grad_ref, s32[8,512]{1,0:T(8,128)S(1)} %slice_select_fusion.2.jitter_ref, f32[8,512]{1,0:T(8,128)S(1)} %slice_bitcast_fusion.edge_ref), custom_call_target="tpu_custom_call" | custom-call | flops 1048576 | bytes 262144 | tf_op jit(solution)/shard_map/node_terms/pallas_call | solution.py:539
  58.8 1.9 %collective-permute-done.10.refs_1_ = bf16[16,32,256]{2,1,0:T(8,128)(2,1)S(1)} collective-permute-done((bf16[16,32,256]{2,1,0:T(8,128)(2,1)S(1)}, bf16[16,32,256]{2,1,0:T(8,128)(2,1)S(1)}, u32[]{:S(2)}, u32[]{:S(2)}) %collective-permute-start.10) | collective-permute-done | bytes 262176 | tf_op jit(solution)/shard_map/ppermute | solution.py:22
  60.6 0.7 %potential_sum.1 = bf16[16,32,256]{2,1,0:T(8,128)(2,1)} custom-call(f32[16,32,256]{2,1,0:T(8,128)S(1)} %slice.127.refs_0_, bf16[16,32,256]{2,1,0:T(8,128)(2,1)S(1)} %collective-permute-done.10.refs_1_), custom_call_target="tpu_custom_call" | custom-call | flops 1048576 | bytes 262144 | tf_op jit(solution)/shard_map/potential_sum/pallas_call | solution.py:548
  (45 shorter events, 0.6 us)
Async XLA Ops:
  0.6 8.3 %copy-start = (s32[5,64]{1,0:T(8,128)S(1)}, s32[5,64]{1,0:T(8,128)}, u32[]{:S(2)}) copy-start(s32[5,64]{1,0:T(8,128)} %param.10) | copy-start | bytes 3844
  1.9 10.0 %collective-permute-start.3 = (bf16[576,256]{1,0:T(8,128)(2,1)S(1)}, bf16[576,256]{1,0:T(8,128)(2,1)S(1)}, u32[]{:S(2)}, u32[]{:S(2)}) collective-permute-start(bf16[576,256]{1,0:T(8,128)(2,1)S(1)} %get-tuple-element.30.refs_0_.refs_8_), channel_id=1, source_target_pairs={{0,2},{2,0},{1,3},{3,1},{4,6},{6,4},{5,7},{7,5},{8,10},{10,8},{9,1... | collective-permute-start | bytes 884744 | tf_op jit(solution)/shard_map/ppermute | solution.py:22
  4.9 7.3 %collective-permute-start.2 = (bf16[576,256]{1,0:T(8,128)(2,1)S(1)}, bf16[576,256]{1,0:T(8,128)(2,1)S(1)}, u32[]{:S(2)}, u32[]{:S(2)}) collective-permute-start(bf16[576,256]{1,0:T(8,128)(2,1)S(1)} %get-tuple-element.30.refs_0_.refs_8_), channel_id=1, source_target_pairs={{0,1},{1,0},{2,3},{3,2},{4,5},{5,4},{6,7},{7,6},{8,9},{9,8},{10,11... | collective-permute-start | bytes 884744 | tf_op jit(solution)/shard_map/ppermute | solution.py:22
  4.9 9.3 %collective-permute-start = (bf16[592,128]{1,0:T(8,128)(2,1)S(1)}, bf16[592,128]{1,0:T(8,128)(2,1)S(1)}, u32[]{:S(2)}, u32[]{:S(2)}) collective-permute-start(bf16[592,128]{1,0:T(8,128)(2,1)S(1)} %get-tuple-element.28), channel_id=1, source_target_pairs={{0,8},{8,12},{12,4},{4,0},{1,9},{9,13},{13,5},{5,1},{2,10},{10,14}... | collective-permute-start | bytes 454664 | tf_op jit(solution)/shard_map/ppermute | solution.py:32
  7.5 6.7 %collective-permute-start.1 = (bf16[512,128]{1,0:T(8,128)(2,1)S(1)}, bf16[512,128]{1,0:T(8,128)(2,1)S(1)}, u32[]{:S(2)}, u32[]{:S(2)}) collective-permute-start(bf16[512,128]{1,0:T(8,128)(2,1)S(1)} %get-tuple-element.29), channel_id=1, source_target_pairs={{0,9},{1,8},{4,1},{5,0},{8,13},{9,12},{12,5},{13,4},{2,11},{3,10},... | collective-permute-start | bytes 393224 | tf_op jit(solution)/shard_map/ppermute | solution.py:44
  11.9 1.6 %collective-permute-start.4 = (bf16[576,256]{1,0:T(8,128)(2,1)S(1)}, bf16[576,256]{1,0:T(8,128)(2,1)S(1)}, u32[]{:S(2)}, u32[]{:S(2)}) collective-permute-start(bf16[576,256]{1,0:T(8,128)(2,1)S(1)} %collective-permute-done.3.refs_0_.refs_9_), channel_id=1, source_target_pairs={{0,1},{1,0},{2,3},{3,2},{4,5},{5,4},{6,7},{7,6},{8,9},{9,8},{10,11... | collective-permute-start | bytes 884744 | tf_op jit(solution)/shard_map/ppermute | solution.py:22
  14.2 12.0 %collective-permute-start.5 = (bf16[592,128]{1,0:T(8,128)(2,1)S(1)}, bf16[592,128]{1,0:T(8,128)(2,1)S(1)}, u32[]{:S(2)}, u32[]{:S(2)}) collective-permute-start(bf16[592,128]{1,0:T(8,128)(2,1)S(1)} %collective-permute-done.refs_1_), channel_id=1, source_target_pairs={{0,8},{8,12},{12,4},{4,0},{1,9},{9,13},{13,5},{5,1},{2,10},{10,14}... | collective-permute-start | bytes 454664 | tf_op jit(solution)/shard_map/ppermute | solution.py:32
  17.1 9.0 %collective-permute-start.6 = (bf16[512,128]{1,0:T(8,128)(2,1)S(1)}, bf16[512,128]{1,0:T(8,128)(2,1)S(1)}, u32[]{:S(2)}, u32[]{:S(2)}) collective-permute-start(bf16[512,128]{1,0:T(8,128)(2,1)S(1)} %collective-permute-done.1.refs_2_), channel_id=1, source_target_pairs={{0,8},{8,12},{12,4},{4,0},{1,9},{9,13},{13,5},{5,1},{2,10},{10,14}... | collective-permute-start | bytes 393224 | tf_op jit(solution)/shard_map/ppermute | solution.py:32
  26.2 8.4 %collective-permute-start.7 = (bf16[592,128]{1,0:T(8,128)(2,1)S(1)}, bf16[592,128]{1,0:T(8,128)(2,1)S(1)}, u32[]{:S(2)}, u32[]{:S(2)}) collective-permute-start(bf16[592,128]{1,0:T(8,128)(2,1)S(1)} %collective-permute-done.5.refs_1_), channel_id=1, source_target_pairs={{0,8},{8,12},{12,4},{4,0},{1,9},{9,13},{13,5},{5,1},{2,10},{10,14}... | collective-permute-start | bytes 454664 | tf_op jit(solution)/shard_map/ppermute | solution.py:32
  26.9 7.7 %collective-permute-start.8 = (bf16[512,128]{1,0:T(8,128)(2,1)S(1)}, bf16[512,128]{1,0:T(8,128)(2,1)S(1)}, u32[]{:S(2)}, u32[]{:S(2)}) collective-permute-start(bf16[512,128]{1,0:T(8,128)(2,1)S(1)} %collective-permute-done.6.refs_2_), channel_id=1, source_target_pairs={{0,8},{8,12},{12,4},{4,0},{1,9},{9,13},{13,5},{5,1},{2,10},{10,14}... | collective-permute-start | bytes 393224 | tf_op jit(solution)/shard_map/ppermute | solution.py:32
  42.4 5.6 %collective-permute-start.11 = (f32[56,128]{1,0:T(8,128)S(1)}, f32[56,128]{1,0:T(8,128)S(1)}, u32[]{:S(2)}, u32[]{:S(2)}) collective-permute-start(f32[56,128]{1,0:T(8,128)S(1)} %get-tuple-element.83), channel_id=1, source_target_pairs={{0,4},{8,0},{12,8},{4,12},{1,5},{9,1},{13,9},{5,13},{2,6},{10,2},{... | collective-permute-start | bytes 86024 | tf_op jit(solution)/shard_map/ppermute | solution.py:32
  44.6 5.7 %collective-permute-start.12 = (f32[56,128]{1,0:T(8,128)S(1)}, f32[56,128]{1,0:T(8,128)S(1)}, u32[]{:S(2)}, u32[]{:S(2)}) collective-permute-start(f32[56,128]{1,0:T(8,128)S(1)} %get-tuple-element.84), channel_id=1, source_target_pairs={{0,12},{8,4},{12,0},{4,8},{1,13},{9,5},{13,1},{5,9},{2,14},{10,6},... | collective-permute-start | bytes 86024 | tf_op jit(solution)/shard_map/ppermute | solution.py:32
  46.7 3.9 %collective-permute-start.13 = (f32[56,128]{1,0:T(8,128)S(1)}, f32[56,128]{1,0:T(8,128)S(1)}, u32[]{:S(2)}, u32[]{:S(2)}) collective-permute-start(f32[56,128]{1,0:T(8,128)S(1)} %get-tuple-element.85), channel_id=1, source_target_pairs={{0,8},{8,12},{12,4},{4,0},{1,9},{9,13},{13,5},{5,1},{2,10},{10,14}... | collective-permute-start | bytes 86024 | tf_op jit(solution)/shard_map/ppermute | solution.py:32
  47.9 2.8 %collective-permute-start.9 = (bf16[16,32,512]{2,1,0:T(8,128)(2,1)S(1)}, bf16[16,32,512]{2,1,0:T(8,128)(2,1)S(1)}, u32[]{:S(2)}, u32[]{:S(2)}) collective-permute-start(bf16[16,32,512]{2,1,0:T(8,128)(2,1)S(1)} %get-tuple-element.47), channel_id=1, source_target_pairs={{0,1},{1,0},{2,3},{3,2},{4,5},{5,4},{6,7},{7,6},{8,9},{9,8},{10,11... | collective-permute-start | bytes 1572872 | tf_op jit(solution)/shard_map/ppermute | solution.py:22
  51.1 5.0 %collective-permute-start.14 = (f32[4,8,512]{2,1,0:T(8,128)S(1)}, f32[4,8,512]{2,1,0:T(8,128)S(1)}, u32[]{:S(2)}, u32[]{:S(2)}) collective-permute-start(f32[4,8,512]{2,1,0:T(8,128)S(1)} %fusion), channel_id=1, source_target_pairs={{0,2},{2,0},{1,3},{3,1},{4,6},{6,4},{5,7},{7,5},{8,10},{10,8},{9,1... | collective-permute-start | bytes 196616 | tf_op jit(solution)/shard_map/ppermute | solution.py:22
  52.4 8.3 %collective-permute-start.10 = (bf16[16,32,256]{2,1,0:T(8,128)(2,1)S(1)}, bf16[16,32,256]{2,1,0:T(8,128)(2,1)S(1)}, u32[]{:S(2)}, u32[]{:S(2)}) collective-permute-start(bf16[16,32,256]{2,1,0:T(8,128)(2,1)S(1)} %slice.308), channel_id=1, source_target_pairs={{0,2},{2,0},{1,3},{3,1},{4,6},{6,4},{5,7},{7,5},{8,10},{10,8},{9,1... | collective-permute-start | bytes 786440 | tf_op jit(solution)/shard_map/ppermute | solution.py:22
  56.1 1.3 %collective-permute-start.15 = (f32[4,8,512]{2,1,0:T(8,128)S(1)}, f32[4,8,512]{2,1,0:T(8,128)S(1)}, u32[]{:S(2)}, u32[]{:S(2)}) collective-permute-start(f32[4,8,512]{2,1,0:T(8,128)S(1)} %select_add_fusion), channel_id=1, source_target_pairs={{0,1},{1,0},{2,3},{3,2},{4,5},{5,4},{6,7},{7,6},{8,9},{9,8},{10,11... | collective-permute-start | bytes 196616 | tf_op jit(solution)/shard_map/ppermute | solution.py:22

commit v11 on v10

--- a/solution.py
+++ b/solution.py
@@ -130,10 +130,8 @@
         lhs_ref[cluster] = jnp.concatenate([*rows, aug, blank], axis=0).T
 
 
-def step_kernel(step, length, rhs, subs, cores, first, last, *refs):
-    items, refs = refs[0], refs[1:]
-    source_refs, refs = refs[:cores], refs[cores:]
-    source_ref = source_refs[0]
+def step_kernel(step, length, rhs, subs, first, last, *refs):
+    items, source_ref, refs = refs[0], refs[1], refs[2:]
     lhs_refs, aug_refs, refs = refs[:subs], refs[subs : 2 * subs], refs[2 * subs :]
     if not first:
         acc_in, refs = refs[0], refs[1:]
@@ -151,6 +149,8 @@
     quarter = source_ref.shape[1]
     base = clusters * rhs
 
+    starts = [0] + list(range(base + 5 * clusters, source_ref.shape[0], base))
+
     there = [
         source_ref[base + coord * clusters : base + (coord + 1) * clusters, :].astype(jnp.float32)
         for coord in range(3)
@@ -166,9 +166,9 @@
     left[...] = jnp.zeros(left.shape, left.dtype)
     for cluster in range(clusters):
         left[cluster, width:rows, quarter:] = aug32[cluster].astype(jnp.bfloat16)
-        for place, ref in enumerate(source_refs):
-            left[cluster, place * rhs : (place + 1) * rhs, :quarter] = ref[
-                cluster * rhs : (cluster + 1) * rhs, :
+        for place, at in enumerate(starts):
+            left[cluster, place * rhs : (place + 1) * rhs, :quarter] = source_ref[
+                at + cluster * rhs : at + (cluster + 1) * rhs, :
             ]
     back[...] = jnp.zeros(back.shape, jnp.float32)
     if first:
@@ -233,16 +233,16 @@
         pot_out_ref[...] = acc[:, rhs:width, :].astype(jnp.bfloat16)
 
 
-def run_step(step, length, items, sources, targets, locals_, rhs, width, carried, last):
+def run_step(step, length, items, source, targets, locals_, rhs, width, carried, last):
     lhss, augs = zip(*targets)
     clusters, _, row_count = augs[0].shape
     subs = len(targets)
     panels = subs * row_count
-    quarter = sources[0].shape[1]
+    quarter = source.shape[1]
     first = carried is None
     vmem = pl.BlockSpec(memory_space=pltpu.VMEM)
     smem = pl.BlockSpec(memory_space=pltpu.SMEM)
-    operands = (items, *sources, *lhss, *augs)
+    operands = (items, source, *lhss, *augs)
     if not first:
         operands += (carried,)
     acc_shape = (clusters, width + AUG, panels)
@@ -268,7 +268,7 @@
         out_shape = (jax.ShapeDtypeStruct(acc_shape, jnp.float32), back_shape)
     pairs = (length - 6) * panels * quarter
     return pl.pallas_call(
-        functools.partial(step_kernel, step, length, rhs, subs, len(sources), first, last),
+        functools.partial(step_kernel, step, length, rhs, subs, first, last),
         out_shape=out_shape,
         in_specs=[smem] + [vmem] * (len(operands) - 1),
         out_specs=(vmem,) * len(out_shape),
@@ -367,13 +367,18 @@
     ring = ring_order(clus_count)
     at_place = [ring.index(index) for index in range(clus_count)]
     ring_place = pick(device, at_place)
-    arrived = [round_ring(parts[0], 1)]
-    for step in range(1, rhs_count):
-
-        def goal(z, c, step=step):
-            return (ring[(at_place[z] + 1) % clus_count], c + step)
-
-        arrived.append(moved(parts[step], ("clus", "rhs"), goal))
+
+    def own_parts(parts, steps):
+        arrived = [round_ring(parts[0], steps)]
+        for step in range(1, rhs_count):
+
+            def goal(z, c, step=step):
+                return (ring[(at_place[z] + steps) % clus_count], c + step)
+
+            arrived.append(moved(parts[step], ("clus", "rhs"), goal))
+        return arrived
+
+    arrived = own_parts(parts, 1)
 
     per_round = 2 * ((clusters // 2 + clus_count - 2) // (clus_count - 1))
     cap = ROUNDS * per_round
@@ -426,17 +431,22 @@
     ]
 
     arrived, targets = lax.optimization_barrier((arrived, targets))
-    sources = arrived
+    source = jnp.concatenate(arrived, axis=0)
+    source, parts = lax.optimization_barrier((source, parts))
+    from_next = own_parts(parts, -1) if clus_count > 2 else None
     carried = None
     backs, jitter_rows = [], [None]
     for step in range(1, clus_count):
-        if step > 1:
+        if 1 < step < clus_count - 1:
             if step > 2:
-                sources, backs[step - 3] = lax.optimization_barrier((sources, backs[step - 3]))
-            sources = [round_ring(source, 1) for source in sources]
+                source, backs[step - 3] = lax.optimization_barrier((source, backs[step - 3]))
+            source = round_ring(source, 1)
+        elif step > 1:
+            from_next, backs[-1] = lax.optimization_barrier((from_next, backs[-1]))
+            source = jnp.concatenate(from_next, axis=0)
         last = step == clus_count - 1
         results = run_step(
-            step - 1, length, items, sources, targets, locals_, rhs, width, carried, last
+            step - 1, length, items, source, targets, locals_, rhs, width, carried, last
         )
         if last:
             pot, pot_out, grad, back = results
@@ -444,7 +454,7 @@
             carried, back = results
         backs.append(back)
         at = clusters * (rhs + 4)
-        jitter_rows.append(sources[0][at : at + clusters])
+        jitter_rows.append(source[at : at + clusters])
 
     grad = in_order([grad[..., at * row_count : (at + 1) * row_count] for at in range(sub_count)])
     low_part = (sub_place == 0) & (core == 0)

time: 61.5 us -> 59.5 us (0.967)
  starting transfers between devices: 19.9 us -> 18.3 us
    ppermute x8 -> x6, starting transfers between devices: 13.3 us -> 10.2 us  [round_ring(): return lax.ppermute(value, 'clus', pairs)]
    ppermute x1 -> x2, starting transfers between devices: 1.41 us -> 2.7 us  [moved(): return lax.ppermute(value, axes, pairs)]
    ppermute x7, waiting for transfers between devices: 8.75 us -> 7.76 us  [shifted(): return lax.ppermute(value, axis, pairs)]
    ppermute x8 -> x6, waiting for transfers between devices: 2.65 us -> 3.32 us  [round_ring(): return lax.ppermute(value, 'clus', pairs)]
  transfers between devices with their start and end apart: 16 -> 15, of which waited for: 8 -> 9; matrix products, arithmetic and copies ran while one was open for 2% -> 3% of each run, Pallas kernels for 28% -> 29%
where the time goes in v11:
time: 59.5 us; the launch traced here: 59.3 us
  Pallas kernels  26.7 us (45%)
  starting transfers between devices  18.3 us (31%)
  waiting for transfers between devices  11.1 us (19%)
  other arithmetic  1.23 us (2%)
  between operations  1.03 us (2%)
  local copies, waits for them, and re-layouts  0.91 us (2%)
    pallas_call x3, Pallas kernels, run_step(): pl.pallas_call(functools.partial(step_kernel, step, length, rhs, subs, fi...  22.7 us
    ppermute x6, starting transfers between devices, round_ring(): return lax.ppermute(value, 'clus', pairs)  10.2 us
    ppermute x7, waiting for transfers between devices, shifted(): return lax.ppermute(value, axis, pairs)  7.76 us
    ppermute x7, starting transfers between devices, shifted(): return lax.ppermute(value, axis, pairs)  5.45 us
    ppermute x6, waiting for transfers between devices, round_ring(): return lax.ppermute(value, 'clus', pairs)  3.32 us
    ppermute x2, starting transfers between devices, moved(): return lax.ppermute(value, axes, pairs)  2.7 us
    pallas_call x1, Pallas kernels, on_device(): pl.pallas_call(node_kernel, out_shape=jax.ShapeDtypeStruct((3, share * pa...  1.32 us
    pallas_call x1, Pallas kernels, on_device(): pl.pallas_call(functools.partial(prepare_kernel, (panels, nodes_total)),...  1.22 us
  transfers between devices with their start and end apart: 15, of which 9 were waited for; matrix products, arithmetic and copies ran while one was open for 3% of the time, Pallas kernels for 29%

profile of v11, /device:TPU:0, one launch (start us, length us, event | category | flops | bytes accessed | tf_op | source)
XLA Modules:
  0.0 59.3 jit_solution(15700071997846006228)
XLA Ops:
  0.6 0.0 copy-start
  0.6 1.2 %prepare.1 = (bf16[592,128]{1,0:T(8,128)(2,1)S(1)}, bf16[512,128]{1,0:T(8,128)(2,1)S(1)}, bf16[576,256]{1,0:T(8,128)(2,1)S(1)}) custom-call(bf16[16,32,256]{2,1,0:T(8,128)(2,1)} %refs_0_.1, bf16[3,16,256]{2,1,0:T(8,128)(2,1)} %bitcast.91, bf16[16,256]{1,0:T(8,128)(2,1)} %refs_2_.1, s32[16,4,256]{2,1,0:T(4,128)} %refs_3_.1, bf16[16,32,256]{2,1,0:T(8,128)(2,1)} %refs_4_.1), custom_call_target="tpu_custom_call" | custom-call | tf_op jit(solution)/shard_map/prepare/pallas_call | solution.py:357
  1.9 3.0 %collective-permute-start.3 = (bf16[576,256]{1,0:T(8,128)(2,1)S(1)}, bf16[576,256]{1,0:T(8,128)(2,1)S(1)}, u32[]{:S(2)}, u32[]{:S(2)}) collective-permute-start(bf16[576,256]{1,0:T(8,128)(2,1)S(1)} %get-tuple-element.33.refs_0_.refs_7_), channel_id=1, source_target_pairs={{0,2},{2,0},{1,3},{3,1},{4,6},{6,4},{5,7},{7,5},{8,10},{10,8},{9,1... | collective-permute-start | bytes 884744 | tf_op jit(solution)/shard_map/ppermute | solution.py:22
  4.9 0.0 collective-permute-start.2
  4.9 2.7 %collective-permute-start.1 = (bf16[512,128]{1,0:T(8,128)(2,1)S(1)}, bf16[512,128]{1,0:T(8,128)(2,1)S(1)}, u32[]{:S(2)}, u32[]{:S(2)}) collective-permute-start(bf16[512,128]{1,0:T(8,128)(2,1)S(1)} %get-tuple-element.41), channel_id=1, source_target_pairs={{0,9},{1,8},{4,1},{5,0},{8,13},{9,12},{12,5},{13,4},{2,11},{3,10},... | collective-permute-start | bytes 393224 | tf_op jit(solution)/shard_map/ppermute | solution.py:44
  7.6 1.6 %collective-permute-start = (bf16[592,128]{1,0:T(8,128)(2,1)S(1)}, bf16[592,128]{1,0:T(8,128)(2,1)S(1)}, u32[]{:S(2)}, u32[]{:S(2)}) collective-permute-start(bf16[592,128]{1,0:T(8,128)(2,1)S(1)} %get-tuple-element.40), channel_id=1, source_target_pairs={{0,8},{8,12},{12,4},{4,0},{1,9},{9,13},{13,5},{5,1},{2,10},{10,14}... | collective-permute-start | bytes 454664 | tf_op jit(solution)/shard_map/ppermute | solution.py:32
  9.2 0.0 copy-done
  9.2 0.1 constant_dynamic-slice_fusion
  9.2 0.1 reshape.294
  9.3 0.1 mul.22
  9.4 0.2 convert_reduce_fusion
  9.6 0.2 convert_reduce_fusion.1
  9.8 0.1 copy.34
  9.9 0.2 select_reduce_fusion
  10.1 1.8 %collective-permute-done.3.refs_0_.refs_8_ = bf16[576,256]{1,0:T(8,128)(2,1)S(1)} collective-permute-done((bf16[576,256]{1,0:T(8,128)(2,1)S(1)}, bf16[576,256]{1,0:T(8,128)(2,1)S(1)}, u32[]{:S(2)}, u32[]{:S(2)}) %collective-permute-start.3) | collective-permute-done | bytes 294944 | tf_op jit(solution)/shard_map/ppermute | solution.py:22
  11.9 0.0 collective-permute-start.4
  11.9 0.1 pad_slice_fusion
  12.0 0.1 pad_add_fusion
  12.0 0.1 reshape.295.refs_0_
  12.1 0.1 pad.40.clone
  12.2 0.0 collective-permute-done.2.refs_1_
  12.2 0.4 targets_0.1
  12.6 0.9 %collective-permute-done.4.refs_1_ = bf16[576,256]{1,0:T(8,128)(2,1)S(1)} collective-permute-done((bf16[576,256]{1,0:T(8,128)(2,1)S(1)}, bf16[576,256]{1,0:T(8,128)(2,1)S(1)}, u32[]{:S(2)}, u32[]{:S(2)}) %collective-permute-start.4) | collective-permute-done | bytes 294944 | tf_op jit(solution)/shard_map/ppermute | solution.py:22
  13.5 0.4 targets_1.1
  13.9 0.0 collective-permute-done.1
  13.9 0.2 collective-permute-done
  14.1 3.4 %collective-permute-start.7 = (bf16[1104,128]{1,0:T(8,128)(2,1)S(1)}, bf16[1104,128]{1,0:T(8,128)(2,1)S(1)}, u32[]{:S(2)}, u32[]{:S(2)}) collective-permute-start(bf16[1104,128]{1,0:T(8,128)(2,1)S(1)} %pad_maximum_fusion.refs_1_), channel_id=1, source_target_pairs={{0,8},{8,12},{12,4},{4,0},{1,9},{9,13},{13,5},{5,1},{2,10},{10,14}... | collective-permute-start | bytes 847880 | tf_op jit(solution)/shard_map/ppermute | solution.py:32
  17.5 0.0 collective-permute-start.6
  17.5 0.8 %collective-permute-start.5 = (bf16[592,128]{1,0:T(8,128)(2,1)S(1)}, bf16[592,128]{1,0:T(8,128)(2,1)S(1)}, u32[]{:S(2)}, u32[]{:S(2)}) collective-permute-start(bf16[592,128]{1,0:T(8,128)(2,1)S(1)} %get-tuple-element.40), channel_id=1, source_target_pairs={{0,4},{8,0},{12,8},{4,12},{1,5},{9,1},{13,9},{5,13},{2,6},{10,2},{... | collective-permute-start | bytes 454664 | tf_op jit(solution)/shard_map/ppermute | solution.py:32
  18.4 6.9 %near_field_0.1 = (f32[16,80,512]{2,1,0:T(8,128)S(1)}, f32[3,16,128]{2,1,0:T(8,128)S(1)}) custom-call(s32[108]{0:T(128)S(1)} %reshape.295.refs_0_, bf16[1104,128]{1,0:T(8,128)(2,1)S(1)} %pad_maximum_fusion.refs_1_, bf16[16,256,128]{2,1,0:T(8,128)(2,1)S(1)} %get-tuple-element.43.refs_2_, bf16[16,256,128]{2,1,0:T(8,128)(2,1)S(1)} %get-tuple-element.44.refs_3_, ...), custom_call_target="tpu_custom_call" | custom-call | flops 692060160 | bytes 6291456 | tf_op jit(solution)/shard_map/near_field_0/pallas_call | solution.py:270
  25.3 0.0 collective-permute-done.7.refs_1_
  25.3 8.3 %near_field_1.1 = (f32[16,80,512]{2,1,0:T(8,128)S(1)}, f32[3,16,128]{2,1,0:T(8,128)S(1)}) custom-call(s32[108]{0:T(128)S(1)} %reshape.295.refs_0_, bf16[1104,128]{1,0:T(8,128)(2,1)S(1)} %collective-permute-done.7.refs_1_, bf16[16,256,128]{2,1,0:T(8,128)(2,1)S(1)} %get-tuple-element.43.refs_2_, bf16[16,256,128]{2,1,0:T(8,128)(2,1)S(1)} %get-tuple-element.44.refs_3_, ...), custom_call_target="tpu_custom_call" | custom-call | flops 692060160 | bytes 6291456 | tf_op jit(solution)/shard_map/near_field_1/pallas_call | solution.py:270
  33.6 0.0 collective-permute-done.6
  33.6 0.0 collective-permute-done.5
  33.6 7.5 %near_field_2.1 = (f32[16,32,512]{2,1,0:T(8,128)S(1)}, bf16[16,32,512]{2,1,0:T(8,128)(2,1)S(1)}, f32[3,16,512]{2,1,0:T(8,128)S(1)}, f32[3,16,128]{2,1,0:T(8,128)S(1)}) custom-call(s32[108]{0:T(128)S(1)} %reshape.295.refs_0_, bf16[1104,128]{1,0:T(8,128)(2,1)S(1)} %pad_maximum_fusion.1.refs_1_, bf16[16,256,128]{2,1,0:T(8,128)(2,1)S(1)} %get-tuple-element.43.refs_2_, ...), custom_call_target="tpu_custom_call" | custom-call | flops 692060160 | bytes 6291456 | tf_op jit(solution)/shard_map/near_field_2/pallas_call | solution.py:270
  41.2 0.1 copy.38
  41.4 0.1 maximum_maximum_fusion
  41.4 1.5 %collective-permute-start.10 = (f32[56,128]{1,0:T(8,128)S(1)}, f32[56,128]{1,0:T(8,128)S(1)}, u32[]{:S(2)}, u32[]{:S(2)}) collective-permute-start(f32[56,128]{1,0:T(8,128)S(1)} %get-tuple-element.89), channel_id=1, source_target_pairs={{0,4},{8,0},{12,8},{4,12},{1,5},{9,1},{13,9},{5,13},{2,6},{10,2},{... | collective-permute-start | bytes 86024 | tf_op jit(solution)/shard_map/ppermute | solution.py:32
  43.0 2.3 %collective-permute-start.11 = (f32[56,128]{1,0:T(8,128)S(1)}, f32[56,128]{1,0:T(8,128)S(1)}, u32[]{:S(2)}, u32[]{:S(2)}) collective-permute-start(f32[56,128]{1,0:T(8,128)S(1)} %get-tuple-element.90), channel_id=1, source_target_pairs={{0,12},{8,4},{12,0},{4,8},{1,13},{9,5},{13,1},{5,9},{2,14},{10,6},... | collective-permute-start | bytes 86024 | tf_op jit(solution)/shard_map/ppermute | solution.py:32
  45.2 0.5 collective-permute-start.12
  45.8 0.2 collective-permute-start.8
  46.0 0.5 collective-permute-done.10
  46.5 2.5 %collective-permute-done.11 = f32[56,128]{1,0:T(8,128)S(1)} collective-permute-done((f32[56,128]{1,0:T(8,128)S(1)}, f32[56,128]{1,0:T(8,128)S(1)}, u32[]{:S(2)}, u32[]{:S(2)}) %collective-permute-start.11) | collective-permute-done | bytes 28704 | tf_op jit(solution)/shard_map/ppermute | solution.py:32
  49.0 0.2 collective-permute-done.12
  49.3 0.0 collective-permute-done.8
  49.3 0.2 convert_add_fusion
  49.8 1.0 %collective-permute-start.13 = (f32[4,8,512]{2,1,0:T(8,128)S(1)}, f32[4,8,512]{2,1,0:T(8,128)S(1)}, u32[]{:S(2)}, u32[]{:S(2)}) collective-permute-start(f32[4,8,512]{2,1,0:T(8,128)S(1)} %fusion), channel_id=1, source_target_pairs={{0,2},{2,0},{1,3},{3,1},{4,6},{6,4},{5,7},{7,5},{8,10},{10,8},{9,1... | collective-permute-start | bytes 196616 | tf_op jit(solution)/shard_map/ppermute | solution.py:22
  50.8 1.1 %collective-permute-start.9 = (bf16[16,32,256]{2,1,0:T(8,128)(2,1)S(1)}, bf16[16,32,256]{2,1,0:T(8,128)(2,1)S(1)}, u32[]{:S(2)}, u32[]{:S(2)}) collective-permute-start(bf16[16,32,256]{2,1,0:T(8,128)(2,1)S(1)} %slice.307), channel_id=1, source_target_pairs={{0,2},{2,0},{1,3},{3,1},{4,6},{6,4},{5,7},{7,5},{8,10},{10,8},{9,1... | collective-permute-start | bytes 786440 | tf_op jit(solution)/shard_map/ppermute | solution.py:22
  52.0 2.8 %collective-permute-done.13 = f32[4,8,512]{2,1,0:T(8,128)S(1)} collective-permute-done((f32[4,8,512]{2,1,0:T(8,128)S(1)}, f32[4,8,512]{2,1,0:T(8,128)S(1)}, u32[]{:S(2)}, u32[]{:S(2)}) %collective-permute-start.13) | collective-permute-done | bytes 65568 | tf_op jit(solution)/shard_map/ppermute | solution.py:22
  54.8 0.1 collective-permute-start.14
  55.0 1.2 %collective-permute-done.14 = f32[4,8,512]{2,1,0:T(8,128)S(1)} collective-permute-done((f32[4,8,512]{2,1,0:T(8,128)S(1)}, f32[4,8,512]{2,1,0:T(8,128)S(1)}, u32[]{:S(2)}, u32[]{:S(2)}) %collective-permute-start.14) | collective-permute-done | bytes 65568 | tf_op jit(solution)/shard_map/ppermute | solution.py:22
  56.2 1.3 %node_terms.1 = f32[3,4096]{1,0:T(4,128)} custom-call(f32[3,8,512]{2,1,0:T(8,128)S(1)} %slice.197.grad_ref, s32[8,512]{1,0:T(8,128)S(1)} %slice_select_fusion.2.jitter_ref, f32[8,512]{1,0:T(8,128)S(1)} %slice_bitcast_fusion.edge_ref), custom_call_target="tpu_custom_call" | custom-call | flops 1048576 | bytes 262144 | tf_op jit(solution)/shard_map/node_terms/pallas_call | solution.py:549
  57.5 1.1 %collective-permute-done.9.refs_1_ = bf16[16,32,256]{2,1,0:T(8,128)(2,1)S(1)} collective-permute-done((bf16[16,32,256]{2,1,0:T(8,128)(2,1)S(1)}, bf16[16,32,256]{2,1,0:T(8,128)(2,1)S(1)}, u32[]{:S(2)}, u32[]{:S(2)}) %collective-permute-start.9) | collective-permute-done | bytes 262176 | tf_op jit(solution)/shard_map/ppermute | solution.py:22
  58.6 0.7 %potential_sum.1 = bf16[16,32,256]{2,1,0:T(8,128)(2,1)} custom-call(f32[16,32,256]{2,1,0:T(8,128)S(1)} %slice.127.refs_0_, bf16[16,32,256]{2,1,0:T(8,128)(2,1)S(1)} %collective-permute-done.9.refs_1_), custom_call_target="tpu_custom_call" | custom-call | flops 1048576 | bytes 262144 | tf_op jit(solution)/shard_map/potential_sum/pallas_call | solution.py:558
  (47 shorter events, 0.6 us)
Async XLA Ops:
  0.6 8.5 %copy-start = (s32[5,64]{1,0:T(8,128)S(1)}, s32[5,64]{1,0:T(8,128)}, u32[]{:S(2)}) copy-start(s32[5,64]{1,0:T(8,128)} %param.10) | copy-start | bytes 3844
  1.9 10.0 %collective-permute-start.3 = (bf16[576,256]{1,0:T(8,128)(2,1)S(1)}, bf16[576,256]{1,0:T(8,128)(2,1)S(1)}, u32[]{:S(2)}, u32[]{:S(2)}) collective-permute-start(bf16[576,256]{1,0:T(8,128)(2,1)S(1)} %get-tuple-element.33.refs_0_.refs_7_), channel_id=1, source_target_pairs={{0,2},{2,0},{1,3},{3,1},{4,6},{6,4},{5,7},{7,5},{8,10},{10,8},{9,1... | collective-permute-start | bytes 884744 | tf_op jit(solution)/shard_map/ppermute | solution.py:22
  4.9 7.3 %collective-permute-start.2 = (bf16[576,256]{1,0:T(8,128)(2,1)S(1)}, bf16[576,256]{1,0:T(8,128)(2,1)S(1)}, u32[]{:S(2)}, u32[]{:S(2)}) collective-permute-start(bf16[576,256]{1,0:T(8,128)(2,1)S(1)} %get-tuple-element.33.refs_0_.refs_7_), channel_id=1, source_target_pairs={{0,1},{1,0},{2,3},{3,2},{4,5},{5,4},{6,7},{7,6},{8,9},{9,8},{10,11... | collective-permute-start | bytes 884744 | tf_op jit(solution)/shard_map/ppermute | solution.py:22
  4.9 9.0 %collective-permute-start.1 = (bf16[512,128]{1,0:T(8,128)(2,1)S(1)}, bf16[512,128]{1,0:T(8,128)(2,1)S(1)}, u32[]{:S(2)}, u32[]{:S(2)}) collective-permute-start(bf16[512,128]{1,0:T(8,128)(2,1)S(1)} %get-tuple-element.41), channel_id=1, source_target_pairs={{0,9},{1,8},{4,1},{5,0},{8,13},{9,12},{12,5},{13,4},{2,11},{3,10},... | collective-permute-start | bytes 393224 | tf_op jit(solution)/shard_map/ppermute | solution.py:44
  7.6 6.5 %collective-permute-start = (bf16[592,128]{1,0:T(8,128)(2,1)S(1)}, bf16[592,128]{1,0:T(8,128)(2,1)S(1)}, u32[]{:S(2)}, u32[]{:S(2)}) collective-permute-start(bf16[592,128]{1,0:T(8,128)(2,1)S(1)} %get-tuple-element.40), channel_id=1, source_target_pairs={{0,8},{8,12},{12,4},{4,0},{1,9},{9,13},{13,5},{5,1},{2,10},{10,14}... | collective-permute-start | bytes 454664 | tf_op jit(solution)/shard_map/ppermute | solution.py:32
  11.9 1.6 %collective-permute-start.4 = (bf16[576,256]{1,0:T(8,128)(2,1)S(1)}, bf16[576,256]{1,0:T(8,128)(2,1)S(1)}, u32[]{:S(2)}, u32[]{:S(2)}) collective-permute-start(bf16[576,256]{1,0:T(8,128)(2,1)S(1)} %collective-permute-done.3.refs_0_.refs_8_), channel_id=1, source_target_pairs={{0,1},{1,0},{2,3},{3,2},{4,5},{5,4},{6,7},{7,6},{8,9},{9,8},{10,11... | collective-permute-start | bytes 884744 | tf_op jit(solution)/shard_map/ppermute | solution.py:22
  14.1 11.2 %collective-permute-start.7 = (bf16[1104,128]{1,0:T(8,128)(2,1)S(1)}, bf16[1104,128]{1,0:T(8,128)(2,1)S(1)}, u32[]{:S(2)}, u32[]{:S(2)}) collective-permute-start(bf16[1104,128]{1,0:T(8,128)(2,1)S(1)} %pad_maximum_fusion.refs_1_), channel_id=1, source_target_pairs={{0,8},{8,12},{12,4},{4,0},{1,9},{9,13},{13,5},{5,1},{2,10},{10,14}... | collective-permute-start | bytes 847880 | tf_op jit(solution)/shard_map/ppermute | solution.py:32
  17.5 16.1 %collective-permute-start.6 = (bf16[512,128]{1,0:T(8,128)(2,1)S(1)}, bf16[512,128]{1,0:T(8,128)(2,1)S(1)}, u32[]{:S(2)}, u32[]{:S(2)}) collective-permute-start(bf16[512,128]{1,0:T(8,128)(2,1)S(1)} %get-tuple-element.41), channel_id=1, source_target_pairs={{0,5},{1,4},{4,13},{5,12},{8,1},{9,0},{12,9},{13,8},{2,7},{3,6},{6... | collective-permute-start | bytes 393224 | tf_op jit(solution)/shard_map/ppermute | solution.py:44
  17.5 16.1 %collective-permute-start.5 = (bf16[592,128]{1,0:T(8,128)(2,1)S(1)}, bf16[592,128]{1,0:T(8,128)(2,1)S(1)}, u32[]{:S(2)}, u32[]{:S(2)}) collective-permute-start(bf16[592,128]{1,0:T(8,128)(2,1)S(1)} %get-tuple-element.40), channel_id=1, source_target_pairs={{0,4},{8,0},{12,8},{4,12},{1,5},{9,1},{13,9},{5,13},{2,6},{10,2},{... | collective-permute-start | bytes 454664 | tf_op jit(solution)/shard_map/ppermute | solution.py:32
  41.4 5.1 %collective-permute-start.10 = (f32[56,128]{1,0:T(8,128)S(1)}, f32[56,128]{1,0:T(8,128)S(1)}, u32[]{:S(2)}, u32[]{:S(2)}) collective-permute-start(f32[56,128]{1,0:T(8,128)S(1)} %get-tuple-element.89), channel_id=1, source_target_pairs={{0,4},{8,0},{12,8},{4,12},{1,5},{9,1},{13,9},{5,13},{2,6},{10,2},{... | collective-permute-start | bytes 86024 | tf_op jit(solution)/shard_map/ppermute | solution.py:32
  43.0 6.0 %collective-permute-start.11 = (f32[56,128]{1,0:T(8,128)S(1)}, f32[56,128]{1,0:T(8,128)S(1)}, u32[]{:S(2)}, u32[]{:S(2)}) collective-permute-start(f32[56,128]{1,0:T(8,128)S(1)} %get-tuple-element.90), channel_id=1, source_target_pairs={{0,12},{8,4},{12,0},{4,8},{1,13},{9,5},{13,1},{5,9},{2,14},{10,6},... | collective-permute-start | bytes 86024 | tf_op jit(solution)/shard_map/ppermute | solution.py:32
  45.2 3.9 %collective-permute-start.12 = (f32[56,128]{1,0:T(8,128)S(1)}, f32[56,128]{1,0:T(8,128)S(1)}, u32[]{:S(2)}, u32[]{:S(2)}) collective-permute-start(f32[56,128]{1,0:T(8,128)S(1)} %get-tuple-element.91), channel_id=1, source_target_pairs={{0,8},{8,12},{12,4},{4,0},{1,9},{9,13},{13,5},{5,1},{2,10},{10,14}... | collective-permute-start | bytes 86024 | tf_op jit(solution)/shard_map/ppermute | solution.py:32
  45.8 3.5 %collective-permute-start.8 = (bf16[16,32,512]{2,1,0:T(8,128)(2,1)S(1)}, bf16[16,32,512]{2,1,0:T(8,128)(2,1)S(1)}, u32[]{:S(2)}, u32[]{:S(2)}) collective-permute-start(bf16[16,32,512]{2,1,0:T(8,128)(2,1)S(1)} %get-tuple-element.53), channel_id=1, source_target_pairs={{0,1},{1,0},{2,3},{3,2},{4,5},{5,4},{6,7},{7,6},{8,9},{9,8},{10,11... | collective-permute-start | bytes 1572872 | tf_op jit(solution)/shard_map/ppermute | solution.py:22
  49.8 5.0 %collective-permute-start.13 = (f32[4,8,512]{2,1,0:T(8,128)S(1)}, f32[4,8,512]{2,1,0:T(8,128)S(1)}, u32[]{:S(2)}, u32[]{:S(2)}) collective-permute-start(f32[4,8,512]{2,1,0:T(8,128)S(1)} %fusion), channel_id=1, source_target_pairs={{0,2},{2,0},{1,3},{3,1},{4,6},{6,4},{5,7},{7,5},{8,10},{10,8},{9,1... | collective-permute-start | bytes 196616 | tf_op jit(solution)/shard_map/ppermute | solution.py:22
  50.8 7.7 %collective-permute-start.9 = (bf16[16,32,256]{2,1,0:T(8,128)(2,1)S(1)}, bf16[16,32,256]{2,1,0:T(8,128)(2,1)S(1)}, u32[]{:S(2)}, u32[]{:S(2)}) collective-permute-start(bf16[16,32,256]{2,1,0:T(8,128)(2,1)S(1)} %slice.307), channel_id=1, source_target_pairs={{0,2},{2,0},{1,3},{3,1},{4,6},{6,4},{5,7},{7,5},{8,10},{10,8},{9,1... | collective-permute-start | bytes 786440 | tf_op jit(solution)/shard_map/ppermute | solution.py:22
  54.8 1.3 %collective-permute-start.14 = (f32[4,8,512]{2,1,0:T(8,128)S(1)}, f32[4,8,512]{2,1,0:T(8,128)S(1)}, u32[]{:S(2)}, u32[]{:S(2)}) collective-permute-start(f32[4,8,512]{2,1,0:T(8,128)S(1)} %select_add_fusion), channel_id=1, source_target_pairs={{0,1},{1,0},{2,3},{3,2},{4,5},{5,4},{6,7},{7,6},{8,9},{9,8},{10,11... | collective-permute-start | bytes 196616 | tf_op jit(solution)/shard_map/ppermute | solution.py:22

commit v12 on v11

--- a/solution.py
+++ b/solution.py
@@ -142,7 +142,7 @@
     else:
         acc, back_ref = refs[:2]
         refs = refs[2:]
-    aug32, left, weight, back, raw_a, raw_b, both_a, both_b = refs
+    aug32, left, weight, back, both_a, both_b = refs
     clusters, rows, panels = acc.shape
     width = rows - AUG
     row_count = panels // subs
@@ -175,22 +175,18 @@
         acc[...] = jnp.zeros(acc.shape, jnp.float32)
     else:
         acc[...] = acc_in[...]
-    raw_b[...] = jnp.ones(raw_b.shape, jnp.float32)
     both_a[...] = jnp.zeros(both_a.shape, both_a.dtype)
 
     def decoded(place):
         code = items[step * length + place]
         return code // (2 * clusters), code % (2 * clusters)
 
-    def products(place, raw):
+    def formed(place, both):
         here, mate = decoded(place)
+        scale = weight[pl.ds(mate, 1), :]
         mate = mate % clusters
         lhs = jnp.concatenate([ref[here] for ref in lhs_refs], axis=0)
-        raw[...] = jnp.dot(lhs, left[mate], preferred_element_type=jnp.float32)
-
-    def pointwise(place, raw, both):
-        _, mate = decoded(place)
-        scale = weight[pl.ds(mate, 1), :]
+        raw = jnp.dot(lhs, left[mate], preferred_element_type=jnp.float32)
         for start in range(0, panels, LANES):
             span = slice(start, start + LANES)
             inverse = lax.rsqrt(raw[span, quarter:])
@@ -215,11 +211,9 @@
     def _(pair):
         turn = 2 * pair + 1
         summed(turn, both_a)
-        pointwise(turn + 1, raw_b, both_b)
-        products(turn + 2, raw_a)
+        formed(turn + 1, both_b)
         summed(turn + 1, both_b)
-        pointwise(turn + 2, raw_a, both_a)
-        products(turn + 3, raw_b)
+        formed(turn + 2, both_a)
 
     for coord in range(3):
         back_ref[coord] = -0.5 * back[:, coord, :] - there[coord] * back[:, 6, :]
@@ -253,7 +247,6 @@
         pltpu.VMEM((clusters + 8, quarter), jnp.float32),
         pltpu.VMEM((clusters, AUG, quarter), jnp.float32),
     ]
-    scratch += [pltpu.VMEM((panels, 2 * quarter), jnp.float32)] * 2
     scratch += [pltpu.VMEM((panels, 2 * quarter), jnp.bfloat16)] * 2
     if last:
         operands += tuple(locals_)
@@ -397,9 +390,9 @@
     slots = jnp.arange(cap, dtype=jnp.int32)
     chosen = member[:, None, :] & (rank[None, None, :] == slots[None, :, None])
     listed = jnp.sum(jnp.where(chosen, code[None, None, :] - clusters, 0), axis=2) + clusters
-    turns = (jnp.sum(member.astype(jnp.int32), axis=1) + 3) // 2
+    turns = (jnp.sum(member.astype(jnp.int32), axis=1) + 2) // 2
     length = cap + 6
-    items = jnp.pad(listed, ((0, 0), (3, 3)), constant_values=clusters)
+    items = jnp.pad(listed, ((0, 0), (2, 4)), constant_values=clusters)
     items = jnp.concatenate([turns[:, None], items[:, 1:]], axis=1).reshape(-1)
 
     locals_ = [local] + [shifted(local, "sub", step) for step in range(1, sub_count)]

time: 59.5 us -> 66.2 us (1.11)
  Pallas kernels: 26.7 us -> 33.4 us
    pallas_call x3, Pallas kernels: 22.7 us -> 29.4 us  [run_step(): pl.pallas_call(functools.partial(step_kernel, step, length, rhs, subs, fi...]
  transfers between devices with their start and end apart: 15 -> 15, of which waited for: 9 -> 9; matrix products, arithmetic and copies ran while one was open for 3% -> 2% of each run, Pallas kernels for 29% -> 33%
where the time goes in v12:
time: 66.2 us; the launch traced here: 66 us
  Pallas kernels  33.4 us (50%)
  starting transfers between devices  18.4 us (28%)
  waiting for transfers between devices  11.1 us (17%)
  other arithmetic  1.23 us (2%)
  between operations  1.03 us (2%)
  local copies, waits for them, and re-layouts  0.91 us (1%)
    pallas_call x3, Pallas kernels, run_step(): pl.pallas_call(functools.partial(step_kernel, step, length, rhs, subs, fi...  29.4 us
    ppermute x6, starting transfers between devices, round_ring(): return lax.ppermute(value, 'clus', pairs)  10.2 us
    ppermute x7, waiting for transfers between devices, shifted(): return lax.ppermute(value, axis, pairs)  7.87 us
    ppermute x7, starting transfers between devices, shifted(): return lax.ppermute(value, axis, pairs)  5.44 us
    ppermute x6, waiting for transfers between devices, round_ring(): return lax.ppermute(value, 'clus', pairs)  3.2 us
    ppermute x2, starting transfers between devices, moved(): return lax.ppermute(value, axes, pairs)  2.7 us
  transfers between devices with their start and end apart: 15, of which 9 were waited for; matrix products, arithmetic and copies ran while one was open for 2% of the time, Pallas kernels for 33%

profile of v12, /device:TPU:0, one launch (start us, length us, event | category | flops | bytes accessed | tf_op | source)
XLA Modules:
  0.0 66.0 jit_solution(9973095780347882709)
XLA Ops:
  0.6 0.0 copy-start
  0.6 1.2 %prepare.1 = (bf16[592,128]{1,0:T(8,128)(2,1)S(1)}, bf16[512,128]{1,0:T(8,128)(2,1)S(1)}, bf16[576,256]{1,0:T(8,128)(2,1)S(1)}) custom-call(bf16[16,32,256]{2,1,0:T(8,128)(2,1)} %refs_0_.1, bf16[3,16,256]{2,1,0:T(8,128)(2,1)} %bitcast.91, bf16[16,256]{1,0:T(8,128)(2,1)} %refs_2_.1, s32[16,4,256]{2,1,0:T(4,128)} %refs_3_.1, bf16[16,32,256]{2,1,0:T(8,128)(2,1)} %refs_4_.1), custom_call_target="tpu_custom_call" | custom-call | tf_op jit(solution)/shard_map/prepare/pallas_call | solution.py:350
  1.9 3.0 %collective-permute-start.3 = (bf16[576,256]{1,0:T(8,128)(2,1)S(1)}, bf16[576,256]{1,0:T(8,128)(2,1)S(1)}, u32[]{:S(2)}, u32[]{:S(2)}) collective-permute-start(bf16[576,256]{1,0:T(8,128)(2,1)S(1)} %get-tuple-element.33.refs_0_.refs_7_), channel_id=1, source_target_pairs={{0,2},{2,0},{1,3},{3,1},{4,6},{6,4},{5,7},{7,5},{8,10},{10,8},{9,1... | collective-permute-start | bytes 884744 | tf_op jit(solution)/shard_map/ppermute | solution.py:22
  4.9 0.0 collective-permute-start.2
  4.9 2.7 %collective-permute-start.1 = (bf16[512,128]{1,0:T(8,128)(2,1)S(1)}, bf16[512,128]{1,0:T(8,128)(2,1)S(1)}, u32[]{:S(2)}, u32[]{:S(2)}) collective-permute-start(bf16[512,128]{1,0:T(8,128)(2,1)S(1)} %get-tuple-element.41), channel_id=1, source_target_pairs={{0,9},{1,8},{4,1},{5,0},{8,13},{9,12},{12,5},{13,4},{2,11},{3,10},... | collective-permute-start | bytes 393224 | tf_op jit(solution)/shard_map/ppermute | solution.py:44
  7.6 1.6 %collective-permute-start = (bf16[592,128]{1,0:T(8,128)(2,1)S(1)}, bf16[592,128]{1,0:T(8,128)(2,1)S(1)}, u32[]{:S(2)}, u32[]{:S(2)}) collective-permute-start(bf16[592,128]{1,0:T(8,128)(2,1)S(1)} %get-tuple-element.40), channel_id=1, source_target_pairs={{0,8},{8,12},{12,4},{4,0},{1,9},{9,13},{13,5},{5,1},{2,10},{10,14}... | collective-permute-start | bytes 454664 | tf_op jit(solution)/shard_map/ppermute | solution.py:32
  9.2 0.0 copy-done
  9.2 0.1 constant_dynamic-slice_fusion
  9.2 0.1 reshape.294
  9.3 0.1 mul.22
  9.4 0.2 convert_reduce_fusion
  9.6 0.2 convert_reduce_fusion.1
  9.8 0.1 copy.34
  9.9 0.2 select_reduce_fusion
  10.1 1.8 %collective-permute-done.3.refs_0_.refs_8_ = bf16[576,256]{1,0:T(8,128)(2,1)S(1)} collective-permute-done((bf16[576,256]{1,0:T(8,128)(2,1)S(1)}, bf16[576,256]{1,0:T(8,128)(2,1)S(1)}, u32[]{:S(2)}, u32[]{:S(2)}) %collective-permute-start.3) | collective-permute-done | bytes 294944 | tf_op jit(solution)/shard_map/ppermute | solution.py:22
  11.9 0.0 collective-permute-start.4
  11.9 0.1 pad_slice_fusion
  12.0 0.1 pad_add_fusion
  12.0 0.1 reshape.295.refs_0_
  12.1 0.1 pad.40.clone
  12.2 0.0 collective-permute-done.2.refs_1_
  12.2 0.4 targets_0.1
  12.6 0.9 %collective-permute-done.4.refs_1_ = bf16[576,256]{1,0:T(8,128)(2,1)S(1)} collective-permute-done((bf16[576,256]{1,0:T(8,128)(2,1)S(1)}, bf16[576,256]{1,0:T(8,128)(2,1)S(1)}, u32[]{:S(2)}, u32[]{:S(2)}) %collective-permute-start.4) | collective-permute-done | bytes 294944 | tf_op jit(solution)/shard_map/ppermute | solution.py:22
  13.5 0.4 targets_1.1
  13.9 0.0 collective-permute-done.1
  13.9 0.2 collective-permute-done
  14.1 3.4 %collective-permute-start.7 = (bf16[1104,128]{1,0:T(8,128)(2,1)S(1)}, bf16[1104,128]{1,0:T(8,128)(2,1)S(1)}, u32[]{:S(2)}, u32[]{:S(2)}) collective-permute-start(bf16[1104,128]{1,0:T(8,128)(2,1)S(1)} %pad_maximum_fusion.refs_1_), channel_id=1, source_target_pairs={{0,8},{8,12},{12,4},{4,0},{1,9},{9,13},{13,5},{5,1},{2,10},{10,14}... | collective-permute-start | bytes 847880 | tf_op jit(solution)/shard_map/ppermute | solution.py:32
  17.5 0.0 collective-permute-start.6
  17.5 0.8 %collective-permute-start.5 = (bf16[592,128]{1,0:T(8,128)(2,1)S(1)}, bf16[592,128]{1,0:T(8,128)(2,1)S(1)}, u32[]{:S(2)}, u32[]{:S(2)}) collective-permute-start(bf16[592,128]{1,0:T(8,128)(2,1)S(1)} %get-tuple-element.40), channel_id=1, source_target_pairs={{0,4},{8,0},{12,8},{4,12},{1,5},{9,1},{13,9},{5,13},{2,6},{10,2},{... | collective-permute-start | bytes 454664 | tf_op jit(solution)/shard_map/ppermute | solution.py:32
  18.4 10.1 %near_field_0.1 = (f32[16,80,512]{2,1,0:T(8,128)S(1)}, f32[3,16,128]{2,1,0:T(8,128)S(1)}) custom-call(s32[108]{0:T(128)S(1)} %reshape.295.refs_0_, bf16[1104,128]{1,0:T(8,128)(2,1)S(1)} %pad_maximum_fusion.refs_1_, bf16[16,256,128]{2,1,0:T(8,128)(2,1)S(1)} %get-tuple-element.43.refs_2_, bf16[16,256,128]{2,1,0:T(8,128)(2,1)S(1)} %get-tuple-element.44.refs_3_, ...), custom_call_target="tpu_custom_call" | custom-call | flops 692060160 | bytes 6291456 | tf_op jit(solution)/shard_map/near_field_0/pallas_call | solution.py:263
  28.5 0.0 collective-permute-done.7.refs_1_
  28.5 9.5 %near_field_1.1 = (f32[16,80,512]{2,1,0:T(8,128)S(1)}, f32[3,16,128]{2,1,0:T(8,128)S(1)}) custom-call(s32[108]{0:T(128)S(1)} %reshape.295.refs_0_, bf16[1104,128]{1,0:T(8,128)(2,1)S(1)} %collective-permute-done.7.refs_1_, bf16[16,256,128]{2,1,0:T(8,128)(2,1)S(1)} %get-tuple-element.43.refs_2_, bf16[16,256,128]{2,1,0:T(8,128)(2,1)S(1)} %get-tuple-element.44.refs_3_, ...), custom_call_target="tpu_custom_call" | custom-call | flops 692060160 | bytes 6291456 | tf_op jit(solution)/shard_map/near_field_1/pallas_call | solution.py:263
  38.1 0.0 collective-permute-done.6
  38.1 0.0 collective-permute-done.5
  38.1 9.7 %near_field_2.1 = (f32[16,32,512]{2,1,0:T(8,128)S(1)}, bf16[16,32,512]{2,1,0:T(8,128)(2,1)S(1)}, f32[3,16,512]{2,1,0:T(8,128)S(1)}, f32[3,16,128]{2,1,0:T(8,128)S(1)}) custom-call(s32[108]{0:T(128)S(1)} %reshape.295.refs_0_, bf16[1104,128]{1,0:T(8,128)(2,1)S(1)} %pad_maximum_fusion.1.refs_1_, bf16[16,256,128]{2,1,0:T(8,128)(2,1)S(1)} %get-tuple-element.43.refs_2_, ...), custom_call_target="tpu_custom_call" | custom-call | flops 692060160 | bytes 6291456 | tf_op jit(solution)/shard_map/near_field_2/pallas_call | solution.py:263
  47.9 0.1 copy.38
  48.1 0.1 maximum_maximum_fusion
  48.1 1.6 %collective-permute-start.10 = (f32[56,128]{1,0:T(8,128)S(1)}, f32[56,128]{1,0:T(8,128)S(1)}, u32[]{:S(2)}, u32[]{:S(2)}) collective-permute-start(f32[56,128]{1,0:T(8,128)S(1)} %get-tuple-element.89), channel_id=1, source_target_pairs={{0,4},{8,0},{12,8},{4,12},{1,5},{9,1},{13,9},{5,13},{2,6},{10,2},{... | collective-permute-start | bytes 86024 | tf_op jit(solution)/shard_map/ppermute | solution.py:32
  49.7 2.0 %collective-permute-start.11 = (f32[56,128]{1,0:T(8,128)S(1)}, f32[56,128]{1,0:T(8,128)S(1)}, u32[]{:S(2)}, u32[]{:S(2)}) collective-permute-start(f32[56,128]{1,0:T(8,128)S(1)} %get-tuple-element.90), channel_id=1, source_target_pairs={{0,12},{8,4},{12,0},{4,8},{1,13},{9,5},{13,1},{5,9},{2,14},{10,6},... | collective-permute-start | bytes 86024 | tf_op jit(solution)/shard_map/ppermute | solution.py:32
  51.8 0.8 %collective-permute-start.12 = (f32[56,128]{1,0:T(8,128)S(1)}, f32[56,128]{1,0:T(8,128)S(1)}, u32[]{:S(2)}, u32[]{:S(2)}) collective-permute-start(f32[56,128]{1,0:T(8,128)S(1)} %get-tuple-element.91), channel_id=1, source_target_pairs={{0,8},{8,12},{12,4},{4,0},{1,9},{9,13},{13,5},{5,1},{2,10},{10,14}... | collective-permute-start | bytes 86024 | tf_op jit(solution)/shard_map/ppermute | solution.py:32
  52.5 0.2 collective-permute-start.8
  52.8 0.5 collective-permute-done.10
  53.2 2.5 %collective-permute-done.11 = f32[56,128]{1,0:T(8,128)S(1)} collective-permute-done((f32[56,128]{1,0:T(8,128)S(1)}, f32[56,128]{1,0:T(8,128)S(1)}, u32[]{:S(2)}, u32[]{:S(2)}) %collective-permute-start.11) | collective-permute-done | bytes 28704 | tf_op jit(solution)/shard_map/ppermute | solution.py:32
  55.7 0.1 collective-permute-done.12
  56.0 0.0 collective-permute-done.8
  56.0 0.2 convert_add_fusion
  56.4 1.1 %collective-permute-start.13 = (f32[4,8,512]{2,1,0:T(8,128)S(1)}, f32[4,8,512]{2,1,0:T(8,128)S(1)}, u32[]{:S(2)}, u32[]{:S(2)}) collective-permute-start(f32[4,8,512]{2,1,0:T(8,128)S(1)} %fusion), channel_id=1, source_target_pairs={{0,2},{2,0},{1,3},{3,1},{4,6},{6,4},{5,7},{7,5},{8,10},{10,8},{9,1... | collective-permute-start | bytes 196616 | tf_op jit(solution)/shard_map/ppermute | solution.py:22
  57.6 1.0 %collective-permute-start.9 = (bf16[16,32,256]{2,1,0:T(8,128)(2,1)S(1)}, bf16[16,32,256]{2,1,0:T(8,128)(2,1)S(1)}, u32[]{:S(2)}, u32[]{:S(2)}) collective-permute-start(bf16[16,32,256]{2,1,0:T(8,128)(2,1)S(1)} %slice.307), channel_id=1, source_target_pairs={{0,2},{2,0},{1,3},{3,1},{4,6},{6,4},{5,7},{7,5},{8,10},{10,8},{9,1... | collective-permute-start | bytes 786440 | tf_op jit(solution)/shard_map/ppermute | solution.py:22
  58.6 2.8 %collective-permute-done.13 = f32[4,8,512]{2,1,0:T(8,128)S(1)} collective-permute-done((f32[4,8,512]{2,1,0:T(8,128)S(1)}, f32[4,8,512]{2,1,0:T(8,128)S(1)}, u32[]{:S(2)}, u32[]{:S(2)}) %collective-permute-start.13) | collective-permute-done | bytes 65568 | tf_op jit(solution)/shard_map/ppermute | solution.py:22
  61.4 0.1 collective-permute-start.14
  61.6 1.2 %collective-permute-done.14 = f32[4,8,512]{2,1,0:T(8,128)S(1)} collective-permute-done((f32[4,8,512]{2,1,0:T(8,128)S(1)}, f32[4,8,512]{2,1,0:T(8,128)S(1)}, u32[]{:S(2)}, u32[]{:S(2)}) %collective-permute-start.14) | collective-permute-done | bytes 65568 | tf_op jit(solution)/shard_map/ppermute | solution.py:22
  62.8 1.3 %node_terms.1 = f32[3,4096]{1,0:T(4,128)} custom-call(f32[3,8,512]{2,1,0:T(8,128)S(1)} %slice.197.grad_ref, s32[8,512]{1,0:T(8,128)S(1)} %slice_select_fusion.2.jitter_ref, f32[8,512]{1,0:T(8,128)S(1)} %slice_bitcast_fusion.edge_ref), custom_call_target="tpu_custom_call" | custom-call | flops 1048576 | bytes 262144 | tf_op jit(solution)/shard_map/node_terms/pallas_call | solution.py:542
  64.1 1.2 %collective-permute-done.9.refs_1_ = bf16[16,32,256]{2,1,0:T(8,128)(2,1)S(1)} collective-permute-done((bf16[16,32,256]{2,1,0:T(8,128)(2,1)S(1)}, bf16[16,32,256]{2,1,0:T(8,128)(2,1)S(1)}, u32[]{:S(2)}, u32[]{:S(2)}) %collective-permute-start.9) | collective-permute-done | bytes 262176 | tf_op jit(solution)/shard_map/ppermute | solution.py:22
  65.3 0.7 %potential_sum.1 = bf16[16,32,256]{2,1,0:T(8,128)(2,1)} custom-call(f32[16,32,256]{2,1,0:T(8,128)S(1)} %slice.127.refs_0_, bf16[16,32,256]{2,1,0:T(8,128)(2,1)S(1)} %collective-permute-done.9.refs_1_), custom_call_target="tpu_custom_call" | custom-call | flops 1048576 | bytes 262144 | tf_op jit(solution)/shard_map/potential_sum/pallas_call | solution.py:551
  (47 shorter events, 0.6 us)
Async XLA Ops:
  0.6 8.5 %copy-start = (s32[5,64]{1,0:T(8,128)S(1)}, s32[5,64]{1,0:T(8,128)}, u32[]{:S(2)}) copy-start(s32[5,64]{1,0:T(8,128)} %param.10) | copy-start | bytes 3844
  1.9 10.0 %collective-permute-start.3 = (bf16[576,256]{1,0:T(8,128)(2,1)S(1)}, bf16[576,256]{1,0:T(8,128)(2,1)S(1)}, u32[]{:S(2)}, u32[]{:S(2)}) collective-permute-start(bf16[576,256]{1,0:T(8,128)(2,1)S(1)} %get-tuple-element.33.refs_0_.refs_7_), channel_id=1, source_target_pairs={{0,2},{2,0},{1,3},{3,1},{4,6},{6,4},{5,7},{7,5},{8,10},{10,8},{9,1... | collective-permute-start | bytes 884744 | tf_op jit(solution)/shard_map/ppermute | solution.py:22
  4.9 7.3 %collective-permute-start.2 = (bf16[576,256]{1,0:T(8,128)(2,1)S(1)}, bf16[576,256]{1,0:T(8,128)(2,1)S(1)}, u32[]{:S(2)}, u32[]{:S(2)}) collective-permute-start(bf16[576,256]{1,0:T(8,128)(2,1)S(1)} %get-tuple-element.33.refs_0_.refs_7_), channel_id=1, source_target_pairs={{0,1},{1,0},{2,3},{3,2},{4,5},{5,4},{6,7},{7,6},{8,9},{9,8},{10,11... | collective-permute-start | bytes 884744 | tf_op jit(solution)/shard_map/ppermute | solution.py:22
  4.9 9.0 %collective-permute-start.1 = (bf16[512,128]{1,0:T(8,128)(2,1)S(1)}, bf16[512,128]{1,0:T(8,128)(2,1)S(1)}, u32[]{:S(2)}, u32[]{:S(2)}) collective-permute-start(bf16[512,128]{1,0:T(8,128)(2,1)S(1)} %get-tuple-element.41), channel_id=1, source_target_pairs={{0,9},{1,8},{4,1},{5,0},{8,13},{9,12},{12,5},{13,4},{2,11},{3,10},... | collective-permute-start | bytes 393224 | tf_op jit(solution)/shard_map/ppermute | solution.py:44
  7.6 6.5 %collective-permute-start = (bf16[592,128]{1,0:T(8,128)(2,1)S(1)}, bf16[592,128]{1,0:T(8,128)(2,1)S(1)}, u32[]{:S(2)}, u32[]{:S(2)}) collective-permute-start(bf16[592,128]{1,0:T(8,128)(2,1)S(1)} %get-tuple-element.40), channel_id=1, source_target_pairs={{0,8},{8,12},{12,4},{4,0},{1,9},{9,13},{13,5},{5,1},{2,10},{10,14}... | collective-permute-start | bytes 454664 | tf_op jit(solution)/shard_map/ppermute | solution.py:32
  11.9 1.6 %collective-permute-start.4 = (bf16[576,256]{1,0:T(8,128)(2,1)S(1)}, bf16[576,256]{1,0:T(8,128)(2,1)S(1)}, u32[]{:S(2)}, u32[]{:S(2)}) collective-permute-start(bf16[576,256]{1,0:T(8,128)(2,1)S(1)} %collective-permute-done.3.refs_0_.refs_8_), channel_id=1, source_target_pairs={{0,1},{1,0},{2,3},{3,2},{4,5},{5,4},{6,7},{7,6},{8,9},{9,8},{10,11... | collective-permute-start | bytes 884744 | tf_op jit(solution)/shard_map/ppermute | solution.py:22
  14.1 14.5 %collective-permute-start.7 = (bf16[1104,128]{1,0:T(8,128)(2,1)S(1)}, bf16[1104,128]{1,0:T(8,128)(2,1)S(1)}, u32[]{:S(2)}, u32[]{:S(2)}) collective-permute-start(bf16[1104,128]{1,0:T(8,128)(2,1)S(1)} %pad_maximum_fusion.refs_1_), channel_id=1, source_target_pairs={{0,8},{8,12},{12,4},{4,0},{1,9},{9,13},{13,5},{5,1},{2,10},{10,14}... | collective-permute-start | bytes 847880 | tf_op jit(solution)/shard_map/ppermute | solution.py:32
  17.5 20.6 %collective-permute-start.6 = (bf16[512,128]{1,0:T(8,128)(2,1)S(1)}, bf16[512,128]{1,0:T(8,128)(2,1)S(1)}, u32[]{:S(2)}, u32[]{:S(2)}) collective-permute-start(bf16[512,128]{1,0:T(8,128)(2,1)S(1)} %get-tuple-element.41), channel_id=1, source_target_pairs={{0,5},{1,4},{4,13},{5,12},{8,1},{9,0},{12,9},{13,8},{2,7},{3,6},{6... | collective-permute-start | bytes 393224 | tf_op jit(solution)/shard_map/ppermute | solution.py:44
  17.5 20.6 %collective-permute-start.5 = (bf16[592,128]{1,0:T(8,128)(2,1)S(1)}, bf16[592,128]{1,0:T(8,128)(2,1)S(1)}, u32[]{:S(2)}, u32[]{:S(2)}) collective-permute-start(bf16[592,128]{1,0:T(8,128)(2,1)S(1)} %get-tuple-element.40), channel_id=1, source_target_pairs={{0,4},{8,0},{12,8},{4,12},{1,5},{9,1},{13,9},{5,13},{2,6},{10,2},{... | collective-permute-start | bytes 454664 | tf_op jit(solution)/shard_map/ppermute | solution.py:32
  48.1 5.1 %collective-permute-start.10 = (f32[56,128]{1,0:T(8,128)S(1)}, f32[56,128]{1,0:T(8,128)S(1)}, u32[]{:S(2)}, u32[]{:S(2)}) collective-permute-start(f32[56,128]{1,0:T(8,128)S(1)} %get-tuple-element.89), channel_id=1, source_target_pairs={{0,4},{8,0},{12,8},{4,12},{1,5},{9,1},{13,9},{5,13},{2,6},{10,2},{... | collective-permute-start | bytes 86024 | tf_op jit(solution)/shard_map/ppermute | solution.py:32
  49.7 6.0 %collective-permute-start.11 = (f32[56,128]{1,0:T(8,128)S(1)}, f32[56,128]{1,0:T(8,128)S(1)}, u32[]{:S(2)}, u32[]{:S(2)}) collective-permute-start(f32[56,128]{1,0:T(8,128)S(1)} %get-tuple-element.90), channel_id=1, source_target_pairs={{0,12},{8,4},{12,0},{4,8},{1,13},{9,5},{13,1},{5,9},{2,14},{10,6},... | collective-permute-start | bytes 86024 | tf_op jit(solution)/shard_map/ppermute | solution.py:32
  51.8 4.1 %collective-permute-start.12 = (f32[56,128]{1,0:T(8,128)S(1)}, f32[56,128]{1,0:T(8,128)S(1)}, u32[]{:S(2)}, u32[]{:S(2)}) collective-permute-start(f32[56,128]{1,0:T(8,128)S(1)} %get-tuple-element.91), channel_id=1, source_target_pairs={{0,8},{8,12},{12,4},{4,0},{1,9},{9,13},{13,5},{5,1},{2,10},{10,14}... | collective-permute-start | bytes 86024 | tf_op jit(solution)/shard_map/ppermute | solution.py:32
  52.5 3.4 %collective-permute-start.8 = (bf16[16,32,512]{2,1,0:T(8,128)(2,1)S(1)}, bf16[16,32,512]{2,1,0:T(8,128)(2,1)S(1)}, u32[]{:S(2)}, u32[]{:S(2)}) collective-permute-start(bf16[16,32,512]{2,1,0:T(8,128)(2,1)S(1)} %get-tuple-element.53), channel_id=1, source_target_pairs={{0,1},{1,0},{2,3},{3,2},{4,5},{5,4},{6,7},{7,6},{8,9},{9,8},{10,11... | collective-permute-start | bytes 1572872 | tf_op jit(solution)/shard_map/ppermute | solution.py:22
  56.4 5.0 %collective-permute-start.13 = (f32[4,8,512]{2,1,0:T(8,128)S(1)}, f32[4,8,512]{2,1,0:T(8,128)S(1)}, u32[]{:S(2)}, u32[]{:S(2)}) collective-permute-start(f32[4,8,512]{2,1,0:T(8,128)S(1)} %fusion), channel_id=1, source_target_pairs={{0,2},{2,0},{1,3},{3,1},{4,6},{6,4},{5,7},{7,5},{8,10},{10,8},{9,1... | collective-permute-start | bytes 196616 | tf_op jit(solution)/shard_map/ppermute | solution.py:22
  57.6 7.7 %collective-permute-start.9 = (bf16[16,32,256]{2,1,0:T(8,128)(2,1)S(1)}, bf16[16,32,256]{2,1,0:T(8,128)(2,1)S(1)}, u32[]{:S(2)}, u32[]{:S(2)}) collective-permute-start(bf16[16,32,256]{2,1,0:T(8,128)(2,1)S(1)} %slice.307), channel_id=1, source_target_pairs={{0,2},{2,0},{1,3},{3,1},{4,6},{6,4},{5,7},{7,5},{8,10},{10,8},{9,1... | collective-permute-start | bytes 786440 | tf_op jit(solution)/shard_map/ppermute | solution.py:22
  61.4 1.3 %collective-permute-start.14 = (f32[4,8,512]{2,1,0:T(8,128)S(1)}, f32[4,8,512]{2,1,0:T(8,128)S(1)}, u32[]{:S(2)}, u32[]{:S(2)}) collective-permute-start(f32[4,8,512]{2,1,0:T(8,128)S(1)} %select_add_fusion), channel_id=1, source_target_pairs={{0,1},{1,0},{2,3},{3,2},{4,5},{5,4},{6,7},{7,6},{8,9},{9,8},{10,11... | collective-permute-start | bytes 196616 | tf_op jit(solution)/shard_map/ppermute | solution.py:22

commit v13 on v11

--- a/solution.py
+++ b/solution.py
@@ -14,6 +14,7 @@
 jitter_reach = 8
 LANES = 128
 AUG = 16
+HALF_ROOT = -0.7213475204444817
 
 
 def shifted(value, axis, steps):
@@ -193,7 +194,7 @@
         scale = weight[pl.ds(mate, 1), :]
         for start in range(0, panels, LANES):
             span = slice(start, start + LANES)
-            inverse = lax.rsqrt(raw[span, quarter:])
+            inverse = lax.exp2(HALF_ROOT * lax.log(raw[span, quarter:]))
             kernel = scale * inverse
             both[span, :quarter] = kernel.astype(jnp.bfloat16)
             weighted = (inverse * inverse) * (kernel * raw[span, :quarter])

time: 59.5 us -> 59.4 us (level)
  no operation moved by 1% of the time
where the time goes in v13:
time: 59.4 us; the launch traced here: 59.3 us
  Pallas kernels  26.7 us (45%)
  starting transfers between devices  18.4 us (31%)
  waiting for transfers between devices  11.1 us (19%)
  other arithmetic  1.23 us (2%)
  between operations  1.03 us (2%)
  local copies, waits for them, and re-layouts  0.91 us (2%)
    pallas_call x3, Pallas kernels, run_step(): pl.pallas_call(functools.partial(step_kernel, step, length, rhs, subs, fi...  22.6 us
    ppermute x6, starting transfers between devices, round_ring(): return lax.ppermute(value, 'clus', pairs)  10.2 us
    ppermute x7, waiting for transfers between devices, shifted(): return lax.ppermute(value, axis, pairs)  7.75 us
    ppermute x7, starting transfers between devices, shifted(): return lax.ppermute(value, axis, pairs)  5.44 us
    ppermute x6, waiting for transfers between devices, round_ring(): return lax.ppermute(value, 'clus', pairs)  3.32 us
    ppermute x2, starting transfers between devices, moved(): return lax.ppermute(value, axes, pairs)  2.7 us
    pallas_call x1, Pallas kernels, on_device(): pl.pallas_call(node_kernel, out_shape=jax.ShapeDtypeStruct((3, share * pa...  1.32 us
    pallas_call x1, Pallas kernels, on_device(): pl.pallas_call(functools.partial(prepare_kernel, (panels, nodes_total)),...  1.22 us
  transfers between devices with their start and end apart: 15, of which 9 were waited for; matrix products, arithmetic and copies ran while one was open for 3% of the time, Pallas kernels for 29%

profile of v13, /device:TPU:0, one launch (start us, length us, event | category | flops | bytes accessed | tf_op | source)
XLA Modules:
  0.0 59.3 jit_solution(9500904529282943419)
XLA Ops:
  0.6 0.0 copy-start
  0.6 1.2 %prepare.1 = (bf16[592,128]{1,0:T(8,128)(2,1)S(1)}, bf16[512,128]{1,0:T(8,128)(2,1)S(1)}, bf16[576,256]{1,0:T(8,128)(2,1)S(1)}) custom-call(bf16[16,32,256]{2,1,0:T(8,128)(2,1)} %refs_0_.1, bf16[3,16,256]{2,1,0:T(8,128)(2,1)} %bitcast.91, bf16[16,256]{1,0:T(8,128)(2,1)} %refs_2_.1, s32[16,4,256]{2,1,0:T(4,128)} %refs_3_.1, bf16[16,32,256]{2,1,0:T(8,128)(2,1)} %refs_4_.1), custom_call_target="tpu_custom_call" | custom-call | tf_op jit(solution)/shard_map/prepare/pallas_call | solution.py:358
  1.9 3.0 %collective-permute-start.3 = (bf16[576,256]{1,0:T(8,128)(2,1)S(1)}, bf16[576,256]{1,0:T(8,128)(2,1)S(1)}, u32[]{:S(2)}, u32[]{:S(2)}) collective-permute-start(bf16[576,256]{1,0:T(8,128)(2,1)S(1)} %get-tuple-element.33.refs_0_.refs_7_), channel_id=1, source_target_pairs={{0,2},{2,0},{1,3},{3,1},{4,6},{6,4},{5,7},{7,5},{8,10},{10,8},{9,1... | collective-permute-start | bytes 884744 | tf_op jit(solution)/shard_map/ppermute | solution.py:23
  4.9 0.0 collective-permute-start.2
  4.9 2.7 %collective-permute-start.1 = (bf16[512,128]{1,0:T(8,128)(2,1)S(1)}, bf16[512,128]{1,0:T(8,128)(2,1)S(1)}, u32[]{:S(2)}, u32[]{:S(2)}) collective-permute-start(bf16[512,128]{1,0:T(8,128)(2,1)S(1)} %get-tuple-element.41), channel_id=1, source_target_pairs={{0,9},{1,8},{4,1},{5,0},{8,13},{9,12},{12,5},{13,4},{2,11},{3,10},... | collective-permute-start | bytes 393224 | tf_op jit(solution)/shard_map/ppermute | solution.py:45
  7.6 1.6 %collective-permute-start = (bf16[592,128]{1,0:T(8,128)(2,1)S(1)}, bf16[592,128]{1,0:T(8,128)(2,1)S(1)}, u32[]{:S(2)}, u32[]{:S(2)}) collective-permute-start(bf16[592,128]{1,0:T(8,128)(2,1)S(1)} %get-tuple-element.40), channel_id=1, source_target_pairs={{0,8},{8,12},{12,4},{4,0},{1,9},{9,13},{13,5},{5,1},{2,10},{10,14}... | collective-permute-start | bytes 454664 | tf_op jit(solution)/shard_map/ppermute | solution.py:33
  9.2 0.0 copy-done
  9.2 0.1 constant_dynamic-slice_fusion
  9.2 0.1 reshape.294
  9.3 0.1 mul.22
  9.4 0.2 convert_reduce_fusion
  9.6 0.2 convert_reduce_fusion.1
  9.8 0.1 copy.34
  9.9 0.2 select_reduce_fusion
  10.1 1.8 %collective-permute-done.3.refs_0_.refs_8_ = bf16[576,256]{1,0:T(8,128)(2,1)S(1)} collective-permute-done((bf16[576,256]{1,0:T(8,128)(2,1)S(1)}, bf16[576,256]{1,0:T(8,128)(2,1)S(1)}, u32[]{:S(2)}, u32[]{:S(2)}) %collective-permute-start.3) | collective-permute-done | bytes 294944 | tf_op jit(solution)/shard_map/ppermute | solution.py:23
  11.9 0.0 collective-permute-start.4
  11.9 0.1 pad_slice_fusion
  12.0 0.1 pad_add_fusion
  12.0 0.1 reshape.295.refs_0_
  12.1 0.1 pad.40.clone
  12.2 0.0 collective-permute-done.2.refs_1_
  12.2 0.4 targets_0.1
  12.6 0.9 %collective-permute-done.4.refs_1_ = bf16[576,256]{1,0:T(8,128)(2,1)S(1)} collective-permute-done((bf16[576,256]{1,0:T(8,128)(2,1)S(1)}, bf16[576,256]{1,0:T(8,128)(2,1)S(1)}, u32[]{:S(2)}, u32[]{:S(2)}) %collective-permute-start.4) | collective-permute-done | bytes 294944 | tf_op jit(solution)/shard_map/ppermute | solution.py:23
  13.5 0.4 targets_1.1
  13.9 0.0 collective-permute-done.1
  13.9 0.2 collective-permute-done
  14.1 3.4 %collective-permute-start.7 = (bf16[1104,128]{1,0:T(8,128)(2,1)S(1)}, bf16[1104,128]{1,0:T(8,128)(2,1)S(1)}, u32[]{:S(2)}, u32[]{:S(2)}) collective-permute-start(bf16[1104,128]{1,0:T(8,128)(2,1)S(1)} %pad_maximum_fusion.refs_1_), channel_id=1, source_target_pairs={{0,8},{8,12},{12,4},{4,0},{1,9},{9,13},{13,5},{5,1},{2,10},{10,14}... | collective-permute-start | bytes 847880 | tf_op jit(solution)/shard_map/ppermute | solution.py:33
  17.5 0.0 collective-permute-start.6
  17.5 0.8 %collective-permute-start.5 = (bf16[592,128]{1,0:T(8,128)(2,1)S(1)}, bf16[592,128]{1,0:T(8,128)(2,1)S(1)}, u32[]{:S(2)}, u32[]{:S(2)}) collective-permute-start(bf16[592,128]{1,0:T(8,128)(2,1)S(1)} %get-tuple-element.40), channel_id=1, source_target_pairs={{0,4},{8,0},{12,8},{4,12},{1,5},{9,1},{13,9},{5,13},{2,6},{10,2},{... | collective-permute-start | bytes 454664 | tf_op jit(solution)/shard_map/ppermute | solution.py:33
  18.4 7.8 %near_field_0.1 = (f32[16,80,512]{2,1,0:T(8,128)S(1)}, f32[3,16,128]{2,1,0:T(8,128)S(1)}) custom-call(s32[108]{0:T(128)S(1)} %reshape.295.refs_0_, bf16[1104,128]{1,0:T(8,128)(2,1)S(1)} %pad_maximum_fusion.refs_1_, bf16[16,256,128]{2,1,0:T(8,128)(2,1)S(1)} %get-tuple-element.43.refs_2_, bf16[16,256,128]{2,1,0:T(8,128)(2,1)S(1)} %get-tuple-element.44.refs_3_, ...), custom_call_target="tpu_custom_call" | custom-call | flops 692060160 | bytes 6291456 | tf_op jit(solution)/shard_map/near_field_0/pallas_call | solution.py:271
  26.2 0.0 collective-permute-done.7.refs_1_
  26.2 7.3 %near_field_1.1 = (f32[16,80,512]{2,1,0:T(8,128)S(1)}, f32[3,16,128]{2,1,0:T(8,128)S(1)}) custom-call(s32[108]{0:T(128)S(1)} %reshape.295.refs_0_, bf16[1104,128]{1,0:T(8,128)(2,1)S(1)} %collective-permute-done.7.refs_1_, bf16[16,256,128]{2,1,0:T(8,128)(2,1)S(1)} %get-tuple-element.43.refs_2_, bf16[16,256,128]{2,1,0:T(8,128)(2,1)S(1)} %get-tuple-element.44.refs_3_, ...), custom_call_target="tpu_custom_call" | custom-call | flops 692060160 | bytes 6291456 | tf_op jit(solution)/shard_map/near_field_1/pallas_call | solution.py:271
  33.5 0.0 collective-permute-done.6
  33.5 0.0 collective-permute-done.5
  33.6 7.5 %near_field_2.1 = (f32[16,32,512]{2,1,0:T(8,128)S(1)}, bf16[16,32,512]{2,1,0:T(8,128)(2,1)S(1)}, f32[3,16,512]{2,1,0:T(8,128)S(1)}, f32[3,16,128]{2,1,0:T(8,128)S(1)}) custom-call(s32[108]{0:T(128)S(1)} %reshape.295.refs_0_, bf16[1104,128]{1,0:T(8,128)(2,1)S(1)} %pad_maximum_fusion.1.refs_1_, bf16[16,256,128]{2,1,0:T(8,128)(2,1)S(1)} %get-tuple-element.43.refs_2_, ...), custom_call_target="tpu_custom_call" | custom-call | flops 692060160 | bytes 6291456 | tf_op jit(solution)/shard_map/near_field_2/pallas_call | solution.py:271
  41.1 0.1 copy.38
  41.3 0.1 maximum_maximum_fusion
  41.4 1.6 %collective-permute-start.10 = (f32[56,128]{1,0:T(8,128)S(1)}, f32[56,128]{1,0:T(8,128)S(1)}, u32[]{:S(2)}, u32[]{:S(2)}) collective-permute-start(f32[56,128]{1,0:T(8,128)S(1)} %get-tuple-element.89), channel_id=1, source_target_pairs={{0,4},{8,0},{12,8},{4,12},{1,5},{9,1},{13,9},{5,13},{2,6},{10,2},{... | collective-permute-start | bytes 86024 | tf_op jit(solution)/shard_map/ppermute | solution.py:33
  43.0 2.3 %collective-permute-start.11 = (f32[56,128]{1,0:T(8,128)S(1)}, f32[56,128]{1,0:T(8,128)S(1)}, u32[]{:S(2)}, u32[]{:S(2)}) collective-permute-start(f32[56,128]{1,0:T(8,128)S(1)} %get-tuple-element.90), channel_id=1, source_target_pairs={{0,12},{8,4},{12,0},{4,8},{1,13},{9,5},{13,1},{5,9},{2,14},{10,6},... | collective-permute-start | bytes 86024 | tf_op jit(solution)/shard_map/ppermute | solution.py:33
  45.3 0.5 collective-permute-start.12
  45.8 0.2 collective-permute-start.8
  46.0 0.5 collective-permute-done.10
  46.5 2.4 %collective-permute-done.11 = f32[56,128]{1,0:T(8,128)S(1)} collective-permute-done((f32[56,128]{1,0:T(8,128)S(1)}, f32[56,128]{1,0:T(8,128)S(1)}, u32[]{:S(2)}, u32[]{:S(2)}) %collective-permute-start.11) | collective-permute-done | bytes 28704 | tf_op jit(solution)/shard_map/ppermute | solution.py:33
  48.9 0.3 collective-permute-done.12
  49.3 0.0 collective-permute-done.8
  49.3 0.2 convert_add_fusion
  49.8 1.0 %collective-permute-start.13 = (f32[4,8,512]{2,1,0:T(8,128)S(1)}, f32[4,8,512]{2,1,0:T(8,128)S(1)}, u32[]{:S(2)}, u32[]{:S(2)}) collective-permute-start(f32[4,8,512]{2,1,0:T(8,128)S(1)} %fusion), channel_id=1, source_target_pairs={{0,2},{2,0},{1,3},{3,1},{4,6},{6,4},{5,7},{7,5},{8,10},{10,8},{9,1... | collective-permute-start | bytes 196616 | tf_op jit(solution)/shard_map/ppermute | solution.py:23
  50.8 1.1 %collective-permute-start.9 = (bf16[16,32,256]{2,1,0:T(8,128)(2,1)S(1)}, bf16[16,32,256]{2,1,0:T(8,128)(2,1)S(1)}, u32[]{:S(2)}, u32[]{:S(2)}) collective-permute-start(bf16[16,32,256]{2,1,0:T(8,128)(2,1)S(1)} %slice.307), channel_id=1, source_target_pairs={{0,2},{2,0},{1,3},{3,1},{4,6},{6,4},{5,7},{7,5},{8,10},{10,8},{9,1... | collective-permute-start | bytes 786440 | tf_op jit(solution)/shard_map/ppermute | solution.py:23
  51.9 2.9 %collective-permute-done.13 = f32[4,8,512]{2,1,0:T(8,128)S(1)} collective-permute-done((f32[4,8,512]{2,1,0:T(8,128)S(1)}, f32[4,8,512]{2,1,0:T(8,128)S(1)}, u32[]{:S(2)}, u32[]{:S(2)}) %collective-permute-start.13) | collective-permute-done | bytes 65568 | tf_op jit(solution)/shard_map/ppermute | solution.py:23
  54.8 0.1 collective-permute-start.14
  55.0 1.2 %collective-permute-done.14 = f32[4,8,512]{2,1,0:T(8,128)S(1)} collective-permute-done((f32[4,8,512]{2,1,0:T(8,128)S(1)}, f32[4,8,512]{2,1,0:T(8,128)S(1)}, u32[]{:S(2)}, u32[]{:S(2)}) %collective-permute-start.14) | collective-permute-done | bytes 65568 | tf_op jit(solution)/shard_map/ppermute | solution.py:23
  56.2 1.3 %node_terms.1 = f32[3,4096]{1,0:T(4,128)} custom-call(f32[3,8,512]{2,1,0:T(8,128)S(1)} %slice.197.grad_ref, s32[8,512]{1,0:T(8,128)S(1)} %slice_select_fusion.2.jitter_ref, f32[8,512]{1,0:T(8,128)S(1)} %slice_bitcast_fusion.edge_ref), custom_call_target="tpu_custom_call" | custom-call | flops 1048576 | bytes 262144 | tf_op jit(solution)/shard_map/node_terms/pallas_call | solution.py:550
  57.5 1.0 %collective-permute-done.9.refs_1_ = bf16[16,32,256]{2,1,0:T(8,128)(2,1)S(1)} collective-permute-done((bf16[16,32,256]{2,1,0:T(8,128)(2,1)S(1)}, bf16[16,32,256]{2,1,0:T(8,128)(2,1)S(1)}, u32[]{:S(2)}, u32[]{:S(2)}) %collective-permute-start.9) | collective-permute-done | bytes 262176 | tf_op jit(solution)/shard_map/ppermute | solution.py:23
  58.5 0.7 %potential_sum.1 = bf16[16,32,256]{2,1,0:T(8,128)(2,1)} custom-call(f32[16,32,256]{2,1,0:T(8,128)S(1)} %slice.127.refs_0_, bf16[16,32,256]{2,1,0:T(8,128)(2,1)S(1)} %collective-permute-done.9.refs_1_), custom_call_target="tpu_custom_call" | custom-call | flops 1048576 | bytes 262144 | tf_op jit(solution)/shard_map/potential_sum/pallas_call | solution.py:559
  (47 shorter events, 0.6 us)
Async XLA Ops:
  0.6 8.5 %copy-start = (s32[5,64]{1,0:T(8,128)S(1)}, s32[5,64]{1,0:T(8,128)}, u32[]{:S(2)}) copy-start(s32[5,64]{1,0:T(8,128)} %param.10) | copy-start | bytes 3844
  1.9 10.0 %collective-permute-start.3 = (bf16[576,256]{1,0:T(8,128)(2,1)S(1)}, bf16[576,256]{1,0:T(8,128)(2,1)S(1)}, u32[]{:S(2)}, u32[]{:S(2)}) collective-permute-start(bf16[576,256]{1,0:T(8,128)(2,1)S(1)} %get-tuple-element.33.refs_0_.refs_7_), channel_id=1, source_target_pairs={{0,2},{2,0},{1,3},{3,1},{4,6},{6,4},{5,7},{7,5},{8,10},{10,8},{9,1... | collective-permute-start | bytes 884744 | tf_op jit(solution)/shard_map/ppermute | solution.py:23
  4.9 7.3 %collective-permute-start.2 = (bf16[576,256]{1,0:T(8,128)(2,1)S(1)}, bf16[576,256]{1,0:T(8,128)(2,1)S(1)}, u32[]{:S(2)}, u32[]{:S(2)}) collective-permute-start(bf16[576,256]{1,0:T(8,128)(2,1)S(1)} %get-tuple-element.33.refs_0_.refs_7_), channel_id=1, source_target_pairs={{0,1},{1,0},{2,3},{3,2},{4,5},{5,4},{6,7},{7,6},{8,9},{9,8},{10,11... | collective-permute-start | bytes 884744 | tf_op jit(solution)/shard_map/ppermute | solution.py:23
  4.9 9.0 %collective-permute-start.1 = (bf16[512,128]{1,0:T(8,128)(2,1)S(1)}, bf16[512,128]{1,0:T(8,128)(2,1)S(1)}, u32[]{:S(2)}, u32[]{:S(2)}) collective-permute-start(bf16[512,128]{1,0:T(8,128)(2,1)S(1)} %get-tuple-element.41), channel_id=1, source_target_pairs={{0,9},{1,8},{4,1},{5,0},{8,13},{9,12},{12,5},{13,4},{2,11},{3,10},... | collective-permute-start | bytes 393224 | tf_op jit(solution)/shard_map/ppermute | solution.py:45
  7.6 6.5 %collective-permute-start = (bf16[592,128]{1,0:T(8,128)(2,1)S(1)}, bf16[592,128]{1,0:T(8,128)(2,1)S(1)}, u32[]{:S(2)}, u32[]{:S(2)}) collective-permute-start(bf16[592,128]{1,0:T(8,128)(2,1)S(1)} %get-tuple-element.40), channel_id=1, source_target_pairs={{0,8},{8,12},{12,4},{4,0},{1,9},{9,13},{13,5},{5,1},{2,10},{10,14}... | collective-permute-start | bytes 454664 | tf_op jit(solution)/shard_map/ppermute | solution.py:33
  11.9 1.6 %collective-permute-start.4 = (bf16[576,256]{1,0:T(8,128)(2,1)S(1)}, bf16[576,256]{1,0:T(8,128)(2,1)S(1)}, u32[]{:S(2)}, u32[]{:S(2)}) collective-permute-start(bf16[576,256]{1,0:T(8,128)(2,1)S(1)} %collective-permute-done.3.refs_0_.refs_8_), channel_id=1, source_target_pairs={{0,1},{1,0},{2,3},{3,2},{4,5},{5,4},{6,7},{7,6},{8,9},{9,8},{10,11... | collective-permute-start | bytes 884744 | tf_op jit(solution)/shard_map/ppermute | solution.py:23
  14.1 12.1 %collective-permute-start.7 = (bf16[1104,128]{1,0:T(8,128)(2,1)S(1)}, bf16[1104,128]{1,0:T(8,128)(2,1)S(1)}, u32[]{:S(2)}, u32[]{:S(2)}) collective-permute-start(bf16[1104,128]{1,0:T(8,128)(2,1)S(1)} %pad_maximum_fusion.refs_1_), channel_id=1, source_target_pairs={{0,8},{8,12},{12,4},{4,0},{1,9},{9,13},{13,5},{5,1},{2,10},{10,14}... | collective-permute-start | bytes 847880 | tf_op jit(solution)/shard_map/ppermute | solution.py:33
  17.5 16.0 %collective-permute-start.6 = (bf16[512,128]{1,0:T(8,128)(2,1)S(1)}, bf16[512,128]{1,0:T(8,128)(2,1)S(1)}, u32[]{:S(2)}, u32[]{:S(2)}) collective-permute-start(bf16[512,128]{1,0:T(8,128)(2,1)S(1)} %get-tuple-element.41), channel_id=1, source_target_pairs={{0,5},{1,4},{4,13},{5,12},{8,1},{9,0},{12,9},{13,8},{2,7},{3,6},{6... | collective-permute-start | bytes 393224 | tf_op jit(solution)/shard_map/ppermute | solution.py:45
  17.5 16.0 %collective-permute-start.5 = (bf16[592,128]{1,0:T(8,128)(2,1)S(1)}, bf16[592,128]{1,0:T(8,128)(2,1)S(1)}, u32[]{:S(2)}, u32[]{:S(2)}) collective-permute-start(bf16[592,128]{1,0:T(8,128)(2,1)S(1)} %get-tuple-element.40), channel_id=1, source_target_pairs={{0,4},{8,0},{12,8},{4,12},{1,5},{9,1},{13,9},{5,13},{2,6},{10,2},{... | collective-permute-start | bytes 454664 | tf_op jit(solution)/shard_map/ppermute | solution.py:33
  41.4 5.1 %collective-permute-start.10 = (f32[56,128]{1,0:T(8,128)S(1)}, f32[56,128]{1,0:T(8,128)S(1)}, u32[]{:S(2)}, u32[]{:S(2)}) collective-permute-start(f32[56,128]{1,0:T(8,128)S(1)} %get-tuple-element.89), channel_id=1, source_target_pairs={{0,4},{8,0},{12,8},{4,12},{1,5},{9,1},{13,9},{5,13},{2,6},{10,2},{... | collective-permute-start | bytes 86024 | tf_op jit(solution)/shard_map/ppermute | solution.py:33
  43.0 5.9 %collective-permute-start.11 = (f32[56,128]{1,0:T(8,128)S(1)}, f32[56,128]{1,0:T(8,128)S(1)}, u32[]{:S(2)}, u32[]{:S(2)}) collective-permute-start(f32[56,128]{1,0:T(8,128)S(1)} %get-tuple-element.90), channel_id=1, source_target_pairs={{0,12},{8,4},{12,0},{4,8},{1,13},{9,5},{13,1},{5,9},{2,14},{10,6},... | collective-permute-start | bytes 86024 | tf_op jit(solution)/shard_map/ppermute | solution.py:33
  45.3 3.9 %collective-permute-start.12 = (f32[56,128]{1,0:T(8,128)S(1)}, f32[56,128]{1,0:T(8,128)S(1)}, u32[]{:S(2)}, u32[]{:S(2)}) collective-permute-start(f32[56,128]{1,0:T(8,128)S(1)} %get-tuple-element.91), channel_id=1, source_target_pairs={{0,8},{8,12},{12,4},{4,0},{1,9},{9,13},{13,5},{5,1},{2,10},{10,14}... | collective-permute-start | bytes 86024 | tf_op jit(solution)/shard_map/ppermute | solution.py:33
  45.8 3.5 %collective-permute-start.8 = (bf16[16,32,512]{2,1,0:T(8,128)(2,1)S(1)}, bf16[16,32,512]{2,1,0:T(8,128)(2,1)S(1)}, u32[]{:S(2)}, u32[]{:S(2)}) collective-permute-start(bf16[16,32,512]{2,1,0:T(8,128)(2,1)S(1)} %get-tuple-element.53), channel_id=1, source_target_pairs={{0,1},{1,0},{2,3},{3,2},{4,5},{5,4},{6,7},{7,6},{8,9},{9,8},{10,11... | collective-permute-start | bytes 1572872 | tf_op jit(solution)/shard_map/ppermute | solution.py:23
  49.8 5.1 %collective-permute-start.13 = (f32[4,8,512]{2,1,0:T(8,128)S(1)}, f32[4,8,512]{2,1,0:T(8,128)S(1)}, u32[]{:S(2)}, u32[]{:S(2)}) collective-permute-start(f32[4,8,512]{2,1,0:T(8,128)S(1)} %fusion), channel_id=1, source_target_pairs={{0,2},{2,0},{1,3},{3,1},{4,6},{6,4},{5,7},{7,5},{8,10},{10,8},{9,1... | collective-permute-start | bytes 196616 | tf_op jit(solution)/shard_map/ppermute | solution.py:23
  50.8 7.7 %collective-permute-start.9 = (bf16[16,32,256]{2,1,0:T(8,128)(2,1)S(1)}, bf16[16,32,256]{2,1,0:T(8,128)(2,1)S(1)}, u32[]{:S(2)}, u32[]{:S(2)}) collective-permute-start(bf16[16,32,256]{2,1,0:T(8,128)(2,1)S(1)} %slice.307), channel_id=1, source_target_pairs={{0,2},{2,0},{1,3},{3,1},{4,6},{6,4},{5,7},{7,5},{8,10},{10,8},{9,1... | collective-permute-start | bytes 786440 | tf_op jit(solution)/shard_map/ppermute | solution.py:23
  54.8 1.3 %collective-permute-start.14 = (f32[4,8,512]{2,1,0:T(8,128)S(1)}, f32[4,8,512]{2,1,0:T(8,128)S(1)}, u32[]{:S(2)}, u32[]{:S(2)}) collective-permute-start(f32[4,8,512]{2,1,0:T(8,128)S(1)} %select_add_fusion), channel_id=1, source_target_pairs={{0,1},{1,0},{2,3},{3,2},{4,5},{5,4},{6,7},{7,6},{8,9},{9,8},{10,11... | collective-permute-start | bytes 196616 | tf_op jit(solution)/shard_map/ppermute | solution.py:23

commit v14 on v11

--- a/solution.py
+++ b/solution.py
@@ -142,7 +142,7 @@
     else:
         acc, back_ref = refs[:2]
         refs = refs[2:]
-    aug32, left, weight, back, raw_a, raw_b, both_a, both_b = refs
+    aug32, left_a, left_b, weight, back, raw_a, raw_b, both = refs
     clusters, rows, panels = acc.shape
     width = rows - AUG
     row_count = panels // subs
@@ -163,63 +163,82 @@
         aug32[:, row, :] = value
     weight[...] = jnp.zeros(weight.shape, jnp.float32)
     weight[:clusters, :] = CP ** (-0.5) * area
-    left[...] = jnp.zeros(left.shape, left.dtype)
+    left_a[...] = jnp.zeros(left_a.shape, left_a.dtype)
+    left_b[...] = jnp.zeros(left_b.shape, left_b.dtype)
     for cluster in range(clusters):
-        left[cluster, width:rows, quarter:] = aug32[cluster].astype(jnp.bfloat16)
+        distance_rows = aug32[cluster].astype(jnp.bfloat16)
+        left_a[cluster, width:rows, quarter:] = distance_rows
+        left_b[cluster, width:rows, :quarter] = distance_rows
         for place, at in enumerate(starts):
-            left[cluster, place * rhs : (place + 1) * rhs, :quarter] = source_ref[
-                at + cluster * rhs : at + (cluster + 1) * rhs, :
-            ]
+            span = slice(place * rhs, (place + 1) * rhs)
+            dens = source_ref[at + cluster * rhs : at + (cluster + 1) * rhs, :]
+            left_a[cluster, span, :quarter] = dens
+            left_b[cluster, span, quarter:] = dens
     back[...] = jnp.zeros(back.shape, jnp.float32)
     if first:
         acc[...] = jnp.zeros(acc.shape, jnp.float32)
     else:
         acc[...] = acc_in[...]
     raw_b[...] = jnp.ones(raw_b.shape, jnp.float32)
-    both_a[...] = jnp.zeros(both_a.shape, both_a.dtype)
+    both[:, : 2 * quarter] = jnp.zeros((panels, 2 * quarter), both.dtype)
+
+    halves = [slice(at * quarter, (at + 1) * quarter) for at in range(4)]
 
     def decoded(place):
         code = items[step * length + place]
         return code // (2 * clusters), code % (2 * clusters)
 
-    def products(place, raw):
+    def products(place, left, raw):
         here, mate = decoded(place)
-        mate = mate % clusters
         lhs = jnp.concatenate([ref[here] for ref in lhs_refs], axis=0)
-        raw[...] = jnp.dot(lhs, left[mate], preferred_element_type=jnp.float32)
-
-    def pointwise(place, raw, both):
+        raw[...] = jnp.dot(lhs, left[mate % clusters], preferred_element_type=jnp.float32)
+
+    def pointwise(place, raw, raw_halves, both_halves):
         _, mate = decoded(place)
         scale = weight[pl.ds(mate, 1), :]
         for start in range(0, panels, LANES):
             span = slice(start, start + LANES)
-            inverse = lax.rsqrt(raw[span, quarter:])
+            inverse = lax.rsqrt(raw[span, raw_halves[1]])
             kernel = scale * inverse
-            both[span, :quarter] = kernel.astype(jnp.bfloat16)
-            weighted = (inverse * inverse) * (kernel * raw[span, :quarter])
-            both[span, quarter:] = weighted.astype(jnp.bfloat16)
-
-    def summed(place, both):
+            both[span, both_halves[0]] = kernel.astype(jnp.bfloat16)
+            weighted = (inverse * inverse) * (kernel * raw[span, raw_halves[0]])
+            both[span, both_halves[1]] = weighted.astype(jnp.bfloat16)
+
+    def summed(place, left, columns):
         here, mate = decoded(place)
-        mate = mate % clusters
         acc[here] += lax.dot_general(
-            left[mate, :rows, :],
-            both[...],
+            left[mate % clusters, :rows, :],
+            both[:, columns],
             (((1,), (1,)), ((), ())),
             preferred_element_type=jnp.float32,
         )
-        aug = jnp.concatenate([ref[here] for ref in aug_refs], axis=1)
-        back[mate] += jnp.dot(aug, both[:, quarter:], preferred_element_type=jnp.float32)
+
+    def source_sums(place):
+        (here_a, mate_a), (here_b, mate_b) = decoded(place), decoded(place + 1)
+        aug = jnp.concatenate(
+            [
+                jnp.concatenate([ref[here] for ref in aug_refs], axis=1)
+                for here in (here_a, here_b)
+            ],
+            axis=0,
+        )
+        sums = jnp.dot(aug, both[:, quarter : 3 * quarter], preferred_element_type=jnp.float32)
+        back[mate_a % clusters] += sums[:AUG, :quarter]
+        back[mate_b % clusters] += sums[AUG:, quarter:]
+
+    forward, backward = (halves[0], halves[1]), (halves[1], halves[0])
+    columns_a, columns_b = slice(0, 2 * quarter), slice(2 * quarter, 4 * quarter)
 
     @pl.loop(0, items[step * length])
     def _(pair):
         turn = 2 * pair + 1
-        summed(turn, both_a)
-        pointwise(turn + 1, raw_b, both_b)
-        products(turn + 2, raw_a)
-        summed(turn + 1, both_b)
-        pointwise(turn + 2, raw_a, both_a)
-        products(turn + 3, raw_b)
+        summed(turn, left_a, columns_a)
+        pointwise(turn + 1, raw_b, backward, (halves[3], halves[2]))
+        products(turn + 2, left_a, raw_a)
+        source_sums(turn)
+        summed(turn + 1, left_b, columns_b)
+        pointwise(turn + 2, raw_a, forward, (halves[0], halves[1]))
+        products(turn + 3, left_b, raw_b)
 
     for coord in range(3):
         back_ref[coord] = -0.5 * back[:, coord, :] - there[coord] * back[:, 6, :]
@@ -250,11 +269,12 @@
     scratch = [
         pltpu.VMEM((clusters, AUG, quarter), jnp.float32),
         pltpu.VMEM((clusters, LANES, 2 * quarter), jnp.bfloat16),
+        pltpu.VMEM((clusters, LANES, 2 * quarter), jnp.bfloat16),
         pltpu.VMEM((clusters + 8, quarter), jnp.float32),
         pltpu.VMEM((clusters, AUG, quarter), jnp.float32),
     ]
     scratch += [pltpu.VMEM((panels, 2 * quarter), jnp.float32)] * 2
-    scratch += [pltpu.VMEM((panels, 2 * quarter), jnp.bfloat16)] * 2
+    scratch += [pltpu.VMEM((panels, 4 * quarter), jnp.bfloat16)]
     if last:
         operands += tuple(locals_)
         out_shape = (

time: 59.5 us -> 59.2 us (level)
  starting transfers between devices: 18.3 us -> 19.1 us
    ppermute x7, waiting for transfers between devices: 7.76 us -> 6.67 us  [shifted(): return lax.ppermute(value, axis, pairs)]
    ppermute x6, starting transfers between devices: 10.2 us -> 11.1 us  [round_ring(): return lax.ppermute(value, 'clus', pairs)]
    ppermute x6, waiting for transfers between devices: 3.32 us -> 3.98 us  [round_ring(): return lax.ppermute(value, 'clus', pairs)]
  transfers between devices with their start and end apart: 15 -> 15, of which waited for: 9 -> 9; matrix products, arithmetic and copies ran while one was open for 3% -> 3% of each run, Pallas kernels for 29% -> 31%
where the time goes in v14:
time: 59.2 us
  Pallas kernels  26.3 us (44%)
  starting transfers between devices  19.1 us (32%)
  waiting for transfers between devices  10.7 us (18%)
  other arithmetic  1.23 us (2%)
  between operations  1.03 us (2%)
  local copies, waits for them, and re-layouts  0.91 us (2%)
    pallas_call x3, Pallas kernels, run_step(): pl.pallas_call(functools.partial(step_kernel, step, length, rhs, subs, fi...  22.2 us
    ppermute x6, starting transfers between devices, round_ring(): return lax.ppermute(value, 'clus', pairs)  11.1 us
    ppermute x7, waiting for transfers between devices, shifted(): return lax.ppermute(value, axis, pairs)  6.67 us
    ppermute x7, starting transfers between devices, shifted(): return lax.ppermute(value, axis, pairs)  5.24 us
    ppermute x6, waiting for transfers between devices, round_ring(): return lax.ppermute(value, 'clus', pairs)  3.98 us
    ppermute x2, starting transfers between devices, moved(): return lax.ppermute(value, axes, pairs)  2.7 us
    pallas_call x1, Pallas kernels, on_device(): pl.pallas_call(node_kernel, out_shape=jax.ShapeDtypeStruct((3, share * pa...  1.32 us
    pallas_call x1, Pallas kernels, on_device(): pl.pallas_call(functools.partial(prepare_kernel, (panels, nodes_total)),...  1.22 us
  transfers between devices with their start and end apart: 15, of which 9 were waited for; matrix products, arithmetic and copies ran while one was open for 3% of the time, Pallas kernels for 31%

profile of v14, /device:TPU:0, one launch (start us, length us, event | category | flops | bytes accessed | tf_op | source)
XLA Modules:
  0.0 59.2 jit_solution(14986288228259995558)
XLA Ops:
  0.6 0.0 copy-start
  0.6 1.2 %prepare.1 = (bf16[592,128]{1,0:T(8,128)(2,1)S(1)}, bf16[512,128]{1,0:T(8,128)(2,1)S(1)}, bf16[576,256]{1,0:T(8,128)(2,1)S(1)}) custom-call(bf16[16,32,256]{2,1,0:T(8,128)(2,1)} %refs_0_.1, bf16[3,16,256]{2,1,0:T(8,128)(2,1)} %bitcast.91, bf16[16,256]{1,0:T(8,128)(2,1)} %refs_2_.1, s32[16,4,256]{2,1,0:T(4,128)} %refs_3_.1, bf16[16,32,256]{2,1,0:T(8,128)(2,1)} %refs_4_.1), custom_call_target="tpu_custom_call" | custom-call | tf_op jit(solution)/shard_map/prepare/pallas_call | solution.py:377
  1.9 3.0 %collective-permute-start.3 = (bf16[576,256]{1,0:T(8,128)(2,1)S(1)}, bf16[576,256]{1,0:T(8,128)(2,1)S(1)}, u32[]{:S(2)}, u32[]{:S(2)}) collective-permute-start(bf16[576,256]{1,0:T(8,128)(2,1)S(1)} %get-tuple-element.33.refs_0_.refs_7_), channel_id=1, source_target_pairs={{0,2},{2,0},{1,3},{3,1},{4,6},{6,4},{5,7},{7,5},{8,10},{10,8},{9,1... | collective-permute-start | bytes 884744 | tf_op jit(solution)/shard_map/ppermute | solution.py:22
  4.9 0.0 collective-permute-start.2
  4.9 2.7 %collective-permute-start.1 = (bf16[512,128]{1,0:T(8,128)(2,1)S(1)}, bf16[512,128]{1,0:T(8,128)(2,1)S(1)}, u32[]{:S(2)}, u32[]{:S(2)}) collective-permute-start(bf16[512,128]{1,0:T(8,128)(2,1)S(1)} %get-tuple-element.41), channel_id=1, source_target_pairs={{0,9},{1,8},{4,1},{5,0},{8,13},{9,12},{12,5},{13,4},{2,11},{3,10},... | collective-permute-start | bytes 393224 | tf_op jit(solution)/shard_map/ppermute | solution.py:44
  7.6 1.6 %collective-permute-start = (bf16[592,128]{1,0:T(8,128)(2,1)S(1)}, bf16[592,128]{1,0:T(8,128)(2,1)S(1)}, u32[]{:S(2)}, u32[]{:S(2)}) collective-permute-start(bf16[592,128]{1,0:T(8,128)(2,1)S(1)} %get-tuple-element.40), channel_id=1, source_target_pairs={{0,8},{8,12},{12,4},{4,0},{1,9},{9,13},{13,5},{5,1},{2,10},{10,14}... | collective-permute-start | bytes 454664 | tf_op jit(solution)/shard_map/ppermute | solution.py:32
  9.2 0.0 copy-done
  9.2 0.1 constant_dynamic-slice_fusion
  9.2 0.1 reshape.294
  9.3 0.1 mul.22
  9.4 0.2 convert_reduce_fusion
  9.6 0.2 convert_reduce_fusion.1
  9.8 0.1 copy.34
  9.9 0.2 select_reduce_fusion
  10.1 1.8 %collective-permute-done.3.refs_0_.refs_8_ = bf16[576,256]{1,0:T(8,128)(2,1)S(1)} collective-permute-done((bf16[576,256]{1,0:T(8,128)(2,1)S(1)}, bf16[576,256]{1,0:T(8,128)(2,1)S(1)}, u32[]{:S(2)}, u32[]{:S(2)}) %collective-permute-start.3) | collective-permute-done | bytes 294944 | tf_op jit(solution)/shard_map/ppermute | solution.py:22
  11.9 0.0 collective-permute-start.4
  11.9 0.1 pad_slice_fusion
  12.0 0.1 pad_add_fusion
  12.0 0.1 reshape.295.refs_0_
  12.1 0.1 pad.40.clone
  12.2 0.0 collective-permute-done.2.refs_1_
  12.2 0.4 targets_0.1
  12.6 0.9 %collective-permute-done.4.refs_1_ = bf16[576,256]{1,0:T(8,128)(2,1)S(1)} collective-permute-done((bf16[576,256]{1,0:T(8,128)(2,1)S(1)}, bf16[576,256]{1,0:T(8,128)(2,1)S(1)}, u32[]{:S(2)}, u32[]{:S(2)}) %collective-permute-start.4) | collective-permute-done | bytes 294944 | tf_op jit(solution)/shard_map/ppermute | solution.py:22
  13.5 0.4 targets_1.1
  13.9 0.0 collective-permute-done.1
  13.9 0.2 collective-permute-done
  14.1 3.4 %collective-permute-start.7 = (bf16[1104,128]{1,0:T(8,128)(2,1)S(1)}, bf16[1104,128]{1,0:T(8,128)(2,1)S(1)}, u32[]{:S(2)}, u32[]{:S(2)}) collective-permute-start(bf16[1104,128]{1,0:T(8,128)(2,1)S(1)} %pad_maximum_fusion.refs_1_), channel_id=1, source_target_pairs={{0,8},{8,12},{12,4},{4,0},{1,9},{9,13},{13,5},{5,1},{2,10},{10,14}... | collective-permute-start | bytes 847880 | tf_op jit(solution)/shard_map/ppermute | solution.py:32
  17.5 0.0 collective-permute-start.6
  17.5 0.8 %collective-permute-start.5 = (bf16[592,128]{1,0:T(8,128)(2,1)S(1)}, bf16[592,128]{1,0:T(8,128)(2,1)S(1)}, u32[]{:S(2)}, u32[]{:S(2)}) collective-permute-start(bf16[592,128]{1,0:T(8,128)(2,1)S(1)} %get-tuple-element.40), channel_id=1, source_target_pairs={{0,4},{8,0},{12,8},{4,12},{1,5},{9,1},{13,9},{5,13},{2,6},{10,2},{... | collective-permute-start | bytes 454664 | tf_op jit(solution)/shard_map/ppermute | solution.py:32
  18.4 8.1 %near_field_0.1 = (f32[16,80,512]{2,1,0:T(8,128)S(1)}, f32[3,16,128]{2,1,0:T(8,128)S(1)}) custom-call(s32[108]{0:T(128)S(1)} %reshape.295.refs_0_, bf16[1104,128]{1,0:T(8,128)(2,1)S(1)} %pad_maximum_fusion.refs_1_, bf16[16,256,128]{2,1,0:T(8,128)(2,1)S(1)} %get-tuple-element.43.refs_2_, bf16[16,256,128]{2,1,0:T(8,128)(2,1)S(1)} %get-tuple-element.44.refs_3_, ...), custom_call_target="tpu_custom_call" | custom-call | flops 692060160 | bytes 6291456 | tf_op jit(solution)/shard_map/near_field_0/pallas_call | solution.py:290
  26.5 0.0 collective-permute-done.7.refs_1_
  26.5 8.1 %near_field_1.1 = (f32[16,80,512]{2,1,0:T(8,128)S(1)}, f32[3,16,128]{2,1,0:T(8,128)S(1)}) custom-call(s32[108]{0:T(128)S(1)} %reshape.295.refs_0_, bf16[1104,128]{1,0:T(8,128)(2,1)S(1)} %collective-permute-done.7.refs_1_, bf16[16,256,128]{2,1,0:T(8,128)(2,1)S(1)} %get-tuple-element.43.refs_2_, bf16[16,256,128]{2,1,0:T(8,128)(2,1)S(1)} %get-tuple-element.44.refs_3_, ...), custom_call_target="tpu_custom_call" | custom-call | flops 692060160 | bytes 6291456 | tf_op jit(solution)/shard_map/near_field_1/pallas_call | solution.py:290
  34.6 0.0 collective-permute-done.6
  34.6 0.0 collective-permute-done.5
  34.7 6.1 %near_field_2.1 = (f32[16,32,512]{2,1,0:T(8,128)S(1)}, bf16[16,32,512]{2,1,0:T(8,128)(2,1)S(1)}, f32[3,16,512]{2,1,0:T(8,128)S(1)}, f32[3,16,128]{2,1,0:T(8,128)S(1)}) custom-call(s32[108]{0:T(128)S(1)} %reshape.295.refs_0_, bf16[1104,128]{1,0:T(8,128)(2,1)S(1)} %pad_maximum_fusion.1.refs_1_, bf16[16,256,128]{2,1,0:T(8,128)(2,1)S(1)} %get-tuple-element.43.refs_2_, ...), custom_call_target="tpu_custom_call" | custom-call | flops 692060160 | bytes 6291456 | tf_op jit(solution)/shard_map/near_field_2/pallas_call | solution.py:290
  40.8 0.1 copy.38
  40.9 0.1 maximum_maximum_fusion
  41.0 2.9 %collective-permute-start.10 = (f32[56,128]{1,0:T(8,128)S(1)}, f32[56,128]{1,0:T(8,128)S(1)}, u32[]{:S(2)}, u32[]{:S(2)}) collective-permute-start(f32[56,128]{1,0:T(8,128)S(1)} %get-tuple-element.89), channel_id=1, source_target_pairs={{0,4},{8,0},{12,8},{4,12},{1,5},{9,1},{13,9},{5,13},{2,6},{10,2},{... | collective-permute-start | bytes 86024 | tf_op jit(solution)/shard_map/ppermute | solution.py:32
  43.9 2.4 %collective-permute-start.11 = (f32[56,128]{1,0:T(8,128)S(1)}, f32[56,128]{1,0:T(8,128)S(1)}, u32[]{:S(2)}, u32[]{:S(2)}) collective-permute-start(f32[56,128]{1,0:T(8,128)S(1)} %get-tuple-element.90), channel_id=1, source_target_pairs={{0,12},{8,4},{12,0},{4,8},{1,13},{9,5},{13,1},{5,9},{2,14},{10,6},... | collective-permute-start | bytes 86024 | tf_op jit(solution)/shard_map/ppermute | solution.py:32
  46.3 0.0 collective-permute-start.12
  46.3 0.0 collective-permute-start.8
  46.4 0.3 collective-permute-done.10
  46.7 2.9 %collective-permute-done.11 = f32[56,128]{1,0:T(8,128)S(1)} collective-permute-done((f32[56,128]{1,0:T(8,128)S(1)}, f32[56,128]{1,0:T(8,128)S(1)}, u32[]{:S(2)}, u32[]{:S(2)}) %collective-permute-start.11) | collective-permute-done | bytes 28704 | tf_op jit(solution)/shard_map/ppermute | solution.py:32
  49.6 0.6 %collective-permute-done.12 = f32[56,128]{1,0:T(8,128)S(1)} collective-permute-done((f32[56,128]{1,0:T(8,128)S(1)}, f32[56,128]{1,0:T(8,128)S(1)}, u32[]{:S(2)}, u32[]{:S(2)}) %collective-permute-start.12) | collective-permute-done | bytes 28704 | tf_op jit(solution)/shard_map/ppermute | solution.py:32
  50.3 0.0 collective-permute-done.8
  50.3 0.2 convert_add_fusion
  50.8 0.8 %collective-permute-start.13 = (f32[4,8,512]{2,1,0:T(8,128)S(1)}, f32[4,8,512]{2,1,0:T(8,128)S(1)}, u32[]{:S(2)}, u32[]{:S(2)}) collective-permute-start(f32[4,8,512]{2,1,0:T(8,128)S(1)} %fusion), channel_id=1, source_target_pairs={{0,2},{2,0},{1,3},{3,1},{4,6},{6,4},{5,7},{7,5},{8,10},{10,8},{9,1... | collective-permute-start | bytes 196616 | tf_op jit(solution)/shard_map/ppermute | solution.py:22
  51.6 1.4 %collective-permute-start.9 = (bf16[16,32,256]{2,1,0:T(8,128)(2,1)S(1)}, bf16[16,32,256]{2,1,0:T(8,128)(2,1)S(1)}, u32[]{:S(2)}, u32[]{:S(2)}) collective-permute-start(bf16[16,32,256]{2,1,0:T(8,128)(2,1)S(1)} %slice.307), channel_id=1, source_target_pairs={{0,2},{2,0},{1,3},{3,1},{4,6},{6,4},{5,7},{7,5},{8,10},{10,8},{9,1... | collective-permute-start | bytes 786440 | tf_op jit(solution)/shard_map/ppermute | solution.py:22
  53.0 2.7 %collective-permute-done.13 = f32[4,8,512]{2,1,0:T(8,128)S(1)} collective-permute-done((f32[4,8,512]{2,1,0:T(8,128)S(1)}, f32[4,8,512]{2,1,0:T(8,128)S(1)}, u32[]{:S(2)}, u32[]{:S(2)}) %collective-permute-start.13) | collective-permute-done | bytes 65568 | tf_op jit(solution)/shard_map/ppermute | solution.py:22
  55.7 0.1 collective-permute-start.14
  55.8 1.2 %collective-permute-done.14 = f32[4,8,512]{2,1,0:T(8,128)S(1)} collective-permute-done((f32[4,8,512]{2,1,0:T(8,128)S(1)}, f32[4,8,512]{2,1,0:T(8,128)S(1)}, u32[]{:S(2)}, u32[]{:S(2)}) %collective-permute-start.14) | collective-permute-done | bytes 65568 | tf_op jit(solution)/shard_map/ppermute | solution.py:22
  57.0 1.3 %node_terms.1 = f32[3,4096]{1,0:T(4,128)} custom-call(f32[3,8,512]{2,1,0:T(8,128)S(1)} %slice.197.grad_ref, s32[8,512]{1,0:T(8,128)S(1)} %slice_select_fusion.2.jitter_ref, f32[8,512]{1,0:T(8,128)S(1)} %slice_bitcast_fusion.edge_ref), custom_call_target="tpu_custom_call" | custom-call | flops 1048576 | bytes 262144 | tf_op jit(solution)/shard_map/node_terms/pallas_call | solution.py:569
  58.4 0.1 collective-permute-done.9.refs_1_
  58.5 0.7 %potential_sum.1 = bf16[16,32,256]{2,1,0:T(8,128)(2,1)} custom-call(f32[16,32,256]{2,1,0:T(8,128)S(1)} %slice.127.refs_0_, bf16[16,32,256]{2,1,0:T(8,128)(2,1)S(1)} %collective-permute-done.9.refs_1_), custom_call_target="tpu_custom_call" | custom-call | flops 1048576 | bytes 262144 | tf_op jit(solution)/shard_map/potential_sum/pallas_call | solution.py:578
  (47 shorter events, 0.6 us)
Async XLA Ops:
  0.6 8.5 %copy-start = (s32[5,64]{1,0:T(8,128)S(1)}, s32[5,64]{1,0:T(8,128)}, u32[]{:S(2)}) copy-start(s32[5,64]{1,0:T(8,128)} %param.10) | copy-start | bytes 3844
  1.9 10.0 %collective-permute-start.3 = (bf16[576,256]{1,0:T(8,128)(2,1)S(1)}, bf16[576,256]{1,0:T(8,128)(2,1)S(1)}, u32[]{:S(2)}, u32[]{:S(2)}) collective-permute-start(bf16[576,256]{1,0:T(8,128)(2,1)S(1)} %get-tuple-element.33.refs_0_.refs_7_), channel_id=1, source_target_pairs={{0,2},{2,0},{1,3},{3,1},{4,6},{6,4},{5,7},{7,5},{8,10},{10,8},{9,1... | collective-permute-start | bytes 884744 | tf_op jit(solution)/shard_map/ppermute | solution.py:22
  4.9 7.3 %collective-permute-start.2 = (bf16[576,256]{1,0:T(8,128)(2,1)S(1)}, bf16[576,256]{1,0:T(8,128)(2,1)S(1)}, u32[]{:S(2)}, u32[]{:S(2)}) collective-permute-start(bf16[576,256]{1,0:T(8,128)(2,1)S(1)} %get-tuple-element.33.refs_0_.refs_7_), channel_id=1, source_target_pairs={{0,1},{1,0},{2,3},{3,2},{4,5},{5,4},{6,7},{7,6},{8,9},{9,8},{10,11... | collective-permute-start | bytes 884744 | tf_op jit(solution)/shard_map/ppermute | solution.py:22
  4.9 9.0 %collective-permute-start.1 = (bf16[512,128]{1,0:T(8,128)(2,1)S(1)}, bf16[512,128]{1,0:T(8,128)(2,1)S(1)}, u32[]{:S(2)}, u32[]{:S(2)}) collective-permute-start(bf16[512,128]{1,0:T(8,128)(2,1)S(1)} %get-tuple-element.41), channel_id=1, source_target_pairs={{0,9},{1,8},{4,1},{5,0},{8,13},{9,12},{12,5},{13,4},{2,11},{3,10},... | collective-permute-start | bytes 393224 | tf_op jit(solution)/shard_map/ppermute | solution.py:44
  7.6 6.5 %collective-permute-start = (bf16[592,128]{1,0:T(8,128)(2,1)S(1)}, bf16[592,128]{1,0:T(8,128)(2,1)S(1)}, u32[]{:S(2)}, u32[]{:S(2)}) collective-permute-start(bf16[592,128]{1,0:T(8,128)(2,1)S(1)} %get-tuple-element.40), channel_id=1, source_target_pairs={{0,8},{8,12},{12,4},{4,0},{1,9},{9,13},{13,5},{5,1},{2,10},{10,14}... | collective-permute-start | bytes 454664 | tf_op jit(solution)/shard_map/ppermute | solution.py:32
  11.9 1.6 %collective-permute-start.4 = (bf16[576,256]{1,0:T(8,128)(2,1)S(1)}, bf16[576,256]{1,0:T(8,128)(2,1)S(1)}, u32[]{:S(2)}, u32[]{:S(2)}) collective-permute-start(bf16[576,256]{1,0:T(8,128)(2,1)S(1)} %collective-permute-done.3.refs_0_.refs_8_), channel_id=1, source_target_pairs={{0,1},{1,0},{2,3},{3,2},{4,5},{5,4},{6,7},{7,6},{8,9},{9,8},{10,11... | collective-permute-start | bytes 884744 | tf_op jit(solution)/shard_map/ppermute | solution.py:22
  14.1 12.4 %collective-permute-start.7 = (bf16[1104,128]{1,0:T(8,128)(2,1)S(1)}, bf16[1104,128]{1,0:T(8,128)(2,1)S(1)}, u32[]{:S(2)}, u32[]{:S(2)}) collective-permute-start(bf16[1104,128]{1,0:T(8,128)(2,1)S(1)} %pad_maximum_fusion.refs_1_), channel_id=1, source_target_pairs={{0,8},{8,12},{12,4},{4,0},{1,9},{9,13},{13,5},{5,1},{2,10},{10,14}... | collective-permute-start | bytes 847880 | tf_op jit(solution)/shard_map/ppermute | solution.py:32
  17.5 17.1 %collective-permute-start.6 = (bf16[512,128]{1,0:T(8,128)(2,1)S(1)}, bf16[512,128]{1,0:T(8,128)(2,1)S(1)}, u32[]{:S(2)}, u32[]{:S(2)}) collective-permute-start(bf16[512,128]{1,0:T(8,128)(2,1)S(1)} %get-tuple-element.41), channel_id=1, source_target_pairs={{0,5},{1,4},{4,13},{5,12},{8,1},{9,0},{12,9},{13,8},{2,7},{3,6},{6... | collective-permute-start | bytes 393224 | tf_op jit(solution)/shard_map/ppermute | solution.py:44
  17.5 17.1 %collective-permute-start.5 = (bf16[592,128]{1,0:T(8,128)(2,1)S(1)}, bf16[592,128]{1,0:T(8,128)(2,1)S(1)}, u32[]{:S(2)}, u32[]{:S(2)}) collective-permute-start(bf16[592,128]{1,0:T(8,128)(2,1)S(1)} %get-tuple-element.40), channel_id=1, source_target_pairs={{0,4},{8,0},{12,8},{4,12},{1,5},{9,1},{13,9},{5,13},{2,6},{10,2},{... | collective-permute-start | bytes 454664 | tf_op jit(solution)/shard_map/ppermute | solution.py:32
  41.0 5.7 %collective-permute-start.10 = (f32[56,128]{1,0:T(8,128)S(1)}, f32[56,128]{1,0:T(8,128)S(1)}, u32[]{:S(2)}, u32[]{:S(2)}) collective-permute-start(f32[56,128]{1,0:T(8,128)S(1)} %get-tuple-element.89), channel_id=1, source_target_pairs={{0,4},{8,0},{12,8},{4,12},{1,5},{9,1},{13,9},{5,13},{2,6},{10,2},{... | collective-permute-start | bytes 86024 | tf_op jit(solution)/shard_map/ppermute | solution.py:32
  43.9 5.7 %collective-permute-start.11 = (f32[56,128]{1,0:T(8,128)S(1)}, f32[56,128]{1,0:T(8,128)S(1)}, u32[]{:S(2)}, u32[]{:S(2)}) collective-permute-start(f32[56,128]{1,0:T(8,128)S(1)} %get-tuple-element.90), channel_id=1, source_target_pairs={{0,12},{8,4},{12,0},{4,8},{1,13},{9,5},{13,1},{5,9},{2,14},{10,6},... | collective-permute-start | bytes 86024 | tf_op jit(solution)/shard_map/ppermute | solution.py:32
  46.3 3.9 %collective-permute-start.12 = (f32[56,128]{1,0:T(8,128)S(1)}, f32[56,128]{1,0:T(8,128)S(1)}, u32[]{:S(2)}, u32[]{:S(2)}) collective-permute-start(f32[56,128]{1,0:T(8,128)S(1)} %get-tuple-element.91), channel_id=1, source_target_pairs={{0,8},{8,12},{12,4},{4,0},{1,9},{9,13},{13,5},{5,1},{2,10},{10,14}... | collective-permute-start | bytes 86024 | tf_op jit(solution)/shard_map/ppermute | solution.py:32
  46.3 4.0 %collective-permute-start.8 = (bf16[16,32,512]{2,1,0:T(8,128)(2,1)S(1)}, bf16[16,32,512]{2,1,0:T(8,128)(2,1)S(1)}, u32[]{:S(2)}, u32[]{:S(2)}) collective-permute-start(bf16[16,32,512]{2,1,0:T(8,128)(2,1)S(1)} %get-tuple-element.53), channel_id=1, source_target_pairs={{0,1},{1,0},{2,3},{3,2},{4,5},{5,4},{6,7},{7,6},{8,9},{9,8},{10,11... | collective-permute-start | bytes 1572872 | tf_op jit(solution)/shard_map/ppermute | solution.py:22
  50.8 4.9 %collective-permute-start.13 = (f32[4,8,512]{2,1,0:T(8,128)S(1)}, f32[4,8,512]{2,1,0:T(8,128)S(1)}, u32[]{:S(2)}, u32[]{:S(2)}) collective-permute-start(f32[4,8,512]{2,1,0:T(8,128)S(1)} %fusion), channel_id=1, source_target_pairs={{0,2},{2,0},{1,3},{3,1},{4,6},{6,4},{5,7},{7,5},{8,10},{10,8},{9,1... | collective-permute-start | bytes 196616 | tf_op jit(solution)/shard_map/ppermute | solution.py:22
  51.6 6.9 %collective-permute-start.9 = (bf16[16,32,256]{2,1,0:T(8,128)(2,1)S(1)}, bf16[16,32,256]{2,1,0:T(8,128)(2,1)S(1)}, u32[]{:S(2)}, u32[]{:S(2)}) collective-permute-start(bf16[16,32,256]{2,1,0:T(8,128)(2,1)S(1)} %slice.307), channel_id=1, source_target_pairs={{0,2},{2,0},{1,3},{3,1},{4,6},{6,4},{5,7},{7,5},{8,10},{10,8},{9,1... | collective-permute-start | bytes 786440 | tf_op jit(solution)/shard_map/ppermute | solution.py:22
  55.7 1.3 %collective-permute-start.14 = (f32[4,8,512]{2,1,0:T(8,128)S(1)}, f32[4,8,512]{2,1,0:T(8,128)S(1)}, u32[]{:S(2)}, u32[]{:S(2)}) collective-permute-start(f32[4,8,512]{2,1,0:T(8,128)S(1)} %select_add_fusion), channel_id=1, source_target_pairs={{0,1},{1,0},{2,3},{3,2},{4,5},{5,4},{6,7},{7,6},{8,9},{9,8},{10,11... | collective-permute-start | bytes 196616 | tf_op jit(solution)/shard_map/ppermute | solution.py:22

commit v15 on v14

--- a/solution.py
+++ b/solution.py
@@ -230,15 +230,15 @@
     columns_a, columns_b = slice(0, 2 * quarter), slice(2 * quarter, 4 * quarter)
 
     @pl.loop(0, items[step * length])
-    def _(pair):
-        turn = 2 * pair + 1
-        summed(turn, left_a, columns_a)
-        pointwise(turn + 1, raw_b, backward, (halves[3], halves[2]))
-        products(turn + 2, left_a, raw_a)
-        source_sums(turn)
-        summed(turn + 1, left_b, columns_b)
-        pointwise(turn + 2, raw_a, forward, (halves[0], halves[1]))
-        products(turn + 3, left_b, raw_b)
+    def _(four):
+        for turn in (4 * four + 1, 4 * four + 3):
+            summed(turn, left_a, columns_a)
+            pointwise(turn + 1, raw_b, backward, (halves[3], halves[2]))
+            products(turn + 2, left_a, raw_a)
+            source_sums(turn)
+            summed(turn + 1, left_b, columns_b)
+            pointwise(turn + 2, raw_a, forward, (halves[0], halves[1]))
+            products(turn + 3, left_b, raw_b)
 
     for coord in range(3):
         back_ref[coord] = -0.5 * back[:, coord, :] - there[coord] * back[:, 6, :]
@@ -286,7 +286,7 @@
         scratch = [pltpu.VMEM(acc_shape, jnp.float32)] + scratch
     else:
         out_shape = (jax.ShapeDtypeStruct(acc_shape, jnp.float32), back_shape)
-    pairs = (length - 6) * panels * quarter
+    pairs = (length - 10) * panels * quarter
     return pl.pallas_call(
         functools.partial(step_kernel, step, length, rhs, subs, first, last),
         out_shape=out_shape,
@@ -417,10 +417,10 @@
     slots = jnp.arange(cap, dtype=jnp.int32)
     chosen = member[:, None, :] & (rank[None, None, :] == slots[None, :, None])
     listed = jnp.sum(jnp.where(chosen, code[None, None, :] - clusters, 0), axis=2) + clusters
-    turns = (jnp.sum(member.astype(jnp.int32), axis=1) + 3) // 2
-    length = cap + 6
-    items = jnp.pad(listed, ((0, 0), (3, 3)), constant_values=clusters)
-    items = jnp.concatenate([turns[:, None], items[:, 1:]], axis=1).reshape(-1)
+    fours = (jnp.sum(member.astype(jnp.int32), axis=1) + 5) // 4
+    length = cap + 10
+    items = jnp.pad(listed, ((0, 0), (3, 7)), constant_values=clusters)
+    items = jnp.concatenate([fours[:, None], items[:, 1:]], axis=1).reshape(-1)
 
     locals_ = [local] + [shifted(local, "sub", step) for step in range(1, sub_count)]
     blocks = [

time: 59.2 us -> 62.6 us (1.057)
  Pallas kernels: 26.3 us -> 29.8 us
  starting transfers between devices: 19.1 us -> 18.4 us
    pallas_call x3, Pallas kernels: 22.2 us -> 25.8 us  [run_step(): pl.pallas_call(functools.partial(step_kernel, step, length, rhs, subs, fi...]
    ppermute x7, waiting for transfers between devices: 6.67 us -> 7.69 us  [shifted(): return lax.ppermute(value, axis, pairs)]
    ppermute x6, starting transfers between devices: 11.1 us -> 10.2 us  [round_ring(): return lax.ppermute(value, 'clus', pairs)]
  transfers between devices with their start and end apart: 15 -> 15, of which waited for: 9 -> 9; matrix products, arithmetic and copies ran while one was open for 3% -> 2% of each run, Pallas kernels for 31% -> 33%
where the time goes in v15:
time: 62.6 us; the launch traced here: 62.5 us
  Pallas kernels  29.8 us (48%)
  starting transfers between devices  18.4 us (29%)
  waiting for transfers between devices  11.1 us (18%)
  other arithmetic  1.23 us (2%)
  between operations  1.03 us (2%)
  local copies, waits for them, and re-layouts  0.91 us (1%)
    pallas_call x3, Pallas kernels, run_step(): pl.pallas_call(functools.partial(step_kernel, step, length, rhs, subs, fi...  25.8 us
    ppermute x6, starting transfers between devices, round_ring(): return lax.ppermute(value, 'clus', pairs)  10.2 us
    ppermute x7, waiting for transfers between devices, shifted(): return lax.ppermute(value, axis, pairs)  7.69 us
    ppermute x7, starting transfers between devices, shifted(): return lax.ppermute(value, axis, pairs)  5.44 us
    ppermute x6, waiting for transfers between devices, round_ring(): return lax.ppermute(value, 'clus', pairs)  3.39 us
    ppermute x2, starting transfers between devices, moved(): return lax.ppermute(value, axes, pairs)  2.7 us
    pallas_call x1, Pallas kernels, on_device(): pl.pallas_call(node_kernel, out_shape=jax.ShapeDtypeStruct((3, share * pa...  1.32 us
  transfers between devices with their start and end apart: 15, of which 9 were waited for; matrix products, arithmetic and copies ran while one was open for 2% of the time, Pallas kernels for 33%

profile of v15, /device:TPU:0, one launch (start us, length us, event | category | flops | bytes accessed | tf_op | source)
XLA Modules:
  0.0 62.5 jit_solution(4382041810627138054)
XLA Ops:
  0.6 0.0 copy-start
  0.6 1.2 %prepare.1 = (bf16[592,128]{1,0:T(8,128)(2,1)S(1)}, bf16[512,128]{1,0:T(8,128)(2,1)S(1)}, bf16[576,256]{1,0:T(8,128)(2,1)S(1)}) custom-call(bf16[16,32,256]{2,1,0:T(8,128)(2,1)} %refs_0_.1, bf16[3,16,256]{2,1,0:T(8,128)(2,1)} %bitcast.91, bf16[16,256]{1,0:T(8,128)(2,1)} %refs_2_.1, s32[16,4,256]{2,1,0:T(4,128)} %refs_3_.1, bf16[16,32,256]{2,1,0:T(8,128)(2,1)} %refs_4_.1), custom_call_target="tpu_custom_call" | custom-call | tf_op jit(solution)/shard_map/prepare/pallas_call | solution.py:377
  1.9 3.0 %collective-permute-start.3 = (bf16[576,256]{1,0:T(8,128)(2,1)S(1)}, bf16[576,256]{1,0:T(8,128)(2,1)S(1)}, u32[]{:S(2)}, u32[]{:S(2)}) collective-permute-start(bf16[576,256]{1,0:T(8,128)(2,1)S(1)} %get-tuple-element.33.refs_0_.refs_7_), channel_id=1, source_target_pairs={{0,2},{2,0},{1,3},{3,1},{4,6},{6,4},{5,7},{7,5},{8,10},{10,8},{9,1... | collective-permute-start | bytes 884744 | tf_op jit(solution)/shard_map/ppermute | solution.py:22
  4.9 0.0 collective-permute-start.2
  4.9 2.7 %collective-permute-start.1 = (bf16[512,128]{1,0:T(8,128)(2,1)S(1)}, bf16[512,128]{1,0:T(8,128)(2,1)S(1)}, u32[]{:S(2)}, u32[]{:S(2)}) collective-permute-start(bf16[512,128]{1,0:T(8,128)(2,1)S(1)} %get-tuple-element.41), channel_id=1, source_target_pairs={{0,9},{1,8},{4,1},{5,0},{8,13},{9,12},{12,5},{13,4},{2,11},{3,10},... | collective-permute-start | bytes 393224 | tf_op jit(solution)/shard_map/ppermute | solution.py:44
  7.6 1.6 %collective-permute-start = (bf16[592,128]{1,0:T(8,128)(2,1)S(1)}, bf16[592,128]{1,0:T(8,128)(2,1)S(1)}, u32[]{:S(2)}, u32[]{:S(2)}) collective-permute-start(bf16[592,128]{1,0:T(8,128)(2,1)S(1)} %get-tuple-element.40), channel_id=1, source_target_pairs={{0,8},{8,12},{12,4},{4,0},{1,9},{9,13},{13,5},{5,1},{2,10},{10,14}... | collective-permute-start | bytes 454664 | tf_op jit(solution)/shard_map/ppermute | solution.py:32
  9.2 0.0 copy-done
  9.2 0.1 constant_dynamic-slice_fusion
  9.2 0.1 reshape.294
  9.3 0.1 mul.22
  9.4 0.2 convert_reduce_fusion
  9.6 0.2 convert_reduce_fusion.1
  9.8 0.1 copy.34
  9.9 0.2 select_reduce_fusion
  10.1 1.8 %collective-permute-done.3.refs_0_.refs_8_ = bf16[576,256]{1,0:T(8,128)(2,1)S(1)} collective-permute-done((bf16[576,256]{1,0:T(8,128)(2,1)S(1)}, bf16[576,256]{1,0:T(8,128)(2,1)S(1)}, u32[]{:S(2)}, u32[]{:S(2)}) %collective-permute-start.3) | collective-permute-done | bytes 294944 | tf_op jit(solution)/shard_map/ppermute | solution.py:22
  11.9 0.0 collective-permute-start.4
  11.9 0.1 pad_slice_fusion
  12.0 0.1 pad_add_fusion
  12.0 0.1 reshape.295.refs_0_
  12.1 0.1 pad.40.clone
  12.2 0.0 collective-permute-done.2.refs_1_
  12.2 0.4 targets_0.1
  12.6 0.9 %collective-permute-done.4.refs_1_ = bf16[576,256]{1,0:T(8,128)(2,1)S(1)} collective-permute-done((bf16[576,256]{1,0:T(8,128)(2,1)S(1)}, bf16[576,256]{1,0:T(8,128)(2,1)S(1)}, u32[]{:S(2)}, u32[]{:S(2)}) %collective-permute-start.4) | collective-permute-done | bytes 294944 | tf_op jit(solution)/shard_map/ppermute | solution.py:22
  13.5 0.4 targets_1.1
  13.9 0.0 collective-permute-done.1
  13.9 0.2 collective-permute-done
  14.1 3.4 %collective-permute-start.7 = (bf16[1104,128]{1,0:T(8,128)(2,1)S(1)}, bf16[1104,128]{1,0:T(8,128)(2,1)S(1)}, u32[]{:S(2)}, u32[]{:S(2)}) collective-permute-start(bf16[1104,128]{1,0:T(8,128)(2,1)S(1)} %pad_maximum_fusion.refs_1_), channel_id=1, source_target_pairs={{0,8},{8,12},{12,4},{4,0},{1,9},{9,13},{13,5},{5,1},{2,10},{10,14}... | collective-permute-start | bytes 847880 | tf_op jit(solution)/shard_map/ppermute | solution.py:32
  17.5 0.0 collective-permute-start.6
  17.5 0.8 %collective-permute-start.5 = (bf16[592,128]{1,0:T(8,128)(2,1)S(1)}, bf16[592,128]{1,0:T(8,128)(2,1)S(1)}, u32[]{:S(2)}, u32[]{:S(2)}) collective-permute-start(bf16[592,128]{1,0:T(8,128)(2,1)S(1)} %get-tuple-element.40), channel_id=1, source_target_pairs={{0,4},{8,0},{12,8},{4,12},{1,5},{9,1},{13,9},{5,13},{2,6},{10,2},{... | collective-permute-start | bytes 454664 | tf_op jit(solution)/shard_map/ppermute | solution.py:32
  18.4 9.2 %near_field_0.1 = (f32[16,80,512]{2,1,0:T(8,128)S(1)}, f32[3,16,128]{2,1,0:T(8,128)S(1)}) custom-call(s32[120]{0:T(128)S(1)} %reshape.295.refs_0_, bf16[1104,128]{1,0:T(8,128)(2,1)S(1)} %pad_maximum_fusion.refs_1_, bf16[16,256,128]{2,1,0:T(8,128)(2,1)S(1)} %get-tuple-element.43.refs_2_, bf16[16,256,128]{2,1,0:T(8,128)(2,1)S(1)} %get-tuple-element.44.refs_3_, ...), custom_call_target="tpu_custom_call" | custom-call | flops 692060160 | bytes 6291456 | tf_op jit(solution)/shard_map/near_field_0/pallas_call | solution.py:290
  27.6 0.0 collective-permute-done.7.refs_1_
  27.6 9.2 %near_field_1.1 = (f32[16,80,512]{2,1,0:T(8,128)S(1)}, f32[3,16,128]{2,1,0:T(8,128)S(1)}) custom-call(s32[120]{0:T(128)S(1)} %reshape.295.refs_0_, bf16[1104,128]{1,0:T(8,128)(2,1)S(1)} %collective-permute-done.7.refs_1_, bf16[16,256,128]{2,1,0:T(8,128)(2,1)S(1)} %get-tuple-element.43.refs_2_, bf16[16,256,128]{2,1,0:T(8,128)(2,1)S(1)} %get-tuple-element.44.refs_3_, ...), custom_call_target="tpu_custom_call" | custom-call | flops 692060160 | bytes 6291456 | tf_op jit(solution)/shard_map/near_field_1/pallas_call | solution.py:290
  36.9 0.0 collective-permute-done.6
  36.9 0.0 collective-permute-done.5
  36.9 7.3 %near_field_2.1 = (f32[16,32,512]{2,1,0:T(8,128)S(1)}, bf16[16,32,512]{2,1,0:T(8,128)(2,1)S(1)}, f32[3,16,512]{2,1,0:T(8,128)S(1)}, f32[3,16,128]{2,1,0:T(8,128)S(1)}) custom-call(s32[120]{0:T(128)S(1)} %reshape.295.refs_0_, bf16[1104,128]{1,0:T(8,128)(2,1)S(1)} %pad_maximum_fusion.1.refs_1_, bf16[16,256,128]{2,1,0:T(8,128)(2,1)S(1)} %get-tuple-element.43.refs_2_, ...), custom_call_target="tpu_custom_call" | custom-call | flops 692060160 | bytes 6291456 | tf_op jit(solution)/shard_map/near_field_2/pallas_call | solution.py:290
  44.3 0.1 copy.38
  44.5 0.1 maximum_maximum_fusion
  44.6 1.6 %collective-permute-start.10 = (f32[56,128]{1,0:T(8,128)S(1)}, f32[56,128]{1,0:T(8,128)S(1)}, u32[]{:S(2)}, u32[]{:S(2)}) collective-permute-start(f32[56,128]{1,0:T(8,128)S(1)} %get-tuple-element.89), channel_id=1, source_target_pairs={{0,4},{8,0},{12,8},{4,12},{1,5},{9,1},{13,9},{5,13},{2,6},{10,2},{... | collective-permute-start | bytes 86024 | tf_op jit(solution)/shard_map/ppermute | solution.py:32
  46.1 2.4 %collective-permute-start.11 = (f32[56,128]{1,0:T(8,128)S(1)}, f32[56,128]{1,0:T(8,128)S(1)}, u32[]{:S(2)}, u32[]{:S(2)}) collective-permute-start(f32[56,128]{1,0:T(8,128)S(1)} %get-tuple-element.90), channel_id=1, source_target_pairs={{0,12},{8,4},{12,0},{4,8},{1,13},{9,5},{13,1},{5,9},{2,14},{10,6},... | collective-permute-start | bytes 86024 | tf_op jit(solution)/shard_map/ppermute | solution.py:32
  48.5 0.4 collective-permute-start.12
  48.9 0.2 collective-permute-start.8
  49.2 0.5 collective-permute-done.10
  49.7 2.4 %collective-permute-done.11 = f32[56,128]{1,0:T(8,128)S(1)} collective-permute-done((f32[56,128]{1,0:T(8,128)S(1)}, f32[56,128]{1,0:T(8,128)S(1)}, u32[]{:S(2)}, u32[]{:S(2)}) %collective-permute-start.11) | collective-permute-done | bytes 28704 | tf_op jit(solution)/shard_map/ppermute | solution.py:32
  52.0 0.4 collective-permute-done.12
  52.5 0.0 collective-permute-done.8
  52.6 0.2 convert_add_fusion
  53.0 1.1 %collective-permute-start.13 = (f32[4,8,512]{2,1,0:T(8,128)S(1)}, f32[4,8,512]{2,1,0:T(8,128)S(1)}, u32[]{:S(2)}, u32[]{:S(2)}) collective-permute-start(f32[4,8,512]{2,1,0:T(8,128)S(1)} %fusion), channel_id=1, source_target_pairs={{0,2},{2,0},{1,3},{3,1},{4,6},{6,4},{5,7},{7,5},{8,10},{10,8},{9,1... | collective-permute-start | bytes 196616 | tf_op jit(solution)/shard_map/ppermute | solution.py:22
  54.1 1.1 %collective-permute-start.9 = (bf16[16,32,256]{2,1,0:T(8,128)(2,1)S(1)}, bf16[16,32,256]{2,1,0:T(8,128)(2,1)S(1)}, u32[]{:S(2)}, u32[]{:S(2)}) collective-permute-start(bf16[16,32,256]{2,1,0:T(8,128)(2,1)S(1)} %slice.307), channel_id=1, source_target_pairs={{0,2},{2,0},{1,3},{3,1},{4,6},{6,4},{5,7},{7,5},{8,10},{10,8},{9,1... | collective-permute-start | bytes 786440 | tf_op jit(solution)/shard_map/ppermute | solution.py:22
  55.2 2.9 %collective-permute-done.13 = f32[4,8,512]{2,1,0:T(8,128)S(1)} collective-permute-done((f32[4,8,512]{2,1,0:T(8,128)S(1)}, f32[4,8,512]{2,1,0:T(8,128)S(1)}, u32[]{:S(2)}, u32[]{:S(2)}) %collective-permute-start.13) | collective-permute-done | bytes 65568 | tf_op jit(solution)/shard_map/ppermute | solution.py:22
  58.1 0.1 collective-permute-start.14
  58.2 1.2 %collective-permute-done.14 = f32[4,8,512]{2,1,0:T(8,128)S(1)} collective-permute-done((f32[4,8,512]{2,1,0:T(8,128)S(1)}, f32[4,8,512]{2,1,0:T(8,128)S(1)}, u32[]{:S(2)}, u32[]{:S(2)}) %collective-permute-start.14) | collective-permute-done | bytes 65568 | tf_op jit(solution)/shard_map/ppermute | solution.py:22
  59.4 1.3 %node_terms.1 = f32[3,4096]{1,0:T(4,128)} custom-call(f32[3,8,512]{2,1,0:T(8,128)S(1)} %slice.197.grad_ref, s32[8,512]{1,0:T(8,128)S(1)} %slice_select_fusion.2.jitter_ref, f32[8,512]{1,0:T(8,128)S(1)} %slice_bitcast_fusion.edge_ref), custom_call_target="tpu_custom_call" | custom-call | flops 1048576 | bytes 262144 | tf_op jit(solution)/shard_map/node_terms/pallas_call | solution.py:569
  60.7 1.0 %collective-permute-done.9.refs_1_ = bf16[16,32,256]{2,1,0:T(8,128)(2,1)S(1)} collective-permute-done((bf16[16,32,256]{2,1,0:T(8,128)(2,1)S(1)}, bf16[16,32,256]{2,1,0:T(8,128)(2,1)S(1)}, u32[]{:S(2)}, u32[]{:S(2)}) %collective-permute-start.9) | collective-permute-done | bytes 262176 | tf_op jit(solution)/shard_map/ppermute | solution.py:22
  61.7 0.7 %potential_sum.1 = bf16[16,32,256]{2,1,0:T(8,128)(2,1)} custom-call(f32[16,32,256]{2,1,0:T(8,128)S(1)} %slice.127.refs_0_, bf16[16,32,256]{2,1,0:T(8,128)(2,1)S(1)} %collective-permute-done.9.refs_1_), custom_call_target="tpu_custom_call" | custom-call | flops 1048576 | bytes 262144 | tf_op jit(solution)/shard_map/potential_sum/pallas_call | solution.py:578
  (47 shorter events, 0.6 us)
Async XLA Ops:
  0.6 8.5 %copy-start = (s32[5,64]{1,0:T(8,128)S(1)}, s32[5,64]{1,0:T(8,128)}, u32[]{:S(2)}) copy-start(s32[5,64]{1,0:T(8,128)} %param.10) | copy-start | bytes 3844
  1.9 10.0 %collective-permute-start.3 = (bf16[576,256]{1,0:T(8,128)(2,1)S(1)}, bf16[576,256]{1,0:T(8,128)(2,1)S(1)}, u32[]{:S(2)}, u32[]{:S(2)}) collective-permute-start(bf16[576,256]{1,0:T(8,128)(2,1)S(1)} %get-tuple-element.33.refs_0_.refs_7_), channel_id=1, source_target_pairs={{0,2},{2,0},{1,3},{3,1},{4,6},{6,4},{5,7},{7,5},{8,10},{10,8},{9,1... | collective-permute-start | bytes 884744 | tf_op jit(solution)/shard_map/ppermute | solution.py:22
  4.9 7.3 %collective-permute-start.2 = (bf16[576,256]{1,0:T(8,128)(2,1)S(1)}, bf16[576,256]{1,0:T(8,128)(2,1)S(1)}, u32[]{:S(2)}, u32[]{:S(2)}) collective-permute-start(bf16[576,256]{1,0:T(8,128)(2,1)S(1)} %get-tuple-element.33.refs_0_.refs_7_), channel_id=1, source_target_pairs={{0,1},{1,0},{2,3},{3,2},{4,5},{5,4},{6,7},{7,6},{8,9},{9,8},{10,11... | collective-permute-start | bytes 884744 | tf_op jit(solution)/shard_map/ppermute | solution.py:22
  4.9 9.0 %collective-permute-start.1 = (bf16[512,128]{1,0:T(8,128)(2,1)S(1)}, bf16[512,128]{1,0:T(8,128)(2,1)S(1)}, u32[]{:S(2)}, u32[]{:S(2)}) collective-permute-start(bf16[512,128]{1,0:T(8,128)(2,1)S(1)} %get-tuple-element.41), channel_id=1, source_target_pairs={{0,9},{1,8},{4,1},{5,0},{8,13},{9,12},{12,5},{13,4},{2,11},{3,10},... | collective-permute-start | bytes 393224 | tf_op jit(solution)/shard_map/ppermute | solution.py:44
  7.6 6.5 %collective-permute-start = (bf16[592,128]{1,0:T(8,128)(2,1)S(1)}, bf16[592,128]{1,0:T(8,128)(2,1)S(1)}, u32[]{:S(2)}, u32[]{:S(2)}) collective-permute-start(bf16[592,128]{1,0:T(8,128)(2,1)S(1)} %get-tuple-element.40), channel_id=1, source_target_pairs={{0,8},{8,12},{12,4},{4,0},{1,9},{9,13},{13,5},{5,1},{2,10},{10,14}... | collective-permute-start | bytes 454664 | tf_op jit(solution)/shard_map/ppermute | solution.py:32
  11.9 1.6 %collective-permute-start.4 = (bf16[576,256]{1,0:T(8,128)(2,1)S(1)}, bf16[576,256]{1,0:T(8,128)(2,1)S(1)}, u32[]{:S(2)}, u32[]{:S(2)}) collective-permute-start(bf16[576,256]{1,0:T(8,128)(2,1)S(1)} %collective-permute-done.3.refs_0_.refs_8_), channel_id=1, source_target_pairs={{0,1},{1,0},{2,3},{3,2},{4,5},{5,4},{6,7},{7,6},{8,9},{9,8},{10,11... | collective-permute-start | bytes 884744 | tf_op jit(solution)/shard_map/ppermute | solution.py:22
  14.1 13.6 %collective-permute-start.7 = (bf16[1104,128]{1,0:T(8,128)(2,1)S(1)}, bf16[1104,128]{1,0:T(8,128)(2,1)S(1)}, u32[]{:S(2)}, u32[]{:S(2)}) collective-permute-start(bf16[1104,128]{1,0:T(8,128)(2,1)S(1)} %pad_maximum_fusion.refs_1_), channel_id=1, source_target_pairs={{0,8},{8,12},{12,4},{4,0},{1,9},{9,13},{13,5},{5,1},{2,10},{10,14}... | collective-permute-start | bytes 847880 | tf_op jit(solution)/shard_map/ppermute | solution.py:32
  17.5 19.4 %collective-permute-start.6 = (bf16[512,128]{1,0:T(8,128)(2,1)S(1)}, bf16[512,128]{1,0:T(8,128)(2,1)S(1)}, u32[]{:S(2)}, u32[]{:S(2)}) collective-permute-start(bf16[512,128]{1,0:T(8,128)(2,1)S(1)} %get-tuple-element.41), channel_id=1, source_target_pairs={{0,5},{1,4},{4,13},{5,12},{8,1},{9,0},{12,9},{13,8},{2,7},{3,6},{6... | collective-permute-start | bytes 393224 | tf_op jit(solution)/shard_map/ppermute | solution.py:44
  17.5 19.4 %collective-permute-start.5 = (bf16[592,128]{1,0:T(8,128)(2,1)S(1)}, bf16[592,128]{1,0:T(8,128)(2,1)S(1)}, u32[]{:S(2)}, u32[]{:S(2)}) collective-permute-start(bf16[592,128]{1,0:T(8,128)(2,1)S(1)} %get-tuple-element.40), channel_id=1, source_target_pairs={{0,4},{8,0},{12,8},{4,12},{1,5},{9,1},{13,9},{5,13},{2,6},{10,2},{... | collective-permute-start | bytes 454664 | tf_op jit(solution)/shard_map/ppermute | solution.py:32
  44.6 5.1 %collective-permute-start.10 = (f32[56,128]{1,0:T(8,128)S(1)}, f32[56,128]{1,0:T(8,128)S(1)}, u32[]{:S(2)}, u32[]{:S(2)}) collective-permute-start(f32[56,128]{1,0:T(8,128)S(1)} %get-tuple-element.89), channel_id=1, source_target_pairs={{0,4},{8,0},{12,8},{4,12},{1,5},{9,1},{13,9},{5,13},{2,6},{10,2},{... | collective-permute-start | bytes 86024 | tf_op jit(solution)/shard_map/ppermute | solution.py:32
  46.1 5.9 %collective-permute-start.11 = (f32[56,128]{1,0:T(8,128)S(1)}, f32[56,128]{1,0:T(8,128)S(1)}, u32[]{:S(2)}, u32[]{:S(2)}) collective-permute-start(f32[56,128]{1,0:T(8,128)S(1)} %get-tuple-element.90), channel_id=1, source_target_pairs={{0,12},{8,4},{12,0},{4,8},{1,13},{9,5},{13,1},{5,9},{2,14},{10,6},... | collective-permute-start | bytes 86024 | tf_op jit(solution)/shard_map/ppermute | solution.py:32
  48.5 3.9 %collective-permute-start.12 = (f32[56,128]{1,0:T(8,128)S(1)}, f32[56,128]{1,0:T(8,128)S(1)}, u32[]{:S(2)}, u32[]{:S(2)}) collective-permute-start(f32[56,128]{1,0:T(8,128)S(1)} %get-tuple-element.91), channel_id=1, source_target_pairs={{0,8},{8,12},{12,4},{4,0},{1,9},{9,13},{13,5},{5,1},{2,10},{10,14}... | collective-permute-start | bytes 86024 | tf_op jit(solution)/shard_map/ppermute | solution.py:32
  48.9 3.6 %collective-permute-start.8 = (bf16[16,32,512]{2,1,0:T(8,128)(2,1)S(1)}, bf16[16,32,512]{2,1,0:T(8,128)(2,1)S(1)}, u32[]{:S(2)}, u32[]{:S(2)}) collective-permute-start(bf16[16,32,512]{2,1,0:T(8,128)(2,1)S(1)} %get-tuple-element.53), channel_id=1, source_target_pairs={{0,1},{1,0},{2,3},{3,2},{4,5},{5,4},{6,7},{7,6},{8,9},{9,8},{10,11... | collective-permute-start | bytes 1572872 | tf_op jit(solution)/shard_map/ppermute | solution.py:22
  53.0 5.1 %collective-permute-start.13 = (f32[4,8,512]{2,1,0:T(8,128)S(1)}, f32[4,8,512]{2,1,0:T(8,128)S(1)}, u32[]{:S(2)}, u32[]{:S(2)}) collective-permute-start(f32[4,8,512]{2,1,0:T(8,128)S(1)} %fusion), channel_id=1, source_target_pairs={{0,2},{2,0},{1,3},{3,1},{4,6},{6,4},{5,7},{7,5},{8,10},{10,8},{9,1... | collective-permute-start | bytes 196616 | tf_op jit(solution)/shard_map/ppermute | solution.py:22
  54.1 7.6 %collective-permute-start.9 = (bf16[16,32,256]{2,1,0:T(8,128)(2,1)S(1)}, bf16[16,32,256]{2,1,0:T(8,128)(2,1)S(1)}, u32[]{:S(2)}, u32[]{:S(2)}) collective-permute-start(bf16[16,32,256]{2,1,0:T(8,128)(2,1)S(1)} %slice.307), channel_id=1, source_target_pairs={{0,2},{2,0},{1,3},{3,1},{4,6},{6,4},{5,7},{7,5},{8,10},{10,8},{9,1... | collective-permute-start | bytes 786440 | tf_op jit(solution)/shard_map/ppermute | solution.py:22
  58.1 1.3 %collective-permute-start.14 = (f32[4,8,512]{2,1,0:T(8,128)S(1)}, f32[4,8,512]{2,1,0:T(8,128)S(1)}, u32[]{:S(2)}, u32[]{:S(2)}) collective-permute-start(f32[4,8,512]{2,1,0:T(8,128)S(1)} %select_add_fusion), channel_id=1, source_target_pairs={{0,1},{1,0},{2,3},{3,2},{4,5},{5,4},{6,7},{7,6},{8,9},{9,8},{10,11... | collective-permute-start | bytes 196616 | tf_op jit(solution)/shard_map/ppermute | solution.py:22

commit v16 on v14

--- a/solution.py
+++ b/solution.py
@@ -188,27 +188,30 @@
         code = items[step * length + place]
         return code // (2 * clusters), code % (2 * clusters)
 
-    def products(place, left, raw):
+    part = max(2 * LANES, panels // 2)
+    spans = [slice(start, start + part) for start in range(0, panels, part)]
+
+    def products(place, left, raw, span):
         here, mate = decoded(place)
-        lhs = jnp.concatenate([ref[here] for ref in lhs_refs], axis=0)
-        raw[...] = jnp.dot(lhs, left[mate % clusters], preferred_element_type=jnp.float32)
-
-    def pointwise(place, raw, raw_halves, both_halves):
+        lhs = jnp.concatenate([ref[here] for ref in lhs_refs], axis=0)[span]
+        raw[span, :] = jnp.dot(lhs, left[mate % clusters], preferred_element_type=jnp.float32)
+
+    def pointwise(place, raw, raw_halves, both_halves, span):
         _, mate = decoded(place)
         scale = weight[pl.ds(mate, 1), :]
-        for start in range(0, panels, LANES):
-            span = slice(start, start + LANES)
-            inverse = lax.rsqrt(raw[span, raw_halves[1]])
+        for start in range(span.start, span.stop, LANES):
+            piece = slice(start, start + LANES)
+            inverse = lax.rsqrt(raw[piece, raw_halves[1]])
             kernel = scale * inverse
-            both[span, both_halves[0]] = kernel.astype(jnp.bfloat16)
-            weighted = (inverse * inverse) * (kernel * raw[span, raw_halves[0]])
-            both[span, both_halves[1]] = weighted.astype(jnp.bfloat16)
-
-    def summed(place, left, columns):
+            both[piece, both_halves[0]] = kernel.astype(jnp.bfloat16)
+            weighted = (inverse * inverse) * (kernel * raw[piece, raw_halves[0]])
+            both[piece, both_halves[1]] = weighted.astype(jnp.bfloat16)
+
+    def summed(place, left, columns, span):
         here, mate = decoded(place)
-        acc[here] += lax.dot_general(
+        acc[here, :, span] += lax.dot_general(
             left[mate % clusters, :rows, :],
-            both[:, columns],
+            both[span, columns],
             (((1,), (1,)), ((), ())),
             preferred_element_type=jnp.float32,
         )
@@ -232,13 +235,15 @@
     @pl.loop(0, items[step * length])
     def _(pair):
         turn = 2 * pair + 1
-        summed(turn, left_a, columns_a)
-        pointwise(turn + 1, raw_b, backward, (halves[3], halves[2]))
-        products(turn + 2, left_a, raw_a)
+        for span in spans:
+            summed(turn, left_a, columns_a, span)
+            pointwise(turn + 1, raw_b, backward, (halves[3], halves[2]), span)
+            products(turn + 2, left_a, raw_a, span)
         source_sums(turn)
-        summed(turn + 1, left_b, columns_b)
-        pointwise(turn + 2, raw_a, forward, (halves[0], halves[1]))
-        products(turn + 3, left_b, raw_b)
+        for span in spans:
+            summed(turn + 1, left_b, columns_b, span)
+            pointwise(turn + 2, raw_a, forward, (halves[0], halves[1]), span)
+            products(turn + 3, left_b, raw_b, span)
 
     for coord in range(3):
         back_ref[coord] = -0.5 * back[:, coord, :] - there[coord] * back[:, 6, :]

time: 59.2 us -> 57.2 us (0.966)
  Pallas kernels: 26.3 us -> 24.5 us
  starting transfers between devices: 19.1 us -> 18.4 us
    pallas_call x3, Pallas kernels: 22.2 us -> 20.4 us  [run_step(): pl.pallas_call(functools.partial(step_kernel, step, length, rhs, subs, fi...]
    ppermute x6, starting transfers between devices: 11.1 us -> 10.4 us  [round_ring(): return lax.ppermute(value, 'clus', pairs)]
  transfers between devices with their start and end apart: 15 -> 15, of which waited for: 9 -> 9; matrix products, arithmetic and copies ran while one was open for 3% -> 3% of each run, Pallas kernels for 31% -> 28%
where the time goes in v16:
time: 57.2 us; the launch traced here: 57.1 us
  Pallas kernels  24.5 us (43%)
  starting transfers between devices  18.4 us (32%)
  waiting for transfers between devices  11.1 us (19%)
  other arithmetic  1.23 us (2%)
  between operations  1.03 us (2%)
  local copies, waits for them, and re-layouts  0.91 us (2%)
    pallas_call x3, Pallas kernels, run_step(): pl.pallas_call(functools.partial(step_kernel, step, length, rhs, subs, fi...  20.4 us
    ppermute x6, starting transfers between devices, round_ring(): return lax.ppermute(value, 'clus', pairs)  10.4 us
    ppermute x7, waiting for transfers between devices, shifted(): return lax.ppermute(value, axis, pairs)  7.1 us
    ppermute x7, starting transfers between devices, shifted(): return lax.ppermute(value, axis, pairs)  5.25 us
    ppermute x6, waiting for transfers between devices, round_ring(): return lax.ppermute(value, 'clus', pairs)  3.97 us
    ppermute x2, starting transfers between devices, moved(): return lax.ppermute(value, axes, pairs)  2.7 us
    pallas_call x1, Pallas kernels, on_device(): pl.pallas_call(node_kernel, out_shape=jax.ShapeDtypeStruct((3, share * pa...  1.32 us
    pallas_call x1, Pallas kernels, on_device(): pl.pallas_call(functools.partial(prepare_kernel, (panels, nodes_total)),...  1.22 us
  transfers between devices with their start and end apart: 15, of which 9 were waited for; matrix products, arithmetic and copies ran while one was open for 3% of the time, Pallas kernels for 28%

profile of v16, /device:TPU:0, one launch (start us, length us, event | category | flops | bytes accessed | tf_op | source)
XLA Modules:
  0.0 57.1 jit_solution(2520537494731235438)
XLA Ops:
  0.6 0.0 copy-start
  0.6 1.2 %prepare.1 = (bf16[592,128]{1,0:T(8,128)(2,1)S(1)}, bf16[512,128]{1,0:T(8,128)(2,1)S(1)}, bf16[576,256]{1,0:T(8,128)(2,1)S(1)}) custom-call(bf16[16,32,256]{2,1,0:T(8,128)(2,1)} %refs_0_.1, bf16[3,16,256]{2,1,0:T(8,128)(2,1)} %bitcast.91, bf16[16,256]{1,0:T(8,128)(2,1)} %refs_2_.1, s32[16,4,256]{2,1,0:T(4,128)} %refs_3_.1, bf16[16,32,256]{2,1,0:T(8,128)(2,1)} %refs_4_.1), custom_call_target="tpu_custom_call" | custom-call | tf_op jit(solution)/shard_map/prepare/pallas_call | solution.py:382
  1.9 3.0 %collective-permute-start.3 = (bf16[576,256]{1,0:T(8,128)(2,1)S(1)}, bf16[576,256]{1,0:T(8,128)(2,1)S(1)}, u32[]{:S(2)}, u32[]{:S(2)}) collective-permute-start(bf16[576,256]{1,0:T(8,128)(2,1)S(1)} %get-tuple-element.33.refs_0_.refs_7_), channel_id=1, source_target_pairs={{0,2},{2,0},{1,3},{3,1},{4,6},{6,4},{5,7},{7,5},{8,10},{10,8},{9,1... | collective-permute-start | bytes 884744 | tf_op jit(solution)/shard_map/ppermute | solution.py:22
  4.9 0.0 collective-permute-start.2
  4.9 2.7 %collective-permute-start.1 = (bf16[512,128]{1,0:T(8,128)(2,1)S(1)}, bf16[512,128]{1,0:T(8,128)(2,1)S(1)}, u32[]{:S(2)}, u32[]{:S(2)}) collective-permute-start(bf16[512,128]{1,0:T(8,128)(2,1)S(1)} %get-tuple-element.41), channel_id=1, source_target_pairs={{0,9},{1,8},{4,1},{5,0},{8,13},{9,12},{12,5},{13,4},{2,11},{3,10},... | collective-permute-start | bytes 393224 | tf_op jit(solution)/shard_map/ppermute | solution.py:44
  7.6 1.6 %collective-permute-start = (bf16[592,128]{1,0:T(8,128)(2,1)S(1)}, bf16[592,128]{1,0:T(8,128)(2,1)S(1)}, u32[]{:S(2)}, u32[]{:S(2)}) collective-permute-start(bf16[592,128]{1,0:T(8,128)(2,1)S(1)} %get-tuple-element.40), channel_id=1, source_target_pairs={{0,8},{8,12},{12,4},{4,0},{1,9},{9,13},{13,5},{5,1},{2,10},{10,14}... | collective-permute-start | bytes 454664 | tf_op jit(solution)/shard_map/ppermute | solution.py:32
  9.2 0.0 copy-done
  9.2 0.1 constant_dynamic-slice_fusion
  9.2 0.1 reshape.294
  9.3 0.1 mul.22
  9.4 0.2 convert_reduce_fusion
  9.6 0.2 convert_reduce_fusion.1
  9.8 0.1 copy.34
  9.9 0.2 select_reduce_fusion
  10.1 1.8 %collective-permute-done.3.refs_0_.refs_8_ = bf16[576,256]{1,0:T(8,128)(2,1)S(1)} collective-permute-done((bf16[576,256]{1,0:T(8,128)(2,1)S(1)}, bf16[576,256]{1,0:T(8,128)(2,1)S(1)}, u32[]{:S(2)}, u32[]{:S(2)}) %collective-permute-start.3) | collective-permute-done | bytes 294944 | tf_op jit(solution)/shard_map/ppermute | solution.py:22
  11.9 0.0 collective-permute-start.4
  11.9 0.1 pad_slice_fusion
  12.0 0.1 pad_add_fusion
  12.0 0.1 reshape.295.refs_0_
  12.1 0.1 pad.40.clone
  12.2 0.0 collective-permute-done.2.refs_1_
  12.2 0.4 targets_0.1
  12.6 0.9 %collective-permute-done.4.refs_1_ = bf16[576,256]{1,0:T(8,128)(2,1)S(1)} collective-permute-done((bf16[576,256]{1,0:T(8,128)(2,1)S(1)}, bf16[576,256]{1,0:T(8,128)(2,1)S(1)}, u32[]{:S(2)}, u32[]{:S(2)}) %collective-permute-start.4) | collective-permute-done | bytes 294944 | tf_op jit(solution)/shard_map/ppermute | solution.py:22
  13.5 0.4 targets_1.1
  13.9 0.0 collective-permute-done.1
  13.9 0.2 collective-permute-done
  14.1 3.4 %collective-permute-start.7 = (bf16[1104,128]{1,0:T(8,128)(2,1)S(1)}, bf16[1104,128]{1,0:T(8,128)(2,1)S(1)}, u32[]{:S(2)}, u32[]{:S(2)}) collective-permute-start(bf16[1104,128]{1,0:T(8,128)(2,1)S(1)} %pad_maximum_fusion.refs_1_), channel_id=1, source_target_pairs={{0,8},{8,12},{12,4},{4,0},{1,9},{9,13},{13,5},{5,1},{2,10},{10,14}... | collective-permute-start | bytes 847880 | tf_op jit(solution)/shard_map/ppermute | solution.py:32
  17.5 0.0 collective-permute-start.6
  17.5 0.8 %collective-permute-start.5 = (bf16[592,128]{1,0:T(8,128)(2,1)S(1)}, bf16[592,128]{1,0:T(8,128)(2,1)S(1)}, u32[]{:S(2)}, u32[]{:S(2)}) collective-permute-start(bf16[592,128]{1,0:T(8,128)(2,1)S(1)} %get-tuple-element.40), channel_id=1, source_target_pairs={{0,4},{8,0},{12,8},{4,12},{1,5},{9,1},{13,9},{5,13},{2,6},{10,2},{... | collective-permute-start | bytes 454664 | tf_op jit(solution)/shard_map/ppermute | solution.py:32
  18.4 6.6 %near_field_0.1 = (f32[16,80,512]{2,1,0:T(8,128)S(1)}, f32[3,16,128]{2,1,0:T(8,128)S(1)}) custom-call(s32[108]{0:T(128)S(1)} %reshape.295.refs_0_, bf16[1104,128]{1,0:T(8,128)(2,1)S(1)} %pad_maximum_fusion.refs_1_, bf16[16,256,128]{2,1,0:T(8,128)(2,1)S(1)} %get-tuple-element.43.refs_2_, bf16[16,256,128]{2,1,0:T(8,128)(2,1)S(1)} %get-tuple-element.44.refs_3_, ...), custom_call_target="tpu_custom_call" | custom-call | flops 692060160 | bytes 6291456 | tf_op jit(solution)/shard_map/near_field_0/pallas_call | solution.py:295
  25.0 0.0 collective-permute-done.7.refs_1_
  25.0 7.0 %near_field_1.1 = (f32[16,80,512]{2,1,0:T(8,128)S(1)}, f32[3,16,128]{2,1,0:T(8,128)S(1)}) custom-call(s32[108]{0:T(128)S(1)} %reshape.295.refs_0_, bf16[1104,128]{1,0:T(8,128)(2,1)S(1)} %collective-permute-done.7.refs_1_, bf16[16,256,128]{2,1,0:T(8,128)(2,1)S(1)} %get-tuple-element.43.refs_2_, bf16[16,256,128]{2,1,0:T(8,128)(2,1)S(1)} %get-tuple-element.44.refs_3_, ...), custom_call_target="tpu_custom_call" | custom-call | flops 692060160 | bytes 6291456 | tf_op jit(solution)/shard_map/near_field_1/pallas_call | solution.py:295
  32.0 0.0 collective-permute-done.6
  32.1 0.0 collective-permute-done.5
  32.1 6.7 %near_field_2.1 = (f32[16,32,512]{2,1,0:T(8,128)S(1)}, bf16[16,32,512]{2,1,0:T(8,128)(2,1)S(1)}, f32[3,16,512]{2,1,0:T(8,128)S(1)}, f32[3,16,128]{2,1,0:T(8,128)S(1)}) custom-call(s32[108]{0:T(128)S(1)} %reshape.295.refs_0_, bf16[1104,128]{1,0:T(8,128)(2,1)S(1)} %pad_maximum_fusion.1.refs_1_, bf16[16,256,128]{2,1,0:T(8,128)(2,1)S(1)} %get-tuple-element.43.refs_2_, ...), custom_call_target="tpu_custom_call" | custom-call | flops 692060160 | bytes 6291456 | tf_op jit(solution)/shard_map/near_field_2/pallas_call | solution.py:295
  38.9 0.1 copy.38
  39.1 0.1 maximum_maximum_fusion
  39.2 2.2 %collective-permute-start.10 = (f32[56,128]{1,0:T(8,128)S(1)}, f32[56,128]{1,0:T(8,128)S(1)}, u32[]{:S(2)}, u32[]{:S(2)}) collective-permute-start(f32[56,128]{1,0:T(8,128)S(1)} %get-tuple-element.89), channel_id=1, source_target_pairs={{0,4},{8,0},{12,8},{4,12},{1,5},{9,1},{13,9},{5,13},{2,6},{10,2},{... | collective-permute-start | bytes 86024 | tf_op jit(solution)/shard_map/ppermute | solution.py:32
  41.3 2.4 %collective-permute-start.11 = (f32[56,128]{1,0:T(8,128)S(1)}, f32[56,128]{1,0:T(8,128)S(1)}, u32[]{:S(2)}, u32[]{:S(2)}) collective-permute-start(f32[56,128]{1,0:T(8,128)S(1)} %get-tuple-element.90), channel_id=1, source_target_pairs={{0,12},{8,4},{12,0},{4,8},{1,13},{9,5},{13,1},{5,9},{2,14},{10,6},... | collective-permute-start | bytes 86024 | tf_op jit(solution)/shard_map/ppermute | solution.py:32
  43.8 0.0 collective-permute-start.12
  43.8 0.0 collective-permute-start.8
  43.8 0.5 collective-permute-done.10
  44.3 2.7 %collective-permute-done.11 = f32[56,128]{1,0:T(8,128)S(1)} collective-permute-done((f32[56,128]{1,0:T(8,128)S(1)}, f32[56,128]{1,0:T(8,128)S(1)}, u32[]{:S(2)}, u32[]{:S(2)}) %collective-permute-start.11) | collective-permute-done | bytes 28704 | tf_op jit(solution)/shard_map/ppermute | solution.py:32
  47.0 0.6 %collective-permute-done.12 = f32[56,128]{1,0:T(8,128)S(1)} collective-permute-done((f32[56,128]{1,0:T(8,128)S(1)}, f32[56,128]{1,0:T(8,128)S(1)}, u32[]{:S(2)}, u32[]{:S(2)}) %collective-permute-start.12) | collective-permute-done | bytes 28704 | tf_op jit(solution)/shard_map/ppermute | solution.py:32
  47.8 0.0 collective-permute-done.8
  47.8 0.2 convert_add_fusion
  48.2 0.8 %collective-permute-start.13 = (f32[4,8,512]{2,1,0:T(8,128)S(1)}, f32[4,8,512]{2,1,0:T(8,128)S(1)}, u32[]{:S(2)}, u32[]{:S(2)}) collective-permute-start(f32[4,8,512]{2,1,0:T(8,128)S(1)} %fusion), channel_id=1, source_target_pairs={{0,2},{2,0},{1,3},{3,1},{4,6},{6,4},{5,7},{7,5},{8,10},{10,8},{9,1... | collective-permute-start | bytes 196616 | tf_op jit(solution)/shard_map/ppermute | solution.py:22
  49.0 1.4 %collective-permute-start.9 = (bf16[16,32,256]{2,1,0:T(8,128)(2,1)S(1)}, bf16[16,32,256]{2,1,0:T(8,128)(2,1)S(1)}, u32[]{:S(2)}, u32[]{:S(2)}) collective-permute-start(bf16[16,32,256]{2,1,0:T(8,128)(2,1)S(1)} %slice.307), channel_id=1, source_target_pairs={{0,2},{2,0},{1,3},{3,1},{4,6},{6,4},{5,7},{7,5},{8,10},{10,8},{9,1... | collective-permute-start | bytes 786440 | tf_op jit(solution)/shard_map/ppermute | solution.py:22
  50.4 2.9 %collective-permute-done.13 = f32[4,8,512]{2,1,0:T(8,128)S(1)} collective-permute-done((f32[4,8,512]{2,1,0:T(8,128)S(1)}, f32[4,8,512]{2,1,0:T(8,128)S(1)}, u32[]{:S(2)}, u32[]{:S(2)}) %collective-permute-start.13) | collective-permute-done | bytes 65568 | tf_op jit(solution)/shard_map/ppermute | solution.py:22
  53.3 0.1 collective-permute-start.14
  53.4 1.2 %collective-permute-done.14 = f32[4,8,512]{2,1,0:T(8,128)S(1)} collective-permute-done((f32[4,8,512]{2,1,0:T(8,128)S(1)}, f32[4,8,512]{2,1,0:T(8,128)S(1)}, u32[]{:S(2)}, u32[]{:S(2)}) %collective-permute-start.14) | collective-permute-done | bytes 65568 | tf_op jit(solution)/shard_map/ppermute | solution.py:22
  54.7 1.3 %node_terms.1 = f32[3,4096]{1,0:T(4,128)} custom-call(f32[3,8,512]{2,1,0:T(8,128)S(1)} %slice.197.grad_ref, s32[8,512]{1,0:T(8,128)S(1)} %slice_select_fusion.2.jitter_ref, f32[8,512]{1,0:T(8,128)S(1)} %slice_bitcast_fusion.edge_ref), custom_call_target="tpu_custom_call" | custom-call | flops 1048576 | bytes 262144 | tf_op jit(solution)/shard_map/node_terms/pallas_call | solution.py:574
  56.0 0.3 collective-permute-done.9.refs_1_
  56.3 0.7 %potential_sum.1 = bf16[16,32,256]{2,1,0:T(8,128)(2,1)} custom-call(f32[16,32,256]{2,1,0:T(8,128)S(1)} %slice.127.refs_0_, bf16[16,32,256]{2,1,0:T(8,128)(2,1)S(1)} %collective-permute-done.9.refs_1_), custom_call_target="tpu_custom_call" | custom-call | flops 1048576 | bytes 262144 | tf_op jit(solution)/shard_map/potential_sum/pallas_call | solution.py:583
  (47 shorter events, 0.6 us)
Async XLA Ops:
  0.6 8.5 %copy-start = (s32[5,64]{1,0:T(8,128)S(1)}, s32[5,64]{1,0:T(8,128)}, u32[]{:S(2)}) copy-start(s32[5,64]{1,0:T(8,128)} %param.10) | copy-start | bytes 3844
  1.9 10.0 %collective-permute-start.3 = (bf16[576,256]{1,0:T(8,128)(2,1)S(1)}, bf16[576,256]{1,0:T(8,128)(2,1)S(1)}, u32[]{:S(2)}, u32[]{:S(2)}) collective-permute-start(bf16[576,256]{1,0:T(8,128)(2,1)S(1)} %get-tuple-element.33.refs_0_.refs_7_), channel_id=1, source_target_pairs={{0,2},{2,0},{1,3},{3,1},{4,6},{6,4},{5,7},{7,5},{8,10},{10,8},{9,1... | collective-permute-start | bytes 884744 | tf_op jit(solution)/shard_map/ppermute | solution.py:22
  4.9 7.3 %collective-permute-start.2 = (bf16[576,256]{1,0:T(8,128)(2,1)S(1)}, bf16[576,256]{1,0:T(8,128)(2,1)S(1)}, u32[]{:S(2)}, u32[]{:S(2)}) collective-permute-start(bf16[576,256]{1,0:T(8,128)(2,1)S(1)} %get-tuple-element.33.refs_0_.refs_7_), channel_id=1, source_target_pairs={{0,1},{1,0},{2,3},{3,2},{4,5},{5,4},{6,7},{7,6},{8,9},{9,8},{10,11... | collective-permute-start | bytes 884744 | tf_op jit(solution)/shard_map/ppermute | solution.py:22
  4.9 9.0 %collective-permute-start.1 = (bf16[512,128]{1,0:T(8,128)(2,1)S(1)}, bf16[512,128]{1,0:T(8,128)(2,1)S(1)}, u32[]{:S(2)}, u32[]{:S(2)}) collective-permute-start(bf16[512,128]{1,0:T(8,128)(2,1)S(1)} %get-tuple-element.41), channel_id=1, source_target_pairs={{0,9},{1,8},{4,1},{5,0},{8,13},{9,12},{12,5},{13,4},{2,11},{3,10},... | collective-permute-start | bytes 393224 | tf_op jit(solution)/shard_map/ppermute | solution.py:44
  7.6 6.5 %collective-permute-start = (bf16[592,128]{1,0:T(8,128)(2,1)S(1)}, bf16[592,128]{1,0:T(8,128)(2,1)S(1)}, u32[]{:S(2)}, u32[]{:S(2)}) collective-permute-start(bf16[592,128]{1,0:T(8,128)(2,1)S(1)} %get-tuple-element.40), channel_id=1, source_target_pairs={{0,8},{8,12},{12,4},{4,0},{1,9},{9,13},{13,5},{5,1},{2,10},{10,14}... | collective-permute-start | bytes 454664 | tf_op jit(solution)/shard_map/ppermute | solution.py:32
  11.9 1.6 %collective-permute-start.4 = (bf16[576,256]{1,0:T(8,128)(2,1)S(1)}, bf16[576,256]{1,0:T(8,128)(2,1)S(1)}, u32[]{:S(2)}, u32[]{:S(2)}) collective-permute-start(bf16[576,256]{1,0:T(8,128)(2,1)S(1)} %collective-permute-done.3.refs_0_.refs_8_), channel_id=1, source_target_pairs={{0,1},{1,0},{2,3},{3,2},{4,5},{5,4},{6,7},{7,6},{8,9},{9,8},{10,11... | collective-permute-start | bytes 884744 | tf_op jit(solution)/shard_map/ppermute | solution.py:22
  14.1 11.0 %collective-permute-start.7 = (bf16[1104,128]{1,0:T(8,128)(2,1)S(1)}, bf16[1104,128]{1,0:T(8,128)(2,1)S(1)}, u32[]{:S(2)}, u32[]{:S(2)}) collective-permute-start(bf16[1104,128]{1,0:T(8,128)(2,1)S(1)} %pad_maximum_fusion.refs_1_), channel_id=1, source_target_pairs={{0,8},{8,12},{12,4},{4,0},{1,9},{9,13},{13,5},{5,1},{2,10},{10,14}... | collective-permute-start | bytes 847880 | tf_op jit(solution)/shard_map/ppermute | solution.py:32
  17.5 14.5 %collective-permute-start.6 = (bf16[512,128]{1,0:T(8,128)(2,1)S(1)}, bf16[512,128]{1,0:T(8,128)(2,1)S(1)}, u32[]{:S(2)}, u32[]{:S(2)}) collective-permute-start(bf16[512,128]{1,0:T(8,128)(2,1)S(1)} %get-tuple-element.41), channel_id=1, source_target_pairs={{0,5},{1,4},{4,13},{5,12},{8,1},{9,0},{12,9},{13,8},{2,7},{3,6},{6... | collective-permute-start | bytes 393224 | tf_op jit(solution)/shard_map/ppermute | solution.py:44
  17.5 14.6 %collective-permute-start.5 = (bf16[592,128]{1,0:T(8,128)(2,1)S(1)}, bf16[592,128]{1,0:T(8,128)(2,1)S(1)}, u32[]{:S(2)}, u32[]{:S(2)}) collective-permute-start(bf16[592,128]{1,0:T(8,128)(2,1)S(1)} %get-tuple-element.40), channel_id=1, source_target_pairs={{0,4},{8,0},{12,8},{4,12},{1,5},{9,1},{13,9},{5,13},{2,6},{10,2},{... | collective-permute-start | bytes 454664 | tf_op jit(solution)/shard_map/ppermute | solution.py:32
  39.2 5.1 %collective-permute-start.10 = (f32[56,128]{1,0:T(8,128)S(1)}, f32[56,128]{1,0:T(8,128)S(1)}, u32[]{:S(2)}, u32[]{:S(2)}) collective-permute-start(f32[56,128]{1,0:T(8,128)S(1)} %get-tuple-element.89), channel_id=1, source_target_pairs={{0,4},{8,0},{12,8},{4,12},{1,5},{9,1},{13,9},{5,13},{2,6},{10,2},{... | collective-permute-start | bytes 86024 | tf_op jit(solution)/shard_map/ppermute | solution.py:32
  41.3 5.7 %collective-permute-start.11 = (f32[56,128]{1,0:T(8,128)S(1)}, f32[56,128]{1,0:T(8,128)S(1)}, u32[]{:S(2)}, u32[]{:S(2)}) collective-permute-start(f32[56,128]{1,0:T(8,128)S(1)} %get-tuple-element.90), channel_id=1, source_target_pairs={{0,12},{8,4},{12,0},{4,8},{1,13},{9,5},{13,1},{5,9},{2,14},{10,6},... | collective-permute-start | bytes 86024 | tf_op jit(solution)/shard_map/ppermute | solution.py:32
  43.8 3.9 %collective-permute-start.12 = (f32[56,128]{1,0:T(8,128)S(1)}, f32[56,128]{1,0:T(8,128)S(1)}, u32[]{:S(2)}, u32[]{:S(2)}) collective-permute-start(f32[56,128]{1,0:T(8,128)S(1)} %get-tuple-element.91), channel_id=1, source_target_pairs={{0,8},{8,12},{12,4},{4,0},{1,9},{9,13},{13,5},{5,1},{2,10},{10,14}... | collective-permute-start | bytes 86024 | tf_op jit(solution)/shard_map/ppermute | solution.py:32
  43.8 4.0 %collective-permute-start.8 = (bf16[16,32,512]{2,1,0:T(8,128)(2,1)S(1)}, bf16[16,32,512]{2,1,0:T(8,128)(2,1)S(1)}, u32[]{:S(2)}, u32[]{:S(2)}) collective-permute-start(bf16[16,32,512]{2,1,0:T(8,128)(2,1)S(1)} %get-tuple-element.53), channel_id=1, source_target_pairs={{0,1},{1,0},{2,3},{3,2},{4,5},{5,4},{6,7},{7,6},{8,9},{9,8},{10,11... | collective-permute-start | bytes 1572872 | tf_op jit(solution)/shard_map/ppermute | solution.py:22
  48.2 5.1 %collective-permute-start.13 = (f32[4,8,512]{2,1,0:T(8,128)S(1)}, f32[4,8,512]{2,1,0:T(8,128)S(1)}, u32[]{:S(2)}, u32[]{:S(2)}) collective-permute-start(f32[4,8,512]{2,1,0:T(8,128)S(1)} %fusion), channel_id=1, source_target_pairs={{0,2},{2,0},{1,3},{3,1},{4,6},{6,4},{5,7},{7,5},{8,10},{10,8},{9,1... | collective-permute-start | bytes 196616 | tf_op jit(solution)/shard_map/ppermute | solution.py:22
  49.0 7.3 %collective-permute-start.9 = (bf16[16,32,256]{2,1,0:T(8,128)(2,1)S(1)}, bf16[16,32,256]{2,1,0:T(8,128)(2,1)S(1)}, u32[]{:S(2)}, u32[]{:S(2)}) collective-permute-start(bf16[16,32,256]{2,1,0:T(8,128)(2,1)S(1)} %slice.307), channel_id=1, source_target_pairs={{0,2},{2,0},{1,3},{3,1},{4,6},{6,4},{5,7},{7,5},{8,10},{10,8},{9,1... | collective-permute-start | bytes 786440 | tf_op jit(solution)/shard_map/ppermute | solution.py:22
  53.3 1.3 %collective-permute-start.14 = (f32[4,8,512]{2,1,0:T(8,128)S(1)}, f32[4,8,512]{2,1,0:T(8,128)S(1)}, u32[]{:S(2)}, u32[]{:S(2)}) collective-permute-start(f32[4,8,512]{2,1,0:T(8,128)S(1)} %select_add_fusion), channel_id=1, source_target_pairs={{0,1},{1,0},{2,3},{3,2},{4,5},{5,4},{6,7},{7,6},{8,9},{9,8},{10,11... | collective-permute-start | bytes 196616 | tf_op jit(solution)/shard_map/ppermute | solution.py:22

commit v17 on v16

--- a/solution.py
+++ b/solution.py
@@ -188,7 +188,7 @@
         code = items[step * length + place]
         return code // (2 * clusters), code % (2 * clusters)
 
-    part = max(2 * LANES, panels // 2)
+    part = LANES
     spans = [slice(start, start + part) for start in range(0, panels, part)]
 
     def products(place, left, raw, span):

time: 57.2 us -> 61.3 us (1.072)
  Pallas kernels: 24.5 us -> 28.5 us
    pallas_call x3, Pallas kernels: 20.4 us -> 24.4 us  [run_step(): pl.pallas_call(functools.partial(step_kernel, step, length, rhs, subs, fi...]
    ppermute x7, waiting for transfers between devices: 7.1 us -> 7.88 us  [shifted(): return lax.ppermute(value, axis, pairs)]
    ppermute x6, waiting for transfers between devices: 3.97 us -> 3.23 us  [round_ring(): return lax.ppermute(value, 'clus', pairs)]
  transfers between devices with their start and end apart: 15 -> 15, of which waited for: 9 -> 9; matrix products, arithmetic and copies ran while one was open for 3% -> 2% of each run, Pallas kernels for 28% -> 30%
where the time goes in v17:
time: 61.3 us; the launch traced here: 61.2 us
  Pallas kernels  28.5 us (46%)
  starting transfers between devices  18.4 us (30%)
  waiting for transfers between devices  11.1 us (18%)
  other arithmetic  1.23 us (2%)
  between operations  1.03 us (2%)
  local copies, waits for them, and re-layouts  0.91 us (1%)
    pallas_call x3, Pallas kernels, run_step(): pl.pallas_call(functools.partial(step_kernel, step, length, rhs, subs, fi...  24.4 us
    ppermute x6, starting transfers between devices, round_ring(): return lax.ppermute(value, 'clus', pairs)  10.2 us
    ppermute x7, waiting for transfers between devices, shifted(): return lax.ppermute(value, axis, pairs)  7.88 us
    ppermute x7, starting transfers between devices, shifted(): return lax.ppermute(value, axis, pairs)  5.44 us
    ppermute x6, waiting for transfers between devices, round_ring(): return lax.ppermute(value, 'clus', pairs)  3.23 us
    ppermute x2, starting transfers between devices, moved(): return lax.ppermute(value, axes, pairs)  2.7 us
    pallas_call x1, Pallas kernels, on_device(): pl.pallas_call(node_kernel, out_shape=jax.ShapeDtypeStruct((3, share * pa...  1.32 us
  transfers between devices with their start and end apart: 15, of which 9 were waited for; matrix products, arithmetic and copies ran while one was open for 2% of the time, Pallas kernels for 30%

profile of v17, /device:TPU:0, one launch (start us, length us, event | category | flops | bytes accessed | tf_op | source)
XLA Modules:
  0.0 61.2 jit_solution(13597537832959940959)
XLA Ops:
  0.6 0.0 copy-start
  0.6 1.2 %prepare.1 = (bf16[592,128]{1,0:T(8,128)(2,1)S(1)}, bf16[512,128]{1,0:T(8,128)(2,1)S(1)}, bf16[576,256]{1,0:T(8,128)(2,1)S(1)}) custom-call(bf16[16,32,256]{2,1,0:T(8,128)(2,1)} %refs_0_.1, bf16[3,16,256]{2,1,0:T(8,128)(2,1)} %bitcast.91, bf16[16,256]{1,0:T(8,128)(2,1)} %refs_2_.1, s32[16,4,256]{2,1,0:T(4,128)} %refs_3_.1, bf16[16,32,256]{2,1,0:T(8,128)(2,1)} %refs_4_.1), custom_call_target="tpu_custom_call" | custom-call | tf_op jit(solution)/shard_map/prepare/pallas_call | solution.py:382
  1.9 3.0 %collective-permute-start.3 = (bf16[576,256]{1,0:T(8,128)(2,1)S(1)}, bf16[576,256]{1,0:T(8,128)(2,1)S(1)}, u32[]{:S(2)}, u32[]{:S(2)}) collective-permute-start(bf16[576,256]{1,0:T(8,128)(2,1)S(1)} %get-tuple-element.33.refs_0_.refs_7_), channel_id=1, source_target_pairs={{0,2},{2,0},{1,3},{3,1},{4,6},{6,4},{5,7},{7,5},{8,10},{10,8},{9,1... | collective-permute-start | bytes 884744 | tf_op jit(solution)/shard_map/ppermute | solution.py:22
  4.9 0.0 collective-permute-start.2
  4.9 2.7 %collective-permute-start.1 = (bf16[512,128]{1,0:T(8,128)(2,1)S(1)}, bf16[512,128]{1,0:T(8,128)(2,1)S(1)}, u32[]{:S(2)}, u32[]{:S(2)}) collective-permute-start(bf16[512,128]{1,0:T(8,128)(2,1)S(1)} %get-tuple-element.41), channel_id=1, source_target_pairs={{0,9},{1,8},{4,1},{5,0},{8,13},{9,12},{12,5},{13,4},{2,11},{3,10},... | collective-permute-start | bytes 393224 | tf_op jit(solution)/shard_map/ppermute | solution.py:44
  7.6 1.6 %collective-permute-start = (bf16[592,128]{1,0:T(8,128)(2,1)S(1)}, bf16[592,128]{1,0:T(8,128)(2,1)S(1)}, u32[]{:S(2)}, u32[]{:S(2)}) collective-permute-start(bf16[592,128]{1,0:T(8,128)(2,1)S(1)} %get-tuple-element.40), channel_id=1, source_target_pairs={{0,8},{8,12},{12,4},{4,0},{1,9},{9,13},{13,5},{5,1},{2,10},{10,14}... | collective-permute-start | bytes 454664 | tf_op jit(solution)/shard_map/ppermute | solution.py:32
  9.2 0.0 copy-done
  9.2 0.1 constant_dynamic-slice_fusion
  9.2 0.1 reshape.294
  9.3 0.1 mul.22
  9.4 0.2 convert_reduce_fusion
  9.6 0.2 convert_reduce_fusion.1
  9.8 0.1 copy.34
  9.9 0.2 select_reduce_fusion
  10.1 1.8 %collective-permute-done.3.refs_0_.refs_8_ = bf16[576,256]{1,0:T(8,128)(2,1)S(1)} collective-permute-done((bf16[576,256]{1,0:T(8,128)(2,1)S(1)}, bf16[576,256]{1,0:T(8,128)(2,1)S(1)}, u32[]{:S(2)}, u32[]{:S(2)}) %collective-permute-start.3) | collective-permute-done | bytes 294944 | tf_op jit(solution)/shard_map/ppermute | solution.py:22
  11.9 0.0 collective-permute-start.4
  11.9 0.1 pad_slice_fusion
  12.0 0.1 pad_add_fusion
  12.0 0.1 reshape.295.refs_0_
  12.1 0.1 pad.40.clone
  12.2 0.0 collective-permute-done.2.refs_1_
  12.2 0.4 targets_0.1
  12.6 0.9 %collective-permute-done.4.refs_1_ = bf16[576,256]{1,0:T(8,128)(2,1)S(1)} collective-permute-done((bf16[576,256]{1,0:T(8,128)(2,1)S(1)}, bf16[576,256]{1,0:T(8,128)(2,1)S(1)}, u32[]{:S(2)}, u32[]{:S(2)}) %collective-permute-start.4) | collective-permute-done | bytes 294944 | tf_op jit(solution)/shard_map/ppermute | solution.py:22
  13.5 0.4 targets_1.1
  13.9 0.0 collective-permute-done.1
  13.9 0.2 collective-permute-done
  14.1 3.4 %collective-permute-start.7 = (bf16[1104,128]{1,0:T(8,128)(2,1)S(1)}, bf16[1104,128]{1,0:T(8,128)(2,1)S(1)}, u32[]{:S(2)}, u32[]{:S(2)}) collective-permute-start(bf16[1104,128]{1,0:T(8,128)(2,1)S(1)} %pad_maximum_fusion.refs_1_), channel_id=1, source_target_pairs={{0,8},{8,12},{12,4},{4,0},{1,9},{9,13},{13,5},{5,1},{2,10},{10,14}... | collective-permute-start | bytes 847880 | tf_op jit(solution)/shard_map/ppermute | solution.py:32
  17.5 0.0 collective-permute-start.6
  17.5 0.8 %collective-permute-start.5 = (bf16[592,128]{1,0:T(8,128)(2,1)S(1)}, bf16[592,128]{1,0:T(8,128)(2,1)S(1)}, u32[]{:S(2)}, u32[]{:S(2)}) collective-permute-start(bf16[592,128]{1,0:T(8,128)(2,1)S(1)} %get-tuple-element.40), channel_id=1, source_target_pairs={{0,4},{8,0},{12,8},{4,12},{1,5},{9,1},{13,9},{5,13},{2,6},{10,2},{... | collective-permute-start | bytes 454664 | tf_op jit(solution)/shard_map/ppermute | solution.py:32
  18.4 7.9 %near_field_0.1 = (f32[16,80,512]{2,1,0:T(8,128)S(1)}, f32[3,16,128]{2,1,0:T(8,128)S(1)}) custom-call(s32[108]{0:T(128)S(1)} %reshape.295.refs_0_, bf16[1104,128]{1,0:T(8,128)(2,1)S(1)} %pad_maximum_fusion.refs_1_, bf16[16,256,128]{2,1,0:T(8,128)(2,1)S(1)} %get-tuple-element.43.refs_2_, bf16[16,256,128]{2,1,0:T(8,128)(2,1)S(1)} %get-tuple-element.44.refs_3_, ...), custom_call_target="tpu_custom_call" | custom-call | flops 692060160 | bytes 6291456 | tf_op jit(solution)/shard_map/near_field_0/pallas_call | solution.py:295
  26.3 0.0 collective-permute-done.7.refs_1_
  26.3 8.4 %near_field_1.1 = (f32[16,80,512]{2,1,0:T(8,128)S(1)}, f32[3,16,128]{2,1,0:T(8,128)S(1)}) custom-call(s32[108]{0:T(128)S(1)} %reshape.295.refs_0_, bf16[1104,128]{1,0:T(8,128)(2,1)S(1)} %collective-permute-done.7.refs_1_, bf16[16,256,128]{2,1,0:T(8,128)(2,1)S(1)} %get-tuple-element.43.refs_2_, bf16[16,256,128]{2,1,0:T(8,128)(2,1)S(1)} %get-tuple-element.44.refs_3_, ...), custom_call_target="tpu_custom_call" | custom-call | flops 692060160 | bytes 6291456 | tf_op jit(solution)/shard_map/near_field_1/pallas_call | solution.py:295
  34.7 0.0 collective-permute-done.6
  34.8 0.0 collective-permute-done.5
  34.8 8.1 %near_field_2.1 = (f32[16,32,512]{2,1,0:T(8,128)S(1)}, bf16[16,32,512]{2,1,0:T(8,128)(2,1)S(1)}, f32[3,16,512]{2,1,0:T(8,128)S(1)}, f32[3,16,128]{2,1,0:T(8,128)S(1)}) custom-call(s32[108]{0:T(128)S(1)} %reshape.295.refs_0_, bf16[1104,128]{1,0:T(8,128)(2,1)S(1)} %pad_maximum_fusion.1.refs_1_, bf16[16,256,128]{2,1,0:T(8,128)(2,1)S(1)} %get-tuple-element.43.refs_2_, ...), custom_call_target="tpu_custom_call" | custom-call | flops 692060160 | bytes 6291456 | tf_op jit(solution)/shard_map/near_field_2/pallas_call | solution.py:295
  43.0 0.1 copy.38
  43.1 0.1 maximum_maximum_fusion
  43.2 1.6 %collective-permute-start.10 = (f32[56,128]{1,0:T(8,128)S(1)}, f32[56,128]{1,0:T(8,128)S(1)}, u32[]{:S(2)}, u32[]{:S(2)}) collective-permute-start(f32[56,128]{1,0:T(8,128)S(1)} %get-tuple-element.89), channel_id=1, source_target_pairs={{0,4},{8,0},{12,8},{4,12},{1,5},{9,1},{13,9},{5,13},{2,6},{10,2},{... | collective-permute-start | bytes 86024 | tf_op jit(solution)/shard_map/ppermute | solution.py:32
  44.8 2.0 %collective-permute-start.11 = (f32[56,128]{1,0:T(8,128)S(1)}, f32[56,128]{1,0:T(8,128)S(1)}, u32[]{:S(2)}, u32[]{:S(2)}) collective-permute-start(f32[56,128]{1,0:T(8,128)S(1)} %get-tuple-element.90), channel_id=1, source_target_pairs={{0,12},{8,4},{12,0},{4,8},{1,13},{9,5},{13,1},{5,9},{2,14},{10,6},... | collective-permute-start | bytes 86024 | tf_op jit(solution)/shard_map/ppermute | solution.py:32
  46.9 0.7 %collective-permute-start.12 = (f32[56,128]{1,0:T(8,128)S(1)}, f32[56,128]{1,0:T(8,128)S(1)}, u32[]{:S(2)}, u32[]{:S(2)}) collective-permute-start(f32[56,128]{1,0:T(8,128)S(1)} %get-tuple-element.91), channel_id=1, source_target_pairs={{0,8},{8,12},{12,4},{4,0},{1,9},{9,13},{13,5},{5,1},{2,10},{10,14}... | collective-permute-start | bytes 86024 | tf_op jit(solution)/shard_map/ppermute | solution.py:32
  47.6 0.2 collective-permute-start.8
  47.9 0.5 collective-permute-done.10
  48.3 2.5 %collective-permute-done.11 = f32[56,128]{1,0:T(8,128)S(1)} collective-permute-done((f32[56,128]{1,0:T(8,128)S(1)}, f32[56,128]{1,0:T(8,128)S(1)}, u32[]{:S(2)}, u32[]{:S(2)}) %collective-permute-start.11) | collective-permute-done | bytes 28704 | tf_op jit(solution)/shard_map/ppermute | solution.py:32
  50.8 0.1 collective-permute-done.12
  51.1 0.0 collective-permute-done.8
  51.1 0.2 convert_add_fusion
  51.5 1.1 %collective-permute-start.13 = (f32[4,8,512]{2,1,0:T(8,128)S(1)}, f32[4,8,512]{2,1,0:T(8,128)S(1)}, u32[]{:S(2)}, u32[]{:S(2)}) collective-permute-start(f32[4,8,512]{2,1,0:T(8,128)S(1)} %fusion), channel_id=1, source_target_pairs={{0,2},{2,0},{1,3},{3,1},{4,6},{6,4},{5,7},{7,5},{8,10},{10,8},{9,1... | collective-permute-start | bytes 196616 | tf_op jit(solution)/shard_map/ppermute | solution.py:22
  52.7 1.0 %collective-permute-start.9 = (bf16[16,32,256]{2,1,0:T(8,128)(2,1)S(1)}, bf16[16,32,256]{2,1,0:T(8,128)(2,1)S(1)}, u32[]{:S(2)}, u32[]{:S(2)}) collective-permute-start(bf16[16,32,256]{2,1,0:T(8,128)(2,1)S(1)} %slice.307), channel_id=1, source_target_pairs={{0,2},{2,0},{1,3},{3,1},{4,6},{6,4},{5,7},{7,5},{8,10},{10,8},{9,1... | collective-permute-start | bytes 786440 | tf_op jit(solution)/shard_map/ppermute | solution.py:22
  53.7 2.8 %collective-permute-done.13 = f32[4,8,512]{2,1,0:T(8,128)S(1)} collective-permute-done((f32[4,8,512]{2,1,0:T(8,128)S(1)}, f32[4,8,512]{2,1,0:T(8,128)S(1)}, u32[]{:S(2)}, u32[]{:S(2)}) %collective-permute-start.13) | collective-permute-done | bytes 65568 | tf_op jit(solution)/shard_map/ppermute | solution.py:22
  56.6 0.1 collective-permute-start.14
  56.7 1.2 %collective-permute-done.14 = f32[4,8,512]{2,1,0:T(8,128)S(1)} collective-permute-done((f32[4,8,512]{2,1,0:T(8,128)S(1)}, f32[4,8,512]{2,1,0:T(8,128)S(1)}, u32[]{:S(2)}, u32[]{:S(2)}) %collective-permute-start.14) | collective-permute-done | bytes 65568 | tf_op jit(solution)/shard_map/ppermute | solution.py:22
  57.9 1.3 %node_terms.1 = f32[3,4096]{1,0:T(4,128)} custom-call(f32[3,8,512]{2,1,0:T(8,128)S(1)} %slice.197.grad_ref, s32[8,512]{1,0:T(8,128)S(1)} %slice_select_fusion.2.jitter_ref, f32[8,512]{1,0:T(8,128)S(1)} %slice_bitcast_fusion.edge_ref), custom_call_target="tpu_custom_call" | custom-call | flops 1048576 | bytes 262144 | tf_op jit(solution)/shard_map/node_terms/pallas_call | solution.py:574
  59.2 1.2 %collective-permute-done.9.refs_1_ = bf16[16,32,256]{2,1,0:T(8,128)(2,1)S(1)} collective-permute-done((bf16[16,32,256]{2,1,0:T(8,128)(2,1)S(1)}, bf16[16,32,256]{2,1,0:T(8,128)(2,1)S(1)}, u32[]{:S(2)}, u32[]{:S(2)}) %collective-permute-start.9) | collective-permute-done | bytes 262176 | tf_op jit(solution)/shard_map/ppermute | solution.py:22
  60.4 0.7 %potential_sum.1 = bf16[16,32,256]{2,1,0:T(8,128)(2,1)} custom-call(f32[16,32,256]{2,1,0:T(8,128)S(1)} %slice.127.refs_0_, bf16[16,32,256]{2,1,0:T(8,128)(2,1)S(1)} %collective-permute-done.9.refs_1_), custom_call_target="tpu_custom_call" | custom-call | flops 1048576 | bytes 262144 | tf_op jit(solution)/shard_map/potential_sum/pallas_call | solution.py:583
  (47 shorter events, 0.6 us)
Async XLA Ops:
  0.6 8.5 %copy-start = (s32[5,64]{1,0:T(8,128)S(1)}, s32[5,64]{1,0:T(8,128)}, u32[]{:S(2)}) copy-start(s32[5,64]{1,0:T(8,128)} %param.10) | copy-start | bytes 3844
  1.9 10.0 %collective-permute-start.3 = (bf16[576,256]{1,0:T(8,128)(2,1)S(1)}, bf16[576,256]{1,0:T(8,128)(2,1)S(1)}, u32[]{:S(2)}, u32[]{:S(2)}) collective-permute-start(bf16[576,256]{1,0:T(8,128)(2,1)S(1)} %get-tuple-element.33.refs_0_.refs_7_), channel_id=1, source_target_pairs={{0,2},{2,0},{1,3},{3,1},{4,6},{6,4},{5,7},{7,5},{8,10},{10,8},{9,1... | collective-permute-start | bytes 884744 | tf_op jit(solution)/shard_map/ppermute | solution.py:22
  4.9 7.3 %collective-permute-start.2 = (bf16[576,256]{1,0:T(8,128)(2,1)S(1)}, bf16[576,256]{1,0:T(8,128)(2,1)S(1)}, u32[]{:S(2)}, u32[]{:S(2)}) collective-permute-start(bf16[576,256]{1,0:T(8,128)(2,1)S(1)} %get-tuple-element.33.refs_0_.refs_7_), channel_id=1, source_target_pairs={{0,1},{1,0},{2,3},{3,2},{4,5},{5,4},{6,7},{7,6},{8,9},{9,8},{10,11... | collective-permute-start | bytes 884744 | tf_op jit(solution)/shard_map/ppermute | solution.py:22
  4.9 9.0 %collective-permute-start.1 = (bf16[512,128]{1,0:T(8,128)(2,1)S(1)}, bf16[512,128]{1,0:T(8,128)(2,1)S(1)}, u32[]{:S(2)}, u32[]{:S(2)}) collective-permute-start(bf16[512,128]{1,0:T(8,128)(2,1)S(1)} %get-tuple-element.41), channel_id=1, source_target_pairs={{0,9},{1,8},{4,1},{5,0},{8,13},{9,12},{12,5},{13,4},{2,11},{3,10},... | collective-permute-start | bytes 393224 | tf_op jit(solution)/shard_map/ppermute | solution.py:44
  7.6 6.5 %collective-permute-start = (bf16[592,128]{1,0:T(8,128)(2,1)S(1)}, bf16[592,128]{1,0:T(8,128)(2,1)S(1)}, u32[]{:S(2)}, u32[]{:S(2)}) collective-permute-start(bf16[592,128]{1,0:T(8,128)(2,1)S(1)} %get-tuple-element.40), channel_id=1, source_target_pairs={{0,8},{8,12},{12,4},{4,0},{1,9},{9,13},{13,5},{5,1},{2,10},{10,14}... | collective-permute-start | bytes 454664 | tf_op jit(solution)/shard_map/ppermute | solution.py:32
  11.9 1.6 %collective-permute-start.4 = (bf16[576,256]{1,0:T(8,128)(2,1)S(1)}, bf16[576,256]{1,0:T(8,128)(2,1)S(1)}, u32[]{:S(2)}, u32[]{:S(2)}) collective-permute-start(bf16[576,256]{1,0:T(8,128)(2,1)S(1)} %collective-permute-done.3.refs_0_.refs_8_), channel_id=1, source_target_pairs={{0,1},{1,0},{2,3},{3,2},{4,5},{5,4},{6,7},{7,6},{8,9},{9,8},{10,11... | collective-permute-start | bytes 884744 | tf_op jit(solution)/shard_map/ppermute | solution.py:22
  14.1 12.3 %collective-permute-start.7 = (bf16[1104,128]{1,0:T(8,128)(2,1)S(1)}, bf16[1104,128]{1,0:T(8,128)(2,1)S(1)}, u32[]{:S(2)}, u32[]{:S(2)}) collective-permute-start(bf16[1104,128]{1,0:T(8,128)(2,1)S(1)} %pad_maximum_fusion.refs_1_), channel_id=1, source_target_pairs={{0,8},{8,12},{12,4},{4,0},{1,9},{9,13},{13,5},{5,1},{2,10},{10,14}... | collective-permute-start | bytes 847880 | tf_op jit(solution)/shard_map/ppermute | solution.py:32
  17.5 17.3 %collective-permute-start.6 = (bf16[512,128]{1,0:T(8,128)(2,1)S(1)}, bf16[512,128]{1,0:T(8,128)(2,1)S(1)}, u32[]{:S(2)}, u32[]{:S(2)}) collective-permute-start(bf16[512,128]{1,0:T(8,128)(2,1)S(1)} %get-tuple-element.41), channel_id=1, source_target_pairs={{0,5},{1,4},{4,13},{5,12},{8,1},{9,0},{12,9},{13,8},{2,7},{3,6},{6... | collective-permute-start | bytes 393224 | tf_op jit(solution)/shard_map/ppermute | solution.py:44
  17.5 17.3 %collective-permute-start.5 = (bf16[592,128]{1,0:T(8,128)(2,1)S(1)}, bf16[592,128]{1,0:T(8,128)(2,1)S(1)}, u32[]{:S(2)}, u32[]{:S(2)}) collective-permute-start(bf16[592,128]{1,0:T(8,128)(2,1)S(1)} %get-tuple-element.40), channel_id=1, source_target_pairs={{0,4},{8,0},{12,8},{4,12},{1,5},{9,1},{13,9},{5,13},{2,6},{10,2},{... | collective-permute-start | bytes 454664 | tf_op jit(solution)/shard_map/ppermute | solution.py:32
  43.2 5.1 %collective-permute-start.10 = (f32[56,128]{1,0:T(8,128)S(1)}, f32[56,128]{1,0:T(8,128)S(1)}, u32[]{:S(2)}, u32[]{:S(2)}) collective-permute-start(f32[56,128]{1,0:T(8,128)S(1)} %get-tuple-element.89), channel_id=1, source_target_pairs={{0,4},{8,0},{12,8},{4,12},{1,5},{9,1},{13,9},{5,13},{2,6},{10,2},{... | collective-permute-start | bytes 86024 | tf_op jit(solution)/shard_map/ppermute | solution.py:32
  44.8 6.0 %collective-permute-start.11 = (f32[56,128]{1,0:T(8,128)S(1)}, f32[56,128]{1,0:T(8,128)S(1)}, u32[]{:S(2)}, u32[]{:S(2)}) collective-permute-start(f32[56,128]{1,0:T(8,128)S(1)} %get-tuple-element.90), channel_id=1, source_target_pairs={{0,12},{8,4},{12,0},{4,8},{1,13},{9,5},{13,1},{5,9},{2,14},{10,6},... | collective-permute-start | bytes 86024 | tf_op jit(solution)/shard_map/ppermute | solution.py:32
  46.9 4.1 %collective-permute-start.12 = (f32[56,128]{1,0:T(8,128)S(1)}, f32[56,128]{1,0:T(8,128)S(1)}, u32[]{:S(2)}, u32[]{:S(2)}) collective-permute-start(f32[56,128]{1,0:T(8,128)S(1)} %get-tuple-element.91), channel_id=1, source_target_pairs={{0,8},{8,12},{12,4},{4,0},{1,9},{9,13},{13,5},{5,1},{2,10},{10,14}... | collective-permute-start | bytes 86024 | tf_op jit(solution)/shard_map/ppermute | solution.py:32
  47.6 3.4 %collective-permute-start.8 = (bf16[16,32,512]{2,1,0:T(8,128)(2,1)S(1)}, bf16[16,32,512]{2,1,0:T(8,128)(2,1)S(1)}, u32[]{:S(2)}, u32[]{:S(2)}) collective-permute-start(bf16[16,32,512]{2,1,0:T(8,128)(2,1)S(1)} %get-tuple-element.53), channel_id=1, source_target_pairs={{0,1},{1,0},{2,3},{3,2},{4,5},{5,4},{6,7},{7,6},{8,9},{9,8},{10,11... | collective-permute-start | bytes 1572872 | tf_op jit(solution)/shard_map/ppermute | solution.py:22
  51.5 5.0 %collective-permute-start.13 = (f32[4,8,512]{2,1,0:T(8,128)S(1)}, f32[4,8,512]{2,1,0:T(8,128)S(1)}, u32[]{:S(2)}, u32[]{:S(2)}) collective-permute-start(f32[4,8,512]{2,1,0:T(8,128)S(1)} %fusion), channel_id=1, source_target_pairs={{0,2},{2,0},{1,3},{3,1},{4,6},{6,4},{5,7},{7,5},{8,10},{10,8},{9,1... | collective-permute-start | bytes 196616 | tf_op jit(solution)/shard_map/ppermute | solution.py:22
  52.7 7.7 %collective-permute-start.9 = (bf16[16,32,256]{2,1,0:T(8,128)(2,1)S(1)}, bf16[16,32,256]{2,1,0:T(8,128)(2,1)S(1)}, u32[]{:S(2)}, u32[]{:S(2)}) collective-permute-start(bf16[16,32,256]{2,1,0:T(8,128)(2,1)S(1)} %slice.307), channel_id=1, source_target_pairs={{0,2},{2,0},{1,3},{3,1},{4,6},{6,4},{5,7},{7,5},{8,10},{10,8},{9,1... | collective-permute-start | bytes 786440 | tf_op jit(solution)/shard_map/ppermute | solution.py:22
  56.6 1.3 %collective-permute-start.14 = (f32[4,8,512]{2,1,0:T(8,128)S(1)}, f32[4,8,512]{2,1,0:T(8,128)S(1)}, u32[]{:S(2)}, u32[]{:S(2)}) collective-permute-start(f32[4,8,512]{2,1,0:T(8,128)S(1)} %select_add_fusion), channel_id=1, source_target_pairs={{0,1},{1,0},{2,3},{3,2},{4,5},{5,4},{6,7},{7,6},{8,9},{9,8},{10,11... | collective-permute-start | bytes 196616 | tf_op jit(solution)/shard_map/ppermute | solution.py:22

commit v18 on v16

--- a/solution.py
+++ b/solution.py
@@ -216,18 +216,16 @@
             preferred_element_type=jnp.float32,
         )
 
-    def source_sums(place):
-        (here_a, mate_a), (here_b, mate_b) = decoded(place), decoded(place + 1)
-        aug = jnp.concatenate(
-            [
-                jnp.concatenate([ref[here] for ref in aug_refs], axis=1)
-                for here in (here_a, here_b)
-            ],
-            axis=0,
+    def source_sums(place, span):
+        aug = [
+            jnp.concatenate([ref[decoded(at)[0]] for ref in aug_refs], axis=1)[:, span]
+            for at in (place, place + 1)
+        ]
+        return jnp.dot(
+            jnp.concatenate(aug, axis=0),
+            both[span, quarter : 3 * quarter],
+            preferred_element_type=jnp.float32,
         )
-        sums = jnp.dot(aug, both[:, quarter : 3 * quarter], preferred_element_type=jnp.float32)
-        back[mate_a % clusters] += sums[:AUG, :quarter]
-        back[mate_b % clusters] += sums[AUG:, quarter:]
 
     forward, backward = (halves[0], halves[1]), (halves[1], halves[0])
     columns_a, columns_b = slice(0, 2 * quarter), slice(2 * quarter, 4 * quarter)
@@ -239,11 +237,14 @@
             summed(turn, left_a, columns_a, span)
             pointwise(turn + 1, raw_b, backward, (halves[3], halves[2]), span)
             products(turn + 2, left_a, raw_a, span)
-        source_sums(turn)
+        sums = jnp.zeros((2 * AUG, 2 * quarter), jnp.float32)
         for span in spans:
+            sums = sums + source_sums(turn, span)
             summed(turn + 1, left_b, columns_b, span)
             pointwise(turn + 2, raw_a, forward, (halves[0], halves[1]), span)
             products(turn + 3, left_b, raw_b, span)
+        back[decoded(turn)[1] % clusters] += sums[:AUG, :quarter]
+        back[decoded(turn + 1)[1] % clusters] += sums[AUG:, quarter:]
 
     for coord in range(3):
         back_ref[coord] = -0.5 * back[:, coord, :] - there[coord] * back[:, 6, :]

time: 57.2 us -> 57.2 us (level)
  transfers between devices with their start and end apart: 15 -> 15, of which waited for: 9 -> 9; matrix products, arithmetic and copies ran while one was open for 3% -> 3% of each run, Pallas kernels for 28% -> 27%
where the time goes in v18:
time: 57.2 us; the launch traced here: 57.1 us
  Pallas kernels  24.4 us (43%)
  starting transfers between devices  18.4 us (32%)
  waiting for transfers between devices  11.1 us (19%)
  other arithmetic  1.23 us (2%)
  between operations  1.03 us (2%)
  local copies, waits for them, and re-layouts  0.91 us (2%)
    pallas_call x3, Pallas kernels, run_step(): pl.pallas_call(functools.partial(step_kernel, step, length, rhs, subs, fi...  20.4 us
    ppermute x6, starting transfers between devices, round_ring(): return lax.ppermute(value, 'clus', pairs)  10.2 us
    ppermute x7, waiting for transfers between devices, shifted(): return lax.ppermute(value, axis, pairs)  7.49 us
    ppermute x7, starting transfers between devices, shifted(): return lax.ppermute(value, axis, pairs)  5.45 us
    ppermute x6, waiting for transfers between devices, round_ring(): return lax.ppermute(value, 'clus', pairs)  3.58 us
    ppermute x2, starting transfers between devices, moved(): return lax.ppermute(value, axes, pairs)  2.7 us
    pallas_call x1, Pallas kernels, on_device(): pl.pallas_call(node_kernel, out_shape=jax.ShapeDtypeStruct((3, share * pa...  1.32 us
    pallas_call x1, Pallas kernels, on_device(): pl.pallas_call(functools.partial(prepare_kernel, (panels, nodes_total)),...  1.22 us
  transfers between devices with their start and end apart: 15, of which 9 were waited for; matrix products, arithmetic and copies ran while one was open for 3% of the time, Pallas kernels for 27%

profile of v18, /device:TPU:0, one launch (start us, length us, event | category | flops | bytes accessed | tf_op | source)
XLA Modules:
  0.0 57.1 jit_solution(405582369206672541)
XLA Ops:
  0.6 0.0 copy-start
  0.6 1.2 %prepare.1 = (bf16[592,128]{1,0:T(8,128)(2,1)S(1)}, bf16[512,128]{1,0:T(8,128)(2,1)S(1)}, bf16[576,256]{1,0:T(8,128)(2,1)S(1)}) custom-call(bf16[16,32,256]{2,1,0:T(8,128)(2,1)} %refs_0_.1, bf16[3,16,256]{2,1,0:T(8,128)(2,1)} %bitcast.91, bf16[16,256]{1,0:T(8,128)(2,1)} %refs_2_.1, s32[16,4,256]{2,1,0:T(4,128)} %refs_3_.1, bf16[16,32,256]{2,1,0:T(8,128)(2,1)} %refs_4_.1), custom_call_target="tpu_custom_call" | custom-call | tf_op jit(solution)/shard_map/prepare/pallas_call | solution.py:383
  1.9 3.0 %collective-permute-start.3 = (bf16[576,256]{1,0:T(8,128)(2,1)S(1)}, bf16[576,256]{1,0:T(8,128)(2,1)S(1)}, u32[]{:S(2)}, u32[]{:S(2)}) collective-permute-start(bf16[576,256]{1,0:T(8,128)(2,1)S(1)} %get-tuple-element.33.refs_0_.refs_7_), channel_id=1, source_target_pairs={{0,2},{2,0},{1,3},{3,1},{4,6},{6,4},{5,7},{7,5},{8,10},{10,8},{9,1... | collective-permute-start | bytes 884744 | tf_op jit(solution)/shard_map/ppermute | solution.py:22
  4.9 0.0 collective-permute-start.2
  4.9 2.7 %collective-permute-start.1 = (bf16[512,128]{1,0:T(8,128)(2,1)S(1)}, bf16[512,128]{1,0:T(8,128)(2,1)S(1)}, u32[]{:S(2)}, u32[]{:S(2)}) collective-permute-start(bf16[512,128]{1,0:T(8,128)(2,1)S(1)} %get-tuple-element.41), channel_id=1, source_target_pairs={{0,9},{1,8},{4,1},{5,0},{8,13},{9,12},{12,5},{13,4},{2,11},{3,10},... | collective-permute-start | bytes 393224 | tf_op jit(solution)/shard_map/ppermute | solution.py:44
  7.6 1.6 %collective-permute-start = (bf16[592,128]{1,0:T(8,128)(2,1)S(1)}, bf16[592,128]{1,0:T(8,128)(2,1)S(1)}, u32[]{:S(2)}, u32[]{:S(2)}) collective-permute-start(bf16[592,128]{1,0:T(8,128)(2,1)S(1)} %get-tuple-element.40), channel_id=1, source_target_pairs={{0,8},{8,12},{12,4},{4,0},{1,9},{9,13},{13,5},{5,1},{2,10},{10,14}... | collective-permute-start | bytes 454664 | tf_op jit(solution)/shard_map/ppermute | solution.py:32
  9.2 0.0 copy-done
  9.2 0.1 constant_dynamic-slice_fusion
  9.2 0.1 reshape.294
  9.3 0.1 mul.22
  9.4 0.2 convert_reduce_fusion
  9.6 0.2 convert_reduce_fusion.1
  9.8 0.1 copy.34
  9.9 0.2 select_reduce_fusion
  10.1 1.8 %collective-permute-done.3.refs_0_.refs_8_ = bf16[576,256]{1,0:T(8,128)(2,1)S(1)} collective-permute-done((bf16[576,256]{1,0:T(8,128)(2,1)S(1)}, bf16[576,256]{1,0:T(8,128)(2,1)S(1)}, u32[]{:S(2)}, u32[]{:S(2)}) %collective-permute-start.3) | collective-permute-done | bytes 294944 | tf_op jit(solution)/shard_map/ppermute | solution.py:22
  11.9 0.0 collective-permute-start.4
  11.9 0.1 pad_slice_fusion
  12.0 0.1 pad_add_fusion
  12.0 0.1 reshape.295.refs_0_
  12.1 0.1 pad.40.clone
  12.2 0.0 collective-permute-done.2.refs_1_
  12.2 0.4 targets_0.1
  12.6 0.9 %collective-permute-done.4.refs_1_ = bf16[576,256]{1,0:T(8,128)(2,1)S(1)} collective-permute-done((bf16[576,256]{1,0:T(8,128)(2,1)S(1)}, bf16[576,256]{1,0:T(8,128)(2,1)S(1)}, u32[]{:S(2)}, u32[]{:S(2)}) %collective-permute-start.4) | collective-permute-done | bytes 294944 | tf_op jit(solution)/shard_map/ppermute | solution.py:22
  13.5 0.4 targets_1.1
  13.9 0.0 collective-permute-done.1
  13.9 0.2 collective-permute-done
  14.1 3.4 %collective-permute-start.7 = (bf16[1104,128]{1,0:T(8,128)(2,1)S(1)}, bf16[1104,128]{1,0:T(8,128)(2,1)S(1)}, u32[]{:S(2)}, u32[]{:S(2)}) collective-permute-start(bf16[1104,128]{1,0:T(8,128)(2,1)S(1)} %pad_maximum_fusion.refs_1_), channel_id=1, source_target_pairs={{0,8},{8,12},{12,4},{4,0},{1,9},{9,13},{13,5},{5,1},{2,10},{10,14}... | collective-permute-start | bytes 847880 | tf_op jit(solution)/shard_map/ppermute | solution.py:32
  17.5 0.0 collective-permute-start.6
  17.5 0.8 %collective-permute-start.5 = (bf16[592,128]{1,0:T(8,128)(2,1)S(1)}, bf16[592,128]{1,0:T(8,128)(2,1)S(1)}, u32[]{:S(2)}, u32[]{:S(2)}) collective-permute-start(bf16[592,128]{1,0:T(8,128)(2,1)S(1)} %get-tuple-element.40), channel_id=1, source_target_pairs={{0,4},{8,0},{12,8},{4,12},{1,5},{9,1},{13,9},{5,13},{2,6},{10,2},{... | collective-permute-start | bytes 454664 | tf_op jit(solution)/shard_map/ppermute | solution.py:32
  18.4 7.0 %near_field_0.1 = (f32[16,80,512]{2,1,0:T(8,128)S(1)}, f32[3,16,128]{2,1,0:T(8,128)S(1)}) custom-call(s32[108]{0:T(128)S(1)} %reshape.295.refs_0_, bf16[1104,128]{1,0:T(8,128)(2,1)S(1)} %pad_maximum_fusion.refs_1_, bf16[16,256,128]{2,1,0:T(8,128)(2,1)S(1)} %get-tuple-element.43.refs_2_, bf16[16,256,128]{2,1,0:T(8,128)(2,1)S(1)} %get-tuple-element.44.refs_3_, ...), custom_call_target="tpu_custom_call" | custom-call | flops 692060160 | bytes 6291456 | tf_op jit(solution)/shard_map/near_field_0/pallas_call | solution.py:296
  25.4 0.0 collective-permute-done.7.refs_1_
  25.4 6.2 %near_field_1.1 = (f32[16,80,512]{2,1,0:T(8,128)S(1)}, f32[3,16,128]{2,1,0:T(8,128)S(1)}) custom-call(s32[108]{0:T(128)S(1)} %reshape.295.refs_0_, bf16[1104,128]{1,0:T(8,128)(2,1)S(1)} %collective-permute-done.7.refs_1_, bf16[16,256,128]{2,1,0:T(8,128)(2,1)S(1)} %get-tuple-element.43.refs_2_, bf16[16,256,128]{2,1,0:T(8,128)(2,1)S(1)} %get-tuple-element.44.refs_3_, ...), custom_call_target="tpu_custom_call" | custom-call | flops 692060160 | bytes 6291456 | tf_op jit(solution)/shard_map/near_field_1/pallas_call | solution.py:296
  31.6 0.0 collective-permute-done.6
  31.7 0.0 collective-permute-done.5
  31.7 7.1 %near_field_2.1 = (f32[16,32,512]{2,1,0:T(8,128)S(1)}, bf16[16,32,512]{2,1,0:T(8,128)(2,1)S(1)}, f32[3,16,512]{2,1,0:T(8,128)S(1)}, f32[3,16,128]{2,1,0:T(8,128)S(1)}) custom-call(s32[108]{0:T(128)S(1)} %reshape.295.refs_0_, bf16[1104,128]{1,0:T(8,128)(2,1)S(1)} %pad_maximum_fusion.1.refs_1_, bf16[16,256,128]{2,1,0:T(8,128)(2,1)S(1)} %get-tuple-element.43.refs_2_, ...), custom_call_target="tpu_custom_call" | custom-call | flops 692060160 | bytes 6291456 | tf_op jit(solution)/shard_map/near_field_2/pallas_call | solution.py:296
  38.9 0.1 copy.38
  39.1 0.1 maximum_maximum_fusion
  39.2 1.8 %collective-permute-start.10 = (f32[56,128]{1,0:T(8,128)S(1)}, f32[56,128]{1,0:T(8,128)S(1)}, u32[]{:S(2)}, u32[]{:S(2)}) collective-permute-start(f32[56,128]{1,0:T(8,128)S(1)} %get-tuple-element.89), channel_id=1, source_target_pairs={{0,4},{8,0},{12,8},{4,12},{1,5},{9,1},{13,9},{5,13},{2,6},{10,2},{... | collective-permute-start | bytes 86024 | tf_op jit(solution)/shard_map/ppermute | solution.py:32
  40.9 2.4 %collective-permute-start.11 = (f32[56,128]{1,0:T(8,128)S(1)}, f32[56,128]{1,0:T(8,128)S(1)}, u32[]{:S(2)}, u32[]{:S(2)}) collective-permute-start(f32[56,128]{1,0:T(8,128)S(1)} %get-tuple-element.90), channel_id=1, source_target_pairs={{0,12},{8,4},{12,0},{4,8},{1,13},{9,5},{13,1},{5,9},{2,14},{10,6},... | collective-permute-start | bytes 86024 | tf_op jit(solution)/shard_map/ppermute | solution.py:32
  43.3 0.2 collective-permute-start.12
  43.6 0.2 collective-permute-start.8
  43.8 0.4 collective-permute-done.10
  44.2 2.4 %collective-permute-done.11 = f32[56,128]{1,0:T(8,128)S(1)} collective-permute-done((f32[56,128]{1,0:T(8,128)S(1)}, f32[56,128]{1,0:T(8,128)S(1)}, u32[]{:S(2)}, u32[]{:S(2)}) %collective-permute-start.11) | collective-permute-done | bytes 28704 | tf_op jit(solution)/shard_map/ppermute | solution.py:32
  46.7 0.6 collective-permute-done.12
  47.4 0.0 collective-permute-done.8
  47.4 0.2 convert_add_fusion
  47.8 1.1 %collective-permute-start.13 = (f32[4,8,512]{2,1,0:T(8,128)S(1)}, f32[4,8,512]{2,1,0:T(8,128)S(1)}, u32[]{:S(2)}, u32[]{:S(2)}) collective-permute-start(f32[4,8,512]{2,1,0:T(8,128)S(1)} %fusion), channel_id=1, source_target_pairs={{0,2},{2,0},{1,3},{3,1},{4,6},{6,4},{5,7},{7,5},{8,10},{10,8},{9,1... | collective-permute-start | bytes 196616 | tf_op jit(solution)/shard_map/ppermute | solution.py:22
  48.9 1.1 %collective-permute-start.9 = (bf16[16,32,256]{2,1,0:T(8,128)(2,1)S(1)}, bf16[16,32,256]{2,1,0:T(8,128)(2,1)S(1)}, u32[]{:S(2)}, u32[]{:S(2)}) collective-permute-start(bf16[16,32,256]{2,1,0:T(8,128)(2,1)S(1)} %slice.307), channel_id=1, source_target_pairs={{0,2},{2,0},{1,3},{3,1},{4,6},{6,4},{5,7},{7,5},{8,10},{10,8},{9,1... | collective-permute-start | bytes 786440 | tf_op jit(solution)/shard_map/ppermute | solution.py:22
  50.0 2.9 %collective-permute-done.13 = f32[4,8,512]{2,1,0:T(8,128)S(1)} collective-permute-done((f32[4,8,512]{2,1,0:T(8,128)S(1)}, f32[4,8,512]{2,1,0:T(8,128)S(1)}, u32[]{:S(2)}, u32[]{:S(2)}) %collective-permute-start.13) | collective-permute-done | bytes 65568 | tf_op jit(solution)/shard_map/ppermute | solution.py:22
  52.9 0.1 collective-permute-start.14
  53.0 1.2 %collective-permute-done.14 = f32[4,8,512]{2,1,0:T(8,128)S(1)} collective-permute-done((f32[4,8,512]{2,1,0:T(8,128)S(1)}, f32[4,8,512]{2,1,0:T(8,128)S(1)}, u32[]{:S(2)}, u32[]{:S(2)}) %collective-permute-start.14) | collective-permute-done | bytes 65568 | tf_op jit(solution)/shard_map/ppermute | solution.py:22
  54.2 1.3 %node_terms.1 = f32[3,4096]{1,0:T(4,128)} custom-call(f32[3,8,512]{2,1,0:T(8,128)S(1)} %slice.197.grad_ref, s32[8,512]{1,0:T(8,128)S(1)} %slice_select_fusion.2.jitter_ref, f32[8,512]{1,0:T(8,128)S(1)} %slice_bitcast_fusion.edge_ref), custom_call_target="tpu_custom_call" | custom-call | flops 1048576 | bytes 262144 | tf_op jit(solution)/shard_map/node_terms/pallas_call | solution.py:575
  55.6 0.7 %collective-permute-done.9.refs_1_ = bf16[16,32,256]{2,1,0:T(8,128)(2,1)S(1)} collective-permute-done((bf16[16,32,256]{2,1,0:T(8,128)(2,1)S(1)}, bf16[16,32,256]{2,1,0:T(8,128)(2,1)S(1)}, u32[]{:S(2)}, u32[]{:S(2)}) %collective-permute-start.9) | collective-permute-done | bytes 262176 | tf_op jit(solution)/shard_map/ppermute | solution.py:22
  56.3 0.7 %potential_sum.1 = bf16[16,32,256]{2,1,0:T(8,128)(2,1)} custom-call(f32[16,32,256]{2,1,0:T(8,128)S(1)} %slice.127.refs_0_, bf16[16,32,256]{2,1,0:T(8,128)(2,1)S(1)} %collective-permute-done.9.refs_1_), custom_call_target="tpu_custom_call" | custom-call | flops 1048576 | bytes 262144 | tf_op jit(solution)/shard_map/potential_sum/pallas_call | solution.py:584
  (47 shorter events, 0.6 us)
Async XLA Ops:
  0.6 8.5 %copy-start = (s32[5,64]{1,0:T(8,128)S(1)}, s32[5,64]{1,0:T(8,128)}, u32[]{:S(2)}) copy-start(s32[5,64]{1,0:T(8,128)} %param.10) | copy-start | bytes 3844
  1.9 10.0 %collective-permute-start.3 = (bf16[576,256]{1,0:T(8,128)(2,1)S(1)}, bf16[576,256]{1,0:T(8,128)(2,1)S(1)}, u32[]{:S(2)}, u32[]{:S(2)}) collective-permute-start(bf16[576,256]{1,0:T(8,128)(2,1)S(1)} %get-tuple-element.33.refs_0_.refs_7_), channel_id=1, source_target_pairs={{0,2},{2,0},{1,3},{3,1},{4,6},{6,4},{5,7},{7,5},{8,10},{10,8},{9,1... | collective-permute-start | bytes 884744 | tf_op jit(solution)/shard_map/ppermute | solution.py:22
  4.9 7.3 %collective-permute-start.2 = (bf16[576,256]{1,0:T(8,128)(2,1)S(1)}, bf16[576,256]{1,0:T(8,128)(2,1)S(1)}, u32[]{:S(2)}, u32[]{:S(2)}) collective-permute-start(bf16[576,256]{1,0:T(8,128)(2,1)S(1)} %get-tuple-element.33.refs_0_.refs_7_), channel_id=1, source_target_pairs={{0,1},{1,0},{2,3},{3,2},{4,5},{5,4},{6,7},{7,6},{8,9},{9,8},{10,11... | collective-permute-start | bytes 884744 | tf_op jit(solution)/shard_map/ppermute | solution.py:22
  4.9 9.0 %collective-permute-start.1 = (bf16[512,128]{1,0:T(8,128)(2,1)S(1)}, bf16[512,128]{1,0:T(8,128)(2,1)S(1)}, u32[]{:S(2)}, u32[]{:S(2)}) collective-permute-start(bf16[512,128]{1,0:T(8,128)(2,1)S(1)} %get-tuple-element.41), channel_id=1, source_target_pairs={{0,9},{1,8},{4,1},{5,0},{8,13},{9,12},{12,5},{13,4},{2,11},{3,10},... | collective-permute-start | bytes 393224 | tf_op jit(solution)/shard_map/ppermute | solution.py:44
  7.6 6.5 %collective-permute-start = (bf16[592,128]{1,0:T(8,128)(2,1)S(1)}, bf16[592,128]{1,0:T(8,128)(2,1)S(1)}, u32[]{:S(2)}, u32[]{:S(2)}) collective-permute-start(bf16[592,128]{1,0:T(8,128)(2,1)S(1)} %get-tuple-element.40), channel_id=1, source_target_pairs={{0,8},{8,12},{12,4},{4,0},{1,9},{9,13},{13,5},{5,1},{2,10},{10,14}... | collective-permute-start | bytes 454664 | tf_op jit(solution)/shard_map/ppermute | solution.py:32
  11.9 1.6 %collective-permute-start.4 = (bf16[576,256]{1,0:T(8,128)(2,1)S(1)}, bf16[576,256]{1,0:T(8,128)(2,1)S(1)}, u32[]{:S(2)}, u32[]{:S(2)}) collective-permute-start(bf16[576,256]{1,0:T(8,128)(2,1)S(1)} %collective-permute-done.3.refs_0_.refs_8_), channel_id=1, source_target_pairs={{0,1},{1,0},{2,3},{3,2},{4,5},{5,4},{6,7},{7,6},{8,9},{9,8},{10,11... | collective-permute-start | bytes 884744 | tf_op jit(solution)/shard_map/ppermute | solution.py:22
  14.1 11.3 %collective-permute-start.7 = (bf16[1104,128]{1,0:T(8,128)(2,1)S(1)}, bf16[1104,128]{1,0:T(8,128)(2,1)S(1)}, u32[]{:S(2)}, u32[]{:S(2)}) collective-permute-start(bf16[1104,128]{1,0:T(8,128)(2,1)S(1)} %pad_maximum_fusion.refs_1_), channel_id=1, source_target_pairs={{0,8},{8,12},{12,4},{4,0},{1,9},{9,13},{13,5},{5,1},{2,10},{10,14}... | collective-permute-start | bytes 847880 | tf_op jit(solution)/shard_map/ppermute | solution.py:32
  17.5 14.2 %collective-permute-start.6 = (bf16[512,128]{1,0:T(8,128)(2,1)S(1)}, bf16[512,128]{1,0:T(8,128)(2,1)S(1)}, u32[]{:S(2)}, u32[]{:S(2)}) collective-permute-start(bf16[512,128]{1,0:T(8,128)(2,1)S(1)} %get-tuple-element.41), channel_id=1, source_target_pairs={{0,5},{1,4},{4,13},{5,12},{8,1},{9,0},{12,9},{13,8},{2,7},{3,6},{6... | collective-permute-start | bytes 393224 | tf_op jit(solution)/shard_map/ppermute | solution.py:44
  17.5 14.2 %collective-permute-start.5 = (bf16[592,128]{1,0:T(8,128)(2,1)S(1)}, bf16[592,128]{1,0:T(8,128)(2,1)S(1)}, u32[]{:S(2)}, u32[]{:S(2)}) collective-permute-start(bf16[592,128]{1,0:T(8,128)(2,1)S(1)} %get-tuple-element.40), channel_id=1, source_target_pairs={{0,4},{8,0},{12,8},{4,12},{1,5},{9,1},{13,9},{5,13},{2,6},{10,2},{... | collective-permute-start | bytes 454664 | tf_op jit(solution)/shard_map/ppermute | solution.py:32
  39.2 5.1 %collective-permute-start.10 = (f32[56,128]{1,0:T(8,128)S(1)}, f32[56,128]{1,0:T(8,128)S(1)}, u32[]{:S(2)}, u32[]{:S(2)}) collective-permute-start(f32[56,128]{1,0:T(8,128)S(1)} %get-tuple-element.89), channel_id=1, source_target_pairs={{0,4},{8,0},{12,8},{4,12},{1,5},{9,1},{13,9},{5,13},{2,6},{10,2},{... | collective-permute-start | bytes 86024 | tf_op jit(solution)/shard_map/ppermute | solution.py:32
  40.9 5.7 %collective-permute-start.11 = (f32[56,128]{1,0:T(8,128)S(1)}, f32[56,128]{1,0:T(8,128)S(1)}, u32[]{:S(2)}, u32[]{:S(2)}) collective-permute-start(f32[56,128]{1,0:T(8,128)S(1)} %get-tuple-element.90), channel_id=1, source_target_pairs={{0,12},{8,4},{12,0},{4,8},{1,13},{9,5},{13,1},{5,9},{2,14},{10,6},... | collective-permute-start | bytes 86024 | tf_op jit(solution)/shard_map/ppermute | solution.py:32
  43.3 3.9 %collective-permute-start.12 = (f32[56,128]{1,0:T(8,128)S(1)}, f32[56,128]{1,0:T(8,128)S(1)}, u32[]{:S(2)}, u32[]{:S(2)}) collective-permute-start(f32[56,128]{1,0:T(8,128)S(1)} %get-tuple-element.91), channel_id=1, source_target_pairs={{0,8},{8,12},{12,4},{4,0},{1,9},{9,13},{13,5},{5,1},{2,10},{10,14}... | collective-permute-start | bytes 86024 | tf_op jit(solution)/shard_map/ppermute | solution.py:32
  43.6 3.8 %collective-permute-start.8 = (bf16[16,32,512]{2,1,0:T(8,128)(2,1)S(1)}, bf16[16,32,512]{2,1,0:T(8,128)(2,1)S(1)}, u32[]{:S(2)}, u32[]{:S(2)}) collective-permute-start(bf16[16,32,512]{2,1,0:T(8,128)(2,1)S(1)} %get-tuple-element.53), channel_id=1, source_target_pairs={{0,1},{1,0},{2,3},{3,2},{4,5},{5,4},{6,7},{7,6},{8,9},{9,8},{10,11... | collective-permute-start | bytes 1572872 | tf_op jit(solution)/shard_map/ppermute | solution.py:22
  47.8 5.1 %collective-permute-start.13 = (f32[4,8,512]{2,1,0:T(8,128)S(1)}, f32[4,8,512]{2,1,0:T(8,128)S(1)}, u32[]{:S(2)}, u32[]{:S(2)}) collective-permute-start(f32[4,8,512]{2,1,0:T(8,128)S(1)} %fusion), channel_id=1, source_target_pairs={{0,2},{2,0},{1,3},{3,1},{4,6},{6,4},{5,7},{7,5},{8,10},{10,8},{9,1... | collective-permute-start | bytes 196616 | tf_op jit(solution)/shard_map/ppermute | solution.py:22
  48.9 7.4 %collective-permute-start.9 = (bf16[16,32,256]{2,1,0:T(8,128)(2,1)S(1)}, bf16[16,32,256]{2,1,0:T(8,128)(2,1)S(1)}, u32[]{:S(2)}, u32[]{:S(2)}) collective-permute-start(bf16[16,32,256]{2,1,0:T(8,128)(2,1)S(1)} %slice.307), channel_id=1, source_target_pairs={{0,2},{2,0},{1,3},{3,1},{4,6},{6,4},{5,7},{7,5},{8,10},{10,8},{9,1... | collective-permute-start | bytes 786440 | tf_op jit(solution)/shard_map/ppermute | solution.py:22
  52.9 1.3 %collective-permute-start.14 = (f32[4,8,512]{2,1,0:T(8,128)S(1)}, f32[4,8,512]{2,1,0:T(8,128)S(1)}, u32[]{:S(2)}, u32[]{:S(2)}) collective-permute-start(f32[4,8,512]{2,1,0:T(8,128)S(1)} %select_add_fusion), channel_id=1, source_target_pairs={{0,1},{1,0},{2,3},{3,2},{4,5},{5,4},{6,7},{7,6},{8,9},{9,8},{10,11... | collective-permute-start | bytes 196616 | tf_op jit(solution)/shard_map/ppermute | solution.py:22

commit v19 on v16

--- a/solution.py
+++ b/solution.py
@@ -236,14 +236,18 @@
     def _(pair):
         turn = 2 * pair + 1
         for span in spans:
+            early, late = slice(span.start, span.start + LANES), slice(span.start + LANES, span.stop)
             summed(turn, left_a, columns_a, span)
-            pointwise(turn + 1, raw_b, backward, (halves[3], halves[2]), span)
+            pointwise(turn + 1, raw_b, backward, (halves[3], halves[2]), early)
             products(turn + 2, left_a, raw_a, span)
+            pointwise(turn + 1, raw_b, backward, (halves[3], halves[2]), late)
         source_sums(turn)
         for span in spans:
+            early, late = slice(span.start, span.start + LANES), slice(span.start + LANES, span.stop)
             summed(turn + 1, left_b, columns_b, span)
-            pointwise(turn + 2, raw_a, forward, (halves[0], halves[1]), span)
+            pointwise(turn + 2, raw_a, forward, (halves[0], halves[1]), early)
             products(turn + 3, left_b, raw_b, span)
+            pointwise(turn + 2, raw_a, forward, (halves[0], halves[1]), late)
 
     for coord in range(3):
         back_ref[coord] = -0.5 * back[:, coord, :] - there[coord] * back[:, 6, :]

time: 57.2 us -> 57.1 us (level)
    ppermute x6, waiting for transfers between devices: 3.97 us -> 3.3 us  [round_ring(): return lax.ppermute(value, 'clus', pairs)]
    ppermute x7, waiting for transfers between devices: 7.1 us -> 7.76 us  [shifted(): return lax.ppermute(value, axis, pairs)]
  transfers between devices with their start and end apart: 15 -> 15, of which waited for: 9 -> 9; matrix products, arithmetic and copies ran while one was open for 3% -> 3% of each run, Pallas kernels for 28% -> 26%
where the time goes in v19:
time: 57.1 us; the launch traced here: 56.9 us
  Pallas kernels  24.3 us (43%)
  starting transfers between devices  18.4 us (32%)
  waiting for transfers between devices  11.1 us (19%)
  other arithmetic  1.23 us (2%)
  between operations  1.03 us (2%)
  local copies, waits for them, and re-layouts  0.91 us (2%)
    pallas_call x3, Pallas kernels, run_step(): pl.pallas_call(functools.partial(step_kernel, step, length, rhs, subs, fi...  20.2 us
    ppermute x6, starting transfers between devices, round_ring(): return lax.ppermute(value, 'clus', pairs)  10.4 us
    ppermute x7, waiting for transfers between devices, shifted(): return lax.ppermute(value, axis, pairs)  7.76 us
    ppermute x7, starting transfers between devices, shifted(): return lax.ppermute(value, axis, pairs)  5.32 us
    ppermute x6, waiting for transfers between devices, round_ring(): return lax.ppermute(value, 'clus', pairs)  3.3 us
    ppermute x2, starting transfers between devices, moved(): return lax.ppermute(value, axes, pairs)  2.7 us
    pallas_call x1, Pallas kernels, on_device(): pl.pallas_call(node_kernel, out_shape=jax.ShapeDtypeStruct((3, share * pa...  1.32 us
    pallas_call x1, Pallas kernels, on_device(): pl.pallas_call(functools.partial(prepare_kernel, (panels, nodes_total)),...  1.22 us
  transfers between devices with their start and end apart: 15, of which 9 were waited for; matrix products, arithmetic and copies ran while one was open for 3% of the time, Pallas kernels for 26%

profile of v19, /device:TPU:0, one launch (start us, length us, event | category | flops | bytes accessed | tf_op | source)
XLA Modules:
  0.0 56.9 jit_solution(12298786752510382207)
XLA Ops:
  0.6 0.0 copy-start
  0.6 1.2 %prepare.1 = (bf16[592,128]{1,0:T(8,128)(2,1)S(1)}, bf16[512,128]{1,0:T(8,128)(2,1)S(1)}, bf16[576,256]{1,0:T(8,128)(2,1)S(1)}) custom-call(bf16[16,32,256]{2,1,0:T(8,128)(2,1)} %refs_0_.1, bf16[3,16,256]{2,1,0:T(8,128)(2,1)} %bitcast.91, bf16[16,256]{1,0:T(8,128)(2,1)} %refs_2_.1, s32[16,4,256]{2,1,0:T(4,128)} %refs_3_.1, bf16[16,32,256]{2,1,0:T(8,128)(2,1)} %refs_4_.1), custom_call_target="tpu_custom_call" | custom-call | tf_op jit(solution)/shard_map/prepare/pallas_call | solution.py:386
  1.9 3.0 %collective-permute-start.3 = (bf16[576,256]{1,0:T(8,128)(2,1)S(1)}, bf16[576,256]{1,0:T(8,128)(2,1)S(1)}, u32[]{:S(2)}, u32[]{:S(2)}) collective-permute-start(bf16[576,256]{1,0:T(8,128)(2,1)S(1)} %get-tuple-element.33.refs_0_.refs_7_), channel_id=1, source_target_pairs={{0,2},{2,0},{1,3},{3,1},{4,6},{6,4},{5,7},{7,5},{8,10},{10,8},{9,1... | collective-permute-start | bytes 884744 | tf_op jit(solution)/shard_map/ppermute | solution.py:22
  4.9 0.0 collective-permute-start.2
  4.9 2.7 %collective-permute-start.1 = (bf16[512,128]{1,0:T(8,128)(2,1)S(1)}, bf16[512,128]{1,0:T(8,128)(2,1)S(1)}, u32[]{:S(2)}, u32[]{:S(2)}) collective-permute-start(bf16[512,128]{1,0:T(8,128)(2,1)S(1)} %get-tuple-element.41), channel_id=1, source_target_pairs={{0,9},{1,8},{4,1},{5,0},{8,13},{9,12},{12,5},{13,4},{2,11},{3,10},... | collective-permute-start | bytes 393224 | tf_op jit(solution)/shard_map/ppermute | solution.py:44
  7.6 1.6 %collective-permute-start = (bf16[592,128]{1,0:T(8,128)(2,1)S(1)}, bf16[592,128]{1,0:T(8,128)(2,1)S(1)}, u32[]{:S(2)}, u32[]{:S(2)}) collective-permute-start(bf16[592,128]{1,0:T(8,128)(2,1)S(1)} %get-tuple-element.40), channel_id=1, source_target_pairs={{0,8},{8,12},{12,4},{4,0},{1,9},{9,13},{13,5},{5,1},{2,10},{10,14}... | collective-permute-start | bytes 454664 | tf_op jit(solution)/shard_map/ppermute | solution.py:32
  9.2 0.0 copy-done
  9.2 0.1 constant_dynamic-slice_fusion
  9.2 0.1 reshape.294
  9.3 0.1 mul.22
  9.4 0.2 convert_reduce_fusion
  9.6 0.2 convert_reduce_fusion.1
  9.8 0.1 copy.34
  9.9 0.2 select_reduce_fusion
  10.1 1.8 %collective-permute-done.3.refs_0_.refs_8_ = bf16[576,256]{1,0:T(8,128)(2,1)S(1)} collective-permute-done((bf16[576,256]{1,0:T(8,128)(2,1)S(1)}, bf16[576,256]{1,0:T(8,128)(2,1)S(1)}, u32[]{:S(2)}, u32[]{:S(2)}) %collective-permute-start.3) | collective-permute-done | bytes 294944 | tf_op jit(solution)/shard_map/ppermute | solution.py:22
  11.9 0.0 collective-permute-start.4
  11.9 0.1 pad_slice_fusion
  12.0 0.1 pad_add_fusion
  12.0 0.1 reshape.295.refs_0_
  12.1 0.1 pad.40.clone
  12.2 0.0 collective-permute-done.2.refs_1_
  12.2 0.4 targets_0.1
  12.6 0.9 %collective-permute-done.4.refs_1_ = bf16[576,256]{1,0:T(8,128)(2,1)S(1)} collective-permute-done((bf16[576,256]{1,0:T(8,128)(2,1)S(1)}, bf16[576,256]{1,0:T(8,128)(2,1)S(1)}, u32[]{:S(2)}, u32[]{:S(2)}) %collective-permute-start.4) | collective-permute-done | bytes 294944 | tf_op jit(solution)/shard_map/ppermute | solution.py:22
  13.5 0.4 targets_1.1
  13.9 0.0 collective-permute-done.1
  13.9 0.2 collective-permute-done
  14.1 3.4 %collective-permute-start.7 = (bf16[1104,128]{1,0:T(8,128)(2,1)S(1)}, bf16[1104,128]{1,0:T(8,128)(2,1)S(1)}, u32[]{:S(2)}, u32[]{:S(2)}) collective-permute-start(bf16[1104,128]{1,0:T(8,128)(2,1)S(1)} %pad_maximum_fusion.refs_1_), channel_id=1, source_target_pairs={{0,8},{8,12},{12,4},{4,0},{1,9},{9,13},{13,5},{5,1},{2,10},{10,14}... | collective-permute-start | bytes 847880 | tf_op jit(solution)/shard_map/ppermute | solution.py:32
  17.5 0.0 collective-permute-start.6
  17.5 0.8 %collective-permute-start.5 = (bf16[592,128]{1,0:T(8,128)(2,1)S(1)}, bf16[592,128]{1,0:T(8,128)(2,1)S(1)}, u32[]{:S(2)}, u32[]{:S(2)}) collective-permute-start(bf16[592,128]{1,0:T(8,128)(2,1)S(1)} %get-tuple-element.40), channel_id=1, source_target_pairs={{0,4},{8,0},{12,8},{4,12},{1,5},{9,1},{13,9},{5,13},{2,6},{10,2},{... | collective-permute-start | bytes 454664 | tf_op jit(solution)/shard_map/ppermute | solution.py:32
  18.4 6.5 %near_field_0.1 = (f32[16,80,512]{2,1,0:T(8,128)S(1)}, f32[3,16,128]{2,1,0:T(8,128)S(1)}) custom-call(s32[108]{0:T(128)S(1)} %reshape.295.refs_0_, bf16[1104,128]{1,0:T(8,128)(2,1)S(1)} %pad_maximum_fusion.refs_1_, bf16[16,256,128]{2,1,0:T(8,128)(2,1)S(1)} %get-tuple-element.43.refs_2_, bf16[16,256,128]{2,1,0:T(8,128)(2,1)S(1)} %get-tuple-element.44.refs_3_, ...), custom_call_target="tpu_custom_call" | custom-call | flops 692060160 | bytes 6291456 | tf_op jit(solution)/shard_map/near_field_0/pallas_call | solution.py:299
  24.9 0.0 collective-permute-done.7.refs_1_
  24.9 6.2 %near_field_1.1 = (f32[16,80,512]{2,1,0:T(8,128)S(1)}, f32[3,16,128]{2,1,0:T(8,128)S(1)}) custom-call(s32[108]{0:T(128)S(1)} %reshape.295.refs_0_, bf16[1104,128]{1,0:T(8,128)(2,1)S(1)} %collective-permute-done.7.refs_1_, bf16[16,256,128]{2,1,0:T(8,128)(2,1)S(1)} %get-tuple-element.43.refs_2_, bf16[16,256,128]{2,1,0:T(8,128)(2,1)S(1)} %get-tuple-element.44.refs_3_, ...), custom_call_target="tpu_custom_call" | custom-call | flops 692060160 | bytes 6291456 | tf_op jit(solution)/shard_map/near_field_1/pallas_call | solution.py:299
  31.1 0.0 collective-permute-done.6
  31.1 0.0 collective-permute-done.5
  31.2 7.5 %near_field_2.1 = (f32[16,32,512]{2,1,0:T(8,128)S(1)}, bf16[16,32,512]{2,1,0:T(8,128)(2,1)S(1)}, f32[3,16,512]{2,1,0:T(8,128)S(1)}, f32[3,16,128]{2,1,0:T(8,128)S(1)}) custom-call(s32[108]{0:T(128)S(1)} %reshape.295.refs_0_, bf16[1104,128]{1,0:T(8,128)(2,1)S(1)} %pad_maximum_fusion.1.refs_1_, bf16[16,256,128]{2,1,0:T(8,128)(2,1)S(1)} %get-tuple-element.43.refs_2_, ...), custom_call_target="tpu_custom_call" | custom-call | flops 692060160 | bytes 6291456 | tf_op jit(solution)/shard_map/near_field_2/pallas_call | solution.py:299
  38.8 0.1 copy.38
  38.9 0.1 maximum_maximum_fusion
  39.0 1.6 %collective-permute-start.10 = (f32[56,128]{1,0:T(8,128)S(1)}, f32[56,128]{1,0:T(8,128)S(1)}, u32[]{:S(2)}, u32[]{:S(2)}) collective-permute-start(f32[56,128]{1,0:T(8,128)S(1)} %get-tuple-element.89), channel_id=1, source_target_pairs={{0,4},{8,0},{12,8},{4,12},{1,5},{9,1},{13,9},{5,13},{2,6},{10,2},{... | collective-permute-start | bytes 86024 | tf_op jit(solution)/shard_map/ppermute | solution.py:32
  40.6 2.3 %collective-permute-start.11 = (f32[56,128]{1,0:T(8,128)S(1)}, f32[56,128]{1,0:T(8,128)S(1)}, u32[]{:S(2)}, u32[]{:S(2)}) collective-permute-start(f32[56,128]{1,0:T(8,128)S(1)} %get-tuple-element.90), channel_id=1, source_target_pairs={{0,12},{8,4},{12,0},{4,8},{1,13},{9,5},{13,1},{5,9},{2,14},{10,6},... | collective-permute-start | bytes 86024 | tf_op jit(solution)/shard_map/ppermute | solution.py:32
  42.9 0.7 %collective-permute-start.12 = (f32[56,128]{1,0:T(8,128)S(1)}, f32[56,128]{1,0:T(8,128)S(1)}, u32[]{:S(2)}, u32[]{:S(2)}) collective-permute-start(f32[56,128]{1,0:T(8,128)S(1)} %get-tuple-element.91), channel_id=1, source_target_pairs={{0,8},{8,12},{12,4},{4,0},{1,9},{9,13},{13,5},{5,1},{2,10},{10,14}... | collective-permute-start | bytes 86024 | tf_op jit(solution)/shard_map/ppermute | solution.py:32
  43.6 0.1 collective-permute-start.8
  43.7 0.4 collective-permute-done.10
  44.1 2.4 %collective-permute-done.11 = f32[56,128]{1,0:T(8,128)S(1)} collective-permute-done((f32[56,128]{1,0:T(8,128)S(1)}, f32[56,128]{1,0:T(8,128)S(1)}, u32[]{:S(2)}, u32[]{:S(2)}) %collective-permute-start.11) | collective-permute-done | bytes 28704 | tf_op jit(solution)/shard_map/ppermute | solution.py:32
  46.5 0.3 collective-permute-done.12
  47.0 0.0 collective-permute-done.8
  47.0 0.2 convert_add_fusion
  47.4 1.0 %collective-permute-start.13 = (f32[4,8,512]{2,1,0:T(8,128)S(1)}, f32[4,8,512]{2,1,0:T(8,128)S(1)}, u32[]{:S(2)}, u32[]{:S(2)}) collective-permute-start(f32[4,8,512]{2,1,0:T(8,128)S(1)} %fusion), channel_id=1, source_target_pairs={{0,2},{2,0},{1,3},{3,1},{4,6},{6,4},{5,7},{7,5},{8,10},{10,8},{9,1... | collective-permute-start | bytes 196616 | tf_op jit(solution)/shard_map/ppermute | solution.py:22
  48.5 1.1 %collective-permute-start.9 = (bf16[16,32,256]{2,1,0:T(8,128)(2,1)S(1)}, bf16[16,32,256]{2,1,0:T(8,128)(2,1)S(1)}, u32[]{:S(2)}, u32[]{:S(2)}) collective-permute-start(bf16[16,32,256]{2,1,0:T(8,128)(2,1)S(1)} %slice.307), channel_id=1, source_target_pairs={{0,2},{2,0},{1,3},{3,1},{4,6},{6,4},{5,7},{7,5},{8,10},{10,8},{9,1... | collective-permute-start | bytes 786440 | tf_op jit(solution)/shard_map/ppermute | solution.py:22
  49.6 2.9 %collective-permute-done.13 = f32[4,8,512]{2,1,0:T(8,128)S(1)} collective-permute-done((f32[4,8,512]{2,1,0:T(8,128)S(1)}, f32[4,8,512]{2,1,0:T(8,128)S(1)}, u32[]{:S(2)}, u32[]{:S(2)}) %collective-permute-start.13) | collective-permute-done | bytes 65568 | tf_op jit(solution)/shard_map/ppermute | solution.py:22
  52.5 0.1 collective-permute-start.14
  52.6 1.2 %collective-permute-done.14 = f32[4,8,512]{2,1,0:T(8,128)S(1)} collective-permute-done((f32[4,8,512]{2,1,0:T(8,128)S(1)}, f32[4,8,512]{2,1,0:T(8,128)S(1)}, u32[]{:S(2)}, u32[]{:S(2)}) %collective-permute-start.14) | collective-permute-done | bytes 65568 | tf_op jit(solution)/shard_map/ppermute | solution.py:22
  53.8 1.3 %node_terms.1 = f32[3,4096]{1,0:T(4,128)} custom-call(f32[3,8,512]{2,1,0:T(8,128)S(1)} %slice.197.grad_ref, s32[8,512]{1,0:T(8,128)S(1)} %slice_select_fusion.2.jitter_ref, f32[8,512]{1,0:T(8,128)S(1)} %slice_bitcast_fusion.edge_ref), custom_call_target="tpu_custom_call" | custom-call | flops 1048576 | bytes 262144 | tf_op jit(solution)/shard_map/node_terms/pallas_call | solution.py:578
  55.1 1.1 %collective-permute-done.9.refs_1_ = bf16[16,32,256]{2,1,0:T(8,128)(2,1)S(1)} collective-permute-done((bf16[16,32,256]{2,1,0:T(8,128)(2,1)S(1)}, bf16[16,32,256]{2,1,0:T(8,128)(2,1)S(1)}, u32[]{:S(2)}, u32[]{:S(2)}) %collective-permute-start.9) | collective-permute-done | bytes 262176 | tf_op jit(solution)/shard_map/ppermute | solution.py:22
  56.2 0.7 %potential_sum.1 = bf16[16,32,256]{2,1,0:T(8,128)(2,1)} custom-call(f32[16,32,256]{2,1,0:T(8,128)S(1)} %slice.127.refs_0_, bf16[16,32,256]{2,1,0:T(8,128)(2,1)S(1)} %collective-permute-done.9.refs_1_), custom_call_target="tpu_custom_call" | custom-call | flops 1048576 | bytes 262144 | tf_op jit(solution)/shard_map/potential_sum/pallas_call | solution.py:587
  (47 shorter events, 0.6 us)
Async XLA Ops:
  0.6 8.5 %copy-start = (s32[5,64]{1,0:T(8,128)S(1)}, s32[5,64]{1,0:T(8,128)}, u32[]{:S(2)}) copy-start(s32[5,64]{1,0:T(8,128)} %param.10) | copy-start | bytes 3844
  1.9 10.0 %collective-permute-start.3 = (bf16[576,256]{1,0:T(8,128)(2,1)S(1)}, bf16[576,256]{1,0:T(8,128)(2,1)S(1)}, u32[]{:S(2)}, u32[]{:S(2)}) collective-permute-start(bf16[576,256]{1,0:T(8,128)(2,1)S(1)} %get-tuple-element.33.refs_0_.refs_7_), channel_id=1, source_target_pairs={{0,2},{2,0},{1,3},{3,1},{4,6},{6,4},{5,7},{7,5},{8,10},{10,8},{9,1... | collective-permute-start | bytes 884744 | tf_op jit(solution)/shard_map/ppermute | solution.py:22
  4.9 7.3 %collective-permute-start.2 = (bf16[576,256]{1,0:T(8,128)(2,1)S(1)}, bf16[576,256]{1,0:T(8,128)(2,1)S(1)}, u32[]{:S(2)}, u32[]{:S(2)}) collective-permute-start(bf16[576,256]{1,0:T(8,128)(2,1)S(1)} %get-tuple-element.33.refs_0_.refs_7_), channel_id=1, source_target_pairs={{0,1},{1,0},{2,3},{3,2},{4,5},{5,4},{6,7},{7,6},{8,9},{9,8},{10,11... | collective-permute-start | bytes 884744 | tf_op jit(solution)/shard_map/ppermute | solution.py:22
  4.9 9.0 %collective-permute-start.1 = (bf16[512,128]{1,0:T(8,128)(2,1)S(1)}, bf16[512,128]{1,0:T(8,128)(2,1)S(1)}, u32[]{:S(2)}, u32[]{:S(2)}) collective-permute-start(bf16[512,128]{1,0:T(8,128)(2,1)S(1)} %get-tuple-element.41), channel_id=1, source_target_pairs={{0,9},{1,8},{4,1},{5,0},{8,13},{9,12},{12,5},{13,4},{2,11},{3,10},... | collective-permute-start | bytes 393224 | tf_op jit(solution)/shard_map/ppermute | solution.py:44
  7.6 6.5 %collective-permute-start = (bf16[592,128]{1,0:T(8,128)(2,1)S(1)}, bf16[592,128]{1,0:T(8,128)(2,1)S(1)}, u32[]{:S(2)}, u32[]{:S(2)}) collective-permute-start(bf16[592,128]{1,0:T(8,128)(2,1)S(1)} %get-tuple-element.40), channel_id=1, source_target_pairs={{0,8},{8,12},{12,4},{4,0},{1,9},{9,13},{13,5},{5,1},{2,10},{10,14}... | collective-permute-start | bytes 454664 | tf_op jit(solution)/shard_map/ppermute | solution.py:32
  11.9 1.6 %collective-permute-start.4 = (bf16[576,256]{1,0:T(8,128)(2,1)S(1)}, bf16[576,256]{1,0:T(8,128)(2,1)S(1)}, u32[]{:S(2)}, u32[]{:S(2)}) collective-permute-start(bf16[576,256]{1,0:T(8,128)(2,1)S(1)} %collective-permute-done.3.refs_0_.refs_8_), channel_id=1, source_target_pairs={{0,1},{1,0},{2,3},{3,2},{4,5},{5,4},{6,7},{7,6},{8,9},{9,8},{10,11... | collective-permute-start | bytes 884744 | tf_op jit(solution)/shard_map/ppermute | solution.py:22
  14.1 10.9 %collective-permute-start.7 = (bf16[1104,128]{1,0:T(8,128)(2,1)S(1)}, bf16[1104,128]{1,0:T(8,128)(2,1)S(1)}, u32[]{:S(2)}, u32[]{:S(2)}) collective-permute-start(bf16[1104,128]{1,0:T(8,128)(2,1)S(1)} %pad_maximum_fusion.refs_1_), channel_id=1, source_target_pairs={{0,8},{8,12},{12,4},{4,0},{1,9},{9,13},{13,5},{5,1},{2,10},{10,14}... | collective-permute-start | bytes 847880 | tf_op jit(solution)/shard_map/ppermute | solution.py:32
  17.5 13.6 %collective-permute-start.6 = (bf16[512,128]{1,0:T(8,128)(2,1)S(1)}, bf16[512,128]{1,0:T(8,128)(2,1)S(1)}, u32[]{:S(2)}, u32[]{:S(2)}) collective-permute-start(bf16[512,128]{1,0:T(8,128)(2,1)S(1)} %get-tuple-element.41), channel_id=1, source_target_pairs={{0,5},{1,4},{4,13},{5,12},{8,1},{9,0},{12,9},{13,8},{2,7},{3,6},{6... | collective-permute-start | bytes 393224 | tf_op jit(solution)/shard_map/ppermute | solution.py:44
  17.5 13.6 %collective-permute-start.5 = (bf16[592,128]{1,0:T(8,128)(2,1)S(1)}, bf16[592,128]{1,0:T(8,128)(2,1)S(1)}, u32[]{:S(2)}, u32[]{:S(2)}) collective-permute-start(bf16[592,128]{1,0:T(8,128)(2,1)S(1)} %get-tuple-element.40), channel_id=1, source_target_pairs={{0,4},{8,0},{12,8},{4,12},{1,5},{9,1},{13,9},{5,13},{2,6},{10,2},{... | collective-permute-start | bytes 454664 | tf_op jit(solution)/shard_map/ppermute | solution.py:32
  39.0 5.1 %collective-permute-start.10 = (f32[56,128]{1,0:T(8,128)S(1)}, f32[56,128]{1,0:T(8,128)S(1)}, u32[]{:S(2)}, u32[]{:S(2)}) collective-permute-start(f32[56,128]{1,0:T(8,128)S(1)} %get-tuple-element.89), channel_id=1, source_target_pairs={{0,4},{8,0},{12,8},{4,12},{1,5},{9,1},{13,9},{5,13},{2,6},{10,2},{... | collective-permute-start | bytes 86024 | tf_op jit(solution)/shard_map/ppermute | solution.py:32
  40.6 5.9 %collective-permute-start.11 = (f32[56,128]{1,0:T(8,128)S(1)}, f32[56,128]{1,0:T(8,128)S(1)}, u32[]{:S(2)}, u32[]{:S(2)}) collective-permute-start(f32[56,128]{1,0:T(8,128)S(1)} %get-tuple-element.90), channel_id=1, source_target_pairs={{0,12},{8,4},{12,0},{4,8},{1,13},{9,5},{13,1},{5,9},{2,14},{10,6},... | collective-permute-start | bytes 86024 | tf_op jit(solution)/shard_map/ppermute | solution.py:32
  42.9 3.9 %collective-permute-start.12 = (f32[56,128]{1,0:T(8,128)S(1)}, f32[56,128]{1,0:T(8,128)S(1)}, u32[]{:S(2)}, u32[]{:S(2)}) collective-permute-start(f32[56,128]{1,0:T(8,128)S(1)} %get-tuple-element.91), channel_id=1, source_target_pairs={{0,8},{8,12},{12,4},{4,0},{1,9},{9,13},{13,5},{5,1},{2,10},{10,14}... | collective-permute-start | bytes 86024 | tf_op jit(solution)/shard_map/ppermute | solution.py:32
  43.6 3.4 %collective-permute-start.8 = (bf16[16,32,512]{2,1,0:T(8,128)(2,1)S(1)}, bf16[16,32,512]{2,1,0:T(8,128)(2,1)S(1)}, u32[]{:S(2)}, u32[]{:S(2)}) collective-permute-start(bf16[16,32,512]{2,1,0:T(8,128)(2,1)S(1)} %get-tuple-element.53), channel_id=1, source_target_pairs={{0,1},{1,0},{2,3},{3,2},{4,5},{5,4},{6,7},{7,6},{8,9},{9,8},{10,11... | collective-permute-start | bytes 1572872 | tf_op jit(solution)/shard_map/ppermute | solution.py:22
  47.4 5.0 %collective-permute-start.13 = (f32[4,8,512]{2,1,0:T(8,128)S(1)}, f32[4,8,512]{2,1,0:T(8,128)S(1)}, u32[]{:S(2)}, u32[]{:S(2)}) collective-permute-start(f32[4,8,512]{2,1,0:T(8,128)S(1)} %fusion), channel_id=1, source_target_pairs={{0,2},{2,0},{1,3},{3,1},{4,6},{6,4},{5,7},{7,5},{8,10},{10,8},{9,1... | collective-permute-start | bytes 196616 | tf_op jit(solution)/shard_map/ppermute | solution.py:22
  48.5 7.7 %collective-permute-start.9 = (bf16[16,32,256]{2,1,0:T(8,128)(2,1)S(1)}, bf16[16,32,256]{2,1,0:T(8,128)(2,1)S(1)}, u32[]{:S(2)}, u32[]{:S(2)}) collective-permute-start(bf16[16,32,256]{2,1,0:T(8,128)(2,1)S(1)} %slice.307), channel_id=1, source_target_pairs={{0,2},{2,0},{1,3},{3,1},{4,6},{6,4},{5,7},{7,5},{8,10},{10,8},{9,1... | collective-permute-start | bytes 786440 | tf_op jit(solution)/shard_map/ppermute | solution.py:22
  52.5 1.3 %collective-permute-start.14 = (f32[4,8,512]{2,1,0:T(8,128)S(1)}, f32[4,8,512]{2,1,0:T(8,128)S(1)}, u32[]{:S(2)}, u32[]{:S(2)}) collective-permute-start(f32[4,8,512]{2,1,0:T(8,128)S(1)} %select_add_fusion), channel_id=1, source_target_pairs={{0,1},{1,0},{2,3},{3,2},{4,5},{5,4},{6,7},{7,6},{8,9},{9,8},{10,11... | collective-permute-start | bytes 196616 | tf_op jit(solution)/shard_map/ppermute | solution.py:22

commit v20 on v16

--- a/solution.py
+++ b/solution.py
@@ -236,14 +236,14 @@
     def _(pair):
         turn = 2 * pair + 1
         for span in spans:
+            products(turn + 2, left_a, raw_a, span)
             summed(turn, left_a, columns_a, span)
             pointwise(turn + 1, raw_b, backward, (halves[3], halves[2]), span)
-            products(turn + 2, left_a, raw_a, span)
         source_sums(turn)
         for span in spans:
+            products(turn + 3, left_b, raw_b, span)
             summed(turn + 1, left_b, columns_b, span)
             pointwise(turn + 2, raw_a, forward, (halves[0], halves[1]), span)
-            products(turn + 3, left_b, raw_b, span)
 
     for coord in range(3):
         back_ref[coord] = -0.5 * back[:, coord, :] - there[coord] * back[:, 6, :]

time: 57.2 us -> 58.6 us (1.024)
  Pallas kernels: 24.5 us -> 25.8 us
    pallas_call x3, Pallas kernels: 20.4 us -> 21.7 us  [run_step(): pl.pallas_call(functools.partial(step_kernel, step, length, rhs, subs, fi...]
  transfers between devices with their start and end apart: 15 -> 15, of which waited for: 9 -> 9; matrix products, arithmetic and copies ran while one was open for 3% -> 3% of each run, Pallas kernels for 28% -> 29%
where the time goes in v20:
time: 58.6 us; the launch traced here: 58.4 us
  Pallas kernels  25.8 us (44%)
  starting transfers between devices  18.4 us (31%)
  waiting for transfers between devices  11.1 us (19%)
  other arithmetic  1.23 us (2%)
  between operations  1.03 us (2%)
  local copies, waits for them, and re-layouts  0.91 us (2%)
    pallas_call x3, Pallas kernels, run_step(): pl.pallas_call(functools.partial(step_kernel, step, length, rhs, subs, fi...  21.7 us
    ppermute x6, starting transfers between devices, round_ring(): return lax.ppermute(value, 'clus', pairs)  10.4 us
    ppermute x7, waiting for transfers between devices, shifted(): return lax.ppermute(value, axis, pairs)  7.09 us
    ppermute x7, starting transfers between devices, shifted(): return lax.ppermute(value, axis, pairs)  5.24 us
    ppermute x6, waiting for transfers between devices, round_ring(): return lax.ppermute(value, 'clus', pairs)  3.98 us
    ppermute x2, starting transfers between devices, moved(): return lax.ppermute(value, axes, pairs)  2.7 us
    pallas_call x1, Pallas kernels, on_device(): pl.pallas_call(node_kernel, out_shape=jax.ShapeDtypeStruct((3, share * pa...  1.32 us
    pallas_call x1, Pallas kernels, on_device(): pl.pallas_call(functools.partial(prepare_kernel, (panels, nodes_total)),...  1.22 us
  transfers between devices with their start and end apart: 15, of which 9 were waited for; matrix products, arithmetic and copies ran while one was open for 3% of the time, Pallas kernels for 29%

profile of v20, /device:TPU:0, one launch (start us, length us, event | category | flops | bytes accessed | tf_op | source)
XLA Modules:
  0.0 58.4 jit_solution(18151305028044827525)
XLA Ops:
  0.6 0.0 copy-start
  0.6 1.2 %prepare.1 = (bf16[592,128]{1,0:T(8,128)(2,1)S(1)}, bf16[512,128]{1,0:T(8,128)(2,1)S(1)}, bf16[576,256]{1,0:T(8,128)(2,1)S(1)}) custom-call(bf16[16,32,256]{2,1,0:T(8,128)(2,1)} %refs_0_.1, bf16[3,16,256]{2,1,0:T(8,128)(2,1)} %bitcast.91, bf16[16,256]{1,0:T(8,128)(2,1)} %refs_2_.1, s32[16,4,256]{2,1,0:T(4,128)} %refs_3_.1, bf16[16,32,256]{2,1,0:T(8,128)(2,1)} %refs_4_.1), custom_call_target="tpu_custom_call" | custom-call | tf_op jit(solution)/shard_map/prepare/pallas_call | solution.py:382
  1.9 3.0 %collective-permute-start.3 = (bf16[576,256]{1,0:T(8,128)(2,1)S(1)}, bf16[576,256]{1,0:T(8,128)(2,1)S(1)}, u32[]{:S(2)}, u32[]{:S(2)}) collective-permute-start(bf16[576,256]{1,0:T(8,128)(2,1)S(1)} %get-tuple-element.33.refs_0_.refs_7_), channel_id=1, source_target_pairs={{0,2},{2,0},{1,3},{3,1},{4,6},{6,4},{5,7},{7,5},{8,10},{10,8},{9,1... | collective-permute-start | bytes 884744 | tf_op jit(solution)/shard_map/ppermute | solution.py:22
  4.9 0.0 collective-permute-start.2
  4.9 2.7 %collective-permute-start.1 = (bf16[512,128]{1,0:T(8,128)(2,1)S(1)}, bf16[512,128]{1,0:T(8,128)(2,1)S(1)}, u32[]{:S(2)}, u32[]{:S(2)}) collective-permute-start(bf16[512,128]{1,0:T(8,128)(2,1)S(1)} %get-tuple-element.41), channel_id=1, source_target_pairs={{0,9},{1,8},{4,1},{5,0},{8,13},{9,12},{12,5},{13,4},{2,11},{3,10},... | collective-permute-start | bytes 393224 | tf_op jit(solution)/shard_map/ppermute | solution.py:44
  7.6 1.6 %collective-permute-start = (bf16[592,128]{1,0:T(8,128)(2,1)S(1)}, bf16[592,128]{1,0:T(8,128)(2,1)S(1)}, u32[]{:S(2)}, u32[]{:S(2)}) collective-permute-start(bf16[592,128]{1,0:T(8,128)(2,1)S(1)} %get-tuple-element.40), channel_id=1, source_target_pairs={{0,8},{8,12},{12,4},{4,0},{1,9},{9,13},{13,5},{5,1},{2,10},{10,14}... | collective-permute-start | bytes 454664 | tf_op jit(solution)/shard_map/ppermute | solution.py:32
  9.2 0.0 copy-done
  9.2 0.1 constant_dynamic-slice_fusion
  9.2 0.1 reshape.294
  9.3 0.1 mul.22
  9.4 0.2 convert_reduce_fusion
  9.6 0.2 convert_reduce_fusion.1
  9.8 0.1 copy.34
  9.9 0.2 select_reduce_fusion
  10.1 1.8 %collective-permute-done.3.refs_0_.refs_8_ = bf16[576,256]{1,0:T(8,128)(2,1)S(1)} collective-permute-done((bf16[576,256]{1,0:T(8,128)(2,1)S(1)}, bf16[576,256]{1,0:T(8,128)(2,1)S(1)}, u32[]{:S(2)}, u32[]{:S(2)}) %collective-permute-start.3) | collective-permute-done | bytes 294944 | tf_op jit(solution)/shard_map/ppermute | solution.py:22
  11.9 0.0 collective-permute-start.4
  11.9 0.1 pad_slice_fusion
  12.0 0.1 pad_add_fusion
  12.0 0.1 reshape.295.refs_0_
  12.1 0.1 pad.40.clone
  12.2 0.0 collective-permute-done.2.refs_1_
  12.2 0.4 targets_0.1
  12.6 0.9 %collective-permute-done.4.refs_1_ = bf16[576,256]{1,0:T(8,128)(2,1)S(1)} collective-permute-done((bf16[576,256]{1,0:T(8,128)(2,1)S(1)}, bf16[576,256]{1,0:T(8,128)(2,1)S(1)}, u32[]{:S(2)}, u32[]{:S(2)}) %collective-permute-start.4) | collective-permute-done | bytes 294944 | tf_op jit(solution)/shard_map/ppermute | solution.py:22
  13.5 0.4 targets_1.1
  13.9 0.0 collective-permute-done.1
  13.9 0.2 collective-permute-done
  14.1 3.4 %collective-permute-start.7 = (bf16[1104,128]{1,0:T(8,128)(2,1)S(1)}, bf16[1104,128]{1,0:T(8,128)(2,1)S(1)}, u32[]{:S(2)}, u32[]{:S(2)}) collective-permute-start(bf16[1104,128]{1,0:T(8,128)(2,1)S(1)} %pad_maximum_fusion.refs_1_), channel_id=1, source_target_pairs={{0,8},{8,12},{12,4},{4,0},{1,9},{9,13},{13,5},{5,1},{2,10},{10,14}... | collective-permute-start | bytes 847880 | tf_op jit(solution)/shard_map/ppermute | solution.py:32
  17.5 0.0 collective-permute-start.6
  17.5 0.8 %collective-permute-start.5 = (bf16[592,128]{1,0:T(8,128)(2,1)S(1)}, bf16[592,128]{1,0:T(8,128)(2,1)S(1)}, u32[]{:S(2)}, u32[]{:S(2)}) collective-permute-start(bf16[592,128]{1,0:T(8,128)(2,1)S(1)} %get-tuple-element.40), channel_id=1, source_target_pairs={{0,4},{8,0},{12,8},{4,12},{1,5},{9,1},{13,9},{5,13},{2,6},{10,2},{... | collective-permute-start | bytes 454664 | tf_op jit(solution)/shard_map/ppermute | solution.py:32
  18.4 7.9 %near_field_0.1 = (f32[16,80,512]{2,1,0:T(8,128)S(1)}, f32[3,16,128]{2,1,0:T(8,128)S(1)}) custom-call(s32[108]{0:T(128)S(1)} %reshape.295.refs_0_, bf16[1104,128]{1,0:T(8,128)(2,1)S(1)} %pad_maximum_fusion.refs_1_, bf16[16,256,128]{2,1,0:T(8,128)(2,1)S(1)} %get-tuple-element.43.refs_2_, bf16[16,256,128]{2,1,0:T(8,128)(2,1)S(1)} %get-tuple-element.44.refs_3_, ...), custom_call_target="tpu_custom_call" | custom-call | flops 692060160 | bytes 6291456 | tf_op jit(solution)/shard_map/near_field_0/pallas_call | solution.py:295
  26.3 0.0 collective-permute-done.7.refs_1_
  26.3 7.0 %near_field_1.1 = (f32[16,80,512]{2,1,0:T(8,128)S(1)}, f32[3,16,128]{2,1,0:T(8,128)S(1)}) custom-call(s32[108]{0:T(128)S(1)} %reshape.295.refs_0_, bf16[1104,128]{1,0:T(8,128)(2,1)S(1)} %collective-permute-done.7.refs_1_, bf16[16,256,128]{2,1,0:T(8,128)(2,1)S(1)} %get-tuple-element.43.refs_2_, bf16[16,256,128]{2,1,0:T(8,128)(2,1)S(1)} %get-tuple-element.44.refs_3_, ...), custom_call_target="tpu_custom_call" | custom-call | flops 692060160 | bytes 6291456 | tf_op jit(solution)/shard_map/near_field_1/pallas_call | solution.py:295
  33.3 0.0 collective-permute-done.6
  33.3 0.0 collective-permute-done.5
  33.4 6.8 %near_field_2.1 = (f32[16,32,512]{2,1,0:T(8,128)S(1)}, bf16[16,32,512]{2,1,0:T(8,128)(2,1)S(1)}, f32[3,16,512]{2,1,0:T(8,128)S(1)}, f32[3,16,128]{2,1,0:T(8,128)S(1)}) custom-call(s32[108]{0:T(128)S(1)} %reshape.295.refs_0_, bf16[1104,128]{1,0:T(8,128)(2,1)S(1)} %pad_maximum_fusion.1.refs_1_, bf16[16,256,128]{2,1,0:T(8,128)(2,1)S(1)} %get-tuple-element.43.refs_2_, ...), custom_call_target="tpu_custom_call" | custom-call | flops 692060160 | bytes 6291456 | tf_op jit(solution)/shard_map/near_field_2/pallas_call | solution.py:295
  40.2 0.1 copy.38
  40.4 0.1 maximum_maximum_fusion
  40.5 2.2 %collective-permute-start.10 = (f32[56,128]{1,0:T(8,128)S(1)}, f32[56,128]{1,0:T(8,128)S(1)}, u32[]{:S(2)}, u32[]{:S(2)}) collective-permute-start(f32[56,128]{1,0:T(8,128)S(1)} %get-tuple-element.89), channel_id=1, source_target_pairs={{0,4},{8,0},{12,8},{4,12},{1,5},{9,1},{13,9},{5,13},{2,6},{10,2},{... | collective-permute-start | bytes 86024 | tf_op jit(solution)/shard_map/ppermute | solution.py:32
  42.7 2.4 %collective-permute-start.11 = (f32[56,128]{1,0:T(8,128)S(1)}, f32[56,128]{1,0:T(8,128)S(1)}, u32[]{:S(2)}, u32[]{:S(2)}) collective-permute-start(f32[56,128]{1,0:T(8,128)S(1)} %get-tuple-element.90), channel_id=1, source_target_pairs={{0,12},{8,4},{12,0},{4,8},{1,13},{9,5},{13,1},{5,9},{2,14},{10,6},... | collective-permute-start | bytes 86024 | tf_op jit(solution)/shard_map/ppermute | solution.py:32
  45.1 0.0 collective-permute-start.12
  45.1 0.0 collective-permute-start.8
  45.2 0.4 collective-permute-done.10
  45.6 2.7 %collective-permute-done.11 = f32[56,128]{1,0:T(8,128)S(1)} collective-permute-done((f32[56,128]{1,0:T(8,128)S(1)}, f32[56,128]{1,0:T(8,128)S(1)}, u32[]{:S(2)}, u32[]{:S(2)}) %collective-permute-start.11) | collective-permute-done | bytes 28704 | tf_op jit(solution)/shard_map/ppermute | solution.py:32
  48.4 0.6 %collective-permute-done.12 = f32[56,128]{1,0:T(8,128)S(1)} collective-permute-done((f32[56,128]{1,0:T(8,128)S(1)}, f32[56,128]{1,0:T(8,128)S(1)}, u32[]{:S(2)}, u32[]{:S(2)}) %collective-permute-start.12) | collective-permute-done | bytes 28704 | tf_op jit(solution)/shard_map/ppermute | solution.py:32
  49.1 0.0 collective-permute-done.8
  49.1 0.2 convert_add_fusion
  49.6 0.8 %collective-permute-start.13 = (f32[4,8,512]{2,1,0:T(8,128)S(1)}, f32[4,8,512]{2,1,0:T(8,128)S(1)}, u32[]{:S(2)}, u32[]{:S(2)}) collective-permute-start(f32[4,8,512]{2,1,0:T(8,128)S(1)} %fusion), channel_id=1, source_target_pairs={{0,2},{2,0},{1,3},{3,1},{4,6},{6,4},{5,7},{7,5},{8,10},{10,8},{9,1... | collective-permute-start | bytes 196616 | tf_op jit(solution)/shard_map/ppermute | solution.py:22
  50.4 1.4 %collective-permute-start.9 = (bf16[16,32,256]{2,1,0:T(8,128)(2,1)S(1)}, bf16[16,32,256]{2,1,0:T(8,128)(2,1)S(1)}, u32[]{:S(2)}, u32[]{:S(2)}) collective-permute-start(bf16[16,32,256]{2,1,0:T(8,128)(2,1)S(1)} %slice.307), channel_id=1, source_target_pairs={{0,2},{2,0},{1,3},{3,1},{4,6},{6,4},{5,7},{7,5},{8,10},{10,8},{9,1... | collective-permute-start | bytes 786440 | tf_op jit(solution)/shard_map/ppermute | solution.py:22
  51.8 2.9 %collective-permute-done.13 = f32[4,8,512]{2,1,0:T(8,128)S(1)} collective-permute-done((f32[4,8,512]{2,1,0:T(8,128)S(1)}, f32[4,8,512]{2,1,0:T(8,128)S(1)}, u32[]{:S(2)}, u32[]{:S(2)}) %collective-permute-start.13) | collective-permute-done | bytes 65568 | tf_op jit(solution)/shard_map/ppermute | solution.py:22
  54.7 0.1 collective-permute-start.14
  54.8 1.2 %collective-permute-done.14 = f32[4,8,512]{2,1,0:T(8,128)S(1)} collective-permute-done((f32[4,8,512]{2,1,0:T(8,128)S(1)}, f32[4,8,512]{2,1,0:T(8,128)S(1)}, u32[]{:S(2)}, u32[]{:S(2)}) %collective-permute-start.14) | collective-permute-done | bytes 65568 | tf_op jit(solution)/shard_map/ppermute | solution.py:22
  56.0 1.3 %node_terms.1 = f32[3,4096]{1,0:T(4,128)} custom-call(f32[3,8,512]{2,1,0:T(8,128)S(1)} %slice.197.grad_ref, s32[8,512]{1,0:T(8,128)S(1)} %slice_select_fusion.2.jitter_ref, f32[8,512]{1,0:T(8,128)S(1)} %slice_bitcast_fusion.edge_ref), custom_call_target="tpu_custom_call" | custom-call | flops 1048576 | bytes 262144 | tf_op jit(solution)/shard_map/node_terms/pallas_call | solution.py:574
  57.4 0.3 collective-permute-done.9.refs_1_
  57.7 0.7 %potential_sum.1 = bf16[16,32,256]{2,1,0:T(8,128)(2,1)} custom-call(f32[16,32,256]{2,1,0:T(8,128)S(1)} %slice.127.refs_0_, bf16[16,32,256]{2,1,0:T(8,128)(2,1)S(1)} %collective-permute-done.9.refs_1_), custom_call_target="tpu_custom_call" | custom-call | flops 1048576 | bytes 262144 | tf_op jit(solution)/shard_map/potential_sum/pallas_call | solution.py:583
  (47 shorter events, 0.6 us)
Async XLA Ops:
  0.6 8.5 %copy-start = (s32[5,64]{1,0:T(8,128)S(1)}, s32[5,64]{1,0:T(8,128)}, u32[]{:S(2)}) copy-start(s32[5,64]{1,0:T(8,128)} %param.10) | copy-start | bytes 3844
  1.9 10.0 %collective-permute-start.3 = (bf16[576,256]{1,0:T(8,128)(2,1)S(1)}, bf16[576,256]{1,0:T(8,128)(2,1)S(1)}, u32[]{:S(2)}, u32[]{:S(2)}) collective-permute-start(bf16[576,256]{1,0:T(8,128)(2,1)S(1)} %get-tuple-element.33.refs_0_.refs_7_), channel_id=1, source_target_pairs={{0,2},{2,0},{1,3},{3,1},{4,6},{6,4},{5,7},{7,5},{8,10},{10,8},{9,1... | collective-permute-start | bytes 884744 | tf_op jit(solution)/shard_map/ppermute | solution.py:22
  4.9 7.3 %collective-permute-start.2 = (bf16[576,256]{1,0:T(8,128)(2,1)S(1)}, bf16[576,256]{1,0:T(8,128)(2,1)S(1)}, u32[]{:S(2)}, u32[]{:S(2)}) collective-permute-start(bf16[576,256]{1,0:T(8,128)(2,1)S(1)} %get-tuple-element.33.refs_0_.refs_7_), channel_id=1, source_target_pairs={{0,1},{1,0},{2,3},{3,2},{4,5},{5,4},{6,7},{7,6},{8,9},{9,8},{10,11... | collective-permute-start | bytes 884744 | tf_op jit(solution)/shard_map/ppermute | solution.py:22
  4.9 9.0 %collective-permute-start.1 = (bf16[512,128]{1,0:T(8,128)(2,1)S(1)}, bf16[512,128]{1,0:T(8,128)(2,1)S(1)}, u32[]{:S(2)}, u32[]{:S(2)}) collective-permute-start(bf16[512,128]{1,0:T(8,128)(2,1)S(1)} %get-tuple-element.41), channel_id=1, source_target_pairs={{0,9},{1,8},{4,1},{5,0},{8,13},{9,12},{12,5},{13,4},{2,11},{3,10},... | collective-permute-start | bytes 393224 | tf_op jit(solution)/shard_map/ppermute | solution.py:44
  7.6 6.5 %collective-permute-start = (bf16[592,128]{1,0:T(8,128)(2,1)S(1)}, bf16[592,128]{1,0:T(8,128)(2,1)S(1)}, u32[]{:S(2)}, u32[]{:S(2)}) collective-permute-start(bf16[592,128]{1,0:T(8,128)(2,1)S(1)} %get-tuple-element.40), channel_id=1, source_target_pairs={{0,8},{8,12},{12,4},{4,0},{1,9},{9,13},{13,5},{5,1},{2,10},{10,14}... | collective-permute-start | bytes 454664 | tf_op jit(solution)/shard_map/ppermute | solution.py:32
  11.9 1.6 %collective-permute-start.4 = (bf16[576,256]{1,0:T(8,128)(2,1)S(1)}, bf16[576,256]{1,0:T(8,128)(2,1)S(1)}, u32[]{:S(2)}, u32[]{:S(2)}) collective-permute-start(bf16[576,256]{1,0:T(8,128)(2,1)S(1)} %collective-permute-done.3.refs_0_.refs_8_), channel_id=1, source_target_pairs={{0,1},{1,0},{2,3},{3,2},{4,5},{5,4},{6,7},{7,6},{8,9},{9,8},{10,11... | collective-permute-start | bytes 884744 | tf_op jit(solution)/shard_map/ppermute | solution.py:22
  14.1 12.2 %collective-permute-start.7 = (bf16[1104,128]{1,0:T(8,128)(2,1)S(1)}, bf16[1104,128]{1,0:T(8,128)(2,1)S(1)}, u32[]{:S(2)}, u32[]{:S(2)}) collective-permute-start(bf16[1104,128]{1,0:T(8,128)(2,1)S(1)} %pad_maximum_fusion.refs_1_), channel_id=1, source_target_pairs={{0,8},{8,12},{12,4},{4,0},{1,9},{9,13},{13,5},{5,1},{2,10},{10,14}... | collective-permute-start | bytes 847880 | tf_op jit(solution)/shard_map/ppermute | solution.py:32
  17.5 15.8 %collective-permute-start.6 = (bf16[512,128]{1,0:T(8,128)(2,1)S(1)}, bf16[512,128]{1,0:T(8,128)(2,1)S(1)}, u32[]{:S(2)}, u32[]{:S(2)}) collective-permute-start(bf16[512,128]{1,0:T(8,128)(2,1)S(1)} %get-tuple-element.41), channel_id=1, source_target_pairs={{0,5},{1,4},{4,13},{5,12},{8,1},{9,0},{12,9},{13,8},{2,7},{3,6},{6... | collective-permute-start | bytes 393224 | tf_op jit(solution)/shard_map/ppermute | solution.py:44
  17.5 15.8 %collective-permute-start.5 = (bf16[592,128]{1,0:T(8,128)(2,1)S(1)}, bf16[592,128]{1,0:T(8,128)(2,1)S(1)}, u32[]{:S(2)}, u32[]{:S(2)}) collective-permute-start(bf16[592,128]{1,0:T(8,128)(2,1)S(1)} %get-tuple-element.40), channel_id=1, source_target_pairs={{0,4},{8,0},{12,8},{4,12},{1,5},{9,1},{13,9},{5,13},{2,6},{10,2},{... | collective-permute-start | bytes 454664 | tf_op jit(solution)/shard_map/ppermute | solution.py:32
  40.5 5.1 %collective-permute-start.10 = (f32[56,128]{1,0:T(8,128)S(1)}, f32[56,128]{1,0:T(8,128)S(1)}, u32[]{:S(2)}, u32[]{:S(2)}) collective-permute-start(f32[56,128]{1,0:T(8,128)S(1)} %get-tuple-element.89), channel_id=1, source_target_pairs={{0,4},{8,0},{12,8},{4,12},{1,5},{9,1},{13,9},{5,13},{2,6},{10,2},{... | collective-permute-start | bytes 86024 | tf_op jit(solution)/shard_map/ppermute | solution.py:32
  42.7 5.7 %collective-permute-start.11 = (f32[56,128]{1,0:T(8,128)S(1)}, f32[56,128]{1,0:T(8,128)S(1)}, u32[]{:S(2)}, u32[]{:S(2)}) collective-permute-start(f32[56,128]{1,0:T(8,128)S(1)} %get-tuple-element.90), channel_id=1, source_target_pairs={{0,12},{8,4},{12,0},{4,8},{1,13},{9,5},{13,1},{5,9},{2,14},{10,6},... | collective-permute-start | bytes 86024 | tf_op jit(solution)/shard_map/ppermute | solution.py:32
  45.1 3.9 %collective-permute-start.12 = (f32[56,128]{1,0:T(8,128)S(1)}, f32[56,128]{1,0:T(8,128)S(1)}, u32[]{:S(2)}, u32[]{:S(2)}) collective-permute-start(f32[56,128]{1,0:T(8,128)S(1)} %get-tuple-element.91), channel_id=1, source_target_pairs={{0,8},{8,12},{12,4},{4,0},{1,9},{9,13},{13,5},{5,1},{2,10},{10,14}... | collective-permute-start | bytes 86024 | tf_op jit(solution)/shard_map/ppermute | solution.py:32
  45.1 4.0 %collective-permute-start.8 = (bf16[16,32,512]{2,1,0:T(8,128)(2,1)S(1)}, bf16[16,32,512]{2,1,0:T(8,128)(2,1)S(1)}, u32[]{:S(2)}, u32[]{:S(2)}) collective-permute-start(bf16[16,32,512]{2,1,0:T(8,128)(2,1)S(1)} %get-tuple-element.53), channel_id=1, source_target_pairs={{0,1},{1,0},{2,3},{3,2},{4,5},{5,4},{6,7},{7,6},{8,9},{9,8},{10,11... | collective-permute-start | bytes 1572872 | tf_op jit(solution)/shard_map/ppermute | solution.py:22
  49.6 5.1 %collective-permute-start.13 = (f32[4,8,512]{2,1,0:T(8,128)S(1)}, f32[4,8,512]{2,1,0:T(8,128)S(1)}, u32[]{:S(2)}, u32[]{:S(2)}) collective-permute-start(f32[4,8,512]{2,1,0:T(8,128)S(1)} %fusion), channel_id=1, source_target_pairs={{0,2},{2,0},{1,3},{3,1},{4,6},{6,4},{5,7},{7,5},{8,10},{10,8},{9,1... | collective-permute-start | bytes 196616 | tf_op jit(solution)/shard_map/ppermute | solution.py:22
  50.4 7.3 %collective-permute-start.9 = (bf16[16,32,256]{2,1,0:T(8,128)(2,1)S(1)}, bf16[16,32,256]{2,1,0:T(8,128)(2,1)S(1)}, u32[]{:S(2)}, u32[]{:S(2)}) collective-permute-start(bf16[16,32,256]{2,1,0:T(8,128)(2,1)S(1)} %slice.307), channel_id=1, source_target_pairs={{0,2},{2,0},{1,3},{3,1},{4,6},{6,4},{5,7},{7,5},{8,10},{10,8},{9,1... | collective-permute-start | bytes 786440 | tf_op jit(solution)/shard_map/ppermute | solution.py:22
  54.7 1.3 %collective-permute-start.14 = (f32[4,8,512]{2,1,0:T(8,128)S(1)}, f32[4,8,512]{2,1,0:T(8,128)S(1)}, u32[]{:S(2)}, u32[]{:S(2)}) collective-permute-start(f32[4,8,512]{2,1,0:T(8,128)S(1)} %select_add_fusion), channel_id=1, source_target_pairs={{0,1},{1,0},{2,3},{3,2},{4,5},{5,4},{6,7},{7,6},{8,9},{9,8},{10,11... | collective-permute-start | bytes 196616 | tf_op jit(solution)/shard_map/ppermute | solution.py:22

commit v21 on v16

--- a/solution.py
+++ b/solution.py
@@ -236,13 +236,13 @@
     def _(pair):
         turn = 2 * pair + 1
         for span in spans:
+            pointwise(turn + 1, raw_b, backward, (halves[3], halves[2]), span)
             summed(turn, left_a, columns_a, span)
-            pointwise(turn + 1, raw_b, backward, (halves[3], halves[2]), span)
             products(turn + 2, left_a, raw_a, span)
         source_sums(turn)
         for span in spans:
+            pointwise(turn + 2, raw_a, forward, (halves[0], halves[1]), span)
             summed(turn + 1, left_b, columns_b, span)
-            pointwise(turn + 2, raw_a, forward, (halves[0], halves[1]), span)
             products(turn + 3, left_b, raw_b, span)
 
     for coord in range(3):

time: 57.2 us -> 57.2 us (level)
  no operation moved by 1% of the time
where the time goes in v21:
time: 57.2 us; the launch traced here: 57.1 us
  Pallas kernels  24.5 us (43%)
  starting transfers between devices  18.4 us (32%)
  waiting for transfers between devices  11.1 us (19%)
  other arithmetic  1.23 us (2%)
  between operations  1.03 us (2%)
  local copies, waits for them, and re-layouts  0.91 us (2%)
    pallas_call x3, Pallas kernels, run_step(): pl.pallas_call(functools.partial(step_kernel, step, length, rhs, subs, fi...  20.4 us
    ppermute x6, starting transfers between devices, round_ring(): return lax.ppermute(value, 'clus', pairs)  10.4 us
    ppermute x7, waiting for transfers between devices, shifted(): return lax.ppermute(value, axis, pairs)  7.1 us
    ppermute x7, starting transfers between devices, shifted(): return lax.ppermute(value, axis, pairs)  5.26 us
    ppermute x6, waiting for transfers between devices, round_ring(): return lax.ppermute(value, 'clus', pairs)  3.97 us
    ppermute x2, starting transfers between devices, moved(): return lax.ppermute(value, axes, pairs)  2.7 us
    pallas_call x1, Pallas kernels, on_device(): pl.pallas_call(node_kernel, out_shape=jax.ShapeDtypeStruct((3, share * pa...  1.32 us
    pallas_call x1, Pallas kernels, on_device(): pl.pallas_call(functools.partial(prepare_kernel, (panels, nodes_total)),...  1.22 us
  transfers between devices with their start and end apart: 15, of which 9 were waited for; matrix products, arithmetic and copies ran while one was open for 3% of the time, Pallas kernels for 28%

profile of v21, /device:TPU:0, one launch (start us, length us, event | category | flops | bytes accessed | tf_op | source)
XLA Modules:
  0.0 57.1 jit_solution(2520537494731235438)
XLA Ops:
  0.6 0.0 copy-start
  0.6 1.2 %prepare.1 = (bf16[592,128]{1,0:T(8,128)(2,1)S(1)}, bf16[512,128]{1,0:T(8,128)(2,1)S(1)}, bf16[576,256]{1,0:T(8,128)(2,1)S(1)}) custom-call(bf16[16,32,256]{2,1,0:T(8,128)(2,1)} %refs_0_.1, bf16[3,16,256]{2,1,0:T(8,128)(2,1)} %bitcast.91, bf16[16,256]{1,0:T(8,128)(2,1)} %refs_2_.1, s32[16,4,256]{2,1,0:T(4,128)} %refs_3_.1, bf16[16,32,256]{2,1,0:T(8,128)(2,1)} %refs_4_.1), custom_call_target="tpu_custom_call" | custom-call | tf_op jit(solution)/shard_map/prepare/pallas_call | solution.py:382
  1.9 3.0 %collective-permute-start.3 = (bf16[576,256]{1,0:T(8,128)(2,1)S(1)}, bf16[576,256]{1,0:T(8,128)(2,1)S(1)}, u32[]{:S(2)}, u32[]{:S(2)}) collective-permute-start(bf16[576,256]{1,0:T(8,128)(2,1)S(1)} %get-tuple-element.33.refs_0_.refs_7_), channel_id=1, source_target_pairs={{0,2},{2,0},{1,3},{3,1},{4,6},{6,4},{5,7},{7,5},{8,10},{10,8},{9,1... | collective-permute-start | bytes 884744 | tf_op jit(solution)/shard_map/ppermute | solution.py:22
  4.9 0.0 collective-permute-start.2
  4.9 2.7 %collective-permute-start.1 = (bf16[512,128]{1,0:T(8,128)(2,1)S(1)}, bf16[512,128]{1,0:T(8,128)(2,1)S(1)}, u32[]{:S(2)}, u32[]{:S(2)}) collective-permute-start(bf16[512,128]{1,0:T(8,128)(2,1)S(1)} %get-tuple-element.41), channel_id=1, source_target_pairs={{0,9},{1,8},{4,1},{5,0},{8,13},{9,12},{12,5},{13,4},{2,11},{3,10},... | collective-permute-start | bytes 393224 | tf_op jit(solution)/shard_map/ppermute | solution.py:44
  7.6 1.6 %collective-permute-start = (bf16[592,128]{1,0:T(8,128)(2,1)S(1)}, bf16[592,128]{1,0:T(8,128)(2,1)S(1)}, u32[]{:S(2)}, u32[]{:S(2)}) collective-permute-start(bf16[592,128]{1,0:T(8,128)(2,1)S(1)} %get-tuple-element.40), channel_id=1, source_target_pairs={{0,8},{8,12},{12,4},{4,0},{1,9},{9,13},{13,5},{5,1},{2,10},{10,14}... | collective-permute-start | bytes 454664 | tf_op jit(solution)/shard_map/ppermute | solution.py:32
  9.2 0.0 copy-done
  9.2 0.1 constant_dynamic-slice_fusion
  9.2 0.1 reshape.294
  9.3 0.1 mul.22
  9.4 0.2 convert_reduce_fusion
  9.6 0.2 convert_reduce_fusion.1
  9.8 0.1 copy.34
  9.9 0.2 select_reduce_fusion
  10.1 1.8 %collective-permute-done.3.refs_0_.refs_8_ = bf16[576,256]{1,0:T(8,128)(2,1)S(1)} collective-permute-done((bf16[576,256]{1,0:T(8,128)(2,1)S(1)}, bf16[576,256]{1,0:T(8,128)(2,1)S(1)}, u32[]{:S(2)}, u32[]{:S(2)}) %collective-permute-start.3) | collective-permute-done | bytes 294944 | tf_op jit(solution)/shard_map/ppermute | solution.py:22
  11.9 0.0 collective-permute-start.4
  11.9 0.1 pad_slice_fusion
  12.0 0.1 pad_add_fusion
  12.0 0.1 reshape.295.refs_0_
  12.1 0.1 pad.40.clone
  12.2 0.0 collective-permute-done.2.refs_1_
  12.2 0.4 targets_0.1
  12.6 0.9 %collective-permute-done.4.refs_1_ = bf16[576,256]{1,0:T(8,128)(2,1)S(1)} collective-permute-done((bf16[576,256]{1,0:T(8,128)(2,1)S(1)}, bf16[576,256]{1,0:T(8,128)(2,1)S(1)}, u32[]{:S(2)}, u32[]{:S(2)}) %collective-permute-start.4) | collective-permute-done | bytes 294944 | tf_op jit(solution)/shard_map/ppermute | solution.py:22
  13.5 0.4 targets_1.1
  13.9 0.0 collective-permute-done.1
  13.9 0.2 collective-permute-done
  14.1 3.4 %collective-permute-start.7 = (bf16[1104,128]{1,0:T(8,128)(2,1)S(1)}, bf16[1104,128]{1,0:T(8,128)(2,1)S(1)}, u32[]{:S(2)}, u32[]{:S(2)}) collective-permute-start(bf16[1104,128]{1,0:T(8,128)(2,1)S(1)} %pad_maximum_fusion.refs_1_), channel_id=1, source_target_pairs={{0,8},{8,12},{12,4},{4,0},{1,9},{9,13},{13,5},{5,1},{2,10},{10,14}... | collective-permute-start | bytes 847880 | tf_op jit(solution)/shard_map/ppermute | solution.py:32
  17.5 0.0 collective-permute-start.6
  17.5 0.8 %collective-permute-start.5 = (bf16[592,128]{1,0:T(8,128)(2,1)S(1)}, bf16[592,128]{1,0:T(8,128)(2,1)S(1)}, u32[]{:S(2)}, u32[]{:S(2)}) collective-permute-start(bf16[592,128]{1,0:T(8,128)(2,1)S(1)} %get-tuple-element.40), channel_id=1, source_target_pairs={{0,4},{8,0},{12,8},{4,12},{1,5},{9,1},{13,9},{5,13},{2,6},{10,2},{... | collective-permute-start | bytes 454664 | tf_op jit(solution)/shard_map/ppermute | solution.py:32
  18.4 7.4 %near_field_0.1 = (f32[16,80,512]{2,1,0:T(8,128)S(1)}, f32[3,16,128]{2,1,0:T(8,128)S(1)}) custom-call(s32[108]{0:T(128)S(1)} %reshape.295.refs_0_, bf16[1104,128]{1,0:T(8,128)(2,1)S(1)} %pad_maximum_fusion.refs_1_, bf16[16,256,128]{2,1,0:T(8,128)(2,1)S(1)} %get-tuple-element.43.refs_2_, bf16[16,256,128]{2,1,0:T(8,128)(2,1)S(1)} %get-tuple-element.44.refs_3_, ...), custom_call_target="tpu_custom_call" | custom-call | flops 692060160 | bytes 6291456 | tf_op jit(solution)/shard_map/near_field_0/pallas_call | solution.py:295
  25.8 0.0 collective-permute-done.7.refs_1_
  25.8 6.2 %near_field_1.1 = (f32[16,80,512]{2,1,0:T(8,128)S(1)}, f32[3,16,128]{2,1,0:T(8,128)S(1)}) custom-call(s32[108]{0:T(128)S(1)} %reshape.295.refs_0_, bf16[1104,128]{1,0:T(8,128)(2,1)S(1)} %collective-permute-done.7.refs_1_, bf16[16,256,128]{2,1,0:T(8,128)(2,1)S(1)} %get-tuple-element.43.refs_2_, bf16[16,256,128]{2,1,0:T(8,128)(2,1)S(1)} %get-tuple-element.44.refs_3_, ...), custom_call_target="tpu_custom_call" | custom-call | flops 692060160 | bytes 6291456 | tf_op jit(solution)/shard_map/near_field_1/pallas_call | solution.py:295
  32.0 0.0 collective-permute-done.6
  32.1 0.0 collective-permute-done.5
  32.1 6.7 %near_field_2.1 = (f32[16,32,512]{2,1,0:T(8,128)S(1)}, bf16[16,32,512]{2,1,0:T(8,128)(2,1)S(1)}, f32[3,16,512]{2,1,0:T(8,128)S(1)}, f32[3,16,128]{2,1,0:T(8,128)S(1)}) custom-call(s32[108]{0:T(128)S(1)} %reshape.295.refs_0_, bf16[1104,128]{1,0:T(8,128)(2,1)S(1)} %pad_maximum_fusion.1.refs_1_, bf16[16,256,128]{2,1,0:T(8,128)(2,1)S(1)} %get-tuple-element.43.refs_2_, ...), custom_call_target="tpu_custom_call" | custom-call | flops 692060160 | bytes 6291456 | tf_op jit(solution)/shard_map/near_field_2/pallas_call | solution.py:295
  38.9 0.1 copy.38
  39.1 0.1 maximum_maximum_fusion
  39.2 2.2 %collective-permute-start.10 = (f32[56,128]{1,0:T(8,128)S(1)}, f32[56,128]{1,0:T(8,128)S(1)}, u32[]{:S(2)}, u32[]{:S(2)}) collective-permute-start(f32[56,128]{1,0:T(8,128)S(1)} %get-tuple-element.89), channel_id=1, source_target_pairs={{0,4},{8,0},{12,8},{4,12},{1,5},{9,1},{13,9},{5,13},{2,6},{10,2},{... | collective-permute-start | bytes 86024 | tf_op jit(solution)/shard_map/ppermute | solution.py:32
  41.3 2.4 %collective-permute-start.11 = (f32[56,128]{1,0:T(8,128)S(1)}, f32[56,128]{1,0:T(8,128)S(1)}, u32[]{:S(2)}, u32[]{:S(2)}) collective-permute-start(f32[56,128]{1,0:T(8,128)S(1)} %get-tuple-element.90), channel_id=1, source_target_pairs={{0,12},{8,4},{12,0},{4,8},{1,13},{9,5},{13,1},{5,9},{2,14},{10,6},... | collective-permute-start | bytes 86024 | tf_op jit(solution)/shard_map/ppermute | solution.py:32
  43.7 0.0 collective-permute-start.12
  43.8 0.0 collective-permute-start.8
  43.8 0.5 collective-permute-done.10
  44.3 2.7 %collective-permute-done.11 = f32[56,128]{1,0:T(8,128)S(1)} collective-permute-done((f32[56,128]{1,0:T(8,128)S(1)}, f32[56,128]{1,0:T(8,128)S(1)}, u32[]{:S(2)}, u32[]{:S(2)}) %collective-permute-start.11) | collective-permute-done | bytes 28704 | tf_op jit(solution)/shard_map/ppermute | solution.py:32
  47.0 0.6 %collective-permute-done.12 = f32[56,128]{1,0:T(8,128)S(1)} collective-permute-done((f32[56,128]{1,0:T(8,128)S(1)}, f32[56,128]{1,0:T(8,128)S(1)}, u32[]{:S(2)}, u32[]{:S(2)}) %collective-permute-start.12) | collective-permute-done | bytes 28704 | tf_op jit(solution)/shard_map/ppermute | solution.py:32
  47.8 0.0 collective-permute-done.8
  47.8 0.2 convert_add_fusion
  48.2 0.8 %collective-permute-start.13 = (f32[4,8,512]{2,1,0:T(8,128)S(1)}, f32[4,8,512]{2,1,0:T(8,128)S(1)}, u32[]{:S(2)}, u32[]{:S(2)}) collective-permute-start(f32[4,8,512]{2,1,0:T(8,128)S(1)} %fusion), channel_id=1, source_target_pairs={{0,2},{2,0},{1,3},{3,1},{4,6},{6,4},{5,7},{7,5},{8,10},{10,8},{9,1... | collective-permute-start | bytes 196616 | tf_op jit(solution)/shard_map/ppermute | solution.py:22
  49.0 1.4 %collective-permute-start.9 = (bf16[16,32,256]{2,1,0:T(8,128)(2,1)S(1)}, bf16[16,32,256]{2,1,0:T(8,128)(2,1)S(1)}, u32[]{:S(2)}, u32[]{:S(2)}) collective-permute-start(bf16[16,32,256]{2,1,0:T(8,128)(2,1)S(1)} %slice.307), channel_id=1, source_target_pairs={{0,2},{2,0},{1,3},{3,1},{4,6},{6,4},{5,7},{7,5},{8,10},{10,8},{9,1... | collective-permute-start | bytes 786440 | tf_op jit(solution)/shard_map/ppermute | solution.py:22
  50.4 2.9 %collective-permute-done.13 = f32[4,8,512]{2,1,0:T(8,128)S(1)} collective-permute-done((f32[4,8,512]{2,1,0:T(8,128)S(1)}, f32[4,8,512]{2,1,0:T(8,128)S(1)}, u32[]{:S(2)}, u32[]{:S(2)}) %collective-permute-start.13) | collective-permute-done | bytes 65568 | tf_op jit(solution)/shard_map/ppermute | solution.py:22
  53.3 0.1 collective-permute-start.14
  53.4 1.2 %collective-permute-done.14 = f32[4,8,512]{2,1,0:T(8,128)S(1)} collective-permute-done((f32[4,8,512]{2,1,0:T(8,128)S(1)}, f32[4,8,512]{2,1,0:T(8,128)S(1)}, u32[]{:S(2)}, u32[]{:S(2)}) %collective-permute-start.14) | collective-permute-done | bytes 65568 | tf_op jit(solution)/shard_map/ppermute | solution.py:22
  54.7 1.3 %node_terms.1 = f32[3,4096]{1,0:T(4,128)} custom-call(f32[3,8,512]{2,1,0:T(8,128)S(1)} %slice.197.grad_ref, s32[8,512]{1,0:T(8,128)S(1)} %slice_select_fusion.2.jitter_ref, f32[8,512]{1,0:T(8,128)S(1)} %slice_bitcast_fusion.edge_ref), custom_call_target="tpu_custom_call" | custom-call | flops 1048576 | bytes 262144 | tf_op jit(solution)/shard_map/node_terms/pallas_call | solution.py:574
  56.0 0.3 collective-permute-done.9.refs_1_
  56.3 0.7 %potential_sum.1 = bf16[16,32,256]{2,1,0:T(8,128)(2,1)} custom-call(f32[16,32,256]{2,1,0:T(8,128)S(1)} %slice.127.refs_0_, bf16[16,32,256]{2,1,0:T(8,128)(2,1)S(1)} %collective-permute-done.9.refs_1_), custom_call_target="tpu_custom_call" | custom-call | flops 1048576 | bytes 262144 | tf_op jit(solution)/shard_map/potential_sum/pallas_call | solution.py:583
  (47 shorter events, 0.6 us)
Async XLA Ops:
  0.6 8.5 %copy-start = (s32[5,64]{1,0:T(8,128)S(1)}, s32[5,64]{1,0:T(8,128)}, u32[]{:S(2)}) copy-start(s32[5,64]{1,0:T(8,128)} %param.10) | copy-start | bytes 3844
  1.9 10.0 %collective-permute-start.3 = (bf16[576,256]{1,0:T(8,128)(2,1)S(1)}, bf16[576,256]{1,0:T(8,128)(2,1)S(1)}, u32[]{:S(2)}, u32[]{:S(2)}) collective-permute-start(bf16[576,256]{1,0:T(8,128)(2,1)S(1)} %get-tuple-element.33.refs_0_.refs_7_), channel_id=1, source_target_pairs={{0,2},{2,0},{1,3},{3,1},{4,6},{6,4},{5,7},{7,5},{8,10},{10,8},{9,1... | collective-permute-start | bytes 884744 | tf_op jit(solution)/shard_map/ppermute | solution.py:22
  4.9 7.3 %collective-permute-start.2 = (bf16[576,256]{1,0:T(8,128)(2,1)S(1)}, bf16[576,256]{1,0:T(8,128)(2,1)S(1)}, u32[]{:S(2)}, u32[]{:S(2)}) collective-permute-start(bf16[576,256]{1,0:T(8,128)(2,1)S(1)} %get-tuple-element.33.refs_0_.refs_7_), channel_id=1, source_target_pairs={{0,1},{1,0},{2,3},{3,2},{4,5},{5,4},{6,7},{7,6},{8,9},{9,8},{10,11... | collective-permute-start | bytes 884744 | tf_op jit(solution)/shard_map/ppermute | solution.py:22
  4.9 9.0 %collective-permute-start.1 = (bf16[512,128]{1,0:T(8,128)(2,1)S(1)}, bf16[512,128]{1,0:T(8,128)(2,1)S(1)}, u32[]{:S(2)}, u32[]{:S(2)}) collective-permute-start(bf16[512,128]{1,0:T(8,128)(2,1)S(1)} %get-tuple-element.41), channel_id=1, source_target_pairs={{0,9},{1,8},{4,1},{5,0},{8,13},{9,12},{12,5},{13,4},{2,11},{3,10},... | collective-permute-start | bytes 393224 | tf_op jit(solution)/shard_map/ppermute | solution.py:44
  7.6 6.5 %collective-permute-start = (bf16[592,128]{1,0:T(8,128)(2,1)S(1)}, bf16[592,128]{1,0:T(8,128)(2,1)S(1)}, u32[]{:S(2)}, u32[]{:S(2)}) collective-permute-start(bf16[592,128]{1,0:T(8,128)(2,1)S(1)} %get-tuple-element.40), channel_id=1, source_target_pairs={{0,8},{8,12},{12,4},{4,0},{1,9},{9,13},{13,5},{5,1},{2,10},{10,14}... | collective-permute-start | bytes 454664 | tf_op jit(solution)/shard_map/ppermute | solution.py:32
  11.9 1.6 %collective-permute-start.4 = (bf16[576,256]{1,0:T(8,128)(2,1)S(1)}, bf16[576,256]{1,0:T(8,128)(2,1)S(1)}, u32[]{:S(2)}, u32[]{:S(2)}) collective-permute-start(bf16[576,256]{1,0:T(8,128)(2,1)S(1)} %collective-permute-done.3.refs_0_.refs_8_), channel_id=1, source_target_pairs={{0,1},{1,0},{2,3},{3,2},{4,5},{5,4},{6,7},{7,6},{8,9},{9,8},{10,11... | collective-permute-start | bytes 884744 | tf_op jit(solution)/shard_map/ppermute | solution.py:22
  14.1 11.7 %collective-permute-start.7 = (bf16[1104,128]{1,0:T(8,128)(2,1)S(1)}, bf16[1104,128]{1,0:T(8,128)(2,1)S(1)}, u32[]{:S(2)}, u32[]{:S(2)}) collective-permute-start(bf16[1104,128]{1,0:T(8,128)(2,1)S(1)} %pad_maximum_fusion.refs_1_), channel_id=1, source_target_pairs={{0,8},{8,12},{12,4},{4,0},{1,9},{9,13},{13,5},{5,1},{2,10},{10,14}... | collective-permute-start | bytes 847880 | tf_op jit(solution)/shard_map/ppermute | solution.py:32
  17.5 14.5 %collective-permute-start.6 = (bf16[512,128]{1,0:T(8,128)(2,1)S(1)}, bf16[512,128]{1,0:T(8,128)(2,1)S(1)}, u32[]{:S(2)}, u32[]{:S(2)}) collective-permute-start(bf16[512,128]{1,0:T(8,128)(2,1)S(1)} %get-tuple-element.41), channel_id=1, source_target_pairs={{0,5},{1,4},{4,13},{5,12},{8,1},{9,0},{12,9},{13,8},{2,7},{3,6},{6... | collective-permute-start | bytes 393224 | tf_op jit(solution)/shard_map/ppermute | solution.py:44
  17.5 14.6 %collective-permute-start.5 = (bf16[592,128]{1,0:T(8,128)(2,1)S(1)}, bf16[592,128]{1,0:T(8,128)(2,1)S(1)}, u32[]{:S(2)}, u32[]{:S(2)}) collective-permute-start(bf16[592,128]{1,0:T(8,128)(2,1)S(1)} %get-tuple-element.40), channel_id=1, source_target_pairs={{0,4},{8,0},{12,8},{4,12},{1,5},{9,1},{13,9},{5,13},{2,6},{10,2},{... | collective-permute-start | bytes 454664 | tf_op jit(solution)/shard_map/ppermute | solution.py:32
  39.2 5.1 %collective-permute-start.10 = (f32[56,128]{1,0:T(8,128)S(1)}, f32[56,128]{1,0:T(8,128)S(1)}, u32[]{:S(2)}, u32[]{:S(2)}) collective-permute-start(f32[56,128]{1,0:T(8,128)S(1)} %get-tuple-element.89), channel_id=1, source_target_pairs={{0,4},{8,0},{12,8},{4,12},{1,5},{9,1},{13,9},{5,13},{2,6},{10,2},{... | collective-permute-start | bytes 86024 | tf_op jit(solution)/shard_map/ppermute | solution.py:32
  41.3 5.7 %collective-permute-start.11 = (f32[56,128]{1,0:T(8,128)S(1)}, f32[56,128]{1,0:T(8,128)S(1)}, u32[]{:S(2)}, u32[]{:S(2)}) collective-permute-start(f32[56,128]{1,0:T(8,128)S(1)} %get-tuple-element.90), channel_id=1, source_target_pairs={{0,12},{8,4},{12,0},{4,8},{1,13},{9,5},{13,1},{5,9},{2,14},{10,6},... | collective-permute-start | bytes 86024 | tf_op jit(solution)/shard_map/ppermute | solution.py:32
  43.7 3.9 %collective-permute-start.12 = (f32[56,128]{1,0:T(8,128)S(1)}, f32[56,128]{1,0:T(8,128)S(1)}, u32[]{:S(2)}, u32[]{:S(2)}) collective-permute-start(f32[56,128]{1,0:T(8,128)S(1)} %get-tuple-element.91), channel_id=1, source_target_pairs={{0,8},{8,12},{12,4},{4,0},{1,9},{9,13},{13,5},{5,1},{2,10},{10,14}... | collective-permute-start | bytes 86024 | tf_op jit(solution)/shard_map/ppermute | solution.py:32
  43.8 4.0 %collective-permute-start.8 = (bf16[16,32,512]{2,1,0:T(8,128)(2,1)S(1)}, bf16[16,32,512]{2,1,0:T(8,128)(2,1)S(1)}, u32[]{:S(2)}, u32[]{:S(2)}) collective-permute-start(bf16[16,32,512]{2,1,0:T(8,128)(2,1)S(1)} %get-tuple-element.53), channel_id=1, source_target_pairs={{0,1},{1,0},{2,3},{3,2},{4,5},{5,4},{6,7},{7,6},{8,9},{9,8},{10,11... | collective-permute-start | bytes 1572872 | tf_op jit(solution)/shard_map/ppermute | solution.py:22
  48.2 5.1 %collective-permute-start.13 = (f32[4,8,512]{2,1,0:T(8,128)S(1)}, f32[4,8,512]{2,1,0:T(8,128)S(1)}, u32[]{:S(2)}, u32[]{:S(2)}) collective-permute-start(f32[4,8,512]{2,1,0:T(8,128)S(1)} %fusion), channel_id=1, source_target_pairs={{0,2},{2,0},{1,3},{3,1},{4,6},{6,4},{5,7},{7,5},{8,10},{10,8},{9,1... | collective-permute-start | bytes 196616 | tf_op jit(solution)/shard_map/ppermute | solution.py:22
  49.0 7.3 %collective-permute-start.9 = (bf16[16,32,256]{2,1,0:T(8,128)(2,1)S(1)}, bf16[16,32,256]{2,1,0:T(8,128)(2,1)S(1)}, u32[]{:S(2)}, u32[]{:S(2)}) collective-permute-start(bf16[16,32,256]{2,1,0:T(8,128)(2,1)S(1)} %slice.307), channel_id=1, source_target_pairs={{0,2},{2,0},{1,3},{3,1},{4,6},{6,4},{5,7},{7,5},{8,10},{10,8},{9,1... | collective-permute-start | bytes 786440 | tf_op jit(solution)/shard_map/ppermute | solution.py:22
  53.3 1.3 %collective-permute-start.14 = (f32[4,8,512]{2,1,0:T(8,128)S(1)}, f32[4,8,512]{2,1,0:T(8,128)S(1)}, u32[]{:S(2)}, u32[]{:S(2)}) collective-permute-start(f32[4,8,512]{2,1,0:T(8,128)S(1)} %select_add_fusion), channel_id=1, source_target_pairs={{0,1},{1,0},{2,3},{3,2},{4,5},{5,4},{6,7},{7,6},{8,9},{9,8},{10,11... | collective-permute-start | bytes 196616 | tf_op jit(solution)/shard_map/ppermute | solution.py:22

commit v22 on v21

--- a/solution.py
+++ b/solution.py
@@ -236,13 +236,15 @@
     def _(pair):
         turn = 2 * pair + 1
         for span in spans:
-            pointwise(turn + 1, raw_b, backward, (halves[3], halves[2]), span)
+            pointwise(turn + 1, raw_b, backward, (halves[3], halves[2]), slice(span.start, span.start + LANES))
             summed(turn, left_a, columns_a, span)
+            pointwise(turn + 1, raw_b, backward, (halves[3], halves[2]), slice(span.start + LANES, span.stop))
             products(turn + 2, left_a, raw_a, span)
         source_sums(turn)
         for span in spans:
-            pointwise(turn + 2, raw_a, forward, (halves[0], halves[1]), span)
+            pointwise(turn + 2, raw_a, forward, (halves[0], halves[1]), slice(span.start, span.start + LANES))
             summed(turn + 1, left_b, columns_b, span)
+            pointwise(turn + 2, raw_a, forward, (halves[0], halves[1]), slice(span.start + LANES, span.stop))
             products(turn + 3, left_b, raw_b, span)
 
     for coord in range(3):

time: 57.2 us -> 57.2 us (level)
    ppermute x7, waiting for transfers between devices: 7.1 us -> 7.69 us  [shifted(): return lax.ppermute(value, axis, pairs)]
  transfers between devices with their start and end apart: 15 -> 15, of which waited for: 9 -> 9; matrix products, arithmetic and copies ran while one was open for 3% -> 3% of each run, Pallas kernels for 28% -> 27%
where the time goes in v22:
time: 57.2 us
  Pallas kernels  24.3 us (42%)
  starting transfers between devices  18.5 us (32%)
  waiting for transfers between devices  11.2 us (20%)
  other arithmetic  1.23 us (2%)
  between operations  1.03 us (2%)
  local copies, waits for them, and re-layouts  0.91 us (2%)
    pallas_call x3, Pallas kernels, run_step(): pl.pallas_call(functools.partial(step_kernel, step, length, rhs, subs, fi...  20.2 us
    ppermute x6, starting transfers between devices, round_ring(): return lax.ppermute(value, 'clus', pairs)  10.6 us
    ppermute x7, waiting for transfers between devices, shifted(): return lax.ppermute(value, axis, pairs)  7.69 us
    ppermute x7, starting transfers between devices, shifted(): return lax.ppermute(value, axis, pairs)  5.24 us
    ppermute x6, waiting for transfers between devices, round_ring(): return lax.ppermute(value, 'clus', pairs)  3.53 us
    ppermute x2, starting transfers between devices, moved(): return lax.ppermute(value, axes, pairs)  2.7 us
    pallas_call x1, Pallas kernels, on_device(): pl.pallas_call(node_kernel, out_shape=jax.ShapeDtypeStruct((3, share * pa...  1.32 us
    pallas_call x1, Pallas kernels, on_device(): pl.pallas_call(functools.partial(prepare_kernel, (panels, nodes_total)),...  1.22 us
  transfers between devices with their start and end apart: 15, of which 9 were waited for; matrix products, arithmetic and copies ran while one was open for 3% of the time, Pallas kernels for 27%

profile of v22, /device:TPU:0, one launch (start us, length us, event | category | flops | bytes accessed | tf_op | source)
XLA Modules:
  0.0 57.2 jit_solution(2884491478472173215)
XLA Ops:
  0.6 0.0 copy-start
  0.6 1.2 %prepare.1 = (bf16[592,128]{1,0:T(8,128)(2,1)S(1)}, bf16[512,128]{1,0:T(8,128)(2,1)S(1)}, bf16[576,256]{1,0:T(8,128)(2,1)S(1)}) custom-call(bf16[16,32,256]{2,1,0:T(8,128)(2,1)} %refs_0_.1, bf16[3,16,256]{2,1,0:T(8,128)(2,1)} %bitcast.91, bf16[16,256]{1,0:T(8,128)(2,1)} %refs_2_.1, s32[16,4,256]{2,1,0:T(4,128)} %refs_3_.1, bf16[16,32,256]{2,1,0:T(8,128)(2,1)} %refs_4_.1), custom_call_target="tpu_custom_call" | custom-call | tf_op jit(solution)/shard_map/prepare/pallas_call | solution.py:384
  1.9 3.0 %collective-permute-start.3 = (bf16[576,256]{1,0:T(8,128)(2,1)S(1)}, bf16[576,256]{1,0:T(8,128)(2,1)S(1)}, u32[]{:S(2)}, u32[]{:S(2)}) collective-permute-start(bf16[576,256]{1,0:T(8,128)(2,1)S(1)} %get-tuple-element.33.refs_0_.refs_7_), channel_id=1, source_target_pairs={{0,2},{2,0},{1,3},{3,1},{4,6},{6,4},{5,7},{7,5},{8,10},{10,8},{9,1... | collective-permute-start | bytes 884744 | tf_op jit(solution)/shard_map/ppermute | solution.py:22
  4.9 0.0 collective-permute-start.2
  4.9 2.7 %collective-permute-start.1 = (bf16[512,128]{1,0:T(8,128)(2,1)S(1)}, bf16[512,128]{1,0:T(8,128)(2,1)S(1)}, u32[]{:S(2)}, u32[]{:S(2)}) collective-permute-start(bf16[512,128]{1,0:T(8,128)(2,1)S(1)} %get-tuple-element.41), channel_id=1, source_target_pairs={{0,9},{1,8},{4,1},{5,0},{8,13},{9,12},{12,5},{13,4},{2,11},{3,10},... | collective-permute-start | bytes 393224 | tf_op jit(solution)/shard_map/ppermute | solution.py:44
  7.6 1.6 %collective-permute-start = (bf16[592,128]{1,0:T(8,128)(2,1)S(1)}, bf16[592,128]{1,0:T(8,128)(2,1)S(1)}, u32[]{:S(2)}, u32[]{:S(2)}) collective-permute-start(bf16[592,128]{1,0:T(8,128)(2,1)S(1)} %get-tuple-element.40), channel_id=1, source_target_pairs={{0,8},{8,12},{12,4},{4,0},{1,9},{9,13},{13,5},{5,1},{2,10},{10,14}... | collective-permute-start | bytes 454664 | tf_op jit(solution)/shard_map/ppermute | solution.py:32
  9.2 0.0 copy-done
  9.2 0.1 constant_dynamic-slice_fusion
  9.2 0.1 reshape.294
  9.3 0.1 mul.22
  9.4 0.2 convert_reduce_fusion
  9.6 0.2 convert_reduce_fusion.1
  9.8 0.1 copy.34
  9.9 0.2 select_reduce_fusion
  10.1 1.8 %collective-permute-done.3.refs_0_.refs_8_ = bf16[576,256]{1,0:T(8,128)(2,1)S(1)} collective-permute-done((bf16[576,256]{1,0:T(8,128)(2,1)S(1)}, bf16[576,256]{1,0:T(8,128)(2,1)S(1)}, u32[]{:S(2)}, u32[]{:S(2)}) %collective-permute-start.3) | collective-permute-done | bytes 294944 | tf_op jit(solution)/shard_map/ppermute | solution.py:22
  11.9 0.0 collective-permute-start.4
  11.9 0.1 pad_slice_fusion
  12.0 0.1 pad_add_fusion
  12.0 0.1 reshape.295.refs_0_
  12.1 0.1 pad.40.clone
  12.2 0.0 collective-permute-done.2.refs_1_
  12.2 0.4 targets_0.1
  12.6 0.9 %collective-permute-done.4.refs_1_ = bf16[576,256]{1,0:T(8,128)(2,1)S(1)} collective-permute-done((bf16[576,256]{1,0:T(8,128)(2,1)S(1)}, bf16[576,256]{1,0:T(8,128)(2,1)S(1)}, u32[]{:S(2)}, u32[]{:S(2)}) %collective-permute-start.4) | collective-permute-done | bytes 294944 | tf_op jit(solution)/shard_map/ppermute | solution.py:22
  13.5 0.4 targets_1.1
  13.9 0.0 collective-permute-done.1
  13.9 0.2 collective-permute-done
  14.1 3.4 %collective-permute-start.7 = (bf16[1104,128]{1,0:T(8,128)(2,1)S(1)}, bf16[1104,128]{1,0:T(8,128)(2,1)S(1)}, u32[]{:S(2)}, u32[]{:S(2)}) collective-permute-start(bf16[1104,128]{1,0:T(8,128)(2,1)S(1)} %pad_maximum_fusion.refs_1_), channel_id=1, source_target_pairs={{0,8},{8,12},{12,4},{4,0},{1,9},{9,13},{13,5},{5,1},{2,10},{10,14}... | collective-permute-start | bytes 847880 | tf_op jit(solution)/shard_map/ppermute | solution.py:32
  17.5 0.0 collective-permute-start.6
  17.5 0.8 %collective-permute-start.5 = (bf16[592,128]{1,0:T(8,128)(2,1)S(1)}, bf16[592,128]{1,0:T(8,128)(2,1)S(1)}, u32[]{:S(2)}, u32[]{:S(2)}) collective-permute-start(bf16[592,128]{1,0:T(8,128)(2,1)S(1)} %get-tuple-element.40), channel_id=1, source_target_pairs={{0,4},{8,0},{12,8},{4,12},{1,5},{9,1},{13,9},{5,13},{2,6},{10,2},{... | collective-permute-start | bytes 454664 | tf_op jit(solution)/shard_map/ppermute | solution.py:32
  18.4 5.8 %near_field_0.1 = (f32[16,80,512]{2,1,0:T(8,128)S(1)}, f32[3,16,128]{2,1,0:T(8,128)S(1)}) custom-call(s32[108]{0:T(128)S(1)} %reshape.295.refs_0_, bf16[1104,128]{1,0:T(8,128)(2,1)S(1)} %pad_maximum_fusion.refs_1_, bf16[16,256,128]{2,1,0:T(8,128)(2,1)S(1)} %get-tuple-element.43.refs_2_, bf16[16,256,128]{2,1,0:T(8,128)(2,1)S(1)} %get-tuple-element.44.refs_3_, ...), custom_call_target="tpu_custom_call" | custom-call | flops 692060160 | bytes 6291456 | tf_op jit(solution)/shard_map/near_field_0/pallas_call | solution.py:297
  24.2 0.6 collective-permute-done.7.refs_1_
  24.7 7.3 %near_field_1.1 = (f32[16,80,512]{2,1,0:T(8,128)S(1)}, f32[3,16,128]{2,1,0:T(8,128)S(1)}) custom-call(s32[108]{0:T(128)S(1)} %reshape.295.refs_0_, bf16[1104,128]{1,0:T(8,128)(2,1)S(1)} %collective-permute-done.7.refs_1_, bf16[16,256,128]{2,1,0:T(8,128)(2,1)S(1)} %get-tuple-element.43.refs_2_, bf16[16,256,128]{2,1,0:T(8,128)(2,1)S(1)} %get-tuple-element.44.refs_3_, ...), custom_call_target="tpu_custom_call" | custom-call | flops 692060160 | bytes 6291456 | tf_op jit(solution)/shard_map/near_field_1/pallas_call | solution.py:297
  32.1 0.0 collective-permute-done.6
  32.1 0.0 collective-permute-done.5
  32.1 7.1 %near_field_2.1 = (f32[16,32,512]{2,1,0:T(8,128)S(1)}, bf16[16,32,512]{2,1,0:T(8,128)(2,1)S(1)}, f32[3,16,512]{2,1,0:T(8,128)S(1)}, f32[3,16,128]{2,1,0:T(8,128)S(1)}) custom-call(s32[108]{0:T(128)S(1)} %reshape.295.refs_0_, bf16[1104,128]{1,0:T(8,128)(2,1)S(1)} %pad_maximum_fusion.1.refs_1_, bf16[16,256,128]{2,1,0:T(8,128)(2,1)S(1)} %get-tuple-element.43.refs_2_, ...), custom_call_target="tpu_custom_call" | custom-call | flops 692060160 | bytes 6291456 | tf_op jit(solution)/shard_map/near_field_2/pallas_call | solution.py:297
  39.3 0.1 copy.38
  39.4 0.1 maximum_maximum_fusion
  39.5 1.3 %collective-permute-start.10 = (f32[56,128]{1,0:T(8,128)S(1)}, f32[56,128]{1,0:T(8,128)S(1)}, u32[]{:S(2)}, u32[]{:S(2)}) collective-permute-start(f32[56,128]{1,0:T(8,128)S(1)} %get-tuple-element.89), channel_id=1, source_target_pairs={{0,4},{8,0},{12,8},{4,12},{1,5},{9,1},{13,9},{5,13},{2,6},{10,2},{... | collective-permute-start | bytes 86024 | tf_op jit(solution)/shard_map/ppermute | solution.py:32
  40.8 2.4 %collective-permute-start.11 = (f32[56,128]{1,0:T(8,128)S(1)}, f32[56,128]{1,0:T(8,128)S(1)}, u32[]{:S(2)}, u32[]{:S(2)}) collective-permute-start(f32[56,128]{1,0:T(8,128)S(1)} %get-tuple-element.90), channel_id=1, source_target_pairs={{0,12},{8,4},{12,0},{4,8},{1,13},{9,5},{13,1},{5,9},{2,14},{10,6},... | collective-permute-start | bytes 86024 | tf_op jit(solution)/shard_map/ppermute | solution.py:32
  43.2 1.0 %collective-permute-start.12 = (f32[56,128]{1,0:T(8,128)S(1)}, f32[56,128]{1,0:T(8,128)S(1)}, u32[]{:S(2)}, u32[]{:S(2)}) collective-permute-start(f32[56,128]{1,0:T(8,128)S(1)} %get-tuple-element.91), channel_id=1, source_target_pairs={{0,8},{8,12},{12,4},{4,0},{1,9},{9,13},{13,5},{5,1},{2,10},{10,14}... | collective-permute-start | bytes 86024 | tf_op jit(solution)/shard_map/ppermute | solution.py:32
  44.3 0.0 collective-permute-start.8
  44.3 0.0 collective-permute-done.10
  44.3 2.2 %collective-permute-done.11 = f32[56,128]{1,0:T(8,128)S(1)} collective-permute-done((f32[56,128]{1,0:T(8,128)S(1)}, f32[56,128]{1,0:T(8,128)S(1)}, u32[]{:S(2)}, u32[]{:S(2)}) %collective-permute-start.11) | collective-permute-done | bytes 28704 | tf_op jit(solution)/shard_map/ppermute | solution.py:32
  46.6 0.5 collective-permute-done.12
  47.2 0.0 collective-permute-done.8
  47.3 0.2 convert_add_fusion
  47.7 1.0 %collective-permute-start.13 = (f32[4,8,512]{2,1,0:T(8,128)S(1)}, f32[4,8,512]{2,1,0:T(8,128)S(1)}, u32[]{:S(2)}, u32[]{:S(2)}) collective-permute-start(f32[4,8,512]{2,1,0:T(8,128)S(1)} %fusion), channel_id=1, source_target_pairs={{0,2},{2,0},{1,3},{3,1},{4,6},{6,4},{5,7},{7,5},{8,10},{10,8},{9,1... | collective-permute-start | bytes 196616 | tf_op jit(solution)/shard_map/ppermute | solution.py:22
  48.7 1.2 %collective-permute-start.9 = (bf16[16,32,256]{2,1,0:T(8,128)(2,1)S(1)}, bf16[16,32,256]{2,1,0:T(8,128)(2,1)S(1)}, u32[]{:S(2)}, u32[]{:S(2)}) collective-permute-start(bf16[16,32,256]{2,1,0:T(8,128)(2,1)S(1)} %slice.307), channel_id=1, source_target_pairs={{0,2},{2,0},{1,3},{3,1},{4,6},{6,4},{5,7},{7,5},{8,10},{10,8},{9,1... | collective-permute-start | bytes 786440 | tf_op jit(solution)/shard_map/ppermute | solution.py:22
  49.9 2.9 %collective-permute-done.13 = f32[4,8,512]{2,1,0:T(8,128)S(1)} collective-permute-done((f32[4,8,512]{2,1,0:T(8,128)S(1)}, f32[4,8,512]{2,1,0:T(8,128)S(1)}, u32[]{:S(2)}, u32[]{:S(2)}) %collective-permute-start.13) | collective-permute-done | bytes 65568 | tf_op jit(solution)/shard_map/ppermute | solution.py:22
  52.8 0.1 collective-permute-start.14
  52.9 1.2 %collective-permute-done.14 = f32[4,8,512]{2,1,0:T(8,128)S(1)} collective-permute-done((f32[4,8,512]{2,1,0:T(8,128)S(1)}, f32[4,8,512]{2,1,0:T(8,128)S(1)}, u32[]{:S(2)}, u32[]{:S(2)}) %collective-permute-start.14) | collective-permute-done | bytes 65568 | tf_op jit(solution)/shard_map/ppermute | solution.py:22
  54.1 1.3 %node_terms.1 = f32[3,4096]{1,0:T(4,128)} custom-call(f32[3,8,512]{2,1,0:T(8,128)S(1)} %slice.197.grad_ref, s32[8,512]{1,0:T(8,128)S(1)} %slice_select_fusion.2.jitter_ref, f32[8,512]{1,0:T(8,128)S(1)} %slice_bitcast_fusion.edge_ref), custom_call_target="tpu_custom_call" | custom-call | flops 1048576 | bytes 262144 | tf_op jit(solution)/shard_map/node_terms/pallas_call | solution.py:576
  55.5 0.9 %collective-permute-done.9.refs_1_ = bf16[16,32,256]{2,1,0:T(8,128)(2,1)S(1)} collective-permute-done((bf16[16,32,256]{2,1,0:T(8,128)(2,1)S(1)}, bf16[16,32,256]{2,1,0:T(8,128)(2,1)S(1)}, u32[]{:S(2)}, u32[]{:S(2)}) %collective-permute-start.9) | collective-permute-done | bytes 262176 | tf_op jit(solution)/shard_map/ppermute | solution.py:22
  56.4 0.7 %potential_sum.1 = bf16[16,32,256]{2,1,0:T(8,128)(2,1)} custom-call(f32[16,32,256]{2,1,0:T(8,128)S(1)} %slice.127.refs_0_, bf16[16,32,256]{2,1,0:T(8,128)(2,1)S(1)} %collective-permute-done.9.refs_1_), custom_call_target="tpu_custom_call" | custom-call | flops 1048576 | bytes 262144 | tf_op jit(solution)/shard_map/potential_sum/pallas_call | solution.py:585
  (47 shorter events, 0.6 us)
Async XLA Ops:
  0.6 8.5 %copy-start = (s32[5,64]{1,0:T(8,128)S(1)}, s32[5,64]{1,0:T(8,128)}, u32[]{:S(2)}) copy-start(s32[5,64]{1,0:T(8,128)} %param.10) | copy-start | bytes 3844
  1.9 10.0 %collective-permute-start.3 = (bf16[576,256]{1,0:T(8,128)(2,1)S(1)}, bf16[576,256]{1,0:T(8,128)(2,1)S(1)}, u32[]{:S(2)}, u32[]{:S(2)}) collective-permute-start(bf16[576,256]{1,0:T(8,128)(2,1)S(1)} %get-tuple-element.33.refs_0_.refs_7_), channel_id=1, source_target_pairs={{0,2},{2,0},{1,3},{3,1},{4,6},{6,4},{5,7},{7,5},{8,10},{10,8},{9,1... | collective-permute-start | bytes 884744 | tf_op jit(solution)/shard_map/ppermute | solution.py:22
  4.9 7.3 %collective-permute-start.2 = (bf16[576,256]{1,0:T(8,128)(2,1)S(1)}, bf16[576,256]{1,0:T(8,128)(2,1)S(1)}, u32[]{:S(2)}, u32[]{:S(2)}) collective-permute-start(bf16[576,256]{1,0:T(8,128)(2,1)S(1)} %get-tuple-element.33.refs_0_.refs_7_), channel_id=1, source_target_pairs={{0,1},{1,0},{2,3},{3,2},{4,5},{5,4},{6,7},{7,6},{8,9},{9,8},{10,11... | collective-permute-start | bytes 884744 | tf_op jit(solution)/shard_map/ppermute | solution.py:22
  4.9 9.0 %collective-permute-start.1 = (bf16[512,128]{1,0:T(8,128)(2,1)S(1)}, bf16[512,128]{1,0:T(8,128)(2,1)S(1)}, u32[]{:S(2)}, u32[]{:S(2)}) collective-permute-start(bf16[512,128]{1,0:T(8,128)(2,1)S(1)} %get-tuple-element.41), channel_id=1, source_target_pairs={{0,9},{1,8},{4,1},{5,0},{8,13},{9,12},{12,5},{13,4},{2,11},{3,10},... | collective-permute-start | bytes 393224 | tf_op jit(solution)/shard_map/ppermute | solution.py:44
  7.6 6.5 %collective-permute-start = (bf16[592,128]{1,0:T(8,128)(2,1)S(1)}, bf16[592,128]{1,0:T(8,128)(2,1)S(1)}, u32[]{:S(2)}, u32[]{:S(2)}) collective-permute-start(bf16[592,128]{1,0:T(8,128)(2,1)S(1)} %get-tuple-element.40), channel_id=1, source_target_pairs={{0,8},{8,12},{12,4},{4,0},{1,9},{9,13},{13,5},{5,1},{2,10},{10,14}... | collective-permute-start | bytes 454664 | tf_op jit(solution)/shard_map/ppermute | solution.py:32
  11.9 1.6 %collective-permute-start.4 = (bf16[576,256]{1,0:T(8,128)(2,1)S(1)}, bf16[576,256]{1,0:T(8,128)(2,1)S(1)}, u32[]{:S(2)}, u32[]{:S(2)}) collective-permute-start(bf16[576,256]{1,0:T(8,128)(2,1)S(1)} %collective-permute-done.3.refs_0_.refs_8_), channel_id=1, source_target_pairs={{0,1},{1,0},{2,3},{3,2},{4,5},{5,4},{6,7},{7,6},{8,9},{9,8},{10,11... | collective-permute-start | bytes 884744 | tf_op jit(solution)/shard_map/ppermute | solution.py:22
  14.1 10.7 %collective-permute-start.7 = (bf16[1104,128]{1,0:T(8,128)(2,1)S(1)}, bf16[1104,128]{1,0:T(8,128)(2,1)S(1)}, u32[]{:S(2)}, u32[]{:S(2)}) collective-permute-start(bf16[1104,128]{1,0:T(8,128)(2,1)S(1)} %pad_maximum_fusion.refs_1_), channel_id=1, source_target_pairs={{0,8},{8,12},{12,4},{4,0},{1,9},{9,13},{13,5},{5,1},{2,10},{10,14}... | collective-permute-start | bytes 847880 | tf_op jit(solution)/shard_map/ppermute | solution.py:32
  17.5 14.6 %collective-permute-start.6 = (bf16[512,128]{1,0:T(8,128)(2,1)S(1)}, bf16[512,128]{1,0:T(8,128)(2,1)S(1)}, u32[]{:S(2)}, u32[]{:S(2)}) collective-permute-start(bf16[512,128]{1,0:T(8,128)(2,1)S(1)} %get-tuple-element.41), channel_id=1, source_target_pairs={{0,5},{1,4},{4,13},{5,12},{8,1},{9,0},{12,9},{13,8},{2,7},{3,6},{6... | collective-permute-start | bytes 393224 | tf_op jit(solution)/shard_map/ppermute | solution.py:44
  17.5 14.6 %collective-permute-start.5 = (bf16[592,128]{1,0:T(8,128)(2,1)S(1)}, bf16[592,128]{1,0:T(8,128)(2,1)S(1)}, u32[]{:S(2)}, u32[]{:S(2)}) collective-permute-start(bf16[592,128]{1,0:T(8,128)(2,1)S(1)} %get-tuple-element.40), channel_id=1, source_target_pairs={{0,4},{8,0},{12,8},{4,12},{1,5},{9,1},{13,9},{5,13},{2,6},{10,2},{... | collective-permute-start | bytes 454664 | tf_op jit(solution)/shard_map/ppermute | solution.py:32
  39.5 4.8 %collective-permute-start.10 = (f32[56,128]{1,0:T(8,128)S(1)}, f32[56,128]{1,0:T(8,128)S(1)}, u32[]{:S(2)}, u32[]{:S(2)}) collective-permute-start(f32[56,128]{1,0:T(8,128)S(1)} %get-tuple-element.89), channel_id=1, source_target_pairs={{0,4},{8,0},{12,8},{4,12},{1,5},{9,1},{13,9},{5,13},{2,6},{10,2},{... | collective-permute-start | bytes 86024 | tf_op jit(solution)/shard_map/ppermute | solution.py:32
  40.8 5.8 %collective-permute-start.11 = (f32[56,128]{1,0:T(8,128)S(1)}, f32[56,128]{1,0:T(8,128)S(1)}, u32[]{:S(2)}, u32[]{:S(2)}) collective-permute-start(f32[56,128]{1,0:T(8,128)S(1)} %get-tuple-element.90), channel_id=1, source_target_pairs={{0,12},{8,4},{12,0},{4,8},{1,13},{9,5},{13,1},{5,9},{2,14},{10,6},... | collective-permute-start | bytes 86024 | tf_op jit(solution)/shard_map/ppermute | solution.py:32
  43.2 3.9 %collective-permute-start.12 = (f32[56,128]{1,0:T(8,128)S(1)}, f32[56,128]{1,0:T(8,128)S(1)}, u32[]{:S(2)}, u32[]{:S(2)}) collective-permute-start(f32[56,128]{1,0:T(8,128)S(1)} %get-tuple-element.91), channel_id=1, source_target_pairs={{0,8},{8,12},{12,4},{4,0},{1,9},{9,13},{13,5},{5,1},{2,10},{10,14}... | collective-permute-start | bytes 86024 | tf_op jit(solution)/shard_map/ppermute | solution.py:32
  44.3 3.0 %collective-permute-start.8 = (bf16[16,32,512]{2,1,0:T(8,128)(2,1)S(1)}, bf16[16,32,512]{2,1,0:T(8,128)(2,1)S(1)}, u32[]{:S(2)}, u32[]{:S(2)}) collective-permute-start(bf16[16,32,512]{2,1,0:T(8,128)(2,1)S(1)} %get-tuple-element.53), channel_id=1, source_target_pairs={{0,1},{1,0},{2,3},{3,2},{4,5},{5,4},{6,7},{7,6},{8,9},{9,8},{10,11... | collective-permute-start | bytes 1572872 | tf_op jit(solution)/shard_map/ppermute | solution.py:22
  47.7 5.1 %collective-permute-start.13 = (f32[4,8,512]{2,1,0:T(8,128)S(1)}, f32[4,8,512]{2,1,0:T(8,128)S(1)}, u32[]{:S(2)}, u32[]{:S(2)}) collective-permute-start(f32[4,8,512]{2,1,0:T(8,128)S(1)} %fusion), channel_id=1, source_target_pairs={{0,2},{2,0},{1,3},{3,1},{4,6},{6,4},{5,7},{7,5},{8,10},{10,8},{9,1... | collective-permute-start | bytes 196616 | tf_op jit(solution)/shard_map/ppermute | solution.py:22
  48.7 7.7 %collective-permute-start.9 = (bf16[16,32,256]{2,1,0:T(8,128)(2,1)S(1)}, bf16[16,32,256]{2,1,0:T(8,128)(2,1)S(1)}, u32[]{:S(2)}, u32[]{:S(2)}) collective-permute-start(bf16[16,32,256]{2,1,0:T(8,128)(2,1)S(1)} %slice.307), channel_id=1, source_target_pairs={{0,2},{2,0},{1,3},{3,1},{4,6},{6,4},{5,7},{7,5},{8,10},{10,8},{9,1... | collective-permute-start | bytes 786440 | tf_op jit(solution)/shard_map/ppermute | solution.py:22
  52.8 1.3 %collective-permute-start.14 = (f32[4,8,512]{2,1,0:T(8,128)S(1)}, f32[4,8,512]{2,1,0:T(8,128)S(1)}, u32[]{:S(2)}, u32[]{:S(2)}) collective-permute-start(f32[4,8,512]{2,1,0:T(8,128)S(1)} %select_add_fusion), channel_id=1, source_target_pairs={{0,1},{1,0},{2,3},{3,2},{4,5},{5,4},{6,7},{7,6},{8,9},{9,8},{10,11... | collective-permute-start | bytes 196616 | tf_op jit(solution)/shard_map/ppermute | solution.py:22
